TPU v7x, 32 devices: a whole 2x2x4 slice. The times are simulated.
32 devices in a mesh: frames: 8 (over z, y), chan: 4 (over x, core).
Axes of the slice: x: 2, y: 2, z: 4, core: 2. Of those that a mesh axis runs over, the one named last changes fastest.
Arguments:
- signal: float32 [512, 32768], P('chan', 'frames'), may hold values from -6 to 6
- dilated_dirs: bfloat16 [3, 7, 512, 512], P(None, None, 'chan'), may hold values from -0.09375 to 0.09375
- dilated_gains: float32 [3, 512], P(None, 'chan'), may hold values from 0.3 to 0.9
- dilated_bias: float32 [3, 512], P(None, 'chan'), may hold values from -1 to 1
- snake_first: float32 [3, 512], P(None, 'chan'), may hold values from 0.3 to 1.2
- snake_second: float32 [3, 512], P(None, 'chan'), may hold values from 0.3 to 1.2
- pointwise_dirs: bfloat16 [3, 512, 512], P(None, 'chan'), may hold values from -0.25 to 0.25
- pointwise_gains: float32 [3, 512], P(None, 'chan'), may hold values from 0.3 to 0.9
- pointwise_bias: float32 [3, 512], P(None, 'chan'), may hold values from -1 to 1
- snake_last: float32 [512], P('chan'), may hold values from 0.3 to 1.2
- strided_dirs: bfloat16 [16, 1024, 512], P(None, 'chan'), may hold values from -0.0625 to 0.0625
- strided_gains: float32 [1024], P('chan'), may hold values from 0.3 to 0.9
- strided_bias: float32 [1024], P('chan'), may hold values from -1 to 1
- latent_proj: bfloat16 [8, 1024], P(None, 'chan'), may hold values from -0.1875 to 0.1875
- latent_bias: float32 [8], replicated, may hold values from -3 to 3
- codebook: float32 [8, 8192], replicated, may hold values from -6 to 6
- output_proj: bfloat16 [1024, 8], P('chan'), may hold values from -2 to 2
- output_bias: float32 [1024], P('chan'), may hold values from -3 to 3
- utterances: int32 [10], replicated, may hold values from 1 to 800, 4096 in all
- code_index: int32 [4096], P('frames'), may hold values from 0 to 8191
- refill_index: int32 [8192], replicated, may hold values from 0 to 4095
- cotangent: bfloat16 [1024, 4096], P('chan', 'frames'), may hold values from -6 to 6
Outputs:
- output: float32 [1024, 4096], P('chan', 'frames')
- grad_signal: float32 [512, 32768], P('chan', 'frames')
- grad_dilated_dirs: float32 [3, 7, 512, 512], P(None, None, 'chan')
- grad_dilated_gains: float32 [3, 512], P(None, 'chan')
- grad_dilated_bias: float32 [3, 512], P(None, 'chan')
- grad_snake_first: float32 [3, 512], P(None, 'chan')
- grad_snake_second: float32 [3, 512], P(None, 'chan')
- grad_pointwise_dirs: float32 [3, 512, 512], P(None, 'chan')
- grad_pointwise_gains: float32 [3, 512], P(None, 'chan')
- grad_pointwise_bias: float32 [3, 512], P(None, 'chan')
- grad_snake_last: float32 [512], P('chan')
- grad_strided_dirs: float32 [16, 1024, 512], P(None, 'chan')
- grad_strided_gains: float32 [1024], P('chan')
- grad_strided_bias: float32 [1024], P('chan')
- grad_latent_proj: float32 [8, 1024], P(None, 'chan')
- grad_latent_bias: float32 [8], replicated
- grad_codebook: float32 [8, 8192], replicated
- grad_output_proj: float32 [1024, 8], P('chan')
- grad_output_bias: float32 [1024], P('chan')
- refreshed: float32 [8, 8192], replicated
All inputs are finite; a program needn't handle non-finite values.
Results may differ from a plain program's by a relative error of at most 0.019.
Values may be sent and summed in bfloat16 or wider, within the bound.
No kernel may reach another device: no remote copies, remote signals or barrier semaphores. Data moves between devices by JAX's collectives and lax.ppermute only.
A program may use at most 256 MiB of HBM per device.

v0:
```python
import jax
import jax.numpy as jnp
from jax import lax
from jax.sharding import PartitionSpec as P

CODES = 8192
STRIDE = 8


norm_eps = 1e-06
commit_weight = 4.0


def with_halo(cells, sides, width):
    for axis, dim in sides:
        count = lax.axis_size(axis)
        ends = count - 1
        head = lax.slice_in_dim(cells, 0, width, axis=dim)
        tail = lax.slice_in_dim(cells, cells.shape[dim] - width, cells.shape[dim], axis=dim)
        cells = jnp.concatenate(
            [
                lax.ppermute(tail, axis, [(i, (i + 1) % count) for i in range(ends)]),
                cells,
                lax.ppermute(head, axis, [((i + 1) % count, i) for i in range(ends)]),
            ],
            axis=dim,
        )
    return cells


def snake_act(value, alpha):
    return value + jnp.sin(alpha[:, None] * value) ** 2 / alpha[:, None]


def snake_back(value, alpha, grad):
    result, pull = jax.vjp(snake_act, value, alpha)
    return pull(grad)


def taps_norm(direction, gain):
    return (
        direction
        * (gain * lax.rsqrt(jnp.sum(direction * direction, axis=(0, 2)) + norm_eps))[None, :, None]
    )


def rows_norm(direction, gain):
    return (
        direction * (gain * lax.rsqrt(jnp.sum(direction * direction, axis=1) + norm_eps))[:, None]
    )


def norm_back(normer, direction, gain, grad):
    result, pull = jax.vjp(normer, direction.astype(jnp.float32), gain)
    return pull(grad)


def unit_scale(value):
    return value * lax.rsqrt(jnp.sum(value * value, axis=0) + 1.0)[None, :]


def place_labels(bounds, first, count, whole):
    spots = first + jnp.arange(count, dtype=jnp.int32)
    found = jnp.sum((spots[:, None] >= bounds[None, :]).astype(jnp.int32), axis=1)
    return jnp.where((spots >= 0) & (spots < whole), found, -1)


def contract_rows(left, right):
    return lax.dot_general(
        left, right, (((1,), (1,)), ((), ())), preferred_element_type=jnp.float32
    )


def contract_cols(left, right):
    return lax.dot_general(
        left, right, (((0,), (0,)), ((), ())), preferred_element_type=jnp.float32
    )


def with_edges(active, margin):
    return with_halo(active, (("frames", 1),), margin)


def all_channels(active):
    return lax.all_gather(active, "chan", axis=0, tiled=True)


def to_owner(grad_full):
    return lax.psum_scatter(
        grad_full.astype(jnp.bfloat16), "chan", scatter_dimension=0, tiled=True
    ).astype(jnp.float32)


def unit_owner(grad_full):
    return lax.psum_scatter(
        grad_full.astype(jnp.bfloat16), "chan", scatter_dimension=0, tiled=True
    ).astype(jnp.float32)


def give_back(grad_ext, margin):
    extent = grad_ext.shape[1] - 2 * margin
    between = jnp.zeros((grad_ext.shape[0], extent - 2 * margin), jnp.float32)
    rims = jnp.concatenate([grad_ext[:, :margin], between, grad_ext[:, -margin:]], axis=1)
    returned = with_halo(rims.astype(jnp.bfloat16), (("frames", 1),), margin).astype(rims.dtype)
    extra = jnp.concatenate([returned[:, :margin], between, returned[:, -margin:]], axis=1)
    return grad_ext[:, margin : margin + extent] + extra


def dilated_conv(wide, weight, masks, spacing, extent):
    result = jnp.zeros((weight.shape[1], extent), jnp.float32)
    for kernel_tap in range(weight.shape[0]):
        start = kernel_tap * spacing
        columns = wide[:, start : start + extent] * masks[kernel_tap].astype(jnp.bfloat16)[None, :]
        result = result + jnp.dot(weight[kernel_tap], columns, preferred_element_type=jnp.float32)
    return result


def dilated_back(wide, masks, spacing, extent, grad_low, back_weight, back_grad):
    pieces = []
    back = jnp.zeros((back_weight.shape[2], wide.shape[1]), jnp.float32)
    for kernel_tap in range(back_weight.shape[0]):
        start = kernel_tap * spacing
        columns = wide[:, start : start + extent] * masks[kernel_tap].astype(jnp.bfloat16)[None, :]
        pieces.append(contract_rows(grad_low, columns))
        spread = (
            contract_cols(back_weight[kernel_tap], back_grad)
            * masks[kernel_tap].astype(jnp.float32)[None, :]
        )
        back = back.at[:, start : start + extent].add(spread)
    return (jnp.stack(pieces), back)


def strided_conv(wide, weight, masks, frames):
    stride = weight.shape[0] // 2
    result = jnp.zeros((weight.shape[1], frames), jnp.float32)
    for kernel_tap in range(weight.shape[0]):
        columns = (
            wide[:, kernel_tap : kernel_tap + stride * frames : stride]
            * masks[kernel_tap].astype(jnp.bfloat16)[None, :]
        )
        result = result + jnp.dot(weight[kernel_tap], columns, preferred_element_type=jnp.float32)
    return result


def strided_back(wide, weight, masks, frames, grad_low):
    stride = weight.shape[0] // 2
    pieces = []
    back = jnp.zeros(wide.shape, jnp.float32)
    for kernel_tap in range(weight.shape[0]):
        columns = (
            wide[:, kernel_tap : kernel_tap + stride * frames : stride]
            * masks[kernel_tap].astype(jnp.bfloat16)[None, :]
        )
        pieces.append(contract_rows(grad_low, columns))
        spread = (
            contract_cols(weight[kernel_tap], grad_low)
            * masks[kernel_tap].astype(jnp.float32)[None, :]
        )
        back = back.at[:, kernel_tap : kernel_tap + stride * frames : stride].add(spread)
    return (jnp.stack(pieces), back)


def local(
    signal,
    dilated_dirs,
    dilated_gains,
    dilated_bias,
    snake_first,
    snake_second,
    pointwise_dirs,
    pointwise_gains,
    pointwise_bias,
    snake_last,
    strided_dirs,
    strided_gains,
    strided_bias,
    latent_proj,
    latent_bias,
    codebook,
    output_proj,
    output_bias,
    utterances,
    code_index,
    refill_index,
    cotangent,
):
    extent = signal.shape[1]
    frames = code_index.shape[0]
    stride = STRIDE
    half = stride // 2
    whole = lax.axis_size("frames") * extent
    anchor = lax.axis_index("frames") * extent
    bounds = jnp.cumsum(utterances) * stride
    units = dilated_dirs.shape[0]
    stream = signal
    saved = []
    for member in range(units):
        spacing = 3**member
        margin = dilated_dirs.shape[1] // 2 * spacing
        labels = place_labels(bounds, anchor - margin, extent + 2 * margin, whole)
        centre = labels[margin : margin + extent]
        masks = [
            labels[kernel_tap * spacing : kernel_tap * spacing + extent] == centre
            for kernel_tap in range(dilated_dirs.shape[1])
        ]
        weight7 = taps_norm(dilated_dirs[member].astype(jnp.float32), dilated_gains[member]).astype(
            jnp.bfloat16
        )
        weight1 = rows_norm(
            pointwise_dirs[member].astype(jnp.float32), pointwise_gains[member]
        ).astype(jnp.bfloat16)
        wide = all_channels(
            with_edges(snake_act(stream, snake_first[member]).astype(jnp.bfloat16), margin)
        )
        middle = dilated_conv(wide, weight7, masks, spacing, extent) + dilated_bias[member][:, None]
        second = all_channels(snake_act(middle, snake_second[member]).astype(jnp.bfloat16))
        saved.append((stream, middle, wide, second, masks, weight7, weight1, spacing, margin))
        stream = (
            stream
            + jnp.dot(weight1, second, preferred_element_type=jnp.float32)
            + pointwise_bias[member][:, None]
        )
    labels3 = place_labels(bounds, anchor - half, extent + 2 * half, whole)
    centre3 = labels3[half : half + stride * frames : stride]
    masks3 = [
        labels3[kernel_tap : kernel_tap + stride * frames : stride] == centre3
        for kernel_tap in range(strided_dirs.shape[0])
    ]
    weights = taps_norm(strided_dirs.astype(jnp.float32), strided_gains).astype(jnp.bfloat16)
    wide_last = all_channels(with_edges(snake_act(stream, snake_last).astype(jnp.bfloat16), half))
    hidden = strided_conv(wide_last, weights, masks3, frames) + strided_bias[:, None]
    latent_terms = jnp.dot(
        latent_proj.astype(jnp.float32),
        hidden,
        precision=lax.Precision.HIGHEST,
        preferred_element_type=jnp.float32,
    )
    latent = lax.psum(latent_terms, "chan") + latent_bias[:, None]
    normed, latent_pull = jax.vjp(unit_scale, latent)
    coded, code_pull = jax.vjp(unit_scale, codebook)
    chosen = jnp.take(coded, code_index, axis=1)
    chosen_low = chosen.astype(jnp.bfloat16)
    output = (
        jnp.dot(output_proj, chosen_low, preferred_element_type=jnp.float32) + output_bias[:, None]
    )
    offsets = refill_index - lax.axis_index("frames") * frames
    inside = ((offsets >= 0) & (offsets < frames)).astype(jnp.float32)
    picked = jnp.take(latent, jnp.clip(offsets, 0, frames - 1), axis=1) * inside[None, :]
    usage = jax.ops.segment_sum(jnp.ones((frames,), jnp.float32), code_index, num_segments=CODES)
    usage, picked = (
        lax.psum(usage.astype(jnp.bfloat16), "frames").astype(jnp.float32),
        lax.psum(picked.astype(jnp.bfloat16), "frames").astype(jnp.float32),
    )
    refreshed = jnp.where(usage[None, :] > 0, codebook, picked)
    dchosen = lax.psum(contract_cols(output_proj, cotangent), "chan")
    spread_diff = 2.0 * commit_weight * (normed - chosen)
    dchosen = dchosen - spread_diff
    (dlatent,) = latent_pull(spread_diff)
    dcoded = jax.ops.segment_sum(dchosen.T, code_index, num_segments=CODES).T
    dproj_out = contract_rows(cotangent, chosen_low)
    dbias_out = jnp.sum(cotangent.astype(jnp.float32), axis=1)
    dbias_latent = jnp.sum(dlatent, axis=1)
    dproj_latent = lax.dot_general(
        dlatent,
        hidden,
        (((1,), (1,)), ((), ())),
        precision=lax.Precision.HIGHEST,
        preferred_element_type=jnp.float32,
    )
    dhidden = lax.dot_general(
        latent_proj.astype(jnp.float32),
        dlatent,
        (((0,), (0,)), ((), ())),
        precision=lax.Precision.HIGHEST,
        preferred_element_type=jnp.float32,
    )
    dbias_strided = jnp.sum(dhidden, axis=1)
    dweights, dwide_last = strided_back(
        wide_last, weights, masks3, frames, dhidden.astype(jnp.bfloat16)
    )
    dactive3 = give_back(to_owner(dwide_last), half)
    grad, dalpha_last = snake_back(stream, snake_last, dactive3)
    unit_sums = [None] * units
    for member in reversed(range(units)):
        stream_in, middle, wide, second, masks, weight7, weight1, spacing, margin = saved[member]
        dbias1 = jnp.sum(grad, axis=1)
        grad_low = grad.astype(jnp.bfloat16)
        dweight1 = contract_rows(grad_low, second)
        dsecond = unit_owner(contract_cols(weight1, grad_low))
        dmiddle, dalpha2 = snake_back(middle, snake_second[member], dsecond)
        dbias7 = jnp.sum(dmiddle, axis=1)
        dmiddle_low = dmiddle.astype(jnp.bfloat16)
        dweight7, dwide = dilated_back(
            wide, masks, spacing, extent, dmiddle_low, weight7, dmiddle_low
        )
        dactive = give_back(unit_owner(dwide), margin)
        dstream_in, dalpha1 = snake_back(stream_in, snake_first[member], dactive)
        grad = grad + dstream_in
        unit_sums[member] = (
            lax.psum(dweight7.astype(jnp.bfloat16), "frames").astype(jnp.float32),
            lax.psum(dweight1.astype(jnp.bfloat16), "frames").astype(jnp.float32),
            lax.psum(dbias7.astype(jnp.bfloat16), "frames").astype(jnp.float32),
            lax.psum(dbias1.astype(jnp.bfloat16), "frames").astype(jnp.float32),
            lax.psum(dalpha1.astype(jnp.bfloat16), "frames").astype(jnp.float32),
            lax.psum(dalpha2.astype(jnp.bfloat16), "frames").astype(jnp.float32),
        )
    stacked = [
        jnp.stack([unit_sums[member][entry] for member in range(units)]) for entry in range(6)
    ]
    tail = (
        lax.psum(dweights.astype(jnp.bfloat16), "frames").astype(jnp.float32),
        lax.psum(dbias_strided.astype(jnp.bfloat16), "frames").astype(jnp.float32),
        lax.psum(dalpha_last.astype(jnp.bfloat16), "frames").astype(jnp.float32),
        lax.psum(dproj_latent.astype(jnp.bfloat16), "frames").astype(jnp.float32),
        lax.psum(dbias_latent.astype(jnp.bfloat16), "frames").astype(jnp.float32),
        lax.psum(dproj_out.astype(jnp.bfloat16), "frames").astype(jnp.float32),
        lax.psum(dbias_out.astype(jnp.bfloat16), "frames").astype(jnp.float32),
        lax.psum(dcoded.astype(jnp.bfloat16), "frames").astype(jnp.float32),
    )
    dweight7s, dweight1s, dbias7s, dbias1s, dalpha1s, dalpha2s = stacked
    (
        dweights,
        dbias_strided,
        dalpha_last,
        dproj_latent,
        dbias_latent,
        dproj_out,
        dbias_out,
        dcoded,
    ) = tail
    dirs7 = []
    gains7 = []
    dirs1 = []
    gains1 = []
    for member in range(units):
        dir_grad, gain_grad = norm_back(
            taps_norm, dilated_dirs[member], dilated_gains[member], dweight7s[member]
        )
        dirs7.append(dir_grad)
        gains7.append(gain_grad)
        dir_grad, gain_grad = norm_back(
            rows_norm, pointwise_dirs[member], pointwise_gains[member], dweight1s[member]
        )
        dirs1.append(dir_grad)
        gains1.append(gain_grad)
    dstrided_dirs, dstrided_gains = norm_back(taps_norm, strided_dirs, strided_gains, dweights)
    (dcodebook,) = code_pull(dcoded)
    return (
        output,
        grad,
        jnp.stack(dirs7),
        jnp.stack(gains7),
        dbias7s,
        dalpha1s,
        dalpha2s,
        jnp.stack(dirs1),
        jnp.stack(gains1),
        dbias1s,
        dalpha_last,
        dstrided_dirs,
        dstrided_gains,
        dbias_strided,
        dproj_latent,
        dbias_latent,
        dcodebook,
        dproj_out,
        dbias_out,
        refreshed,
    )


def solution(mesh):
    in_specs = (
        P("chan", "frames"),
        P(None, None, "chan", None),
        P(None, "chan"),
        P(None, "chan"),
        P(None, "chan"),
        P(None, "chan"),
        P(None, "chan", None),
        P(None, "chan"),
        P(None, "chan"),
        P("chan"),
        P(None, "chan", None),
        P("chan"),
        P("chan"),
        P(None, "chan"),
        P(),
        P(),
        P("chan", None),
        P("chan"),
        P(),
        P("frames"),
        P(),
        P("chan", "frames"),
    )
    out_specs = (
        P("chan", "frames"),
        P("chan", "frames"),
        P(None, None, "chan", None),
        P(None, "chan"),
        P(None, "chan"),
        P(None, "chan"),
        P(None, "chan"),
        P(None, "chan", None),
        P(None, "chan"),
        P(None, "chan"),
        P("chan"),
        P(None, "chan", None),
        P("chan"),
        P("chan"),
        P(None, "chan"),
        P(),
        P(),
        P("chan", None),
        P("chan"),
        P(),
    )
    return jax.shard_map(local, mesh=mesh, in_specs=in_specs, out_specs=out_specs, check_vma=False)
```

profile of v0, /device:TPU:0, one launch (start us, length us, event | category | flops | bytes accessed | tf_op | source)
XLA Modules:
  0.0 2604.4 jit_solution(393344105747571610)
XLA Ops:
  37.0 31.4 %all-gather.8.cloned.1.call-done = bf16[512,4102]{1,0:T(8,128)(2,1)} async-done(((bf16[128,4102]{1,0:T(8,128)(2,1)}), bf16[512,4102]{1,0:T(8,128)(2,1)}) %all-gather.8.cloned.1.call-update) | async-done | bytes 4200464 | tf_op jit(solution)/shard_map/all_gather | solution.py:85
  91.3 34.3 %all-gather.10.cloned.1.call-done = bf16[512,4096]{1,0:T(8,128)(2,1)} async-done(((bf16[128,4096]{1,0:T(8,128)(2,1)}), bf16[512,4096]{1,0:T(8,128)(2,1)}) %all-gather.10.cloned.1.call-update) | async-done | bytes 4194320 | tf_op jit(solution)/shard_map/all_gather | solution.py:85
  151.2 34.1 %all-gather.12.cloned.1.call-done = bf16[512,4114]{1,0:T(8,128)(2,1)} async-done(((bf16[128,4114]{1,0:T(8,128)(2,1)}), bf16[512,4114]{1,0:T(8,128)(2,1)}) %all-gather.12.cloned.1.call-update) | async-done | bytes 4212752 | tf_op jit(solution)/shard_map/all_gather | solution.py:85
  208.2 34.6 %all-gather.14.cloned.1.call-done = bf16[512,4096]{1,0:T(8,128)(2,1)} async-done(((bf16[128,4096]{1,0:T(8,128)(2,1)}), bf16[512,4096]{1,0:T(8,128)(2,1)}) %all-gather.14.cloned.1.call-update) | async-done | bytes 4194320 | tf_op jit(solution)/shard_map/all_gather | solution.py:85
  266.3 34.1 %all-gather.16.cloned.1.call-done = bf16[512,4150]{1,0:T(8,128)(2,1)} async-done(((bf16[128,4150]{1,0:T(8,128)(2,1)}), bf16[512,4150]{1,0:T(8,128)(2,1)}) %all-gather.16.cloned.1.call-update) | async-done | bytes 4249616 | tf_op jit(solution)/shard_map/all_gather | solution.py:85
  323.0 34.6 %all-gather.18.cloned.1.call-done = bf16[512,4096]{1,0:T(8,128)(2,1)} async-done(((bf16[128,4096]{1,0:T(8,128)(2,1)}), bf16[512,4096]{1,0:T(8,128)(2,1)}) %all-gather.18.cloned.1.call-update) | async-done | bytes 4194320 | tf_op jit(solution)/shard_map/all_gather | solution.py:85
  400.1 15.2 all-gather.20.cloned.1.call-done
  415.3 21.0 slice.1103
  438.4 21.0 slice.1114
  461.0 21.0 slice.1099
  483.5 21.2 slice.1106
  506.2 21.0 slice.1109
  529.3 21.0 slice.1112
  551.8 21.0 slice.1117
  574.3 21.1 slice.1120
  597.5 21.0 slice.1123
  620.0 21.5 slice.1126
  643.6 21.1 slice.1129
  666.9 21.1 slice.1132
  690.1 21.1 slice.1135
  713.3 21.1 slice.1138
  735.9 21.3 slice.1141
  758.7 21.0 slice.1144
  1034.6 46.5 %reduce-scatter.22.cloned.1.call-done = bf16[128,4104]{1,0:T(8,128)(2,1)} async-done(((bf16[512,4104]{1,0:T(8,128)(2,1)}), bf16[128,4104]{1,0:T(8,128)(2,1)}) %reduce-scatter.22.cloned.1.call-update) | async-done | bytes 1050640 | tf_op jit(solution)/shard_map/reduce_scatter | solution.py:89
  1114.8 40.1 %reduce-scatter.24.cloned.1.call-done = bf16[128,4096]{1,0:T(8,128)(2,1)} async-done(((bf16[512,4096]{1,0:T(8,128)(2,1)}), bf16[128,4096]{1,0:T(8,128)(2,1)}) %reduce-scatter.24.cloned.1.call-update) | async-done | bytes 1048592 | tf_op jit(solution)/shard_map/reduce_scatter | solution.py:95
  1179.0 43.2 %scatter-add.248 = f32[512,4150]{1,0:T(8,128)} dynamic-update-slice(f32[512,4150]{1,0:T(8,128)} %scatter-add.247, f32[512,4096]{1,0:T(8,128)} %add_select_fusion.14, s32[]{:T(128)} %constant.605.clone.1, s32[]{:T(128)} %constant.631.clone.1) | dynamic-update-slice | bytes 16777220 | tf_op jit(solution)/shard_map/scatter-add | solution.py:129
  1232.0 43.2 %scatter-add.249 = f32[512,4150]{1,0:T(8,128)} dynamic-update-slice(f32[512,4150]{1,0:T(8,128)} %scatter-add.248, f32[512,4096]{1,0:T(8,128)} %add_select_fusion.13, s32[]{:T(128)} %constant.605.clone.1, s32[]{:T(128)} %constant.642.clone.1) | dynamic-update-slice | bytes 16777220 | tf_op jit(solution)/shard_map/scatter-add | solution.py:129
  1285.2 43.6 %scatter-add.250 = f32[512,4150]{1,0:T(8,128)} dynamic-update-slice(f32[512,4150]{1,0:T(8,128)} %scatter-add.249, f32[512,4096]{1,0:T(8,128)} %add_select_fusion.12, s32[]{:T(128)} %constant.605.clone.1, s32[]{:T(128)} %constant.643.clone.1) | dynamic-update-slice | bytes 16777220 | tf_op jit(solution)/shard_map/scatter-add | solution.py:129
  1338.7 43.2 %scatter-add.251 = f32[512,4150]{1,0:T(8,128)} dynamic-update-slice(f32[512,4150]{1,0:T(8,128)} %scatter-add.250, f32[512,4096]{1,0:T(8,128)} %add_select_fusion.11, s32[]{:T(128)} %constant.605.clone.1, s32[]{:T(128)} %constant.644.clone.1) | dynamic-update-slice | bytes 16777220 | tf_op jit(solution)/shard_map/scatter-add | solution.py:129
  1391.8 43.2 %scatter-add.252 = f32[512,4150]{1,0:T(8,128)} dynamic-update-slice(f32[512,4150]{1,0:T(8,128)} %scatter-add.251, f32[512,4096]{1,0:T(8,128)} %add_select_fusion.10, s32[]{:T(128)} %constant.605.clone.1, s32[]{:T(128)} %constant.645.clone.1) | dynamic-update-slice | bytes 16777220 | tf_op jit(solution)/shard_map/scatter-add | solution.py:129
  1444.3 43.2 %scatter-add.253 = f32[512,4150]{1,0:T(8,128)} dynamic-update-slice(f32[512,4150]{1,0:T(8,128)} %scatter-add.252, f32[512,4096]{1,0:T(8,128)} %slice_add_fusion.2, s32[]{:T(128)} %constant.605.clone.1, s32[]{:T(128)} %constant.640.clone.1) | dynamic-update-slice | bytes 16777220 | tf_op jit(solution)/shard_map/scatter-add | solution.py:129
  1493.5 45.5 %reduce-scatter.26.cloned.1.call-done = bf16[128,4150]{1,0:T(8,128)(2,1)} async-done(((bf16[512,4150]{1,0:T(8,128)(2,1)}), bf16[128,4150]{1,0:T(8,128)(2,1)}) %reduce-scatter.26.cloned.1.call-update) | async-done | bytes 1062416 | tf_op jit(solution)/shard_map/reduce_scatter | solution.py:95
  1580.0 40.6 %reduce-scatter.28.cloned.1.call-done = bf16[128,4096]{1,0:T(8,128)(2,1)} async-done(((bf16[512,4096]{1,0:T(8,128)(2,1)}), bf16[128,4096]{1,0:T(8,128)(2,1)}) %reduce-scatter.28.cloned.1.call-update) | async-done | bytes 1048592 | tf_op jit(solution)/shard_map/reduce_scatter | solution.py:95
  1642.8 43.2 %scatter-add.255 = f32[512,4114]{1,0:T(8,128)} dynamic-update-slice(f32[512,4114]{1,0:T(8,128)} %scatter-add.254, f32[512,4096]{1,0:T(8,128)} %add_select_fusion.9, s32[]{:T(128)} %constant.605.clone.1, s32[]{:T(128)} %constant.626.clone.1) | dynamic-update-slice | bytes 16777220 | tf_op jit(solution)/shard_map/scatter-add | solution.py:129
  1695.8 43.2 %scatter-add.256 = f32[512,4114]{1,0:T(8,128)} dynamic-update-slice(f32[512,4114]{1,0:T(8,128)} %scatter-add.255, f32[512,4096]{1,0:T(8,128)} %add_select_fusion.8, s32[]{:T(128)} %constant.605.clone.1, s32[]{:T(128)} %constant.629.clone.1) | dynamic-update-slice | bytes 16777220 | tf_op jit(solution)/shard_map/scatter-add | solution.py:129
  1748.9 43.4 %scatter-add.257 = f32[512,4114]{1,0:T(8,128)} dynamic-update-slice(f32[512,4114]{1,0:T(8,128)} %scatter-add.256, f32[512,4096]{1,0:T(8,128)} %add_select_fusion.7, s32[]{:T(128)} %constant.605.clone.1, s32[]{:T(128)} %constant.631.clone.1) | dynamic-update-slice | bytes 16777220 | tf_op jit(solution)/shard_map/scatter-add | solution.py:129
  1802.1 43.2 %scatter-add.258 = f32[512,4114]{1,0:T(8,128)} dynamic-update-slice(f32[512,4114]{1,0:T(8,128)} %scatter-add.257, f32[512,4096]{1,0:T(8,128)} %add_select_fusion.6, s32[]{:T(128)} %constant.605.clone.1, s32[]{:T(128)} %constant.634.clone.1) | dynamic-update-slice | bytes 16777220 | tf_op jit(solution)/shard_map/scatter-add | solution.py:129
  1855.0 43.2 %scatter-add.259 = f32[512,4114]{1,0:T(8,128)} dynamic-update-slice(f32[512,4114]{1,0:T(8,128)} %scatter-add.258, f32[512,4096]{1,0:T(8,128)} %add_select_fusion.5, s32[]{:T(128)} %constant.605.clone.1, s32[]{:T(128)} %constant.637.clone.1) | dynamic-update-slice | bytes 16777220 | tf_op jit(solution)/shard_map/scatter-add | solution.py:129
  1907.5 43.2 %scatter-add.260 = f32[512,4114]{1,0:T(8,128)} dynamic-update-slice(f32[512,4114]{1,0:T(8,128)} %scatter-add.259, f32[512,4096]{1,0:T(8,128)} %slice_add_fusion.1, s32[]{:T(128)} %constant.605.clone.1, s32[]{:T(128)} %constant.642.clone.1) | dynamic-update-slice | bytes 16777220 | tf_op jit(solution)/shard_map/scatter-add | solution.py:129
  1957.6 28.0 %gather_fusion.1 = f32[8192,8]{1,0:T(8,128)} fusion(f32[8,512]{0,1:T(8,128)S(1)} %copy.248, s32[8192]{0:T(1024)S(1)} %fusion.336), kind=kCustom, calls=%fused_computation.1 | custom fusion | bytes 557056 | tf_op jit(solution)/shard_map/jit(_take)/gather | solution.py:248
  2154.7 43.4 %scatter-add.262 = f32[512,4102]{1,0:T(8,128)} dynamic-update-slice(f32[512,4102]{1,0:T(8,128)} %scatter-add.261, f32[512,4096]{1,0:T(8,128)} %add_select_fusion.4, s32[]{:T(128)} %constant.605.clone.1, s32[]{:T(128)} %constant.624.clone.1) | dynamic-update-slice | bytes 16777220 | tf_op jit(solution)/shard_map/scatter-add | solution.py:129
  2207.9 43.3 %scatter-add.263 = f32[512,4102]{1,0:T(8,128)} dynamic-update-slice(f32[512,4102]{1,0:T(8,128)} %scatter-add.262, f32[512,4096]{1,0:T(8,128)} %add_select_fusion.3, s32[]{:T(128)} %constant.605.clone.1, s32[]{:T(128)} %constant.625.clone.1) | dynamic-update-slice | bytes 16777220 | tf_op jit(solution)/shard_map/scatter-add | solution.py:129
  2261.2 43.5 %scatter-add.264 = f32[512,4102]{1,0:T(8,128)} dynamic-update-slice(f32[512,4102]{1,0:T(8,128)} %scatter-add.263, f32[512,4096]{1,0:T(8,128)} %add_select_fusion.2, s32[]{:T(128)} %constant.605.clone.1, s32[]{:T(128)} %constant.626.clone.1) | dynamic-update-slice | bytes 16777220 | tf_op jit(solution)/shard_map/scatter-add | solution.py:129
  2314.6 43.8 %scatter-add.265 = f32[512,4102]{1,0:T(8,128)} dynamic-update-slice(f32[512,4102]{1,0:T(8,128)} %scatter-add.264, f32[512,4096]{1,0:T(8,128)} %add_select_fusion.1, s32[]{:T(128)} %constant.605.clone.1, s32[]{:T(128)} %constant.627.clone.1) | dynamic-update-slice | bytes 16777220 | tf_op jit(solution)/shard_map/scatter-add | solution.py:129
  2368.3 43.5 %scatter-add.266 = f32[512,4102]{1,0:T(8,128)} dynamic-update-slice(f32[512,4102]{1,0:T(8,128)} %scatter-add.265, f32[512,4096]{1,0:T(8,128)} %add_select_fusion, s32[]{:T(128)} %constant.605.clone.1, s32[]{:T(128)} %constant.628.clone.1) | dynamic-update-slice | bytes 16777220 | tf_op jit(solution)/shard_map/scatter-add | solution.py:129
  2421.2 43.2 %scatter-add.267 = f32[512,4102]{1,0:T(8,128)} dynamic-update-slice(f32[512,4102]{1,0:T(8,128)} %scatter-add.266, f32[512,4096]{1,0:T(8,128)} %slice_add_fusion, s32[]{:T(128)} %constant.605.clone.1, s32[]{:T(128)} %constant.629.clone.1) | dynamic-update-slice | bytes 16777220 | tf_op jit(solution)/shard_map/scatter-add | solution.py:129
  2501.3 14.9 reduce-scatter.34.cloned.1.call-done
  2546.4 35.5 %all-reduce.4 = (bf16[1,128]{1,0:T(2,128)(2,1)S(1)}, bf16[1,128]{1,0:T(2,128)(2,1)S(1)}, bf16[1,128]{1,0:T(2,128)(2,1)S(1)}, bf16[1,128]{1,0:T(2,128)(2,1)S(1)},...) all-reduce(bf16[1,128]{1,0:T(2,128)(2,1)S(1)} %bitcast.666, ...), channel_id=1, replica_groups=mesh['frames'=8,'chan'=4] {'frames'}, use_global_device_ids=true, to_apply=%region_68.69 | all-reduce | flops 14472 | bytes 57888 | tf_op jit(solution)/shard_map/psum | solution.py:302
  (972 shorter events, 1000.2 us)
Async XLA Ops:
  7.2 774.8 %copy-start = (bf16[8,256]{1,0:T(8,128)(2,1)S(1)}, bf16[8,256]{1,0:T(8,128)(2,1)}, u32[]{:S(2)}) copy-start(bf16[8,256]{1,0:T(8,128)(2,1)} %param.77) | copy-start | bytes 12292
  7.3 61.2 %all-gather.8.cloned.1.call-start = ((), (), s32[]{:S(2)}) async-start(), calls=%async_computation.7 | async-start | bytes 5406720 | tf_op jit(solution)/shard_map/all_gather | solution.py:85
  8.2 234.6 %copy-start.206 = (f32[128]{0:T(128)}, f32[128]{0:T(128)S(1)}, u32[]{:S(2)}) copy-start(f32[128]{0:T(128)S(1)} %get-tuple-element.645) | copy-start | bytes 1540
  17.6 6.5 collective-permute-start
  22.5 5.8 collective-permute-start.1
  31.9 93.8 %all-gather.10.cloned.1.call-start = ((), (), s32[]{:S(2)}) async-start(), calls=%async_computation.8 | async-start | bytes 5242880 | tf_op jit(solution)/shard_map/all_gather | solution.py:85
  33.7 164.0 %copy-start.198 = (f32[128]{0:T(128)}, f32[128]{0:T(128)S(1)}, u32[]{:S(2)}) copy-start(f32[128]{0:T(128)S(1)} %get-tuple-element.638) | copy-start | bytes 1540
  91.0 94.3 %all-gather.12.cloned.1.call-start = ((), (), s32[]{:S(2)}) async-start(), calls=%async_computation.9 | async-start | bytes 5406720 | tf_op jit(solution)/shard_map/all_gather | solution.py:85
  91.3 1015.6 %copy-start.136 = (f32[128]{0:T(128)}, f32[128]{0:T(128)S(1)}, u32[]{:S(2)}) copy-start(f32[128]{0:T(128)S(1)} %get-tuple-element.630) | copy-start | bytes 1540
  137.2 5.0 collective-permute-start.2
  140.6 5.8 collective-permute-start.3
  150.0 92.8 %all-gather.14.cloned.1.call-start = ((), (), s32[]{:S(2)}) async-start(), calls=%async_computation.10 | async-start | bytes 5242880 | tf_op jit(solution)/shard_map/all_gather | solution.py:85
  208.1 92.3 %all-gather.16.cloned.1.call-start = ((), (), s32[]{:S(2)}) async-start(), calls=%async_computation.11 | async-start | bytes 5406720 | tf_op jit(solution)/shard_map/all_gather | solution.py:85
  253.5 5.0 collective-permute-start.4
  256.9 5.8 collective-permute-start.5
  265.1 92.6 %all-gather.18.cloned.1.call-start = ((), (), s32[]{:S(2)}) async-start(), calls=%async_computation.12 | async-start | bytes 5242880 | tf_op jit(solution)/shard_map/all_gather | solution.py:85
  323.0 92.3 %all-gather.20.cloned.1.call-start = ((), (), s32[]{:S(2)}) async-start(), calls=%async_computation.13 | async-start | bytes 5406720 | tf_op jit(solution)/shard_map/all_gather | solution.py:85
  368.4 5.0 collective-permute-start.6
  371.8 5.8 collective-permute-start.7
  380.0 701.1 %reduce-scatter.22.cloned.1.call-start = ((), (), s32[]{:S(2)}) async-start(), calls=%async_computation.14 | async-start | bytes 5406720 | tf_op jit(solution)/shard_map/reduce_scatter | solution.py:89
  383.9 188.9 %copy-start.230 = (bf16[512]{0:T(512)(128)(2,1)}, bf16[512]{0:T(512)(128)(2,1)S(1)}, u32[]{:S(2)}) copy-start(bf16[512]{0:T(512)(128)(2,1)S(1)} %convert_element_type.627) | copy-start | bytes 3076
  383.9 211.5 %copy-start.228 = (bf16[512]{0:T(512)(128)(2,1)}, bf16[512]{0:T(512)(128)(2,1)S(1)}, u32[]{:S(2)}) copy-start(bf16[512]{0:T(512)(128)(2,1)S(1)} %convert_element_type.628) | copy-start | bytes 3076
  383.9 234.6 %copy-start.226 = (bf16[512]{0:T(512)(128)(2,1)}, bf16[512]{0:T(512)(128)(2,1)S(1)}, u32[]{:S(2)}) copy-start(bf16[512]{0:T(512)(128)(2,1)S(1)} %convert_element_type.629) | copy-start | bytes 3076
  384.0 257.6 %copy-start.224 = (bf16[512]{0:T(512)(128)(2,1)}, bf16[512]{0:T(512)(128)(2,1)S(1)}, u32[]{:S(2)}) copy-start(bf16[512]{0:T(512)(128)(2,1)S(1)} %convert_element_type.630) | copy-start | bytes 3076
  384.0 280.8 %copy-start.222 = (bf16[512]{0:T(512)(128)(2,1)}, bf16[512]{0:T(512)(128)(2,1)S(1)}, u32[]{:S(2)}) copy-start(bf16[512]{0:T(512)(128)(2,1)S(1)} %convert_element_type.631) | copy-start | bytes 3076
  384.0 304.0 %copy-start.220 = (bf16[512]{0:T(512)(128)(2,1)}, bf16[512]{0:T(512)(128)(2,1)S(1)}, u32[]{:S(2)}) copy-start(bf16[512]{0:T(512)(128)(2,1)S(1)} %convert_element_type.632) | copy-start | bytes 3076
  384.0 327.1 %copy-start.218 = (bf16[512]{0:T(512)(128)(2,1)}, bf16[512]{0:T(512)(128)(2,1)S(1)}, u32[]{:S(2)}) copy-start(bf16[512]{0:T(512)(128)(2,1)S(1)} %convert_element_type.633) | copy-start | bytes 3076
  384.0 350.3 %copy-start.216 = (bf16[512]{0:T(512)(128)(2,1)}, bf16[512]{0:T(512)(128)(2,1)S(1)}, u32[]{:S(2)}) copy-start(bf16[512]{0:T(512)(128)(2,1)S(1)} %convert_element_type.634) | copy-start | bytes 3076
  384.1 373.1 %copy-start.214 = (bf16[512]{0:T(512)(128)(2,1)}, bf16[512]{0:T(512)(128)(2,1)S(1)}, u32[]{:S(2)}) copy-start(bf16[512]{0:T(512)(128)(2,1)S(1)} %convert_element_type.635) | copy-start | bytes 3076
  384.1 395.6 %copy-start.212 = (bf16[512]{0:T(512)(128)(2,1)}, bf16[512]{0:T(512)(128)(2,1)S(1)}, u32[]{:S(2)}) copy-start(bf16[512]{0:T(512)(128)(2,1)S(1)} %convert_element_type.636) | copy-start | bytes 3076
  392.3 401.1 %copy-start.81 = (f32[512,8]{0,1:T(8,128)}, f32[512,8]{0,1:T(8,128)S(1)}, u32[]{:S(2)}) copy-start(f32[512,8]{0,1:T(8,128)S(1)} %copy.209) | copy-start | bytes 49156
  392.6 400.9 %copy-start.130 = (pred[512]{0:T(512)(128)(4,1)}, pred[512]{0:T(512)(128)(4,1)S(1)}, u32[]{:S(2)}) copy-start(pred[512]{0:T(512)(128)(4,1)S(1)} %compare_and_fusion.1) | copy-start | bytes 1540
  1034.5 120.5 %reduce-scatter.24.cloned.1.call-start = ((), (), s32[]{:S(2)}) async-start(), calls=%async_computation.15 | async-start | bytes 5242880 | tf_op jit(solution)/shard_map/reduce_scatter | solution.py:95
  1081.9 5.0 collective-permute-start.8
  1085.3 5.8 collective-permute-start.9
  1106.9 453.0 %copy-start.14 = (f32[128,4096]{1,0:T(8,128)}, f32[128,4096]{1,0:T(8,128)S(1)}, u32[]{:S(2)}) copy-start(f32[128,4096]{1,0:T(8,128)S(1)} %get-tuple-element.508) | copy-start | bytes 6291460
  1110.3 428.6 %reduce-scatter.26.cloned.1.call-start = ((), (), s32[]{:S(2)}) async-start(), calls=%async_computation.16 | async-start | bytes 5406720 | tf_op jit(solution)/shard_map/reduce_scatter | solution.py:95
  1493.5 127.1 %reduce-scatter.28.cloned.1.call-start = ((), (), s32[]{:S(2)}) async-start(), calls=%async_computation.17 | async-start | bytes 5242880 | tf_op jit(solution)/shard_map/reduce_scatter | solution.py:95
  1539.8 5.2 collective-permute-start.10
  1543.2 5.8 collective-permute-start.11
  1575.9 430.4 %reduce-scatter.30.cloned.1.call-start = ((), (), s32[]{:S(2)}) async-start(), calls=%async_computation.18 | async-start | bytes 5406720 | tf_op jit(solution)/shard_map/reduce_scatter | solution.py:95
  1956.7 150.7 %reduce-scatter.32.cloned.1.call-start = ((), (), s32[]{:S(2)}) async-start(), calls=%async_computation.19 | async-start | bytes 5242880 | tf_op jit(solution)/shard_map/reduce_scatter | solution.py:95
  2007.2 5.8 collective-permute-start.12
  2010.6 5.8 collective-permute-start.13
  2041.8 438.3 %all-reduce.8.cloned.1.call-start = ((), (), s32[]{:S(2)}) async-start(), calls=%async_computation.21 | async-start | bytes 19136512 | tf_op jit(solution)/shard_map/psum | solution.py:300
  2139.0 377.2 %reduce-scatter.34.cloned.1.call-start = ((), (), s32[]{:S(2)}) async-start(), calls=%async_computation.20 | async-start | bytes 5406720 | tf_op jit(solution)/shard_map/reduce_scatter | solution.py:95
  2517.1 5.3 collective-permute-start.14
  2520.5 5.8 collective-permute-start.15
  (244 other events, 4676.2 us)
Sparse Core Ops, SparseCore 0:
  32.0 36.3 all-gather.7
  91.1 34.4 all-gather.9
  150.1 35.1 all-gather.11
  208.2 34.4 all-gather.13
  265.2 35.1 all-gather.15
  323.1 34.4 all-gather.17
  380.1 35.1 all-gather.19
  1034.7 46.3 reduce-scatter.21
  1110.5 44.4 reduce-scatter.23
  1493.6 45.3 reduce-scatter.25
  1576.1 44.4 reduce-scatter.27
  1956.8 45.3 reduce-scatter.29
  2041.9 44.4 reduce-scatter.31
  2139.1 308.3 all-reduce.7
  2470.5 45.6 reduce-scatter.33
where the time goes:
time: 2640 us; the launch traced here: 2600 us
  local copies, waits for them, and re-layouts  1280 us (48%)
  waiting for transfers between devices  440 us (17%)
  matrix products  427 us (16%)
  other arithmetic  349 us (13%)
  blocking collectives  45.9 us (2%)
  starting transfers between devices  40.3 us (2%)
    scatter-add x21, local copies, waits for them, and re-layouts, dilated_back(): back = back.at[:, start:start + extent].add(spread)  792 us
    slice x16, local copies, waits for them, and re-layouts, strided_conv(): wide[:, kernel_tap:kernel_tap + stride * frames:stride]  338 us
    all_gather x7, waiting for transfers between devices, all_channels(): return lax.all_gather(active, 'chan', axis=0, tiled=True)  218 us
    dot_general x41, matrix products, contract_cols(): lax.dot_general(left, right, (((0,), (0,)), ((), ())), preferred_element_...  211 us
    scatter-add x16, other arithmetic, strided_back(): back.at[:, kernel_tap:kernel_tap + stride * frames:stride].add(spread)  166 us
    reduce_scatter x6, waiting for transfers between devices, unit_owner(): lax.psum_scatter(grad_full.astype(jnp.bfloat16), 'chan', scatter_dimensio...  141 us
    dot_general x41, matrix products, contract_rows(): lax.dot_general(left, right, (((1,), (1,)), ((), ())), preferred_element_...  92.1 us
    reduce_sum x7, other arithmetic, snake_act(): return value + jnp.sin(alpha[:, None] * value) ** 2 / alpha[:, None]  76.6 us
  transfers between devices with their start and end apart: 31, of which 25 were waited for; matrix products, arithmetic and copies ran while one was open for 19% of the time, Pallas kernels for 0%

commit v1 on v0

v1 whole, which is shorter than its diff:
```python
import jax
import jax.numpy as jnp
from jax import lax
from jax.experimental import pallas as pl
from jax.experimental.pallas import tpu as pltpu
from jax.sharding import PartitionSpec as P

CODES = 8192
STRIDE = 8
NORM_EPS = 1e-06
COMMIT = 4.0

BF = jnp.bfloat16
F32 = jnp.float32

SEG = 16
HALO = 128
LEAD = 28
CHUNK = 256
VMEM = 60 * 2**20

INV_PI = 0.3183098861837907
PI_HIGH = 3.140625
PI_LOW = 0.000967653589793116


def reduced(angle):
    turns = jnp.round(angle * INV_PI)
    return (angle - turns * PI_HIGH) - turns * PI_LOW


def sin_over(square):
    return 0.999999995 + square * (
        -0.166666573 + square * (8.33303355e-03 + square * (-1.98077678e-04 + square * 2.60223459e-06))
    )


def cos_of(square):
    return 0.999999948 + square * (
        -4.99998973e-01
        + square * (4.16633930e-02 + square * (-1.38522741e-03 + square * 2.31212358e-05))
    )


def snake(value, alpha, inverse):
    angle = reduced(alpha * value)
    square = angle * angle
    part = sin_over(square)
    return value + (square * part * part) * inverse


def snake_parts(value, alpha, inverse):
    angle = reduced(alpha * value)
    square = angle * angle
    part = sin_over(square)
    sine2 = (square * part * part) * inverse
    double = 2.0 * angle * part * cos_of(square)
    return value + sine2, 1.0 + double, (value * double - sine2) * inverse


def lanes4(mask):
    return jnp.concatenate([mask] * 4, axis=1)


def own_mask(start, count, span, own):
    row = lax.broadcasted_iota(jnp.int32, (count, 128), 0) + start
    place = (row & (SEG - 1)) * span + (row >> 4)
    return jnp.where((place >= HALO) & (place < HALO + own), 1.0, 0.0).astype(F32)


def fold(values):
    rows, cols = values.shape
    return values.reshape(rows // 8, 8, cols).sum(axis=0)


def load_weights(pieces, weights, sems):
    me = lax.axis_index("chan")
    copies = []
    for p, piece in enumerate(pieces):
        rows = piece.shape[1]
        slot = pl.multiple_of((me ^ p) * rows, rows)
        copy = pltpu.make_async_copy(piece, weights.at[:, pl.ds(slot, rows), :], sems.at[p])
        copy.start()
        copies.append(copy)
    return copies


def fill_masks(mask, labels, spacing, rows):
    base = LEAD * SEG
    here = labels[pl.ds(base, rows), :]
    for tap in range(7):
        there = labels[pl.ds(base + (tap - 3) * spacing * SEG, rows), :]
        mask[tap] = jnp.where(there == here, 1.0, 0.0).astype(BF)


def fill_ends(wide, full, margin, rows):
    edge = margin * SEG
    wide[pl.ds(0, edge), :] = full[pl.ds(8 + rows - edge - 1, edge), :].astype(BF)
    wide[pl.ds(edge + rows, edge), :] = full[pl.ds(8 + 1, edge), :].astype(BF)


def dot_nt(left, right):
    return lax.dot_general(left, right, (((1,), (1,)), ((), ())), preferred_element_type=F32)


def dot_nn(left, right):
    return lax.dot_general(left, right, (((1,), (0,)), ((), ())), preferred_element_type=F32)


def dot_tn(left, right):
    return lax.dot_general(left, right, (((0,), (0,)), ((), ())), preferred_element_type=F32)


A1, I1, A2, I2, S7, B7, S1, B1 = range(8)


def unit_forward(stream, pieces, vecs, labels, spacing):
    rows, chans = stream.shape
    margin = 3 * spacing

    def kernel(s_ref, p0, p1, p2, p3, v_ref, l_ref, out_ref, mid_ref, weights, wide, full, mask, sems):
        copies = load_weights((p0, p1, p2, p3), weights, sems)
        fill_masks(mask, l_ref, spacing, rows)

        @pl.loop(0, rows, step=CHUNK)
        def _(start):
            start = pl.multiple_of(start, CHUNK)
            act = snake(s_ref[pl.ds(start, CHUNK), :], v_ref[A1 : A1 + 1, :], v_ref[I1 : I1 + 1, :])
            full[pl.ds(8 + start, CHUNK), :] = act
            wide[pl.ds(margin * SEG + start, CHUNK), :] = act.astype(BF)

        fill_ends(wide, full, margin, rows)
        for copy in copies:
            copy.wait()

        @pl.loop(0, rows, step=CHUNK)
        def _(start):
            start = pl.multiple_of(start, CHUNK)
            total = None
            for tap in range(7):
                columns = wide[pl.ds(start + tap * spacing * SEG, CHUNK), :]
                if tap != 3:
                    columns = columns * lanes4(mask[tap, pl.ds(start, CHUNK), :])
                term = dot_nt(columns, weights[tap])
                total = term if total is None else total + term
            middle = total * v_ref[S7 : S7 + 1, :] + v_ref[B7 : B7 + 1, :]
            mid_ref[pl.ds(start, CHUNK), :] = middle
            second = snake(middle, v_ref[A2 : A2 + 1, :], v_ref[I2 : I2 + 1, :]).astype(BF)
            term = dot_nt(second, weights[7])
            out_ref[pl.ds(start, CHUNK), :] = (
                s_ref[pl.ds(start, CHUNK), :] + term * v_ref[S1 : S1 + 1, :] + v_ref[B1 : B1 + 1, :]
            )

    whole = pl.BlockSpec(memory_space=pltpu.VMEM)
    held = pl.BlockSpec(memory_space=pl.ANY)
    return pl.pallas_call(
        kernel,
        out_shape=[jax.ShapeDtypeStruct((rows, chans), F32)] * 2,
        in_specs=[whole] + [held] * 4 + [whole] * 2,
        out_specs=[whole] * 2,
        scratch_shapes=[
            pltpu.VMEM((8, chans, chans), BF),
            pltpu.VMEM((rows + 2 * margin * SEG, chans), BF),
            pltpu.VMEM((rows + 16, chans), F32),
            pltpu.VMEM((7, rows, 128), BF),
            pltpu.SemaphoreType.DMA((4,)),
        ],
        compiler_params=pltpu.CompilerParams(vmem_limit_bytes=VMEM),
        cost_estimate=pl.CostEstimate(
            flops=2 * rows * 8 * chans * chans, bytes_accessed=16 * 2**20, transcendentals=0
        ),
        name=f"unit_forward_{spacing}",
    )(stream, *pieces, vecs, labels)


def unit_weights_back(grad, stream, middle, piece1s, vecs, labels, spacing, own):
    rows, chans = stream.shape
    margin = 3 * spacing
    span = rows // SEG
    part = chans // 4

    def kernel(
        g_ref, s_ref, m_ref, p0, p1, p2, p3, v_ref, l_ref,
        d_ref, keep_ref, send_ref, sum_ref,
        w1, wide, full, mask, low_t, mid_t, second, results, sums, sems, out_sems,
    ):
        me = lax.axis_index("chan")
        copies = []
        for p, piece in enumerate((p0, p1, p2, p3)):
            slot = pl.multiple_of((me ^ p) * part, part)
            copy = pltpu.make_async_copy(piece.at[7], w1.at[pl.ds(slot, part), :], sems.at[p])
            copy.start()
            copies.append(copy)
        fill_masks(mask, l_ref, spacing, rows)
        sums[...] = jnp.zeros_like(sums)
        for copy in copies:
            copy.wait()

        @pl.loop(0, rows, step=CHUNK)
        def _(start):
            start = pl.multiple_of(start, CHUNK)
            here = pl.ds(start, CHUNK)
            mine = lanes4(own_mask(start, CHUNK, span, own))
            act = snake(s_ref[here, :], v_ref[A1 : A1 + 1, :], v_ref[I1 : I1 + 1, :])
            full[pl.ds(8 + start, CHUNK), :] = act
            wide[pl.ds(margin * SEG + start, CHUNK), :] = act.astype(BF)
            grad_here = g_ref[here, :]
            scaled = grad_here * v_ref[S1 : S1 + 1, :]
            low_t[:, here] = (scaled * mine).T.astype(BF)
            back = dot_nn(scaled.astype(BF), w1[...])
            value, slope, by_alpha = snake_parts(
                m_ref[here, :], v_ref[A2 : A2 + 1, :], v_ref[I2 : I2 + 1, :]
            )
            second[here, :] = value.astype(BF)
            dmiddle = back * slope
            mine_mid = dmiddle * mine
            sums[0] += fold(grad_here * mine)
            sums[1] += fold(mine_mid)
            sums[2] += fold(back * by_alpha * mine)
            d_ref[here, :] = (dmiddle * v_ref[S7 : S7 + 1, :]).astype(BF)
            mid_t[:, here] = (mine_mid * v_ref[S7 : S7 + 1, :]).T.astype(BF)

        fill_ends(wide, full, margin, rows)
        sum_ref[...] = jnp.concatenate(
            [sums[i].sum(axis=0, keepdims=True) for i in range(3)] + [jnp.zeros((5, chans), F32)], axis=0
        )
        results[7] = dot_nn(low_t[...], second[...]).astype(BF)

        @pl.loop(0, 7)
        def _(tap):
            columns = wide[pl.ds(pl.multiple_of(tap * (spacing * SEG), SEG), rows), :]
            columns = columns * lanes4(mask[tap])
            results[tap] = dot_nn(mid_t[...], columns).astype(BF)

        outs = []
        for p, target in enumerate((keep_ref.at[0], send_ref.at[0], keep_ref.at[1], send_ref.at[1])):
            slot = pl.multiple_of((me ^ p) * part, part)
            copy = pltpu.make_async_copy(results.at[:, pl.ds(slot, part), :], target, out_sems.at[p])
            copy.start()
            outs.append(copy)
        for copy in outs:
            copy.wait()

    whole = pl.BlockSpec(memory_space=pltpu.VMEM)
    held = pl.BlockSpec(memory_space=pl.ANY)
    return pl.pallas_call(
        kernel,
        out_shape=[
            jax.ShapeDtypeStruct((rows, chans), BF),
            jax.ShapeDtypeStruct((2, 8, part, chans), BF),
            jax.ShapeDtypeStruct((2, 8, part, chans), BF),
            jax.ShapeDtypeStruct((8, chans), F32),
        ],
        in_specs=[whole] * 3 + [held] * 4 + [whole] * 2,
        out_specs=[whole, held, held, whole],
        scratch_shapes=[
            pltpu.VMEM((chans, chans), BF),
            pltpu.VMEM((rows + 2 * margin * SEG, chans), BF),
            pltpu.VMEM((rows + 16, chans), F32),
            pltpu.VMEM((7, rows, 128), BF),
            pltpu.VMEM((chans, rows), BF),
            pltpu.VMEM((chans, rows), BF),
            pltpu.VMEM((rows, chans), BF),
            pltpu.VMEM((8, chans, chans), BF),
            pltpu.VMEM((3, 8, chans), F32),
            pltpu.SemaphoreType.DMA((4,)),
            pltpu.SemaphoreType.DMA((4,)),
        ],
        compiler_params=pltpu.CompilerParams(vmem_limit_bytes=VMEM),
        cost_estimate=pl.CostEstimate(
            flops=2 * rows * 9 * chans * chans, bytes_accessed=20 * 2**20, transcendentals=0
        ),
        name=f"unit_weights_back_{spacing}",
    )(grad, stream, middle, *piece1s, vecs, labels)


def unit_input_back(grad, stream, scaled, pieces, vecs, labels, spacing, own):
    rows, chans = stream.shape
    margin = 3 * spacing
    span = rows // SEG

    def kernel(g_ref, s_ref, d_ref, p0, p1, p2, p3, v_ref, l_ref, out_ref, sum_ref, weights, wide, full, mask, sums, sems):
        copies = load_weights((p0, p1, p2, p3), weights, sems)
        fill_masks(mask, l_ref, spacing, rows)
        sums[...] = jnp.zeros_like(sums)

        @pl.loop(0, rows, step=CHUNK)
        def _(start):
            start = pl.multiple_of(start, CHUNK)
            value = d_ref[pl.ds(start, CHUNK), :]
            full[pl.ds(8 + start, CHUNK), :] = value.astype(F32)
            wide[pl.ds(margin * SEG + start, CHUNK), :] = value

        fill_ends(wide, full, margin, rows)
        for copy in copies:
            copy.wait()

        @pl.loop(0, rows, step=CHUNK)
        def _(start):
            start = pl.multiple_of(start, CHUNK)
            here = pl.ds(start, CHUNK)
            total = None
            for tap in range(7):
                columns = wide[pl.ds(start + (6 - tap) * spacing * SEG, CHUNK), :]
                if tap != 3:
                    columns = columns * lanes4(mask[6 - tap, pl.ds(start, CHUNK), :])
                term = dot_nn(columns, weights[tap])
                total = term if total is None else total + term
            mine = lanes4(own_mask(start, CHUNK, span, own))
            value, slope, by_alpha = snake_parts(
                s_ref[here, :], v_ref[A1 : A1 + 1, :], v_ref[I1 : I1 + 1, :]
            )
            sums[...] += fold(total * by_alpha * mine)
            out_ref[here, :] = g_ref[here, :] + total * slope

        sum_ref[...] = jnp.concatenate(
            [sums[...].sum(axis=0, keepdims=True), jnp.zeros((7, chans), F32)], axis=0
        )

    whole = pl.BlockSpec(memory_space=pltpu.VMEM)
    held = pl.BlockSpec(memory_space=pl.ANY)
    return pl.pallas_call(
        kernel,
        out_shape=[jax.ShapeDtypeStruct((rows, chans), F32), jax.ShapeDtypeStruct((8, chans), F32)],
        in_specs=[whole] * 3 + [held] * 4 + [whole] * 2,
        out_specs=[whole] * 2,
        scratch_shapes=[
            pltpu.VMEM((8, chans, chans), BF),
            pltpu.VMEM((rows + 2 * margin * SEG, chans), BF),
            pltpu.VMEM((rows + 16, chans), F32),
            pltpu.VMEM((7, rows, 128), BF),
            pltpu.VMEM((8, chans), F32),
            pltpu.SemaphoreType.DMA((4,)),
        ],
        compiler_params=pltpu.CompilerParams(vmem_limit_bytes=VMEM),
        cost_estimate=pl.CostEstimate(
            flops=2 * rows * 7 * chans * chans, bytes_accessed=16 * 2**20, transcendentals=0
        ),
        name=f"unit_input_back_{spacing}",
    )(grad, stream, scaled, *pieces, vecs, labels)


def enter(pieces, own):
    part, count = pieces[0].shape
    span = count // SEG

    def kernel(p0, p1, p2, p3, out_ref, turned, placed):
        me = lax.axis_index("chan")
        for p, piece in enumerate((p0, p1, p2, p3)):
            turned[...] = piece[...].astype(F32).T
            for a in range(SEG):
                placed[pl.ds(a, span, stride=SEG), :] = turned[pl.ds(a * span, span), :]
            out_ref[:, pl.ds(pl.multiple_of((me ^ p) * part, part), part)] = placed[...]

    whole = pl.BlockSpec(memory_space=pltpu.VMEM)
    return pl.pallas_call(
        kernel,
        out_shape=jax.ShapeDtypeStruct((count, 4 * part), F32),
        in_specs=[whole] * 4,
        out_specs=whole,
        scratch_shapes=[pltpu.VMEM((count, part), F32)] * 2,
        compiler_params=pltpu.CompilerParams(vmem_limit_bytes=VMEM),
        name="enter",
    )(*pieces)


def leave(grad, own):
    rows, chans = grad.shape
    span = rows // SEG
    part = chans // 4

    def kernel(g_ref, o0, o1, o2, o3, ordered, placed):
        me = lax.axis_index("chan")
        for p, out in enumerate((o0, o1, o2, o3)):
            placed[...] = g_ref[:, pl.ds(pl.multiple_of((me ^ p) * part, part), part)]
            for a in range(SEG):
                ordered[pl.ds(a * span, span), :] = placed[pl.ds(a, span, stride=SEG), :]
            out[...] = ordered[pl.ds(HALO, own), :].T.astype(out.dtype)

    whole = pl.BlockSpec(memory_space=pltpu.VMEM)
    return pl.pallas_call(
        kernel,
        out_shape=[jax.ShapeDtypeStruct((part, own), F32)] + [jax.ShapeDtypeStruct((part, own), BF)] * 3,
        in_specs=[whole],
        out_specs=[whole] * 4,
        scratch_shapes=[pltpu.VMEM((rows, part), F32)] * 2,
        compiler_params=pltpu.CompilerParams(vmem_limit_bytes=VMEM),
        name="leave",
    )(grad)


def bottleneck(stream, joined, vecs, labels, chosen, picked_grad, own):
    rows, chans = stream.shape
    span = rows // SEG
    groups = span // STRIDE
    count = groups * SEG
    taps = joined.shape[0]
    edge = 16 * SEG

    def kernel(s_ref, q_ref, v_ref, l_ref, c_ref, o_ref, g_ref, lat_ref, dch_ref, m_ref, sum_ref, wide, full, codes, sums):
        @pl.loop(0, rows, step=CHUNK)
        def _(start):
            start = pl.multiple_of(start, CHUNK)
            act = snake(s_ref[pl.ds(start, CHUNK), :], v_ref[0:1, :], v_ref[1:2, :])
            full[pl.ds(8 + start, CHUNK), :] = act
            wide[pl.ds(edge + start, CHUNK), :] = act.astype(BF)

        wide[pl.ds(0, edge), :] = full[pl.ds(8 + rows - edge - 1, edge), :].astype(BF)
        wide[pl.ds(edge + rows, edge), :] = full[pl.ds(8 + 1, edge), :].astype(BF)

        def tap_mask(tap, first, amount):
            base = (LEAD + first * STRIDE) * SEG
            pieces = []
            for g in range(amount):
                start = base + g * STRIDE * SEG
                there = l_ref[pl.ds(start + (tap - 4) * SEG, SEG), :]
                pieces.append(jnp.where(there == l_ref[pl.ds(start, SEG), :], 1.0, 0.0).astype(F32))
            return jnp.concatenate(pieces, axis=0)

        def tap_columns(tap):
            base = edge + (tap - 4) * SEG
            picked = jnp.concatenate(
                [wide[pl.ds(base + g * STRIDE * SEG, SEG), :] for g in range(groups)], axis=0
            )
            return picked * lanes4(tap_mask(tap, 0, groups).astype(BF))

        total = jnp.zeros((count, 128), F32)
        for tap in range(taps):
            total = total + dot_nt(tap_columns(tap), q_ref[tap])
        lane = lax.broadcasted_iota(jnp.int32, (count, 128), 1)
        latent = jnp.where(lane < 8, total + pltpu.roll(total, 112, 1) + v_ref[2:3, :128], 0.0)
        lat_ref[...] = latent
        inverse = lax.rsqrt(jnp.sum(latent * latent, axis=1, keepdims=True) + 1.0)
        normed = latent * inverse
        spread = (2.0 * COMMIT) * (normed - c_ref[...])
        row = lax.broadcasted_iota(jnp.int32, (count, 128), 0)
        place = (row & (SEG - 1)) * groups + (row >> 4)
        mine = (place >= HALO // STRIDE) & (place < (HALO + own) // STRIDE)
        dch_ref[...] = jnp.where(mine, o_ref[...] - spread, 0.0)
        dlatent = (spread - normed * jnp.sum(normed * spread, axis=1, keepdims=True)) * inverse

        def split(values):
            high = values.astype(BF).astype(F32)
            return high + pltpu.roll(values - high, 8, 1), pltpu.roll(high, 16, 1)

        dmine = jnp.where(mine, dlatent, 0.0)
        sum_ref[1:2, :] = jnp.concatenate([jnp.sum(dmine, axis=0, keepdims=True)] * 4, axis=1)
        pair, _unused = split(dmine)
        pair = pair.astype(BF)
        for tap in range(taps):
            both = dot_tn(pair, tap_columns(tap))
            m_ref[tap] = both[0:8, :] + both[8:16, :]

        pair, again = split(dlatent)
        codes[pl.ds(8 + SEG, count), :] = pair + again
        codes[pl.ds(8, SEG), :] = codes[pl.ds(8 + count - 1, SEG), :]
        codes[pl.ds(8 + SEG + count, SEG), :] = codes[pl.ds(8 + SEG + 1, SEG), :]
        sums[...] = jnp.zeros_like(sums)
        for rest in range(STRIDE):
            total = None
            for tap in (rest - 4, rest + 4, rest + 12):
                if 0 <= tap < taps:
                    hop = (tap - 4 - rest) // STRIDE
                    left = codes[pl.ds(8 + SEG - hop * SEG, count), :] * tap_mask(tap, -hop, groups)
                    term = dot_nn(left.astype(BF), q_ref[tap])
                    total = term if total is None else total + term
            for g in range(groups):
                here = pl.ds((g * STRIDE + rest) * SEG, SEG)
                part = total[g * SEG : (g + 1) * SEG, :]
                value, slope, by_alpha = snake_parts(s_ref[here, :], v_ref[0:1, :], v_ref[1:2, :])
                g_ref[here, :] = part * slope
                mask = lanes4(own_mask((g * STRIDE + rest) * SEG, SEG, span, own))
                sums[...] += fold(part * by_alpha * mask)
        sum_ref[0:1, :] = sums[...].sum(axis=0, keepdims=True)
        sum_ref[2:8, :] = jnp.zeros((6, chans), F32)

    whole = pl.BlockSpec(memory_space=pltpu.VMEM)
    return pl.pallas_call(
        kernel,
        out_shape=[
            jax.ShapeDtypeStruct((rows, chans), F32),
            jax.ShapeDtypeStruct((count, 128), F32),
            jax.ShapeDtypeStruct((count, 128), F32),
            jax.ShapeDtypeStruct((taps, 8, chans), F32),
            jax.ShapeDtypeStruct((8, chans), F32),
        ],
        in_specs=[whole] * 6,
        out_specs=[whole] * 5,
        scratch_shapes=[
            pltpu.VMEM((rows + 2 * edge, chans), BF),
            pltpu.VMEM((rows + 16, chans), F32),
            pltpu.VMEM((count + 2 * SEG + 16, 128), F32),
            pltpu.VMEM((8, chans), F32),
        ],
        compiler_params=pltpu.CompilerParams(vmem_limit_bytes=VMEM),
        cost_estimate=pl.CostEstimate(
            flops=2 * rows * 4 * chans * chans, bytes_accessed=12 * 2**20, transcendentals=0
        ),
        name="bottleneck",
    )(stream, joined, vecs, labels, chosen, picked_grad)


def swap(value, axis, bit):
    count = lax.axis_size(axis)
    return lax.ppermute(value, axis, [(i, i ^ (1 << bit)) for i in range(count)])


def bits_of(axis):
    count = lax.axis_size(axis)
    return [(axis, bit) for bit in range(count.bit_length() - 1)]


def total_over(value, steps):
    for axis, bit in steps:
        value = value + swap(value, axis, bit)
    return value


def spread_sum(value, steps):
    value = value.astype(BF)
    for axis, bit in steps:
        half = value.shape[0] // 2
        low, high = value[:half], value[half:]
        upper = ((lax.axis_index(axis) >> bit) & 1) == 1
        got = swap(jnp.where(upper, low, high), axis, bit)
        value = (jnp.where(upper, high, low).astype(F32) + got.astype(F32)).astype(BF)
    for axis, bit in reversed(steps):
        upper = ((lax.axis_index(axis) >> bit) & 1) == 1
        got = swap(value, axis, bit)
        value = jnp.concatenate([jnp.where(upper, got, value), jnp.where(upper, value, got)], axis=0)
    return value


def from_owners(value):
    far = swap(value, "chan", 1)
    return [value, swap(value, "chan", 0), far, swap(far, "chan", 0)]


def to_peer(value, peer):
    return lax.ppermute(value, "chan", [(i, i ^ peer) for i in range(4)])


def terms(value, count):
    parts = []
    for _ in range(count):
        part = value.astype(BF)
        parts.append(part)
        value = value - part.astype(F32)
    return parts


def local(
    signal,
    dilated_dirs,
    dilated_gains,
    dilated_bias,
    snake_first,
    snake_second,
    pointwise_dirs,
    pointwise_gains,
    pointwise_bias,
    snake_last,
    strided_dirs,
    strided_gains,
    strided_bias,
    latent_proj,
    latent_bias,
    codebook,
    output_proj,
    output_bias,
    utterances,
    code_index,
    refill_index,
    cotangent,
):
    part, extent = signal.shape
    chans = 4 * part
    own = extent // 4
    frames = code_index.shape[0]
    own_frames = frames // 4
    whole = lax.axis_size("frames") * extent
    units = dilated_dirs.shape[0]
    span = (own + 2 * HALO) // SEG
    me = lax.axis_index("chan")
    block = lax.axis_index("frames")
    ring = lax.axis_size("frames")
    origin = block * extent + me * own

    low = signal.astype(BF)
    right = [(i, i + 1) for i in range(ring - 1)]
    left = [(i + 1, i) for i in range(ring - 1)]
    wide = jnp.concatenate(
        [
            lax.ppermute(low[:, extent - HALO :], "frames", right),
            low,
            lax.ppermute(low[:, :HALO], "frames", left),
        ],
        axis=1,
    )
    pieces = []
    for peer in range(4):
        piece = lax.dynamic_slice_in_dim(wide, (me ^ peer) * own, own + 2 * HALO, axis=1)
        pieces.append(piece if peer == 0 else to_peer(piece, peer))
    stream = enter(pieces, own)

    weights = []
    for member in range(units):
        joined = jnp.concatenate([dilated_dirs[member], pointwise_dirs[member][None]], axis=0)
        weights.append(from_owners(joined))

    square7 = jnp.sum(jnp.square(dilated_dirs.astype(F32)), axis=(1, 3)) + NORM_EPS
    square1 = jnp.sum(jnp.square(pointwise_dirs.astype(F32)), axis=2) + NORM_EPS
    scale7 = dilated_gains * lax.rsqrt(square7)
    scale1 = pointwise_gains * lax.rsqrt(square1)
    mine = [snake_first, 1.0 / snake_first, snake_second, 1.0 / snake_second, scale7, dilated_bias, scale1, pointwise_bias]
    packed = jnp.concatenate(
        [jnp.stack(mine, axis=1).reshape(8 * units, part), snake_last[None], (1.0 / snake_last)[None], jnp.zeros((6, part), F32)]
    )
    vecs = jnp.zeros((packed.shape[0], chans), F32)
    for peer in range(4):
        got = packed if peer == 0 else to_peer(packed, peer)
        vecs = lax.dynamic_update_slice(vecs, got, (0, (me ^ peer) * part))

    bounds = jnp.cumsum(utterances) * STRIDE
    b_place = jnp.arange(-LEAD, span + LEAD, dtype=jnp.int32)
    spots = (origin - HALO + b_place[:, None] + span * jnp.arange(SEG, dtype=jnp.int32)[None, :]).reshape(-1)
    found = jnp.sum((spots[:, None] >= bounds[None, :]).astype(F32), axis=1)
    found = jnp.where((spots >= 0) & (spots < whole), found, -1.0)
    labels = jnp.broadcast_to(found[:, None], (found.shape[0], 128))

    squares = jnp.sum(jnp.square(strided_dirs.astype(F32)), axis=(0, 2)) + NORM_EPS
    scales = strided_gains * lax.rsqrt(squares)
    project = latent_proj.astype(F32) * scales[None, :]
    split = jnp.concatenate(terms(project, 3), axis=0)
    taps = strided_dirs.shape[0]
    mixed = lax.dot_general(split, strided_dirs, (((1,), (1,)), ((), ())), preferred_element_type=F32)
    mixed = mixed[0:8] + mixed[8:16] + mixed[16:24]
    shift = jnp.sum(latent_proj.astype(F32) * strided_bias[None, :], axis=1)
    mixed = jnp.concatenate([mixed.reshape(8 * taps, chans), jnp.broadcast_to(jnp.pad(shift, (0, 0))[:, None], (8, chans))])
    mixed = total_over(mixed, bits_of("chan"))
    shift = mixed[8 * taps :, 0] + latent_bias
    mixed = mixed[: 8 * taps].reshape(8, taps, chans).transpose(1, 0, 2)
    high, rest = terms(mixed, 2)
    joined = jnp.concatenate([high, high, rest, jnp.zeros((taps, 104, chans), BF)], axis=1)

    coded_scale = lax.rsqrt(jnp.sum(codebook * codebook, axis=0) + 1.0)
    coded = codebook * coded_scale[None, :]
    table = jnp.concatenate(terms(coded, 3), axis=0)
    extra = HALO // STRIDE
    around = jnp.concatenate(
        [
            lax.ppermute(code_index[frames - extra :], "frames", right),
            code_index,
            lax.ppermute(code_index[:extra], "frames", left),
        ]
    )
    span_frames = span // STRIDE
    near = lax.dynamic_slice_in_dim(around, me * own_frames, own_frames + 2 * extra)
    near = near.reshape(SEG, span_frames).T.reshape(-1)
    wanted = jnp.concatenate([near, code_index])
    hot = (wanted[:, None] == jnp.arange(CODES, dtype=jnp.int32)[None, :]).astype(BF)
    found = lax.dot_general(hot, table, (((1,), (1,)), ((), ())), preferred_element_type=F32)
    found = found[:, 0:8] + found[:, 8:16] + found[:, 16:24]
    chosen = jnp.pad(found[: near.shape[0]], ((0, 0), (0, 120)))
    chosen_low = found[near.shape[0] :].astype(BF)
    output = (
        lax.dot_general(output_proj, chosen_low, (((1,), (1,)), ((), ())), preferred_element_type=F32)
        + output_bias[:, None]
    )
    dproj_out = lax.dot_general(cotangent, chosen_low, (((1,), (0,)), ((), ())), preferred_element_type=F32)
    dbias_out = jnp.sum(cotangent.astype(F32), axis=1)
    pulled = lax.dot_general(cotangent, output_proj, (((0,), (0,)), ((), ())), preferred_element_type=F32)
    mine_pulled = None
    for peer in range(4):
        piece = lax.dynamic_slice_in_dim(pulled, (me ^ peer) * own_frames, own_frames, axis=0)
        piece = piece if peer == 0 else to_peer(piece, peer)
        mine_pulled = piece if mine_pulled is None else mine_pulled + piece
    mine_pulled = jnp.pad(mine_pulled, ((extra, extra), (0, 120)))
    mine_pulled = mine_pulled.reshape(SEG, span_frames, 128).transpose(1, 0, 2).reshape(-1, 128)
    sums_out = jnp.concatenate([dproj_out, dbias_out[:, None]], axis=1)
    sums_out = total_over(sums_out, bits_of("frames"))

    saved = []
    for member in range(units):
        vec = vecs[8 * member : 8 * member + 8]
        result, middle = unit_forward(stream, weights[member], vec, labels, 3**member)
        saved.append((stream, middle, vec))
        stream = result

    tail_vecs = jnp.concatenate(
        [vecs[8 * units : 8 * units + 2], jnp.pad(shift, (0, chans - 8))[None], jnp.zeros((5, chans), F32)]
    )
    grad, latent, dchosen, mixed_grad, last_sums = bottleneck(
        stream, joined, tail_vecs, labels, chosen, mine_pulled, own
    )

    place = (
        jnp.arange(SEG, dtype=jnp.int32)[None, :] * span_frames + jnp.arange(span_frames, dtype=jnp.int32)[:, None]
    ).reshape(-1)
    owned = (place >= extra) & (place < extra + own_frames)
    place = jnp.where(owned, place - extra + block * frames + me * own_frames, -1)
    dchosen = dchosen[:, :8]
    rows_in = jnp.concatenate(terms(dchosen, 2) + [owned.astype(BF)[:, None]], axis=1)
    hot = (near[:, None] == jnp.arange(CODES, dtype=jnp.int32)[None, :]).astype(BF)
    into = lax.dot_general(rows_in, hot, (((0,), (0,)), ((), ())), preferred_element_type=F32)
    hot = (place[:, None] == refill_index[None, :]).astype(BF)
    picked = lax.dot_general(
        latent[:, :8].astype(BF), hot, (((0,), (0,)), ((), ())), preferred_element_type=F32
    )
    everything = bits_of("chan") + bits_of("frames")
    payload = jnp.concatenate(
        [
            (into[0:8] + into[8:16]).astype(BF).reshape(8 * CODES // 128, 128),
            picked.astype(BF).reshape(8 * CODES // 128, 128),
            into[16].astype(BF).reshape(CODES // 128, 128),
            mixed_grad.astype(BF).reshape(taps * 8 * chans // 128, 128),
        ],
        axis=0,
    )
    payload = jnp.pad(payload, ((0, -payload.shape[0] % 2048), (0, 0)))
    payload = spread_sum(payload, everything)

    pieces_sum, small = [None] * units, [None] * units
    for member in reversed(range(units)):
        stream_in, middle, vec = saved[member]
        spacing = 3**member
        scaled, keep, send, sums_a = unit_weights_back(
            grad, stream_in, middle, weights[member], vec, labels, spacing, own
        )
        got = swap(send, "chan", 0)
        near2 = (keep.astype(F32) + got.astype(F32)).astype(BF)
        got = swap(near2[1], "chan", 1)
        mine2 = (near2[0].astype(F32) + got.astype(F32)).astype(BF).reshape(8 * part, chans)
        pieces_sum[member] = spread_sum(mine2, bits_of("frames")).reshape(8, part, chans)
        grad, sums_b = unit_input_back(
            grad, stream_in, scaled, weights[member], vec, labels, spacing, own
        )
        small[member] = jnp.concatenate([sums_a[:3], sums_b[:1]], axis=0)

    outs = leave(grad, own)
    grad_signal = jnp.zeros((part, extent), F32)
    for peer in range(4):
        got = outs[0] if peer == 0 else to_peer(outs[peer], peer).astype(F32)
        grad_signal = lax.dynamic_update_slice(grad_signal, got, (0, (me ^ peer) * own))

    small = jnp.concatenate(small + [last_sums[0:2], jnp.zeros((2, chans), F32)], axis=0)
    small = total_over(small, everything)
    mine_small = lax.dynamic_slice_in_dim(small, me * part, part, axis=1)
    dbias1 = mine_small[0 : 4 * units : 4]
    dbias7 = mine_small[1 : 4 * units : 4]
    dalpha2 = mine_small[2 : 4 * units : 4]
    dalpha1 = mine_small[3 : 4 * units : 4]
    dalpha_last = mine_small[4 * units]
    dbias_latent = small[4 * units + 1, :8]

    size = 8 * CODES // 128
    dcoded = payload[:size].reshape(8, CODES).astype(F32)
    picked = payload[size : 2 * size].reshape(8, CODES).astype(F32)
    usage = payload[2 * size : 2 * size + CODES // 128].reshape(CODES)
    mixed_grad = payload[2 * size + CODES // 128 :][: taps * 8 * chans // 128].reshape(taps, 8, chans)
    refreshed = jnp.where(usage[None, :] > 0, codebook, picked)
    dcodebook = (dcoded - coded * jnp.sum(coded * dcoded, axis=0)[None, :]) * coded_scale[None, :]

    meeting = lax.dot_general(
        strided_dirs, mixed_grad, (((0, 2), (0, 2)), ((), ())), preferred_element_type=F32
    )
    dproj_latent = (meeting * scales[:, None]).T + dbias_latent[:, None] * strided_bias[None, :]
    dbias_strided = jnp.sum(latent_proj.astype(F32) * dbias_latent[:, None], axis=0)
    along = jnp.sum(meeting * latent_proj.astype(F32).T, axis=1)
    dstrided_gains = along * lax.rsqrt(squares)
    dweights = lax.dot_general(latent_proj, mixed_grad, (((0,), (1,)), ((), ())), preferred_element_type=F32)
    dstrided_dirs = scales[None, :, None] * dweights.transpose(1, 0, 2) - strided_dirs.astype(F32) * (
        scales * along / squares
    )[None, :, None]

    dirs7, gains7, dirs1, gains1 = [], [], [], []
    for member in range(units):
        total = pieces_sum[member].astype(F32)
        value7 = dilated_dirs[member].astype(F32)
        along7 = jnp.sum(total[:7] * value7, axis=(0, 2))
        dirs7.append(total[:7] - value7 * (along7 / square7[member])[None, :, None])
        gains7.append(along7 / dilated_gains[member])
        value1 = pointwise_dirs[member].astype(F32)
        along1 = jnp.sum(total[7] * value1, axis=1)
        dirs1.append(total[7] - value1 * (along1 / square1[member])[:, None])
        gains1.append(along1 / pointwise_gains[member])
    return (
        output,
        grad_signal,
        jnp.stack(dirs7),
        jnp.stack(gains7),
        dbias7,
        dalpha1,
        dalpha2,
        jnp.stack(dirs1),
        jnp.stack(gains1),
        dbias1,
        dalpha_last,
        dstrided_dirs,
        dstrided_gains,
        dbias_strided,
        dproj_latent,
        dbias_latent,
        dcodebook,
        sums_out[:, :8],
        sums_out[:, 8],
        refreshed,
    )


def solution(mesh):
    in_specs = (
        P("chan", "frames"),
        P(None, None, "chan", None),
        P(None, "chan"),
        P(None, "chan"),
        P(None, "chan"),
        P(None, "chan"),
        P(None, "chan", None),
        P(None, "chan"),
        P(None, "chan"),
        P("chan"),
        P(None, "chan", None),
        P("chan"),
        P("chan"),
        P(None, "chan"),
        P(),
        P(),
        P("chan", None),
        P("chan"),
        P(),
        P("frames"),
        P(),
        P("chan", "frames"),
    )
    out_specs = (
        P("chan", "frames"),
        P("chan", "frames"),
        P(None, None, "chan", None),
        P(None, "chan"),
        P(None, "chan"),
        P(None, "chan"),
        P(None, "chan"),
        P(None, "chan", None),
        P(None, "chan"),
        P(None, "chan"),
        P("chan"),
        P(None, "chan", None),
        P("chan"),
        P("chan"),
        P(None, "chan"),
        P(),
        P(),
        P("chan", None),
        P("chan"),
        P(),
    )
    return jax.shard_map(local, mesh=mesh, in_specs=in_specs, out_specs=out_specs, check_vma=False)
```

time: 2640 us -> 643 us (0.24); the launches traced: 2600 us -> 636 us
  local copies, waits for them, and re-layouts: 1280 us -> 72.6 us
  matrix products: 427 us -> 21.1 us
  other arithmetic: 349 us -> 71.8 us
  waiting for transfers between devices: 440 us -> 218 us
  Pallas kernels: 0 us -> 181 us
  blocking collectives: 45.9 us -> 0 us
  starting transfers between devices: 40.3 us -> 69.3 us
    scatter-add x22 -> x0, local copies, waits for them, and re-layouts: 796 us -> none  [the longest x21 792 us: dilated_back(): back = back.at[:, start:start + extent].add(spread)]
    dot_general x126 -> x9, matrix products: 427 us -> 21.1 us  [the longest x1 4.86 us: local(): lax.dot_general(latent_proj, mixed_grad, (((0,), (1,)), ((), ())), prefer...]
    slice x44 -> x26, local copies, waits for them, and re-layouts: 348 us -> 16.8 us  [the longest x6 5.69 us: local(): small[member] = jnp.concatenate([sums_a[:3], sums_b[:1]], axis=0)]
    all_gather x7 -> x0, waiting for transfers between devices: 218 us -> none  [all_channels(): return lax.all_gather(active, 'chan', axis=0, tiled=True)]
    reduce_scatter x7 -> x0, waiting for transfers between devices: 188 us -> none  [the longest x6 141 us: unit_owner(): lax.psum_scatter(grad_full.astype(jnp.bfloat16), 'chan', scatter_dimensio...]
    ppermute x16 -> x69, waiting for transfers between devices: 33.8 us -> 218 us  [the longest x53 161 us: swap(): return lax.ppermute(value, axis, [(i, i ^ 1 << bit) for i in range(count)])]
    pallas_call x0 -> x12, Pallas kernels: none -> 181 us  [the longest x3 70.3 us: unit_weights_back(): pl.pallas_call(kernel, out_shape=[jax.ShapeDtypeStruct((rows, chans), BF)...]
    scatter-add x18 -> x0, other arithmetic: 174 us -> none  [the longest x16 166 us: strided_back(): back.at[:, kernel_tap:kernel_tap + stride * frames:stride].add(spread)]
  transfers between devices with their start and end apart: 31 -> 69, of which waited for: 25 -> 25; matrix products, arithmetic and copies ran while one was open for 19% -> 21% of each run, Pallas kernels for 0% -> 24%
where the time goes in v1:
time: 643 us; the launch traced here: 636 us
  waiting for transfers between devices  218 us (34%)
  Pallas kernels  181 us (28%)
  local copies, waits for them, and re-layouts  72.6 us (11%)
  other arithmetic  71.8 us (11%)
  starting transfers between devices  69.3 us (11%)
  matrix products  21.1 us (3%)
    ppermute x53, waiting for transfers between devices, swap(): return lax.ppermute(value, axis, [(i, i ^ 1 << bit) for i in range(count)])  161 us
    pallas_call x3, Pallas kernels, unit_weights_back(): pl.pallas_call(kernel, out_shape=[jax.ShapeDtypeStruct((rows, chans), BF)...  70.3 us
    ppermute x12, waiting for transfers between devices, to_peer(): return lax.ppermute(value, 'chan', [(i, i ^ peer) for i in range(4)])  57.5 us
    ppermute x53, starting transfers between devices, swap(): return lax.ppermute(value, axis, [(i, i ^ 1 << bit) for i in range(count)])  49.8 us
    pallas_call x3, Pallas kernels, unit_input_back(): pl.pallas_call(kernel, out_shape=[jax.ShapeDtypeStruct((rows, chans), F32...  46.7 us
    pallas_call x3, Pallas kernels, unit_forward(): pl.pallas_call(kernel, out_shape=[jax.ShapeDtypeStruct((rows, chans), F32...  43.7 us
    unnamed x136, local copies, waits for them, and re-layouts  23.9 us
  transfers between devices with their start and end apart: 69, of which 25 were waited for; matrix products, arithmetic and copies ran while one was open for 21% of the time, Pallas kernels for 24%

profile of v1, /device:TPU:0, one launch (start us, length us, event | category | flops | bytes accessed | tf_op | source)
XLA Modules:
  0.0 636.2 jit_solution(17289006121282837587)
XLA Ops:
  9.1 4.2 collective-permute-start
  22.6 6.4 %copy.108 = bf16[16,256,512]{1,2,0:T(8,128)(2,1)} copy(bf16[16,256,512]{2,1,0:T(8,128)(2,1)} %param.32) | data formatting | bytes 8388608 | tf_op args[10]
  29.0 3.5 fusion.2
  47.0 4.5 collective-permute-start.2
  54.1 4.5 fusion
  65.0 21.3 %collective-permute-done.23 = f32[128,8]{0,1:T(8,128)S(1)} collective-permute-done((f32[128,8]{0,1:T(8,128)S(1)}, f32[128,8]{0,1:T(8,128)S(1)}, u32[]{:S(2)}, u32[]{:S(2)}) %collective-permute-start.23) | collective-permute-done | bytes 4128 | tf_op jit(solution)/shard_map/ppermute | solution.py:540
  95.8 23.9 %collective-permute-done.5.p2 = bf16[128,1280]{1,0:T(8,128)(2,1)} collective-permute-done((bf16[128,1280]{1,0:T(8,128)(2,1)}, bf16[128,1280]{1,0:T(8,128)(2,1)}, u32[]{:S(2)}, u32[]{:S(2)}) %collective-permute-start.5) | collective-permute-done | bytes 327712 | tf_op jit(solution)/shard_map/ppermute | solution.py:540
  121.8 4.9 collective-permute-done.6.p3
  131.1 3.9 enter.1.s_ref
  135.0 20.1 %collective-permute-done.20 = f32[136,512]{1,0:T(8,128)S(1)} collective-permute-done((f32[136,512]{1,0:T(8,128)S(1)}, f32[136,512]{1,0:T(8,128)S(1)}, u32[]{:S(2)}, u32[]{:S(2)}) %collective-permute-start.20) | collective-permute-done | bytes 278560 | tf_op jit(solution)/shard_map/ppermute | solution.py:505
  162.1 14.6 %unit_forward_1.1 = (f32[1280,512]{1,0:T(8,128)}, f32[1280,512]{1,0:T(8,128)}) custom-call(f32[1280,512]{1,0:T(8,128)} %enter.1.s_ref, bf16[8,128,512]{2,1,0:T(8,128)(2,1)} %pad_maximum_fusion.2.p0, bf16[8,128,512]{2,1,0:T(8,128)(2,1)} %collective-permute-done.7.p1, bf16[8,128,512]{2,1,0:T(8,128)(2,1)} %collective-permute-done.8.p2, ...), custom_call_target="tpu_custom_call" | custom-call | flops 5368709120 | bytes 16777216 | tf_op jit(solution)/shard_map/unit_forward_1/pallas_call | solution.py:156
  176.7 14.5 %unit_forward_3.1 = (f32[1280,512]{1,0:T(8,128)}, f32[1280,512]{1,0:T(8,128)}) custom-call(f32[1280,512]{1,0:T(8,128)} %get-tuple-element.53.s_ref, bf16[8,128,512]{2,1,0:T(8,128)(2,1)} %pad_maximum_fusion.3.p0, bf16[8,128,512]{2,1,0:T(8,128)(2,1)} %collective-permute-done.13.p1, bf16[8,128,512]{2,1,0:T(8,128)(2,1)} %collective-permute-done.14.p2, ...), custom_call_target="tpu_custom_call" | custom-call | flops 5368709120 | bytes 16777216 | tf_op jit(solution)/shard_map/unit_forward_3/pallas_call | solution.py:156
  191.2 14.6 %unit_forward_9.1 = (f32[1280,512]{1,0:T(8,128)}, f32[1280,512]{1,0:T(8,128)}) custom-call(f32[1280,512]{1,0:T(8,128)} %get-tuple-element.54.s_ref, bf16[8,128,512]{2,1,0:T(8,128)(2,1)} %pad_maximum_fusion.4.p0, bf16[8,128,512]{2,1,0:T(8,128)(2,1)} %collective-permute-done.16.p1, bf16[8,128,512]{2,1,0:T(8,128)(2,1)} %collective-permute-done.17.p2, ...), custom_call_target="tpu_custom_call" | custom-call | flops 5368709120 | bytes 16777216 | tf_op jit(solution)/shard_map/unit_forward_9/pallas_call | solution.py:156
  205.9 12.6 %bottleneck.1 = (f32[1280,512]{1,0:T(8,128)}, f32[160,128]{1,0:T(8,128)}, f32[160,128]{1,0:T(8,128)}, f32[16,8,512]{2,1,0:T(8,128)}, f32[8,512]{1,0:T(8,128)}) custom-call(f32[1280,512]{1,0:T(8,128)} %get-tuple-element.55.s_ref, bf16[16,128,512]{2,1,0:T(8,128)(2,1)} %maximum_maximum_fusion.q_ref, f32[8,512]{1,0:T(8,128)} %maximum_maximum_fusion.2.v_ref, ...), custom_call_target="tpu_custom_call" | custom-call | flops 2684354560 | bytes 12582912 | tf_op jit(solution)/shard_map/bottleneck/pallas_call | solution.py:478
  234.4 23.5 %unit_weights_back_9.1 = (bf16[1280,512]{1,0:T(8,128)(2,1)}, bf16[2,8,128,512]{3,2,1,0:T(8,128)(2,1)}, bf16[2,8,128,512]{3,2,1,0:T(8,128)(2,1)}, f32[8,512]{1,0:T(8,128)}) custom-call(f32[1280,512]{1,0:T(8,128)} %get-tuple-element.56.g_ref, f32[1280,512]{1,0:T(8,128)} %get-tuple-element.54.s_ref, f32[1280,512]{1,0:T(8,128)} %get-tuple-element.57.m_ref, ...), custom_call_target="tpu_custom_call" | custom-call | flops 6039797760 | bytes 20971520 | tf_op jit(solution)/shard_map/unit_weights_back_9/pallas_call | solution.py:246
  257.9 15.5 %unit_input_back_9.1 = (f32[1280,512]{1,0:T(8,128)}, f32[8,512]{1,0:T(8,128)}) custom-call(f32[1280,512]{1,0:T(8,128)} %get-tuple-element.56.g_ref, f32[1280,512]{1,0:T(8,128)} %get-tuple-element.54.s_ref, bf16[1280,512]{1,0:T(8,128)(2,1)} %get-tuple-element.58.d_ref, bf16[8,128,512]{2,1,0:T(8,128)(2,1)} %pad_maximum_fusion.4.p0, ...), custom_call_target="tpu_custom_call" | custom-call | flops 4697620480 | bytes 16777216 | tf_op jit(solution)/shard_map/unit_input_back_9/pallas_call | solution.py:322
  273.4 23.5 %unit_weights_back_3.1 = (bf16[1280,512]{1,0:T(8,128)(2,1)}, bf16[2,8,128,512]{3,2,1,0:T(8,128)(2,1)}, bf16[2,8,128,512]{3,2,1,0:T(8,128)(2,1)}, f32[8,512]{1,0:T(8,128)}) custom-call(f32[1280,512]{1,0:T(8,128)} %get-tuple-element.59.g_ref, f32[1280,512]{1,0:T(8,128)} %get-tuple-element.53.s_ref, f32[1280,512]{1,0:T(8,128)} %get-tuple-element.60.m_ref, ...), custom_call_target="tpu_custom_call" | custom-call | flops 6039797760 | bytes 20971520 | tf_op jit(solution)/shard_map/unit_weights_back_3/pallas_call | solution.py:246
  296.9 15.6 %unit_input_back_3.1 = (f32[1280,512]{1,0:T(8,128)}, f32[8,512]{1,0:T(8,128)}) custom-call(f32[1280,512]{1,0:T(8,128)} %get-tuple-element.59.g_ref, f32[1280,512]{1,0:T(8,128)} %get-tuple-element.53.s_ref, bf16[1280,512]{1,0:T(8,128)(2,1)} %get-tuple-element.61.d_ref, bf16[8,128,512]{2,1,0:T(8,128)(2,1)} %pad_maximum_fusion.3.p0, ...), custom_call_target="tpu_custom_call" | custom-call | flops 4697620480 | bytes 16777216 | tf_op jit(solution)/shard_map/unit_input_back_3/pallas_call | solution.py:322
  312.4 23.4 %unit_weights_back_1.1 = (bf16[1280,512]{1,0:T(8,128)(2,1)}, bf16[2,8,128,512]{3,2,1,0:T(8,128)(2,1)}, bf16[2,8,128,512]{3,2,1,0:T(8,128)(2,1)}, f32[8,512]{1,0:T(8,128)}) custom-call(f32[1280,512]{1,0:T(8,128)} %get-tuple-element.62.g_ref, f32[1280,512]{1,0:T(8,128)} %enter.1.s_ref, f32[1280,512]{1,0:T(8,128)} %get-tuple-element.63.m_ref, ...), custom_call_target="tpu_custom_call" | custom-call | flops 6039797760 | bytes 20971520 | tf_op jit(solution)/shard_map/unit_weights_back_1/pallas_call | solution.py:246
  335.8 15.7 %unit_input_back_1.1 = (f32[1280,512]{1,0:T(8,128)}, f32[8,512]{1,0:T(8,128)}) custom-call(f32[1280,512]{1,0:T(8,128)} %get-tuple-element.62.g_ref, f32[1280,512]{1,0:T(8,128)} %enter.1.s_ref, bf16[1280,512]{1,0:T(8,128)(2,1)} %get-tuple-element.64.d_ref, bf16[8,128,512]{2,1,0:T(8,128)(2,1)} %pad_maximum_fusion.2.p0, ...), custom_call_target="tpu_custom_call" | custom-call | flops 4697620480 | bytes 16777216 | tf_op jit(solution)/shard_map/unit_input_back_1/pallas_call | solution.py:322
  359.1 2.7 concatenate.111
  362.8 2.7 collective-permute-start.66
  377.8 2.6 collective-permute-start.68
  391.8 3.5 leave.1
  397.3 2.7 collective-permute-start.60
  419.4 5.2 collective-permute-done.64
  426.8 6.2 collective-permute-done.26
  444.3 4.7 fusion.61
  449.6 4.9 fusion.3
  454.4 9.5 %copy.116 = f32[16,256,512]{2,1,0:T(8,128)} copy(f32[16,256,512]{1,2,0:T(8,128)} %fusion.3) | data formatting | bytes 16777216
  463.9 2.9 add_convert_fusion.1
  475.7 17.3 %collective-permute-done.36 = bf16[8,128,512]{2,1,0:T(8,128)(2,1)S(1)} collective-permute-done((bf16[8,128,512]{2,1,0:T(8,128)(2,1)S(1)}, bf16[8,128,512]{2,1,0:T(8,128)(2,1)S(1)}, u32[]{:S(2)}, u32[]{:S(2)}) %collective-permute-start.36) | collective-permute-done | bytes 1048608 | tf_op jit(solution)/shard_map/ppermute | solution.py:505
  494.3 21.2 %collective-permute-done.44 = bf16[8,128,512]{2,1,0:T(8,128)(2,1)S(1)} collective-permute-done((bf16[8,128,512]{2,1,0:T(8,128)(2,1)S(1)}, bf16[8,128,512]{2,1,0:T(8,128)(2,1)S(1)}, u32[]{:S(2)}, u32[]{:S(2)}) %collective-permute-start.44) | collective-permute-done | bytes 1048608 | tf_op jit(solution)/shard_map/ppermute | solution.py:505
  516.8 20.0 %collective-permute-done.28 = bf16[8,128,512]{2,1,0:T(8,128)(2,1)S(1)} collective-permute-done((bf16[8,128,512]{2,1,0:T(8,128)(2,1)S(1)}, bf16[8,128,512]{2,1,0:T(8,128)(2,1)S(1)}, u32[]{:S(2)}, u32[]{:S(2)}) %collective-permute-start.28) | collective-permute-done | bytes 1048608 | tf_op jit(solution)/shard_map/ppermute | solution.py:505
  540.8 9.2 %collective-permute-done.29 = bf16[512,512]{1,0:T(8,128)(2,1)S(1)} collective-permute-done((bf16[512,512]{1,0:T(8,128)(2,1)S(1)}, bf16[512,512]{1,0:T(8,128)(2,1)S(1)}, u32[]{:S(2)}, u32[]{:S(2)}) %collective-permute-start.29) | collective-permute-done | bytes 524320 | tf_op jit(solution)/shard_map/ppermute | solution.py:505
  554.3 6.5 %collective-permute-done.30 = bf16[256,512]{1,0:T(8,128)(2,1)S(1)} collective-permute-done((bf16[256,512]{1,0:T(8,128)(2,1)S(1)}, bf16[256,512]{1,0:T(8,128)(2,1)S(1)}, u32[]{:S(2)}, u32[]{:S(2)}) %collective-permute-start.30) | collective-permute-done | bytes 262176 | tf_op jit(solution)/shard_map/ppermute | solution.py:505
  561.4 2.7 collective-permute-start.40
  564.0 8.5 %collective-permute-done.47 = bf16[128,512]{1,0:T(8,128)(2,1)S(1)} collective-permute-done((bf16[128,512]{1,0:T(8,128)(2,1)S(1)}, bf16[128,512]{1,0:T(8,128)(2,1)S(1)}, u32[]{:S(2)}, u32[]{:S(2)}) %collective-permute-start.47) | collective-permute-done | bytes 131104 | tf_op jit(solution)/shard_map/ppermute | solution.py:505
  572.7 2.7 collective-permute-done.31
  575.7 6.7 %collective-permute-done.40 = bf16[128,512]{1,0:T(8,128)(2,1)S(1)} collective-permute-done((bf16[128,512]{1,0:T(8,128)(2,1)S(1)}, bf16[128,512]{1,0:T(8,128)(2,1)S(1)}, u32[]{:S(2)}, u32[]{:S(2)}) %collective-permute-start.40) | collective-permute-done | bytes 131104 | tf_op jit(solution)/shard_map/ppermute | solution.py:505
  582.5 2.7 collective-permute-done.48
  587.5 4.9 collective-permute-done.41
  593.0 5.0 collective-permute-done.49
  598.6 3.3 collective-permute-done.33
  604.1 3.3 collective-permute-done.42
  607.9 10.7 %collective-permute-done.50 = bf16[512,512]{1,0:T(8,128)(2,1)S(1)} collective-permute-done((bf16[512,512]{1,0:T(8,128)(2,1)S(1)}, bf16[512,512]{1,0:T(8,128)(2,1)S(1)}, u32[]{:S(2)}, u32[]{:S(2)}) %collective-permute-start.50) | collective-permute-done | bytes 524320 | tf_op jit(solution)/shard_map/ppermute | solution.py:505
  619.2 8.3 %collective-permute-done.34 = bf16[512,512]{1,0:T(8,128)(2,1)S(1)} collective-permute-done((bf16[512,512]{1,0:T(8,128)(2,1)S(1)}, bf16[512,512]{1,0:T(8,128)(2,1)S(1)}, u32[]{:S(2)}, u32[]{:S(2)}) %collective-permute-start.34) | collective-permute-done | bytes 524320 | tf_op jit(solution)/shard_map/ppermute | solution.py:505
  632.2 3.1 pad_maximum_fusion
  (459 shorter events, 179.6 us)
Async XLA Ops:
  5.4 81.8 %collective-permute-start.10 = (f32[32,128]{1,0:T(8,128)}, f32[32,128]{1,0:T(8,128)}, u32[]{:S(2)}, u32[]{:S(2)}) collective-permute-start(f32[32,128]{1,0:T(8,128)} %get-tuple-element.284), channel_id=1, source_target_pairs={{0,1},{1,0},{2,3},{3,2},{4,5},{5,4},{6,7},{7,6},{8,9},{9,8},{10,11... | collective-permute-start | bytes 49160 | tf_op jit(solution)/shard_map/ppermute | solution.py:540
  5.9 82.0 %collective-permute-start.11 = (f32[32,128]{1,0:T(8,128)}, f32[32,128]{1,0:T(8,128)}, u32[]{:S(2)}, u32[]{:S(2)}) collective-permute-start(f32[32,128]{1,0:T(8,128)} %get-tuple-element.284), channel_id=1, source_target_pairs={{0,2},{1,3},{2,0},{3,1},{4,6},{5,7},{6,4},{7,5},{8,10},{9,11},{10,... | collective-permute-start | bytes 49160 | tf_op jit(solution)/shard_map/ppermute | solution.py:540
  8.4 79.6 %collective-permute-start.12 = (f32[32,128]{1,0:T(8,128)}, f32[32,128]{1,0:T(8,128)}, u32[]{:S(2)}, u32[]{:S(2)}) collective-permute-start(f32[32,128]{1,0:T(8,128)} %get-tuple-element.284), channel_id=1, source_target_pairs={{0,3},{1,2},{2,1},{3,0},{4,7},{5,6},{6,5},{7,4},{8,11},{9,10},{10,... | collective-permute-start | bytes 49160 | tf_op jit(solution)/shard_map/ppermute | solution.py:540
  9.1 37.8 %collective-permute-start = (s32[16]{0:T(128)}, s32[16]{0:T(128)}, u32[]{:S(2)}, u32[]{:S(2)}) collective-permute-start(s32[16]{0:T(128)} %get-tuple-element.305), channel_id=1, source_target_pairs={{0,4},{4,8},{8,12},{12,16},{16,20},{20,24},{24,28},{1,5},{5,9},{9,... | collective-permute-start | bytes 200 | tf_op jit(solution)/shard_map/ppermute | solution.py:652
  13.3 38.2 %collective-permute-start.1 = (s32[16]{0:T(128)}, s32[16]{0:T(128)}, u32[]{:S(2)}, u32[]{:S(2)}) collective-permute-start(s32[16]{0:T(128)} %get-tuple-element.306), channel_id=1, source_target_pairs={{4,0},{8,4},{12,8},{16,12},{20,16},{24,20},{28,24},{5,1},{9,5},{13... | collective-permute-start | bytes 200 | tf_op jit(solution)/shard_map/ppermute | solution.py:654
  47.0 12.9 %collective-permute-start.2 = (bf16[128,128]{1,0:T(8,128)(2,1)}, bf16[128,128]{1,0:T(8,128)(2,1)S(1)}, u32[]{:S(2)}, u32[]{:S(2)}) collective-permute-start(bf16[128,128]{1,0:T(8,128)(2,1)} %get-tuple-element.241), channel_id=1, source_target_pairs={{0,4},{4,8},{8,12},{12,16},{16,20},{20,24},{24,28},{1,5},{5,9},{9,... | collective-permute-start | bytes 98312 | tf_op jit(solution)/shard_map/ppermute | solution.py:594
  61.5 68.1 %collective-permute-start.8 = (bf16[8,128,512]{2,1,0:T(8,128)(2,1)}, bf16[8,128,512]{2,1,0:T(8,128)(2,1)}, u32[]{:S(2)}, u32[]{:S(2)}) collective-permute-start(bf16[8,128,512]{2,1,0:T(8,128)(2,1)} %pad_maximum_fusion.2.p0), channel_id=1, source_target_pairs={{0,2},{1,3},{2,0},{3,1},{4,6},{5,7},{6,4},{7,5},{8,10},{9,11},{10,... | collective-permute-start | bytes 3145736 | tf_op jit(solution)/shard_map/ppermute | solution.py:505
  63.5 22.8 %collective-permute-start.23 = (f32[128,8]{0,1:T(8,128)S(1)}, f32[128,8]{0,1:T(8,128)S(1)}, u32[]{:S(2)}, u32[]{:S(2)}) collective-permute-start(f32[128,8]{0,1:T(8,128)S(1)} %get-tuple-element.282), channel_id=1, source_target_pairs={{0,3},{1,2},{2,1},{3,0},{4,7},{5,6},{6,5},{7,4},{8,11},{9,10},{10,... | collective-permute-start | bytes 12296 | tf_op jit(solution)/shard_map/ppermute | solution.py:540
  86.3 70.7 %collective-permute-start.14 = (bf16[8,128,512]{2,1,0:T(8,128)(2,1)}, bf16[8,128,512]{2,1,0:T(8,128)(2,1)}, u32[]{:S(2)}, u32[]{:S(2)}) collective-permute-start(bf16[8,128,512]{2,1,0:T(8,128)(2,1)} %pad_maximum_fusion.3.p0), channel_id=1, source_target_pairs={{0,2},{1,3},{2,0},{3,1},{4,6},{5,7},{6,4},{7,5},{8,10},{9,11},{10,... | collective-permute-start | bytes 3145736 | tf_op jit(solution)/shard_map/ppermute | solution.py:505
  88.0 31.7 %collective-permute-start.5 = (bf16[128,1280]{1,0:T(8,128)(2,1)}, bf16[128,1280]{1,0:T(8,128)(2,1)}, u32[]{:S(2)}, u32[]{:S(2)}) collective-permute-start(bf16[128,1280]{1,0:T(8,128)(2,1)} %get-tuple-element.226), channel_id=1, source_target_pairs={{0,2},{1,3},{2,0},{3,1},{4,6},{5,7},{6,4},{7,5},{8,10},{9,11},{10,... | collective-permute-start | bytes 983048 | tf_op jit(solution)/shard_map/ppermute | solution.py:540
  93.4 33.3 %collective-permute-start.6 = (bf16[128,1280]{1,0:T(8,128)(2,1)}, bf16[128,1280]{1,0:T(8,128)(2,1)}, u32[]{:S(2)}, u32[]{:S(2)}) collective-permute-start(bf16[128,1280]{1,0:T(8,128)(2,1)} %get-tuple-element.225), channel_id=1, source_target_pairs={{0,3},{1,2},{2,1},{3,0},{4,7},{5,6},{6,5},{7,4},{8,11},{9,10},{10,... | collective-permute-start | bytes 983048 | tf_op jit(solution)/shard_map/ppermute | solution.py:540
  95.4 64.1 %collective-permute-start.7 = (bf16[8,128,512]{2,1,0:T(8,128)(2,1)}, bf16[8,128,512]{2,1,0:T(8,128)(2,1)}, u32[]{:S(2)}, u32[]{:S(2)}) collective-permute-start(bf16[8,128,512]{2,1,0:T(8,128)(2,1)} %pad_maximum_fusion.2.p0), channel_id=1, source_target_pairs={{0,1},{1,0},{2,3},{3,2},{4,5},{5,4},{6,7},{7,6},{8,9},{9,8},{10,11... | collective-permute-start | bytes 3145736 | tf_op jit(solution)/shard_map/ppermute | solution.py:505
  119.7 39.9 %collective-permute-start.17 = (bf16[8,128,512]{2,1,0:T(8,128)(2,1)}, bf16[8,128,512]{2,1,0:T(8,128)(2,1)}, u32[]{:S(2)}, u32[]{:S(2)}) collective-permute-start(bf16[8,128,512]{2,1,0:T(8,128)(2,1)} %pad_maximum_fusion.4.p0), channel_id=1, source_target_pairs={{0,2},{1,3},{2,0},{3,1},{4,6},{5,7},{6,4},{7,5},{8,10},{9,11},{10,... | collective-permute-start | bytes 3145736 | tf_op jit(solution)/shard_map/ppermute | solution.py:505
  126.7 28.4 %collective-permute-start.20 = (f32[136,512]{1,0:T(8,128)S(1)}, f32[136,512]{1,0:T(8,128)S(1)}, u32[]{:S(2)}, u32[]{:S(2)}) collective-permute-start(f32[136,512]{1,0:T(8,128)S(1)} %fusion.75), channel_id=1, source_target_pairs={{0,2},{1,3},{2,0},{3,1},{4,6},{5,7},{6,4},{7,5},{8,10},{9,11},{10,... | collective-permute-start | bytes 835592 | tf_op jit(solution)/shard_map/ppermute | solution.py:505
  129.7 31.0 %collective-permute-start.9 = (bf16[8,128,512]{2,1,0:T(8,128)(2,1)}, bf16[8,128,512]{2,1,0:T(8,128)(2,1)}, u32[]{:S(2)}, u32[]{:S(2)}) collective-permute-start(bf16[8,128,512]{2,1,0:T(8,128)(2,1)} %collective-permute-done.8.p2), channel_id=1, source_target_pairs={{0,1},{1,0},{2,3},{3,2},{4,5},{5,4},{6,7},{7,6},{8,9},{9,8},{10,11... | collective-permute-start | bytes 3145736 | tf_op jit(solution)/shard_map/ppermute | solution.py:505
  155.8 21.0 %collective-permute-start.13 = (bf16[8,128,512]{2,1,0:T(8,128)(2,1)}, bf16[8,128,512]{2,1,0:T(8,128)(2,1)}, u32[]{:S(2)}, u32[]{:S(2)}) collective-permute-start(bf16[8,128,512]{2,1,0:T(8,128)(2,1)} %pad_maximum_fusion.3.p0), channel_id=1, source_target_pairs={{0,1},{1,0},{2,3},{3,2},{4,5},{5,4},{6,7},{7,6},{8,9},{9,8},{10,11... | collective-permute-start | bytes 3145736 | tf_op jit(solution)/shard_map/ppermute | solution.py:505
  157.1 19.7 %collective-permute-start.15 = (bf16[8,128,512]{2,1,0:T(8,128)(2,1)}, bf16[8,128,512]{2,1,0:T(8,128)(2,1)}, u32[]{:S(2)}, u32[]{:S(2)}) collective-permute-start(bf16[8,128,512]{2,1,0:T(8,128)(2,1)} %collective-permute-done.14.p2), channel_id=1, source_target_pairs={{0,1},{1,0},{2,3},{3,2},{4,5},{5,4},{6,7},{7,6},{8,9},{9,8},{10,11... | collective-permute-start | bytes 3145736 | tf_op jit(solution)/shard_map/ppermute | solution.py:505
  159.5 31.7 %collective-permute-start.16 = (bf16[8,128,512]{2,1,0:T(8,128)(2,1)}, bf16[8,128,512]{2,1,0:T(8,128)(2,1)}, u32[]{:S(2)}, u32[]{:S(2)}) collective-permute-start(bf16[8,128,512]{2,1,0:T(8,128)(2,1)} %pad_maximum_fusion.4.p0), channel_id=1, source_target_pairs={{0,1},{1,0},{2,3},{3,2},{4,5},{5,4},{6,7},{7,6},{8,9},{9,8},{10,11... | collective-permute-start | bytes 3145736 | tf_op jit(solution)/shard_map/ppermute | solution.py:505
  159.6 31.6 %collective-permute-start.18 = (bf16[8,128,512]{2,1,0:T(8,128)(2,1)}, bf16[8,128,512]{2,1,0:T(8,128)(2,1)}, u32[]{:S(2)}, u32[]{:S(2)}) collective-permute-start(bf16[8,128,512]{2,1,0:T(8,128)(2,1)} %collective-permute-done.17.p2), channel_id=1, source_target_pairs={{0,1},{1,0},{2,3},{3,2},{4,5},{5,4},{6,7},{7,6},{8,9},{9,8},{10,11... | collective-permute-start | bytes 3145736 | tf_op jit(solution)/shard_map/ppermute | solution.py:505
  234.3 132.9 %collective-permute-start.56 = (bf16[1024,128]{1,0:T(8,128)(2,1)}, bf16[1024,128]{1,0:T(8,128)(2,1)}, u32[]{:S(2)}, u32[]{:S(2)}) collective-permute-start(bf16[1024,128]{1,0:T(8,128)(2,1)} %broadcast_select_fusion.14), channel_id=1, source_target_pairs={{0,1},{1,0},{2,3},{3,2},{4,5},{5,4},{6,7},{7,6},{8,9},{9,8},{10,11... | collective-permute-start | bytes 786440 | tf_op jit(solution)/shard_map/ppermute | solution.py:505
  377.8 11.6 %collective-permute-start.68 = (f32[256,9]{0,1:T(8,128)}, f32[256,9]{0,1:T(8,128)}, u32[]{:S(2)}, u32[]{:S(2)}) collective-permute-start(f32[256,9]{0,1:T(8,128)} %add.399), channel_id=1, source_target_pairs={{0,16},{4,20},{8,24},{12,28},{16,0},{20,4},{24,8},{28,12},{1,17},{... | collective-permute-start | bytes 27656 | tf_op jit(solution)/shard_map/ppermute | solution.py:505
  381.8 13.5 %collective-permute-start.54 = (f32[16,512]{1,0:T(8,128)}, f32[16,512]{1,0:T(8,128)}, u32[]{:S(2)}, u32[]{:S(2)}) collective-permute-start(f32[16,512]{1,0:T(8,128)} %add.380), channel_id=1, source_target_pairs={{0,8},{4,12},{8,0},{12,4},{16,24},{20,28},{24,16},{28,20},{1,9},{5... | collective-permute-start | bytes 98312 | tf_op jit(solution)/shard_map/ppermute | solution.py:505
  384.9 11.6 %collective-permute-start.59 = (bf16[128,128]{1,0:T(8,128)(2,1)S(1)}, bf16[128,128]{1,0:T(8,128)(2,1)}, u32[]{:S(2)}, u32[]{:S(2)}) collective-permute-start(bf16[128,128]{1,0:T(8,128)(2,1)S(1)} %broadcast_select_fusion.42), channel_id=1, source_target_pairs={{0,8},{4,12},{8,0},{12,4},{16,24},{20,28},{24,16},{28,20},{1,9},{5... | collective-permute-start | bytes 98312 | tf_op jit(solution)/shard_map/ppermute | solution.py:505
  391.3 72.6 %collective-permute-start.35 = (bf16[2,8,128,512]{3,2,1,0:T(8,128)(2,1)}, bf16[2,8,128,512]{3,2,1,0:T(8,128)(2,1)}, u32[]{:S(2)}, u32[]{:S(2)}) collective-permute-start(bf16[2,8,128,512]{3,2,1,0:T(8,128)(2,1)} %get-tuple-element.73), channel_id=1, source_target_pairs={{0,1},{1,0},{2,3},{3,2},{4,5},{5,4},{6,7},{7,6},{8,9},{9,8},{10,11... | collective-permute-start | bytes 6291464 | tf_op jit(solution)/shard_map/ppermute | solution.py:505
  391.3 76.6 %collective-permute-start.43 = (bf16[2,8,128,512]{3,2,1,0:T(8,128)(2,1)}, bf16[2,8,128,512]{3,2,1,0:T(8,128)(2,1)}, u32[]{:S(2)}, u32[]{:S(2)}) collective-permute-start(bf16[2,8,128,512]{3,2,1,0:T(8,128)(2,1)} %get-tuple-element.75), channel_id=1, source_target_pairs={{0,1},{1,0},{2,3},{3,2},{4,5},{5,4},{6,7},{7,6},{8,9},{9,8},{10,11... | collective-permute-start | bytes 6291464 | tf_op jit(solution)/shard_map/ppermute | solution.py:505
  391.8 80.0 %collective-permute-start.27 = (bf16[2,8,128,512]{3,2,1,0:T(8,128)(2,1)}, bf16[2,8,128,512]{3,2,1,0:T(8,128)(2,1)}, u32[]{:S(2)}, u32[]{:S(2)}) collective-permute-start(bf16[2,8,128,512]{3,2,1,0:T(8,128)(2,1)} %get-tuple-element.71), channel_id=1, source_target_pairs={{0,1},{1,0},{2,3},{3,2},{4,5},{5,4},{6,7},{7,6},{8,9},{9,8},{10,11... | collective-permute-start | bytes 6291464 | tf_op jit(solution)/shard_map/ppermute | solution.py:505
  402.3 14.3 %collective-permute-start.24 = (bf16[128,1024]{1,0:T(8,128)(2,1)}, bf16[128,1024]{1,0:T(8,128)(2,1)}, u32[]{:S(2)}, u32[]{:S(2)}) collective-permute-start(bf16[128,1024]{1,0:T(8,128)(2,1)} %get-tuple-element.67), channel_id=1, source_target_pairs={{0,1},{1,0},{2,3},{3,2},{4,5},{5,4},{6,7},{7,6},{8,9},{9,8},{10,11... | collective-permute-start | bytes 786440 | tf_op jit(solution)/shard_map/ppermute | solution.py:540
  466.9 26.1 %collective-permute-start.36 = (bf16[8,128,512]{2,1,0:T(8,128)(2,1)S(1)}, bf16[8,128,512]{2,1,0:T(8,128)(2,1)S(1)}, u32[]{:S(2)}, u32[]{:S(2)}) collective-permute-start(bf16[8,128,512]{2,1,0:T(8,128)(2,1)S(1)} %slice_bitcast_fusion.2), channel_id=1, source_target_pairs={{0,2},{1,3},{2,0},{3,1},{4,6},{5,7},{6,4},{7,5},{8,10},{9,11},{10,... | collective-permute-start | bytes 3145736 | tf_op jit(solution)/shard_map/ppermute | solution.py:505
  470.8 44.7 %collective-permute-start.44 = (bf16[8,128,512]{2,1,0:T(8,128)(2,1)S(1)}, bf16[8,128,512]{2,1,0:T(8,128)(2,1)S(1)}, u32[]{:S(2)}, u32[]{:S(2)}) collective-permute-start(bf16[8,128,512]{2,1,0:T(8,128)(2,1)S(1)} %slice_bitcast_fusion), channel_id=1, source_target_pairs={{0,2},{1,3},{2,0},{3,1},{4,6},{5,7},{6,4},{7,5},{8,10},{9,11},{10,... | collective-permute-start | bytes 3145736 | tf_op jit(solution)/shard_map/ppermute | solution.py:505
  474.7 62.0 %collective-permute-start.28 = (bf16[8,128,512]{2,1,0:T(8,128)(2,1)S(1)}, bf16[8,128,512]{2,1,0:T(8,128)(2,1)S(1)}, u32[]{:S(2)}, u32[]{:S(2)}) collective-permute-start(bf16[8,128,512]{2,1,0:T(8,128)(2,1)S(1)} %slice_bitcast_fusion.4), channel_id=1, source_target_pairs={{0,2},{1,3},{2,0},{3,1},{4,6},{5,7},{6,4},{7,5},{8,10},{9,11},{10,... | collective-permute-start | bytes 3145736 | tf_op jit(solution)/shard_map/ppermute | solution.py:505
  493.5 44.7 %collective-permute-start.37 = (bf16[512,512]{1,0:T(8,128)(2,1)S(1)}, bf16[512,512]{1,0:T(8,128)(2,1)S(1)}, u32[]{:S(2)}, u32[]{:S(2)}) collective-permute-start(bf16[512,512]{1,0:T(8,128)(2,1)S(1)} %bitcast.194), channel_id=1, source_target_pairs={{0,4},{4,0},{8,12},{12,8},{16,20},{20,16},{24,28},{28,24},{1,5},{5... | collective-permute-start | bytes 1572872 | tf_op jit(solution)/shard_map/ppermute | solution.py:505
  515.9 23.3 %collective-permute-start.45 = (bf16[512,512]{1,0:T(8,128)(2,1)S(1)}, bf16[512,512]{1,0:T(8,128)(2,1)S(1)}, u32[]{:S(2)}, u32[]{:S(2)}) collective-permute-start(bf16[512,512]{1,0:T(8,128)(2,1)S(1)} %bitcast.195), channel_id=1, source_target_pairs={{0,4},{4,0},{8,12},{12,8},{16,20},{20,16},{24,28},{28,24},{1,5},{5... | collective-permute-start | bytes 1572872 | tf_op jit(solution)/shard_map/ppermute | solution.py:505
  537.2 12.8 %collective-permute-start.29 = (bf16[512,512]{1,0:T(8,128)(2,1)S(1)}, bf16[512,512]{1,0:T(8,128)(2,1)S(1)}, u32[]{:S(2)}, u32[]{:S(2)}) collective-permute-start(bf16[512,512]{1,0:T(8,128)(2,1)S(1)} %bitcast.196), channel_id=1, source_target_pairs={{0,4},{4,0},{8,12},{12,8},{16,20},{20,16},{24,28},{28,24},{1,5},{5... | collective-permute-start | bytes 1572872 | tf_op jit(solution)/shard_map/ppermute | solution.py:505
  538.4 12.6 %collective-permute-start.38 = (bf16[256,512]{1,0:T(8,128)(2,1)S(1)}, bf16[256,512]{1,0:T(8,128)(2,1)S(1)}, u32[]{:S(2)}, u32[]{:S(2)}) collective-permute-start(bf16[256,512]{1,0:T(8,128)(2,1)S(1)} %broadcast_select_fusion.20), channel_id=1, source_target_pairs={{0,8},{4,12},{8,0},{12,4},{16,24},{20,28},{24,16},{28,20},{1,9},{5... | collective-permute-start | bytes 786440 | tf_op jit(solution)/shard_map/ppermute | solution.py:505
  539.5 13.7 %collective-permute-start.46 = (bf16[256,512]{1,0:T(8,128)(2,1)S(1)}, bf16[256,512]{1,0:T(8,128)(2,1)S(1)}, u32[]{:S(2)}, u32[]{:S(2)}) collective-permute-start(bf16[256,512]{1,0:T(8,128)(2,1)S(1)} %broadcast_select_fusion.17), channel_id=1, source_target_pairs={{0,8},{4,12},{8,0},{12,4},{16,24},{20,28},{24,16},{28,20},{1,9},{5... | collective-permute-start | bytes 786440 | tf_op jit(solution)/shard_map/ppermute | solution.py:505
  550.2 10.6 %collective-permute-start.30 = (bf16[256,512]{1,0:T(8,128)(2,1)S(1)}, bf16[256,512]{1,0:T(8,128)(2,1)S(1)}, u32[]{:S(2)}, u32[]{:S(2)}) collective-permute-start(bf16[256,512]{1,0:T(8,128)(2,1)S(1)} %broadcast_select_fusion.23), channel_id=1, source_target_pairs={{0,8},{4,12},{8,0},{12,4},{16,24},{20,28},{24,16},{28,20},{1,9},{5... | collective-permute-start | bytes 786440 | tf_op jit(solution)/shard_map/ppermute | solution.py:505
  551.1 10.2 %collective-permute-start.39 = (bf16[128,512]{1,0:T(8,128)(2,1)S(1)}, bf16[128,512]{1,0:T(8,128)(2,1)S(1)}, u32[]{:S(2)}, u32[]{:S(2)}) collective-permute-start(bf16[128,512]{1,0:T(8,128)(2,1)S(1)} %broadcast_select_fusion.33), channel_id=1, source_target_pairs={{0,16},{4,20},{8,24},{12,28},{16,0},{20,4},{24,8},{28,12},{1,17},{... | collective-permute-start | bytes 393224 | tf_op jit(solution)/shard_map/ppermute | solution.py:505
  553.3 19.2 %collective-permute-start.47 = (bf16[128,512]{1,0:T(8,128)(2,1)S(1)}, bf16[128,512]{1,0:T(8,128)(2,1)S(1)}, u32[]{:S(2)}, u32[]{:S(2)}) collective-permute-start(bf16[128,512]{1,0:T(8,128)(2,1)S(1)} %broadcast_select_fusion.30), channel_id=1, source_target_pairs={{0,16},{4,20},{8,24},{12,28},{16,0},{20,4},{24,8},{28,12},{1,17},{... | collective-permute-start | bytes 393224 | tf_op jit(solution)/shard_map/ppermute | solution.py:505
  560.9 14.4 %collective-permute-start.31 = (bf16[128,512]{1,0:T(8,128)(2,1)S(1)}, bf16[128,512]{1,0:T(8,128)(2,1)S(1)}, u32[]{:S(2)}, u32[]{:S(2)}) collective-permute-start(bf16[128,512]{1,0:T(8,128)(2,1)S(1)} %broadcast_select_fusion.36), channel_id=1, source_target_pairs={{0,16},{4,20},{8,24},{12,28},{16,0},{20,4},{24,8},{28,12},{1,17},{... | collective-permute-start | bytes 393224 | tf_op jit(solution)/shard_map/ppermute | solution.py:505
  561.4 21.0 %collective-permute-start.40 = (bf16[128,512]{1,0:T(8,128)(2,1)S(1)}, bf16[128,512]{1,0:T(8,128)(2,1)S(1)}, u32[]{:S(2)}, u32[]{:S(2)}) collective-permute-start(bf16[128,512]{1,0:T(8,128)(2,1)S(1)} %add_convert_fusion.9), channel_id=1, source_target_pairs={{0,16},{4,20},{8,24},{12,28},{16,0},{20,4},{24,8},{28,12},{1,17},{... | collective-permute-start | bytes 393224 | tf_op jit(solution)/shard_map/ppermute | solution.py:505
  572.6 12.6 %collective-permute-start.48 = (bf16[128,512]{1,0:T(8,128)(2,1)S(1)}, bf16[128,512]{1,0:T(8,128)(2,1)S(1)}, u32[]{:S(2)}, u32[]{:S(2)}) collective-permute-start(bf16[128,512]{1,0:T(8,128)(2,1)S(1)} %add_convert_fusion.8), channel_id=1, source_target_pairs={{0,16},{4,20},{8,24},{12,28},{16,0},{20,4},{24,8},{28,12},{1,17},{... | collective-permute-start | bytes 393224 | tf_op jit(solution)/shard_map/ppermute | solution.py:505
  575.4 11.3 %collective-permute-start.32 = (bf16[128,512]{1,0:T(8,128)(2,1)S(1)}, bf16[128,512]{1,0:T(8,128)(2,1)S(1)}, u32[]{:S(2)}, u32[]{:S(2)}) collective-permute-start(bf16[128,512]{1,0:T(8,128)(2,1)S(1)} %add_convert_fusion.10), channel_id=1, source_target_pairs={{0,16},{4,20},{8,24},{12,28},{16,0},{20,4},{24,8},{28,12},{1,17},{... | collective-permute-start | bytes 393224 | tf_op jit(solution)/shard_map/ppermute | solution.py:505
  582.5 9.9 %collective-permute-start.41 = (bf16[256,512]{1,0:T(8,128)(2,1)S(1)}, bf16[256,512]{1,0:T(8,128)(2,1)S(1)}, u32[]{:S(2)}, u32[]{:S(2)}) collective-permute-start(bf16[256,512]{1,0:T(8,128)(2,1)S(1)} %pad_maximum_fusion.11), channel_id=1, source_target_pairs={{0,8},{4,12},{8,0},{12,4},{16,24},{20,28},{24,16},{28,20},{1,9},{5... | collective-permute-start | bytes 786440 | tf_op jit(solution)/shard_map/ppermute | solution.py:505
  585.3 12.7 %collective-permute-start.49 = (bf16[256,512]{1,0:T(8,128)(2,1)S(1)}, bf16[256,512]{1,0:T(8,128)(2,1)S(1)}, u32[]{:S(2)}, u32[]{:S(2)}) collective-permute-start(bf16[256,512]{1,0:T(8,128)(2,1)S(1)} %pad_maximum_fusion.12), channel_id=1, source_target_pairs={{0,8},{4,12},{8,0},{12,4},{16,24},{20,28},{24,16},{28,20},{1,9},{5... | collective-permute-start | bytes 786440 | tf_op jit(solution)/shard_map/ppermute | solution.py:505
  586.8 15.2 %collective-permute-start.33 = (bf16[256,512]{1,0:T(8,128)(2,1)S(1)}, bf16[256,512]{1,0:T(8,128)(2,1)S(1)}, u32[]{:S(2)}, u32[]{:S(2)}) collective-permute-start(bf16[256,512]{1,0:T(8,128)(2,1)S(1)} %pad_maximum_fusion.10), channel_id=1, source_target_pairs={{0,8},{4,12},{8,0},{12,4},{16,24},{20,28},{24,16},{28,20},{1,9},{5... | collective-permute-start | bytes 786440 | tf_op jit(solution)/shard_map/ppermute | solution.py:505
  592.5 14.9 %collective-permute-start.42 = (bf16[512,512]{1,0:T(8,128)(2,1)S(1)}, bf16[512,512]{1,0:T(8,128)(2,1)S(1)}, u32[]{:S(2)}, u32[]{:S(2)}) collective-permute-start(bf16[512,512]{1,0:T(8,128)(2,1)S(1)} %pad_maximum_fusion.7), channel_id=1, source_target_pairs={{0,4},{4,0},{8,12},{12,8},{16,20},{20,16},{24,28},{28,24},{1,5},{5... | collective-permute-start | bytes 1572872 | tf_op jit(solution)/shard_map/ppermute | solution.py:505
  598.1 20.5 %collective-permute-start.50 = (bf16[512,512]{1,0:T(8,128)(2,1)S(1)}, bf16[512,512]{1,0:T(8,128)(2,1)S(1)}, u32[]{:S(2)}, u32[]{:S(2)}) collective-permute-start(bf16[512,512]{1,0:T(8,128)(2,1)S(1)} %pad_maximum_fusion.8), channel_id=1, source_target_pairs={{0,4},{4,0},{8,12},{12,8},{16,20},{20,16},{24,28},{28,24},{1,5},{5... | collective-permute-start | bytes 1572872 | tf_op jit(solution)/shard_map/ppermute | solution.py:505
  602.1 25.4 %collective-permute-start.34 = (bf16[512,512]{1,0:T(8,128)(2,1)S(1)}, bf16[512,512]{1,0:T(8,128)(2,1)S(1)}, u32[]{:S(2)}, u32[]{:S(2)}) collective-permute-start(bf16[512,512]{1,0:T(8,128)(2,1)S(1)} %pad_maximum_fusion.6), channel_id=1, source_target_pairs={{0,4},{4,0},{8,12},{12,8},{16,20},{20,16},{24,28},{28,24},{1,5},{5... | collective-permute-start | bytes 1572872 | tf_op jit(solution)/shard_map/ppermute | solution.py:505
  (85 other events, 600.0 us)

commit v2 on v1

v2 whole, which is shorter than its diff:
```python
import jax
import jax.numpy as jnp
from jax import lax
from jax.experimental import pallas as pl
from jax.experimental.pallas import tpu as pltpu
from jax.sharding import PartitionSpec as P

CODES = 8192
STRIDE = 8
NORM_EPS = 1e-06
COMMIT = 4.0

BF = jnp.bfloat16
F32 = jnp.float32

SEG = 16
HALO = 128
LEAD = 28
CHUNK = 256
VMEM = 60 * 2**20
def cost(micros):
    return pl.CostEstimate(flops=int(micros * 1.15e9), bytes_accessed=0, transcendentals=0)

SIN = (3.1415902692655564, -5.1674066428989045, 2.5440093135845245, -0.5594585999205443)
COS = (0.9999999532244686, -4.934792826917481, 4.0584112640152465, -1.331875904720673, 0.21968809492172123)


def by_powers(square, factors):
    total = factors[-1]
    for factor in factors[-2::-1]:
        total = factor + square * total
    return total


def snake(value, turn, inverse):
    angle = turn * value
    angle = angle - jnp.round(angle)
    square = angle * angle
    part = by_powers(square, SIN)
    return value + (square * part) * (part * inverse)


def snake_parts(value, turn, inverse):
    angle = turn * value
    angle = angle - jnp.round(angle)
    square = angle * angle
    part = by_powers(square, SIN)
    sine2 = (square * part) * (part * inverse)
    double = (angle * part) * (2.0 * by_powers(square, COS))
    return value + sine2, 1.0 + double, (value * double - sine2) * inverse


def terms(value, count):
    parts = []
    for _ in range(count):
        part = value.astype(BF)
        parts.append(part)
        value = value - part.astype(F32)
    return parts


def lanes4(mask):
    return jnp.concatenate([mask] * 4, axis=1)


def own_mask(start, count, span, own):
    row = lax.broadcasted_iota(jnp.int32, (count, 128), 0) + start
    place = (row & (SEG - 1)) * span + (row >> 4)
    return jnp.where((place >= HALO) & (place < HALO + own), 1.0, 0.0).astype(F32)


def fold(values):
    rows, cols = values.shape
    return values.reshape(rows // 8, 8, cols).sum(axis=0)


def load_weights(pieces, member, weights, sems):
    me = lax.axis_index("chan")
    first = (lax.axis_index("frames") & 1) * 4
    own7, own1, near7, near1 = (piece.at[member] for piece in pieces[:4])
    rows = own1.shape[0]

    def place(peer):
        return pl.ds(pl.multiple_of((me ^ peer) * rows, rows), rows)

    moves = [
        (own7, weights.at[pl.ds(0, 7), place(0), :]),
        (own1, weights.at[7, place(0), :]),
        (near7, weights.at[pl.ds(0, 7), place(1), :]),
        (near1, weights.at[7, place(1), :]),
    ]
    if len(pieces) == 6:
        moves += [(pieces[4], weights.at[:, place(2), :]), (pieces[5], weights.at[:, place(3), :])]
    else:
        moves += [
            (pieces[4], weights.at[pl.ds(first, 4), place(2), :]),
            (pieces[5], weights.at[pl.ds(4 - first, 4), place(2), :]),
            (pieces[6], weights.at[pl.ds(first, 4), place(3), :]),
            (pieces[7], weights.at[pl.ds(4 - first, 4), place(3), :]),
        ]
    copies = []
    for piece, target in moves:
        copy = pltpu.make_async_copy(piece, target, sems.at[len(copies)])
        copy.start()
        copies.append(copy)
    return copies


def fill_masks(mask, labels, spacing, rows):
    base = LEAD * SEG
    here = labels[pl.ds(base, rows), :]
    for tap in range(7):
        there = labels[pl.ds(base + (tap - 3) * spacing * SEG, rows), :]
        mask[tap] = jnp.where(there == here, 1.0, 0.0).astype(BF)


def fill_ends(wide, turn, margin, rows):
    edge = margin * SEG
    turn[pl.ds(8, edge + SEG), :] = wide[pl.ds(rows - SEG, edge + SEG), :].astype(F32)
    wide[pl.ds(0, edge), :] = turn[pl.ds(8 + SEG - 1, edge), :].astype(BF)
    turn[pl.ds(8, edge + SEG), :] = wide[pl.ds(edge, edge + SEG), :].astype(F32)
    wide[pl.ds(edge + rows, edge), :] = turn[pl.ds(8 + 1, edge), :].astype(BF)


class Stream:
    def __init__(self, source, target, sems):
        self.source, self.target, self.sems = source, target, sems

    def copy(self, chunk):
        here = pl.ds(chunk * CHUNK, CHUNK)
        return pltpu.make_async_copy(self.source.at[here], self.target.at[here], self.sems.at[chunk])

    def start(self, chunk):
        self.copy(chunk).start()

    def wait(self, chunk):
        self.copy(chunk).wait()


def dot_nt(left, right):
    return lax.dot_general(left, right, (((1,), (1,)), ((), ())), preferred_element_type=F32)


def dot_nn(left, right):
    return lax.dot_general(left, right, (((1,), (0,)), ((), ())), preferred_element_type=F32)


def dot_tn(left, right):
    return lax.dot_general(left, right, (((0,), (0,)), ((), ())), preferred_element_type=F32)


A1, I1, A2, I2, S7, B7, S1, B1 = range(8)


def unit_forward(stream, pieces, member, vecs, labels):
    spacing = 3**member
    rows, chans = stream.shape
    margin = 3 * spacing
    chunks = rows // CHUNK
    wide_rows = rows + 2 * margin * SEG

    def kernel(s_ref, *refs):
        parts, refs = refs[: len(pieces)], refs[len(pieces) :]
        (
            v_ref, l_ref, out_ref, mid_ref, wide_ref, w1_ref,
            weights, wide, turn, mask, stream_in, result, middle, total0, total1, sems, s_sems, o_sems, m_sems, end_sems,
        ) = refs
        incoming = Stream(s_ref, stream_in, s_sems)
        outgoing, outgoing_mid = Stream(result, out_ref, o_sems), Stream(middle, mid_ref, m_sems)
        for chunk in range(chunks):
            incoming.start(chunk)
        copies = load_weights(parts, member, weights, sems)
        fill_masks(mask, l_ref, spacing, rows)
        for chunk in range(chunks):
            incoming.wait(chunk)
            here = pl.ds(chunk * CHUNK, CHUNK)
            act = snake(stream_in[here, :], v_ref[A1 : A1 + 1, :], v_ref[I1 : I1 + 1, :])
            wide[pl.ds(margin * SEG + chunk * CHUNK, CHUNK), :] = act.astype(BF)
        fill_ends(wide, turn, margin, rows)
        keep_wide = pltpu.make_async_copy(wide, wide_ref, end_sems.at[0])
        keep_wide.start()
        for copy in copies:
            copy.wait()
        keep_w1 = pltpu.make_async_copy(weights.at[7], w1_ref, end_sems.at[1])
        keep_w1.start()

        def convolve(chunk, total_ref):
            total = None
            for tap in range(7):
                columns = wide[pl.ds(chunk * CHUNK + tap * spacing * SEG, CHUNK), :]
                if tap != 3:
                    columns = columns * lanes4(mask[tap, pl.ds(chunk * CHUNK, CHUNK), :])
                term = dot_nt(columns, weights[tap])
                total = term if total is None else total + term
            total_ref[...] = total

        def finish(chunk, total_ref):
            here = pl.ds(chunk * CHUNK, CHUNK)
            value = total_ref[...] * v_ref[S7 : S7 + 1, :] + v_ref[B7 : B7 + 1, :]
            middle[here, :] = value
            second = snake(value, v_ref[A2 : A2 + 1, :], v_ref[I2 : I2 + 1, :]).astype(BF)
            term = dot_nt(second, weights[7])
            result[here, :] = stream_in[here, :] + term * v_ref[S1 : S1 + 1, :] + v_ref[B1 : B1 + 1, :]

        totals = (total0, total1)
        convolve(0, totals[0])
        for chunk in range(chunks):
            if chunk + 1 < chunks:
                convolve(chunk + 1, totals[(chunk + 1) % 2])
            finish(chunk, totals[chunk % 2])
            outgoing_mid.start(chunk)
            outgoing.start(chunk)
        keep_wide.wait()
        keep_w1.wait()
        for chunk in range(chunks):
            outgoing_mid.wait(chunk)
            outgoing.wait(chunk)

    whole = pl.BlockSpec(memory_space=pltpu.VMEM)
    held = pl.BlockSpec(memory_space=pl.ANY)
    return pl.pallas_call(
        kernel,
        out_shape=[
            jax.ShapeDtypeStruct((rows, chans), F32),
            jax.ShapeDtypeStruct((rows, chans), F32),
            jax.ShapeDtypeStruct((wide_rows, chans), BF),
            jax.ShapeDtypeStruct((chans, chans), BF),
        ],
        in_specs=[held] * (1 + len(pieces)) + [whole] * 2,
        out_specs=[held] * 4,
        scratch_shapes=[
            pltpu.VMEM((8, chans, chans), BF),
            pltpu.VMEM((wide_rows, chans), BF),
            pltpu.VMEM((margin * SEG + SEG + 16, chans), F32),
            pltpu.VMEM((7, rows, 128), BF),
            pltpu.VMEM((rows, chans), F32),
            pltpu.VMEM((rows, chans), F32),
            pltpu.VMEM((rows, chans), F32),
            pltpu.VMEM((CHUNK, chans), F32),
            pltpu.VMEM((CHUNK, chans), F32),
            pltpu.SemaphoreType.DMA((8,)),
            pltpu.SemaphoreType.DMA((chunks,)),
            pltpu.SemaphoreType.DMA((chunks,)),
            pltpu.SemaphoreType.DMA((chunks,)),
            pltpu.SemaphoreType.DMA((2,)),
        ],
        compiler_params=pltpu.CompilerParams(vmem_limit_bytes=VMEM),
        cost_estimate=cost(12),
        name=f"unit_forward_{spacing}",
    )(stream, *pieces, vecs, labels)


class Names:
    def __init__(self, names, refs):
        self.__dict__.update(zip(names, refs, strict=True))


def units_back(vecs, labels, own, rows, chans, into=None, weights=None, others=()):
    span = rows // SEG
    part = chans // 4
    chunks = rows // CHUNK
    held, whole = pl.BlockSpec(memory_space=pl.ANY), pl.BlockSpec(memory_space=pltpu.VMEM)
    f32_rows, bf_rows = jax.ShapeDtypeStruct((rows, chans), F32), jax.ShapeDtypeStruct((rows, chans), BF)
    ins, outs, scratch = {"labels": (labels, whole)}, {}, {"mask": pltpu.VMEM((7, rows, 128), BF)}
    name, micros = "units_back", 20
    if into is not None:
        member_c, grad, stream, scaled, pieces = into
        spacing_c = 3**member_c
        margin_c = 3 * spacing_c
        name, micros = f"{name}_into_{spacing_c}", micros + 30
        ins |= {"grad": (grad, held), "stream": (stream, held), "scaled": (scaled, held)}
        ins |= {f"piece{n}": (piece, held) for n, piece in enumerate(pieces)}
        ins["vec_c"] = (vecs[member_c], whole)
        ins |= {f"other{n}": (other, whole) for n, other in enumerate(others)}
        outs |= {"out": (f32_rows, held), "sums_c": (jax.ShapeDtypeStruct((8 + 8 * len(others), chans), F32), whole)}
        scratch |= {
            "weights": pltpu.VMEM((8, chans, chans), BF),
            "wide_c": pltpu.VMEM((rows + 2 * margin_c * SEG, chans), BF),
            "turn": pltpu.VMEM((margin_c * SEG + SEG + 16, chans), F32),
            "total_c": pltpu.VMEM((8, chans), F32),
            "stream_in": pltpu.VMEM((rows, chans), F32),
            "result": pltpu.VMEM((rows, chans), F32),
            "back": pltpu.VMEM((rows, chans), F32),
            "w_sems": pltpu.SemaphoreType.DMA((8,)),
            "s_sems": pltpu.SemaphoreType.DMA((chunks,)),
            "o_sems": pltpu.SemaphoreType.DMA((chunks,)),
            "d_sem": pltpu.SemaphoreType.DMA((1,)),
        }
    else:
        ins["grad"] = (weights[1], held)
    scratch |= {"grad_in": pltpu.VMEM((rows, chans), F32), "g_sems": pltpu.SemaphoreType.DMA((chunks,))}
    if weights is not None:
        member_a, _, middle, wide_act, weight1 = weights
        spacing_a = 3**member_a
        name, micros = f"{name}_weights_{spacing_a}", micros + 14
        ins |= {"middle": (middle, held), "wide": (wide_act, held), "w1": (weight1, whole), "vec_a": (vecs[member_a], whole)}
        outs |= {
            "scaled_out": (bf_rows, held),
            "keep": (jax.ShapeDtypeStruct((2, 8, part, chans), BF), held),
            "send": (jax.ShapeDtypeStruct((2, 8, part, chans), BF), held),
            "sums_a": (jax.ShapeDtypeStruct((8, chans), F32), whole),
        }
        scratch |= {
            "middle_in": pltpu.VMEM((rows, chans), F32),
            "wide_a": pltpu.VMEM(wide_act.shape, BF),
            "scaled_a": pltpu.VMEM((rows, chans), BF),
            "low_t": pltpu.VMEM((chans, rows), BF),
            "mid_t": pltpu.VMEM((chans, rows), BF),
            "second": pltpu.VMEM((rows, chans), BF),
            "results": pltpu.VMEM((8, chans, chans), BF),
            "total_a": pltpu.VMEM((3, 8, chans), F32),
            "m_sems": pltpu.SemaphoreType.DMA((chunks,)),
            "x_sem": pltpu.SemaphoreType.DMA((1,)),
            "a_sems": pltpu.SemaphoreType.DMA((chunks,)),
            "r_sems": pltpu.SemaphoreType.DMA((8, 4)),
        }

    def go_into(r):
        get_scaled = pltpu.make_async_copy(r.scaled, r.wide_c.at[pl.ds(margin_c * SEG, rows)], r.d_sem.at[0])
        get_scaled.start()
        parts = [getattr(r, f"piece{n}") for n in range(len(pieces))]
        copies = load_weights(parts, member_c, r.weights, r.w_sems)
        incoming_grad, incoming = Stream(r.grad, r.grad_in, r.g_sems), Stream(r.stream, r.stream_in, r.s_sems)
        outgoing = Stream(r.result, r.out, r.o_sems)
        fill_masks(r.mask, r.labels, spacing_c, rows)
        r.total_c[...] = jnp.zeros_like(r.total_c)
        get_scaled.wait()
        fill_ends(r.wide_c, r.turn, margin_c, rows)
        for copy in copies:
            copy.wait()
        for chunk in range(chunks):
            incoming.start(chunk)
            incoming_grad.start(chunk)
        if weights is not None:
            start_weights(r)
        for chunk in range(chunks):
            total = None
            for tap in range(7):
                columns = r.wide_c[pl.ds(chunk * CHUNK + (6 - tap) * spacing_c * SEG, CHUNK), :]
                if tap != 3:
                    columns = columns * lanes4(r.mask[6 - tap, pl.ds(chunk * CHUNK, CHUNK), :])
                term = dot_nn(columns, r.weights[tap])
                total = term if total is None else total + term
            r.back[pl.ds(chunk * CHUNK, CHUNK), :] = total

        @pl.loop(0, chunks)
        def _(chunk):
            incoming.wait(chunk)
            incoming_grad.wait(chunk)
            here = pl.ds(chunk * CHUNK, CHUNK)
            total = r.back[here, :]
            mine = lanes4(own_mask(chunk * CHUNK, CHUNK, span, own))
            _, slope, by_alpha = snake_parts(r.stream_in[here, :], r.vec_c[A1 : A1 + 1, :], r.vec_c[I1 : I1 + 1, :])
            r.total_c[...] += fold(total * by_alpha * mine)
            r.result[here, :] = r.grad_in[here, :] + total * slope
            outgoing.start(chunk)

        r.sums_c[0:8, :] = jnp.concatenate(
            [r.total_c[...].sum(axis=0, keepdims=True), jnp.zeros((7, chans), F32)], axis=0
        )
        for n in range(len(others)):
            r.sums_c[8 * n + 8 : 8 * n + 16, :] = getattr(r, f"other{n}")[...]
        return outgoing

    def start_weights(r):
        incoming_mid = Stream(r.middle, r.middle_in, r.m_sems)
        for chunk in range(chunks):
            incoming_mid.start(chunk)
        pltpu.make_async_copy(r.wide, r.wide_a, r.x_sem.at[0]).start()

    def go_weights(r):
        me = lax.axis_index("chan")
        incoming, incoming_mid = Stream(r.grad, r.grad_in, r.g_sems), Stream(r.middle, r.middle_in, r.m_sems)
        outgoing = Stream(r.scaled_a, r.scaled_out, r.a_sems)
        grads = r.grad_in if into is None else r.result
        fill_masks(r.mask, r.labels, spacing_a, rows)
        r.total_a[...] = jnp.zeros_like(r.total_a)
        for chunk in range(chunks):
            if into is None:
                incoming.wait(chunk)
            incoming_mid.wait(chunk)
            here = pl.ds(chunk * CHUNK, CHUNK)
            mine = lanes4(own_mask(chunk * CHUNK, CHUNK, span, own))
            grad_here = grads[here, :]
            scaled_here = grad_here * r.vec_a[S1 : S1 + 1, :]
            r.low_t[:, here] = (scaled_here * mine).astype(BF).T
            back = dot_nn(scaled_here.astype(BF), r.w1[...])
            value, slope, by_alpha = snake_parts(
                r.middle_in[here, :], r.vec_a[A2 : A2 + 1, :], r.vec_a[I2 : I2 + 1, :]
            )
            r.second[here, :] = value.astype(BF)
            dmiddle = back * slope
            mine_mid = dmiddle * mine
            r.total_a[0] += fold(grad_here * mine)
            r.total_a[1] += fold(mine_mid)
            r.total_a[2] += fold(back * by_alpha * mine)
            r.scaled_a[here, :] = (dmiddle * r.vec_a[S7 : S7 + 1, :]).astype(BF)
            outgoing.start(chunk)
            r.mid_t[:, here] = (mine_mid * r.vec_a[S7 : S7 + 1, :]).astype(BF).T

        r.sums_a[...] = jnp.concatenate(
            [r.total_a[i].sum(axis=0, keepdims=True) for i in range(3)] + [jnp.zeros((5, chans), F32)], axis=0
        )
        r.results[7] = dot_nn(r.low_t[...], r.second[...]).astype(BF)
        pltpu.make_async_copy(r.wide, r.wide_a, r.x_sem.at[0]).wait()
        targets = (r.keep.at[0], r.send.at[0], r.keep.at[1], r.send.at[1])

        def out(tap, p):
            slot = pl.multiple_of((me ^ p) * part, part)
            return pltpu.make_async_copy(
                r.results.at[tap, pl.ds(slot, part), :], targets[p].at[tap], r.r_sems.at[tap, p]
            )

        for p in range(4):
            out(7, p).start()
        for tap in range(7):
            columns = r.wide_a[pl.ds(tap * (spacing_a * SEG), rows), :]
            if tap != 3:
                columns = columns * lanes4(r.mask[tap])
            r.results[tap] = dot_nn(r.mid_t[...], columns).astype(BF)
            for p in range(4):
                out(tap, p).start()
        for tap in range(8):
            for p in range(4):
                out(tap, p).wait()
        for chunk in range(chunks):
            outgoing.wait(chunk)

    def kernel(*refs):
        r = Names([*ins, *outs, *scratch], refs)
        outgoing = None
        if into is None:
            incoming = Stream(r.grad, r.grad_in, r.g_sems)
            for chunk in range(chunks):
                incoming.start(chunk)
            start_weights(r)
        else:
            outgoing = go_into(r)
        if weights is not None:
            go_weights(r)
        if outgoing is not None:
            for chunk in range(chunks):
                outgoing.wait(chunk)

    results = pl.pallas_call(
        kernel,
        out_shape=[shape for shape, _ in outs.values()],
        in_specs=[spec for _, spec in ins.values()],
        out_specs=[spec for _, spec in outs.values()],
        scratch_shapes=list(scratch.values()),
        compiler_params=pltpu.CompilerParams(vmem_limit_bytes=VMEM),
        cost_estimate=cost(micros),
        name=name,
    )(*[value for value, _ in ins.values()])
    return dict(zip(outs, results, strict=True))


def halve(dilated, pointwise):
    units, _, part, chans = dilated.shape

    def kernel(d_ref, q_ref, f0, f1, f2, held, sems, out_sems):
        first = pl.multiple_of((lax.axis_index("frames") & 1) * 4, 4)
        copies = []
        for u in range(units):
            copies.append(pltpu.make_async_copy(d_ref.at[u], held.at[u, pl.ds(0, 7)], sems.at[u]))
            copies.append(pltpu.make_async_copy(q_ref.at[u], held.at[u, 7], sems.at[units + u]))
        for copy in copies:
            copy.start()
        outs = [
            pltpu.make_async_copy(held.at[0, pl.ds(first, 4)], f0, out_sems.at[0]),
            pltpu.make_async_copy(held.at[1, pl.ds(first, 4)], f1, out_sems.at[1]),
            pltpu.make_async_copy(held.at[2], f2, out_sems.at[2]),
        ]
        for u, out in enumerate(outs):
            copies[2 * u].wait()
            copies[2 * u + 1].wait()
            out.start()
        for out in outs:
            out.wait()

    held = pl.BlockSpec(memory_space=pl.ANY)
    return pl.pallas_call(
        kernel,
        out_shape=[
            jax.ShapeDtypeStruct((4, part, chans), BF),
            jax.ShapeDtypeStruct((4, part, chans), BF),
            jax.ShapeDtypeStruct((8, part, chans), BF),
        ],
        in_specs=[held] * 2,
        out_specs=[held] * 3,
        scratch_shapes=[
            pltpu.VMEM((units, 8, part, chans), BF),
            pltpu.SemaphoreType.DMA((2 * units,)),
            pltpu.SemaphoreType.DMA((units,)),
        ],
        compiler_params=pltpu.CompilerParams(vmem_limit_bytes=VMEM),
        cost_estimate=cost(0.1),
        name="halve",
    )(dilated, pointwise)


def cut(signal):
    part, extent = signal.shape
    own = extent // 4

    def kernel(s_ref, p0, p1, p2, p3, e0, e1, e2, e3, low):
        me = lax.axis_index("chan")
        low[...] = s_ref[...].astype(BF)
        for p, (piece, end) in enumerate(((p0, e0), (p1, e1), (p2, e2), (p3, e3))):
            owner = me ^ p
            start = pl.multiple_of(owner * own, own)
            piece[:, HALO : HALO + own] = low[:, pl.ds(start, own)]
            before = pl.multiple_of(jnp.maximum(start - HALO, 0), HALO)
            piece[:, 0:HALO] = low[:, pl.ds(before, HALO)]
            behind = pl.multiple_of(jnp.minimum(start + own, extent - HALO), HALO)
            piece[:, HALO + own : 2 * HALO + own] = low[:, pl.ds(behind, HALO)]
            outer = pl.multiple_of(jnp.where(owner == 0, extent - HALO, 0), HALO)
            end[...] = low[:, pl.ds(outer, HALO)]

    whole = pl.BlockSpec(memory_space=pltpu.VMEM)
    outs = pl.pallas_call(
        kernel,
        out_shape=[jax.ShapeDtypeStruct((part, own + 2 * HALO), BF)] * 4 + [jax.ShapeDtypeStruct((part, HALO), BF)] * 4,
        in_specs=[whole],
        out_specs=[whole] * 8,
        scratch_shapes=[pltpu.VMEM((part, extent), BF)],
        compiler_params=pltpu.CompilerParams(vmem_limit_bytes=VMEM),
        cost_estimate=cost(0.1),
        name="cut",
    )(signal)
    return outs[0:4], outs[4:8]


def enter(pieces, ends, own):
    part, count = pieces[0].shape
    span = count // SEG

    def kernel(p0, p1, p2, p3, e0, e1, e2, e3, out_ref, turned, placed):
        me = lax.axis_index("chan")
        for p, (piece, end) in enumerate(((p0, e0), (p1, e1), (p2, e2), (p3, e3))):
            turned[...] = piece[...].astype(F32).T

            @pl.when(me == 0)
            def _(end=end):
                turned[0:HALO, :] = end[...].astype(F32).T

            @pl.when(me == 3)
            def _(end=end):
                turned[HALO + own : 2 * HALO + own, :] = end[...].astype(F32).T

            for a in range(SEG):
                placed[pl.ds(a, span, stride=SEG), :] = turned[pl.ds(a * span, span), :]
            out_ref[:, pl.ds(pl.multiple_of((me ^ p) * part, part), part)] = placed[...]

    whole = pl.BlockSpec(memory_space=pltpu.VMEM)
    return pl.pallas_call(
        kernel,
        out_shape=jax.ShapeDtypeStruct((count, 4 * part), F32),
        in_specs=[whole] * 8,
        out_specs=whole,
        scratch_shapes=[pltpu.VMEM((count, part), F32)] * 2,
        compiler_params=pltpu.CompilerParams(vmem_limit_bytes=VMEM),
        cost_estimate=cost(0.1),
        name="enter",
    )(*pieces, *ends)


def lane_sums(squares):
    return jnp.sum(squares.T, axis=0, keepdims=True)


def vectors(dilated, pointwise, gains7, gains1, bias7, bias1, first, second, last, project, cotangent):
    units, taps, part, chans = dilated.shape
    own_frames = cotangent.shape[1] // 4

    def kernel(d_ref, q_ref, g7, g1, b7, b1, a1, a2, a3, p_ref, t_ref, o0, o1, o2, o3, out_ref, pulled):
        out_ref[...] = jnp.zeros_like(out_ref)
        for u in range(units):
            total = jnp.zeros((part, 128), F32)
            for tap in range(taps):
                value = d_ref[u, tap].astype(F32)
                value = value * value
                for g in range(chans // 128):
                    total = total + value[:, g * 128 : (g + 1) * 128]
            value = q_ref[u].astype(F32)
            value = value * value
            total1 = jnp.zeros((part, 128), F32)
            for g in range(chans // 128):
                total1 = total1 + value[:, g * 128 : (g + 1) * 128]
            here = slice(u, u + 1)
            rows = (
                a1[here, :] * (1.0 / jnp.pi),
                1.0 / a1[here, :],
                a2[here, :] * (1.0 / jnp.pi),
                1.0 / a2[here, :],
                g7[here, :] * lax.rsqrt(lane_sums(total) + NORM_EPS),
                b7[here, :],
                g1[here, :] * lax.rsqrt(lane_sums(total1) + NORM_EPS),
                b1[here, :],
            )
            for n, row in enumerate(rows):
                out_ref[8 * u + n : 8 * u + n + 1, :] = row
        out_ref[8 * units : 8 * units + 1, :] = a3[...] * (1.0 / jnp.pi)
        out_ref[8 * units + 1 : 8 * units + 2, :] = 1.0 / a3[...]
        pulled[...] = dot_tn(p_ref[...], t_ref[...])[0:8, :]
        me = lax.axis_index("chan")
        for p, piece in enumerate((o0, o1, o2, o3)):
            piece[0 : 8 * units + 8, :] = out_ref[...]
            frames = pl.ds(pl.multiple_of((me ^ p) * own_frames, own_frames), own_frames)
            piece[8 * units + 8 : 8 * units + 16, :] = pulled[:, frames]

    whole = pl.BlockSpec(memory_space=pltpu.VMEM)
    return pl.pallas_call(
        kernel,
        out_shape=[jax.ShapeDtypeStruct((8 * units + 16, part), F32)] * 4,
        in_specs=[whole] * 11,
        out_specs=[whole] * 4,
        scratch_shapes=[
            pltpu.VMEM((8 * units + 8, part), F32),
            pltpu.VMEM((8, cotangent.shape[1]), F32),
        ],
        compiler_params=pltpu.CompilerParams(vmem_limit_bytes=VMEM),
        cost_estimate=cost(0.1),
        name="vectors",
    )(dilated, pointwise, gains7, gains1, bias7, bias1, first, second, last[None], project, cotangent)


def merge_strided(strided, gains, bias, project):
    taps, rows, chans = strided.shape

    def kernel(w_ref, g_ref, b_ref, p_ref, out_ref, norm_ref):
        total = jnp.zeros((rows, 128), F32)
        for tap in range(taps):
            value = w_ref[tap].astype(F32)
            value = value * value
            for g in range(chans // 128):
                total = total + value[:, g * 128 : (g + 1) * 128]
        inverse = lax.rsqrt(lane_sums(total) + NORM_EPS)
        scale = g_ref[...] * inverse
        norm_ref[...] = jnp.zeros_like(norm_ref)
        norm_ref[0:1, :] = scale
        norm_ref[1:2, :] = scale * inverse * inverse
        norm_ref[2:3, :] = inverse
        plain = p_ref[...].astype(F32)
        scaled = plain * scale
        split = jnp.concatenate(terms(scaled, 3), axis=0)
        for tap in range(taps):
            three = dot_nn(split, w_ref[tap])
            out_ref[8 * tap : 8 * tap + 8, :] = three[0:8] + three[8:16] + three[16:24]
        shift = jnp.sum(plain * b_ref[...], axis=1, keepdims=True)
        out_ref[8 * taps : 8 * taps + 8, :] = jnp.broadcast_to(shift, (8, chans))

    whole = pl.BlockSpec(memory_space=pltpu.VMEM)
    return pl.pallas_call(
        kernel,
        out_shape=[jax.ShapeDtypeStruct((8 * taps + 8, chans), F32), jax.ShapeDtypeStruct((8, rows), F32)],
        in_specs=[whole] * 4,
        out_specs=[whole] * 2,
        compiler_params=pltpu.CompilerParams(vmem_limit_bytes=VMEM),
        cost_estimate=cost(0.1),
        name="merge_strided",
    )(strided, gains[None], bias[None], project)


def look_up(wanted, codebook, project, cotangent, near_count):
    count = wanted.shape[0]
    codes = codebook.shape[1]
    rows, frames = cotangent.shape
    step = 512

    def kernel(i_ref, c_ref, p_ref, t_ref, near_ref, out_ref, sum_ref, found):
        found[...] = jnp.zeros_like(found)
        lane = lax.broadcasted_iota(jnp.int32, (count, 128), 1)

        @pl.loop(0, codes, step=step)
        def _(start):
            start = pl.multiple_of(start, step)
            book = c_ref[:, pl.ds(start, step)]
            book = book * lax.rsqrt(jnp.sum(book * book, axis=0, keepdims=True) + 1.0)
            table = jnp.concatenate(terms(book, 3) + [jnp.zeros((104, step), BF)], axis=0)
            wants = i_ref[...] - start
            hot = jnp.concatenate(
                [jnp.where(wants == lane + g * 128, 1.0, 0.0).astype(BF) for g in range(step // 128)], axis=1
            )
            found[...] += dot_nt(hot, table)

        total = found[...]
        total = total + pltpu.roll(total, 120, 1) + pltpu.roll(total, 112, 1)
        total = jnp.where(lane < 8, total, 0.0)
        near_ref[...] = total[:near_count]
        low = jnp.where((lane >= 8) & (lane < 11), 1.0, total)[near_count:].astype(BF)
        out_ref[...] = dot_nt(p_ref[...], low)
        sum_ref[...] = dot_nn(t_ref[...], low)

    whole = pl.BlockSpec(memory_space=pltpu.VMEM)
    return pl.pallas_call(
        kernel,
        out_shape=[
            jax.ShapeDtypeStruct((near_count, 128), F32),
            jax.ShapeDtypeStruct((rows, frames), F32),
            jax.ShapeDtypeStruct((rows, 128), F32),
        ],
        in_specs=[whole] * 4,
        out_specs=[whole] * 3,
        scratch_shapes=[pltpu.VMEM((count, 128), F32)],
        compiler_params=pltpu.CompilerParams(vmem_limit_bytes=VMEM),
        cost_estimate=cost(0.1),
        name="look_up",
    )(wanted, codebook, project, cotangent)


def code_payload(dchosen, latent, mixed_grad, near, place, refill, after_this):
    count = dchosen.shape[0]
    taps, _, chans = mixed_grad.shape
    blocks, step = refill.shape

    rows = 24 * blocks + 8 * taps
    quarter = rows // 4

    def kernel(d_ref, l_ref, m_ref, n_ref, p_ref, r_ref, _, o0, o1, o2, o3, out_ref):
        lane = lax.broadcasted_iota(jnp.int32, (count, 128), 1)
        owned = p_ref[...] >= 0
        grads = d_ref[...]
        high = grads.astype(BF).astype(F32)
        left = high + pltpu.roll(grads - high, 8, 1) + jnp.where((lane == 16) & owned, 1.0, 0.0)
        left = left.astype(BF)
        right = l_ref[...].astype(BF)

        @pl.loop(0, blocks)
        def _(block):
            wants = n_ref[...] - block * step
            hot = jnp.concatenate(
                [jnp.where(wants == lane + g * 128, 1.0, 0.0).astype(BF) for g in range(step // 128)], axis=1
            )
            into = dot_tn(left, hot)
            wanted = r_ref[pl.ds(block, 1), :]
            hot = jnp.concatenate(
                [
                    jnp.where(p_ref[...] == wanted[:, g * 128 : (g + 1) * 128], 1.0, 0.0).astype(BF)
                    for g in range(step // 128)
                ],
                axis=1,
            )
            picked = dot_tn(right, hot)
            start = pl.multiple_of(block * 24, 8)
            out_ref[pl.ds(start, 24), :] = jnp.concatenate(
                [into[0:8] + into[8:16], picked[0:8], into[16:24]], axis=0
            )

        for tap in range(taps):
            out_ref[24 * blocks + 8 * tap : 24 * blocks + 8 * tap + 8, :] = m_ref[tap]
        me = lax.axis_index("chan")
        for p, piece in enumerate((o0, o1, o2, o3)):
            piece[...] = out_ref[pl.ds(pl.multiple_of((me ^ p) * quarter, 8), quarter), :].astype(BF)

    whole = pl.BlockSpec(memory_space=pltpu.VMEM)
    held = pl.BlockSpec(memory_space=pl.ANY)
    return pl.pallas_call(
        kernel,
        out_shape=[jax.ShapeDtypeStruct((quarter, chans), BF)] * 4,
        in_specs=[whole] * 6 + [held],
        out_specs=[whole] * 4,
        scratch_shapes=[pltpu.VMEM((rows, chans), F32)],
        compiler_params=pltpu.CompilerParams(vmem_limit_bytes=VMEM),
        cost_estimate=cost(0.1),
        name="code_payload",
    )(dchosen, latent, mixed_grad, near, place, refill, after_this)


def strided_back(strided, mixed_grad, project, norms):
    taps, rows, chans = strided.shape
    group = 4

    def kernel(w_ref, m_ref, p_ref, n_ref, out_ref, vec_ref, total, factor, split):
        phase, step = pl.program_id(0), pl.program_id(1)

        @pl.when((phase == 0) & (step == 0))
        def _():
            total[...] = jnp.zeros_like(total)

        @pl.when(phase == 0)
        def _():
            meeting = total[...]
            for tap in range(group):
                meeting = meeting + dot_nt(m_ref[tap], w_ref[tap])
            total[...] = meeting

        @pl.when((phase == 1) & (step == 0))
        def _():
            plain = p_ref[...].astype(F32)
            along = jnp.sum(plain * total[...], axis=0, keepdims=True)
            vec_ref[...] = jnp.zeros_like(vec_ref)
            vec_ref[0:8, :] = total[...] * n_ref[0:1, :]
            vec_ref[8:9, :] = along * n_ref[2:3, :]
            factor[...] = jnp.broadcast_to(along * n_ref[1:2, :], (128, rows)).T
            split[...] = jnp.concatenate(terms(plain * n_ref[0:1, :], 3), axis=0)

        @pl.when(phase == 1)
        def _():
            for tap in range(group):
                three = jnp.concatenate([m_ref[tap]] * 3, axis=0)
                out_ref[tap] = dot_tn(split[...], three) - w_ref[tap].astype(F32) * lanes4(factor[...])

    whole = pl.BlockSpec(memory_space=pltpu.VMEM)
    return pl.pallas_call(
        kernel,
        grid=(2, taps // group),
        out_shape=[jax.ShapeDtypeStruct((taps, rows, chans), F32), jax.ShapeDtypeStruct((16, rows), F32)],
        in_specs=[
            pl.BlockSpec((group, rows, chans), lambda phase, step: (step, 0, 0)),
            pl.BlockSpec((group, 8, chans), lambda phase, step: (step, 0, 0)),
            whole,
            whole,
        ],
        out_specs=[
            pl.BlockSpec((group, rows, chans), lambda phase, step: (phase * step, 0, 0)),
            pl.BlockSpec((16, rows), lambda phase, step: (0, 0)),
        ],
        scratch_shapes=[pltpu.VMEM((8, rows), F32), pltpu.VMEM((rows, 128), F32), pltpu.VMEM((24, rows), BF)],
        compiler_params=pltpu.CompilerParams(vmem_limit_bytes=VMEM),
        cost_estimate=cost(0.1),
        name="strided_back",
    )(strided, mixed_grad, project, norms)


def norm_back(total, dilated, pointwise, gains, member, earlier):
    units, _, part, chans = dilated.shape

    def kernel(*refs):
        held, w_ref, q_ref, g_ref = refs[0], refs[1].at[0], refs[2], refs[3].at[0]
        out7, out1, out_g, res7, res1, row_g, sems = refs[-7:]

        def grad_of(tap):
            return held[tap * part : (tap + 1) * part, :].astype(F32)

        def weight_of(tap):
            return (q_ref[0] if tap == 7 else w_ref[tap]).astype(F32)

        def one(taps):
            square = jnp.zeros((part, 128), F32)
            along = jnp.zeros((part, 128), F32)
            for tap in taps:
                value, grad = weight_of(tap), grad_of(tap)
                both, value2 = value * grad, value * value
                for g in range(chans // 128):
                    cols = slice(g * 128, (g + 1) * 128)
                    square = square + value2[:, cols]
                    along = along + both[:, cols]
            square_sum = jnp.sum(square, axis=1, keepdims=True) + NORM_EPS
            factor = jnp.sum(along, axis=1, keepdims=True) / square_sum
            return lane_sums(along), factor

        along, factor = one(range(7))
        row_g[...] = jnp.zeros_like(row_g)
        row_g[0:1, :] = along / g_ref[0:1, :]
        outs = []
        for tap in range(7):
            res7[tap] = grad_of(tap) - weight_of(tap) * factor
            outs.append(pltpu.make_async_copy(res7.at[tap], out7.at[member, tap], sems.at[tap]))
            outs[-1].start()
        along, factor = one((7,))
        row_g[1:2, :] = along / g_ref[1:2, :]
        res1[...] = grad_of(7) - weight_of(7) * factor
        outs.append(pltpu.make_async_copy(res1, out1.at[member], sems.at[7]))
        outs[-1].start()
        outs.append(pltpu.make_async_copy(row_g, out_g.at[member], sems.at[8]))
        outs[-1].start()
        for copy in outs:
            copy.wait()

    whole = pl.BlockSpec(memory_space=pltpu.VMEM)
    held = pl.BlockSpec(memory_space=pl.ANY)
    return pl.pallas_call(
        kernel,
        grid=(1,),
        out_shape=[
            jax.ShapeDtypeStruct((units, 7, part, chans), F32),
            jax.ShapeDtypeStruct((units, part, chans), F32),
            jax.ShapeDtypeStruct((units, 8, part), F32),
        ],
        in_specs=[
            whole,
            pl.BlockSpec((1, 7, part, chans), lambda step: (member, 0, 0, 0)),
            pl.BlockSpec((1, part, chans), lambda step: (member, 0, 0)),
            pl.BlockSpec((1, 2, part), lambda step: (member, 0, 0)),
        ]
        + [held] * len(earlier),
        out_specs=[held] * 3,
        input_output_aliases={4 + n: n for n in range(len(earlier))},
        scratch_shapes=[
            pltpu.VMEM((7, part, chans), F32),
            pltpu.VMEM((part, chans), F32),
            pltpu.VMEM((8, part), F32),
            pltpu.SemaphoreType.DMA((9,)),
        ],
        compiler_params=pltpu.CompilerParams(vmem_limit_bytes=VMEM),
        cost_estimate=cost(0.1),
        name=f"norm_back_{member}",
    )(total, dilated, pointwise, gains, *earlier)


def leave(grad, own):
    rows, chans = grad.shape
    span = rows // SEG
    part = chans // 4

    def kernel(g_ref, o0, o1, o2, o3, ordered, placed):
        me = lax.axis_index("chan")
        for p, out in enumerate((o0, o1, o2, o3)):
            placed[...] = g_ref[:, pl.ds(pl.multiple_of((me ^ p) * part, part), part)]
            for a in range(SEG):
                ordered[pl.ds(a * span, span), :] = placed[pl.ds(a, span, stride=SEG), :]
            out[...] = ordered[pl.ds(HALO, own), :].T.astype(out.dtype)

    whole = pl.BlockSpec(memory_space=pltpu.VMEM)
    return pl.pallas_call(
        kernel,
        out_shape=[jax.ShapeDtypeStruct((part, own), F32)] + [jax.ShapeDtypeStruct((part, own), BF)] * 3,
        in_specs=[whole],
        out_specs=[whole] * 4,
        scratch_shapes=[pltpu.VMEM((rows, part), F32)] * 2,
        compiler_params=pltpu.CompilerParams(vmem_limit_bytes=VMEM),
        cost_estimate=cost(0.1),
        name="leave",
    )(grad)


def bottleneck(stream, merged, vecs, labels, chosen, picked_grad, own):
    rows, chans = stream.shape
    span = rows // SEG
    groups = span // STRIDE
    count = groups * SEG
    taps = merged.shape[0] // 8 - 1
    edge = 16 * SEG

    def kernel(
        s_ref, w_ref, v_ref, l_ref, c_ref, o_ref, g_ref, lat_ref, dch_ref, m_ref, sum_ref,
        q_ref, wide, full, codes, sums,
    ):
        blank = jnp.zeros((104, chans), BF)
        for tap in range(taps):
            high, rest = terms(w_ref[8 * tap : 8 * tap + 8, :], 2)
            q_ref[tap] = jnp.concatenate([high, high, rest, blank], axis=0)
        shift = jnp.sum(
            jnp.where(
                lax.broadcasted_iota(jnp.int32, (8, 128), 0) == lax.broadcasted_iota(jnp.int32, (8, 128), 1),
                w_ref[8 * taps : 8 * taps + 8, 0:128],
                0.0,
            ),
            axis=0,
            keepdims=True,
        )

        @pl.loop(0, rows, step=CHUNK)
        def _(start):
            start = pl.multiple_of(start, CHUNK)
            act = snake(s_ref[pl.ds(start, CHUNK), :], v_ref[0:1, :], v_ref[1:2, :])
            full[pl.ds(8 + start, CHUNK), :] = act
            wide[pl.ds(edge + start, CHUNK), :] = act.astype(BF)

        wide[pl.ds(0, edge), :] = full[pl.ds(8 + rows - edge - 1, edge), :].astype(BF)
        wide[pl.ds(edge + rows, edge), :] = full[pl.ds(8 + 1, edge), :].astype(BF)

        def tap_mask(tap, first, amount):
            base = (LEAD + first * STRIDE) * SEG
            pieces = []
            for g in range(amount):
                start = base + g * STRIDE * SEG
                there = l_ref[pl.ds(start + (tap - 4) * SEG, SEG), :]
                pieces.append(jnp.where(there == l_ref[pl.ds(start, SEG), :], 1.0, 0.0).astype(F32))
            return jnp.concatenate(pieces, axis=0)

        def tap_columns(tap):
            base = edge + (tap - 4) * SEG
            picked = jnp.concatenate(
                [wide[pl.ds(base + g * STRIDE * SEG, SEG), :] for g in range(groups)], axis=0
            )
            return picked * lanes4(tap_mask(tap, 0, groups).astype(BF))

        total = jnp.zeros((count, 128), F32)
        for tap in range(taps):
            total = total + dot_nt(tap_columns(tap), q_ref[tap])
        lane = lax.broadcasted_iota(jnp.int32, (count, 128), 1)
        latent = jnp.where(lane < 8, total + pltpu.roll(total, 112, 1) + shift + v_ref[2:3, :128], 0.0)
        lat_ref[...] = latent
        inverse = lax.rsqrt(jnp.sum(latent * latent, axis=1, keepdims=True) + 1.0)
        normed = latent * inverse
        spread = (2.0 * COMMIT) * (normed - c_ref[...])
        row = lax.broadcasted_iota(jnp.int32, (count, 128), 0)
        place = (row & (SEG - 1)) * groups + (row >> 4)
        mine = (place >= HALO // STRIDE) & (place < (HALO + own) // STRIDE)
        dch_ref[...] = jnp.where(mine, o_ref[...] - spread, 0.0)
        dlatent = (spread - normed * jnp.sum(normed * spread, axis=1, keepdims=True)) * inverse

        def split(values):
            high = values.astype(BF).astype(F32)
            return high + pltpu.roll(values - high, 8, 1), pltpu.roll(high, 16, 1)

        dmine = jnp.where(mine, dlatent, 0.0)
        sum_ref[1:2, :] = jnp.concatenate([jnp.sum(dmine, axis=0, keepdims=True)] * 4, axis=1)
        pair, _unused = split(dmine)
        pair = pair.astype(BF)
        for tap in range(taps):
            both = dot_tn(pair, tap_columns(tap))
            m_ref[tap] = both[0:8, :] + both[8:16, :]

        pair, again = split(dlatent)
        codes[pl.ds(8 + SEG, count), :] = pair + again
        codes[pl.ds(8, SEG), :] = codes[pl.ds(8 + count - 1, SEG), :]
        codes[pl.ds(8 + SEG + count, SEG), :] = codes[pl.ds(8 + SEG + 1, SEG), :]
        sums[...] = jnp.zeros_like(sums)
        for rest in range(STRIDE):
            total = None
            for tap in (rest - 4, rest + 4, rest + 12):
                if 0 <= tap < taps:
                    hop = (tap - 4 - rest) // STRIDE
                    left = codes[pl.ds(8 + SEG - hop * SEG, count), :] * tap_mask(tap, -hop, groups)
                    term = dot_nn(left.astype(BF), q_ref[tap])
                    total = term if total is None else total + term
            for g in range(groups):
                here = pl.ds((g * STRIDE + rest) * SEG, SEG)
                part = total[g * SEG : (g + 1) * SEG, :]
                value, slope, by_alpha = snake_parts(s_ref[here, :], v_ref[0:1, :], v_ref[1:2, :])
                g_ref[here, :] = part * slope
                mask = lanes4(own_mask((g * STRIDE + rest) * SEG, SEG, span, own))
                sums[...] += fold(part * by_alpha * mask)
        sum_ref[0:1, :] = sums[...].sum(axis=0, keepdims=True)
        sum_ref[2:8, :] = jnp.zeros((6, chans), F32)

    whole = pl.BlockSpec(memory_space=pltpu.VMEM)
    return pl.pallas_call(
        kernel,
        out_shape=[
            jax.ShapeDtypeStruct((rows, chans), F32),
            jax.ShapeDtypeStruct((count, 128), F32),
            jax.ShapeDtypeStruct((count, 128), F32),
            jax.ShapeDtypeStruct((taps, 8, chans), F32),
            jax.ShapeDtypeStruct((8, chans), F32),
        ],
        in_specs=[whole] * 6,
        out_specs=[whole] * 5,
        scratch_shapes=[
            pltpu.VMEM((taps, 128, chans), BF),
            pltpu.VMEM((rows + 2 * edge, chans), BF),
            pltpu.VMEM((rows + 16, chans), F32),
            pltpu.VMEM((count + 2 * SEG + 16, 128), F32),
            pltpu.VMEM((8, chans), F32),
        ],
        compiler_params=pltpu.CompilerParams(vmem_limit_bytes=VMEM),
        cost_estimate=cost(11),
        name="bottleneck",
    )(stream, merged, vecs, labels, chosen, picked_grad)


def swap(value, axis, bit):
    count = lax.axis_size(axis)
    return lax.ppermute(value, axis, [(i, i ^ (1 << bit)) for i in range(count)])


def bits_of(axis):
    count = lax.axis_size(axis)
    return [(axis, bit) for bit in range(count.bit_length() - 1)]


def total_over(value, steps):
    for axis, bit in steps:
        value = value + swap(value, axis, bit)
    return value


def bit_of(axis, bit):
    return (lax.axis_index(axis) >> bit) & 1


def halves_of(value, step):
    axis, bit = step
    half = value.shape[0] // 2
    mine = bit_of(axis, bit)
    kept = lax.dynamic_slice_in_dim(value, mine * half, half)
    return kept, lax.dynamic_slice_in_dim(value, (1 - mine) * half, half).astype(BF)


def add_up(kept, got):
    return (kept.astype(F32) + got.astype(F32)).astype(BF)


def sum_halves(terms_in, rows, step, micros=0.1):
    chans = terms_in[0][0][0].shape[-1]
    flat = [ref for block in terms_in for ref, _ in block]
    half = rows // 2 if step else rows

    def kernel(*refs):
        refs = list(refs)
        ins = [refs.pop(0) for _ in flat]
        outs = refs[: 2 if step else 1]
        total, sems = refs[-2:] if step else (outs[0], None)
        at, start = 0, 0
        for block in terms_in:
            value = None
            for _, index in block:
                ref = ins[at] if index is None else ins[at].at[index]
                term = ref[...].astype(F32)
                value = term if value is None else value + term
                at += 1
            value = value.astype(BF).reshape(-1, chans)
            total[start : start + value.shape[0], :] = value
            start += value.shape[0]
        if start < rows:
            total[start:rows, :] = jnp.zeros((rows - start, chans), BF)
        if step:
            mine = bit_of(*step)
            copies = []
            for n, out in enumerate(outs):
                place = pl.multiple_of((mine if n == 0 else 1 - mine) * half, 16)
                copies.append(pltpu.make_async_copy(total.at[pl.ds(place, half)], out, sems.at[n]))
                copies[-1].start()
            for copy in copies:
                copy.wait()

    def spec(ref, index):
        if index is None:
            return pl.BlockSpec(memory_space=pltpu.VMEM)
        return pl.BlockSpec((1,) + ref.shape[1:], lambda n: (index,) + (0,) * (ref.ndim - 1))

    flat_pairs = [pair for block in terms_in for pair in block]
    terms_in = [[(ref, None if index is None else 0) for ref, index in block] for block in terms_in]
    return pl.pallas_call(
        kernel,
        grid=(1,),
        out_shape=[jax.ShapeDtypeStruct((half, chans), BF)] * (2 if step else 1),
        in_specs=[spec(ref, index) for ref, index in flat_pairs],
        out_specs=[pl.BlockSpec(memory_space=pl.ANY)] * 2 if step else [pl.BlockSpec(memory_space=pltpu.VMEM)],
        scratch_shapes=[pltpu.VMEM((rows, chans), BF), pltpu.SemaphoreType.DMA((2,))] if step else [],
        compiler_params=pltpu.CompilerParams(vmem_limit_bytes=VMEM),
        cost_estimate=cost(micros),
        name="sum_halves",
    )(*flat)


def join(mine, got, step):
    rows, chans = mine.shape

    def kernel(m_ref, g_ref, out_ref):
        upper = bit_of(*step)
        out_ref[pl.ds(pl.multiple_of(upper * rows, 16), rows), :] = m_ref[...]
        out_ref[pl.ds(pl.multiple_of((1 - upper) * rows, 16), rows), :] = g_ref[...]

    whole = pl.BlockSpec(memory_space=pltpu.VMEM)
    return pl.pallas_call(
        kernel,
        out_shape=jax.ShapeDtypeStruct((2 * rows, chans), BF),
        in_specs=[whole] * 2,
        out_specs=whole,
        compiler_params=pltpu.CompilerParams(vmem_limit_bytes=VMEM),
        cost_estimate=cost(0.1),
        name="join",
    )(mine, got)


class Chain:
    def __init__(self, terms_in, rows, steps, micros=0.1):
        self.adds, self.joins = list(steps), list(reversed(steps))
        self.rows = rows
        self.kept, self.sent = sum_halves(terms_in, rows, self.adds[0], micros)
        self.whole = None
        self.left = 2 * len(steps)
        self.start()

    def start(self):
        self.got = swap(self.sent, *(self.adds[0] if self.adds else self.joins[0]))

    def step(self, token):
        got = after(self.got, token)
        self.left -= 1
        if self.adds:
            self.adds.pop(0)
            self.rows //= 2
            terms_in = [[(self.kept, None), (got, None)]]
            if self.adds:
                self.kept, self.sent = sum_halves(terms_in, self.rows, self.adds[0])
            else:
                self.sent = sum_halves(terms_in, self.rows, None)[0]
        else:
            self.sent = self.whole = join(self.sent, got, self.joins.pop(0))
        if self.left:
            self.start()
        return self.sent


def after(value, *others):
    return lax.optimization_barrier((value, *others))[0]


def to_peer(value, peer):
    return lax.ppermute(value, "chan", [(i, i ^ peer) for i in range(4)])


def local(
    signal,
    dilated_dirs,
    dilated_gains,
    dilated_bias,
    snake_first,
    snake_second,
    pointwise_dirs,
    pointwise_gains,
    pointwise_bias,
    snake_last,
    strided_dirs,
    strided_gains,
    strided_bias,
    latent_proj,
    latent_bias,
    codebook,
    output_proj,
    output_bias,
    utterances,
    code_index,
    refill_index,
    cotangent,
):
    part, extent = signal.shape
    chans = 4 * part
    own = extent // 4
    frames = code_index.shape[0]
    own_frames = frames // 4
    whole = lax.axis_size("frames") * extent
    units = dilated_dirs.shape[0]
    span = (own + 2 * HALO) // SEG
    span_frames = span // STRIDE
    extra = HALO // STRIDE
    me = lax.axis_index("chan")
    block = lax.axis_index("frames")
    ring = lax.axis_size("frames")
    origin = block * extent + me * own
    over_chan, over_frames = bits_of("chan"), bits_of("frames")

    halves = halve(dilated_dirs, pointwise_dirs)
    far = [swap(halves[0], "chan", 1)]
    close = [swap(after(dilated_dirs, halves[0]), "chan", 0), swap(after(pointwise_dirs, halves[0]), "chan", 0)]

    project = jnp.concatenate(
        [output_proj] + [term[:, None] for term in terms(output_bias, 3)] + [jnp.zeros((output_bias.shape[0], 117), BF)],
        axis=1,
    )
    packed = vectors(
        after(dilated_dirs, halves[0]), pointwise_dirs, dilated_gains, pointwise_gains, dilated_bias, pointwise_bias,
        snake_first, snake_second, snake_last, project, cotangent,
    )
    packed = [packed[0]] + [to_peer(packed[peer], peer) for peer in (1, 2, 3)]
    code_ends = after(code_index, packed[0])
    around = jnp.concatenate(
        [
            lax.ppermute(code_ends[frames - extra :], "frames", [(i, i + 1) for i in range(ring - 1)]),
            code_index,
            lax.ppermute(code_ends[:extra], "frames", [(i + 1, i) for i in range(ring - 1)]),
        ]
    )

    pieces, ends = cut(after(signal, packed[0]))
    pieces = [pieces[0]] + [to_peer(pieces[peer], peer) for peer in (1, 2, 3)]
    ends = [
        lax.ppermute(
            ends[peer],
            ("frames", "chan"),
            [(4 * (f + 1) + (3 ^ peer), 4 * f + 3) for f in range(ring - 1)]
            + [(4 * f + peer, 4 * (f + 1)) for f in range(ring - 1)],
        )
        for peer in range(4)
    ]
    rest = [swap(far[0], "frames", 0)]
    far_close = [swap(far[0], "chan", 0)]
    rest_close = [swap(rest[0], "chan", 0)]
    for member in (1, 2):
        far.append(swap(after(halves[member], *pieces), "chan", 1))
    lines = packed[0].shape[0] - 8
    vecs = jnp.zeros((lines, chans), F32)
    mine_pulled = None
    for peer in range(4):
        got = packed[peer]
        vecs = lax.dynamic_update_slice(vecs, got[:lines], (0, (me ^ peer) * part))
        mine_pulled = got[lines:] if mine_pulled is None else mine_pulled + got[lines:]
    mine_pulled = jnp.pad(mine_pulled, ((0, 120), (extra, extra)))
    mine_pulled = mine_pulled.reshape(128, SEG, span_frames).transpose(2, 1, 0).reshape(-1, 128)

    bounds = jnp.cumsum(utterances) * STRIDE
    b_place = jnp.arange(-LEAD, span + LEAD, dtype=jnp.int32)
    spots = (origin - HALO + b_place[:, None] + span * jnp.arange(SEG, dtype=jnp.int32)[None, :]).reshape(-1)
    found = jnp.sum((spots[:, None] >= bounds[None, :]).astype(F32), axis=1)
    found = jnp.where((spots >= 0) & (spots < whole), found, -1.0)
    labels = jnp.broadcast_to(found[:, None], (found.shape[0], 128))

    place = (
        jnp.arange(SEG, dtype=jnp.int32)[None, :] * span_frames + jnp.arange(span_frames, dtype=jnp.int32)[:, None]
    ).reshape(-1)
    owned = (place >= extra) & (place < extra + own_frames)
    place = jnp.where(owned, place - extra + block * frames + me * own_frames, -1)
    place = jnp.broadcast_to(place[:, None], (place.shape[0], 128))
    refill = refill_index.reshape(-1, 512)
    near = lax.dynamic_slice_in_dim(around, me * own_frames, own_frames + 2 * extra)
    near = near.reshape(SEG, span_frames).T.reshape(-1)
    wanted = jnp.broadcast_to(jnp.concatenate([near, code_index])[:, None], (near.shape[0] + frames, 128))
    *held, labels, vecs, mine_pulled, place, refill, wanted, _ = lax.optimization_barrier(
        (*pieces, *ends, labels, vecs, mine_pulled, place, refill, wanted, far[0])
    )
    near_rows = wanted[: near.shape[0]]
    stream = enter(held[:4], held[4:], own)

    def unit(member, stream, *far_pieces):
        pieces = (dilated_dirs, pointwise_dirs, *close, *far_pieces)
        vec = vecs[8 * member : 8 * member + 8]
        result, middle, wide, weight1 = unit_forward(stream, pieces, member, vec, labels)
        saved.append((stream, middle, wide, vec, weight1, pieces))
        return result

    saved = []
    stream = unit(0, stream, far[0], rest[0], far_close[0], rest_close[0])
    rest.append(swap(after(far[1], stream), "frames", 0))
    far_close.append(swap(after(far[1], stream), "chan", 0))

    chosen, output, sums_out = look_up(after(wanted, stream), codebook, project, cotangent, near.shape[0])
    rest_close.append(swap(after(rest[1], chosen), "chan", 0))
    stream = unit(1, after(stream, chosen), far[1], rest[1], far_close[1], rest_close[1])
    far_close.append(swap(after(far[2], stream), "chan", 0))
    merged, norms = merge_strided(strided_dirs, strided_gains, strided_bias, after(latent_proj, stream))
    merged = merged + swap(merged, "chan", 0)
    got = swap(merged, "chan", 1)
    stream = unit(2, after(stream, merged), far[2], far_close[2])
    merged = merged + after(got, stream)
    tail_vecs = jnp.concatenate(
        [
            vecs[8 * units : 8 * units + 2],
            jnp.pad(latent_bias, (0, chans - latent_bias.shape[0]))[None],
            jnp.zeros((5, chans), F32),
        ]
    )
    grad, latent, dchosen, mixed_grad, last_sums = bottleneck(
        stream, merged, tail_vecs, labels, chosen, mine_pulled, own
    )

    bit0, bit1 = over_chan

    unit_vecs = [saved[member][3] for member in range(units)]
    rows = grad.shape[0]

    def weights_of(member, grad=None):
        _, middle, wide, _, weight1, _ = saved[member]
        return (member, grad, middle, wide, weight1)

    def into_of(member, grad, scaled):
        return (member, grad, saved[member][0], scaled, saved[member][5])

    back2 = units_back(unit_vecs, labels, own, rows, chans, weights=weights_of(2, grad))
    keep2 = back2["keep"]
    near2 = swap(back2["send"], "chan", 0)
    chain_rows = -(-(8 * part + 128) // (16 * ring)) * 16 * ring
    codes = code_payload(dchosen, latent, mixed_grad, near_rows, place, refill, back2["sums_a"])
    codes = [codes[0]] + [to_peer(codes[peer], peer) for peer in (1, 2, 3)]
    near2 = after(near2, codes[0])
    far2 = add_up(keep2[1], near2[1])
    x2 = swap(far2, "chan", 1)
    back1 = units_back(
        unit_vecs, labels, own, rows, chans, into_of(2, after(grad, far2), back2["scaled_out"]), weights_of(1)
    )
    keep1 = back1["keep"]
    near1 = swap(back1["send"], "chan", 0)
    x2, *codes, _ = lax.optimization_barrier((x2, *codes, back1["sums_a"]))
    chain2 = Chain(
        [[(keep2, 0), (near2, 0), (x2, None)], [(piece, None) for piece in codes]], chain_rows, over_frames, 20
    )
    far1 = add_up(keep1[1], after(near1, chain2.sent)[1])
    x1 = swap(far1, "chan", 1)
    back0 = units_back(
        unit_vecs, labels, own, rows, chans,
        into_of(1, after(back1["out"], far1), back1["scaled_out"]), weights_of(0),
    )
    keep0 = back0["keep"]
    near0 = swap(back0["send"], "chan", 0)
    token = chain2.step(back0["sums_a"])
    more = sums_out[:, :16].astype(BF).reshape(-1, chans)
    more = jnp.pad(more, ((0, 16 - more.shape[0]), (0, 0)))
    chain1 = Chain([[(keep1, 0), (near1, 0), (after(x1, token), None)], [(more, None)]], chain_rows, over_frames)
    last = units_back(
        unit_vecs, labels, own, rows, chans, into_of(0, after(back0["out"], chain1.sent), back0["scaled_out"]),
        others=(back0["sums_a"], back0["sums_c"], back1["sums_a"], back1["sums_c"], back2["sums_a"], last_sums),
    )
    grad, small = last["out"], last["sums_c"]

    token = chain2.step(grad)
    token = chain1.step(token)
    far0 = add_up(keep0[1], after(near0, token)[1])
    x0 = swap(far0, "chan", 1)
    small_steps = [bit0] + over_frames + [bit1]
    small_got = swap(small, *small_steps[0])
    outs = leave(after(grad, far0), own)
    sent_outs = [outs[0]] + [to_peer(outs[peer], peer) for peer in (1, 2, 3)]
    token = outs[0]

    def small_step():
        nonlocal small, small_got, token
        small = small + after(small_got, token)
        small_steps.pop(0)
        if small_steps:
            small_got = swap(small, *small_steps[0])
        token = small

    half = len(over_frames)
    small_step()
    token = chain2.step(token)
    token = chain1.step(token)
    small_step()
    token = chain2.step(token)
    chain0 = Chain([[(keep0, 0), (near0, 0), (after(x0, token), None)]], 8 * part, over_frames)
    token = chain0.sent
    grad_signal = jnp.zeros((part, extent), F32)
    for peer in range(4):
        got = after(sent_outs[peer], token).astype(F32)
        grad_signal = lax.dynamic_update_slice(grad_signal, got, (0, (me ^ peer) * own))
    token = grad_signal
    while len(small_steps) > 2:
        small_step()
    while chain1.left > half:
        token = chain1.step(token)
    token = chain0.step(token)
    small_step()
    while chain2.left > 1:
        token = chain2.step(token)
    token = chain1.step(token)
    token = chain0.step(token)
    small_step()
    while chain1.left > 1:
        token = chain1.step(token)
    while chain0.left > half:
        token = chain0.step(token)
    token = chain2.step(token)
    quarter = codes[0].shape[0]
    total2 = chain2.whole
    codes_mine = total2[8 * part : 8 * part + quarter]
    got_codes = [codes_mine] + [to_peer(codes_mine, peer) for peer in (1, 2, 3)]
    gains = jnp.stack([dilated_gains, pointwise_gains], axis=1)
    results = norm_back(after(total2, token), dilated_dirs, pointwise_dirs, gains, 2, ())
    token = chain0.step(results[0])
    payload = jnp.zeros((4 * quarter, chans), BF)
    for peer in range(4):
        got = after(got_codes[peer], token)
        payload = lax.dynamic_update_slice_in_dim(payload, got, (me ^ peer) * quarter, 0)
    blocks = codebook.shape[1] // 512
    dstrided_dirs, meeting = strided_back(strided_dirs, payload[24 * blocks :].reshape(-1, 8, chans), latent_proj, norms)
    token = dstrided_dirs
    while chain0.left > 1:
        token = chain0.step(token)
    token = chain1.step(token)
    results = norm_back(chain1.whole, dilated_dirs, pointwise_dirs, gains, 1, results)
    payload = after(payload, token)
    codes = codebook.shape[1]
    blocks = codes // 512
    by_code = payload[: 24 * blocks].reshape(blocks, 24, 512).transpose(1, 0, 2).reshape(24, codes).astype(F32)
    dcoded, picked, usage = by_code[0:8], by_code[8:16], by_code[16]
    refreshed = jnp.where(usage[None, :] > 0, codebook, picked)
    coded_scale = lax.rsqrt(jnp.sum(codebook * codebook, axis=0) + 1.0)
    coded = codebook * coded_scale[None, :]
    dcodebook = (dcoded - coded * jnp.sum(coded * dcoded, axis=0)[None, :]) * coded_scale[None, :]

    token = lax.optimization_barrier((results[0], refreshed, dcodebook))[0]
    chain0.step(token)
    total0 = chain0.whole
    results = norm_back(total0, dilated_dirs, pointwise_dirs, gains, 0, results)
    sums_out = chain1.whole[8 * part : 8 * part + output_bias.shape[0] * 16 // chans].astype(F32).reshape(-1, 16)
    mine_small = lax.dynamic_slice_in_dim(small, me * part, part, axis=1)
    dbias_latent = small[6 * 8 + 1, :8]
    dbias1, dbias7, dalpha2 = mine_small[8:48:16], mine_small[9:48:16], mine_small[10:48:16]
    dalpha1 = mine_small[0:48:16]
    dalpha_last = mine_small[6 * 8]
    dproj_latent = meeting[0:8] + dbias_latent[:, None] * strided_bias[None, :]
    dbias_strided = jnp.sum(latent_proj.astype(F32) * dbias_latent[:, None], axis=0)
    return (
        output,
        grad_signal,
        results[0],
        results[2][:, 0],
        dbias7,
        dalpha1,
        dalpha2,
        results[1],
        results[2][:, 1],
        dbias1,
        dalpha_last,
        dstrided_dirs,
        meeting[8],
        dbias_strided,
        dproj_latent,
        dbias_latent,
        dcodebook,
        sums_out[:, :8],
        sums_out[:, 8],
        refreshed,
    )


def solution(mesh):
    in_specs = (
        P("chan", "frames"),
        P(None, None, "chan", None),
        P(None, "chan"),
        P(None, "chan"),
        P(None, "chan"),
        P(None, "chan"),
        P(None, "chan", None),
        P(None, "chan"),
        P(None, "chan"),
        P("chan"),
        P(None, "chan", None),
        P("chan"),
        P("chan"),
        P(None, "chan"),
        P(),
        P(),
        P("chan", None),
        P("chan"),
        P(),
        P("frames"),
        P(),
        P("chan", "frames"),
    )
    out_specs = (
        P("chan", "frames"),
        P("chan", "frames"),
        P(None, None, "chan", None),
        P(None, "chan"),
        P(None, "chan"),
        P(None, "chan"),
        P(None, "chan"),
        P(None, "chan", None),
        P(None, "chan"),
        P(None, "chan"),
        P("chan"),
        P(None, "chan", None),
        P("chan"),
        P("chan"),
        P(None, "chan"),
        P(),
        P(),
        P("chan", None),
        P("chan"),
        P(),
    )
    return jax.shard_map(local, mesh=mesh, in_specs=in_specs, out_specs=out_specs, check_vma=False)
```

time: 643 us -> 403 us (0.63)
  waiting for transfers between devices: 218 us -> 43.6 us
  other arithmetic: 71.8 us -> 14.9 us
  Pallas kernels: 181 us -> 227 us
  local copies, waits for them, and re-layouts: 72.6 us -> 32.3 us
  matrix products: 21.1 us -> 0 us
  starting transfers between devices: 69.3 us -> 77.5 us
    ppermute x53 -> x43, waiting for transfers between devices: 161 us -> 33 us  [swap(): return lax.ppermute(value, axis, [(i, i ^ 1 << bit) for i in range(count)])]
    pallas_call x6 -> x35, Pallas kernels: 117 us -> 172 us  [the longest x4 77.6 us: units_back(): pl.pallas_call(kernel, out_shape=[shape for shape, _ in outs.values()], i...]
    ppermute x12 -> x15, waiting for transfers between devices: 57.5 us -> 10.7 us  [to_peer(): return lax.ppermute(value, 'chan', [(i, i ^ peer) for i in range(4)])]
    dot_general x9 -> x0, matrix products: 21.1 us -> none  [the longest x1 4.86 us: local(): lax.dot_general(latent_proj, mixed_grad, (((0,), (1,)), ((), ())), prefer...]
    convert_element_type x28 -> x4, other arithmetic: 18.2 us -> 5.45 us  [the longest x3 5.36 us: add_up(): return (kept.astype(F32) + got.astype(F32)).astype(BF)]
    concatenate x21 -> x3, other arithmetic: 10.3 us -> 0.82 us  [the longest x1 0.67 us: local(): jnp.concatenate([vecs[8 * units:8 * units + 2], jnp.pad(latent_bias, (0,...]
    ppermute x12 -> x15, starting transfers between devices: 7.98 us -> 17.2 us  [to_peer(): return lax.ppermute(value, 'chan', [(i, i ^ peer) for i in range(4)])]
    reduce_sum x6 -> x1, other arithmetic: 8.76 us -> 0.09 us  [local(): jnp.sum(coded * dcoded, axis=0)[None, :]]
  transfers between devices with their start and end apart: 69 -> 64, of which waited for: 25 -> 13; matrix products, arithmetic and copies ran while one was open for 21% -> 7% of each run, Pallas kernels for 24% -> 48%
where the time goes in v2:
time: 403 us; the launch traced here: 397 us
  Pallas kernels  227 us (56%)
  starting transfers between devices  77.5 us (19%)
  waiting for transfers between devices  43.6 us (11%)
  local copies, waits for them, and re-layouts  32.3 us (8%)
  other arithmetic  14.9 us (4%)
    pallas_call x4, Pallas kernels, units_back(): pl.pallas_call(kernel, out_shape=[shape for shape, _ in outs.values()], i...  77.6 us
    ppermute x43, starting transfers between devices, swap(): return lax.ppermute(value, axis, [(i, i ^ 1 << bit) for i in range(count)])  48.8 us
    pallas_call x3, Pallas kernels, unit_forward(): pl.pallas_call(kernel, out_shape=[jax.ShapeDtypeStruct((rows, chans), F32...  35.2 us
    ppermute x43, waiting for transfers between devices, swap(): return lax.ppermute(value, axis, [(i, i ^ 1 << bit) for i in range(count)])  33 us
    pallas_call x12, Pallas kernels, sum_halves(): pl.pallas_call(kernel, grid=(1,), out_shape=[jax.ShapeDtypeStruct((half,...  27.3 us
    pallas_call x9, Pallas kernels, join(): pl.pallas_call(kernel, out_shape=jax.ShapeDtypeStruct((2 * rows, chans),...  17.8 us
    ppermute x15, starting transfers between devices, to_peer(): return lax.ppermute(value, 'chan', [(i, i ^ peer) for i in range(4)])  17.2 us
    unnamed x123, local copies, waits for them, and re-layouts  15.7 us
  transfers between devices with their start and end apart: 64, of which 13 were waited for; matrix products, arithmetic and copies ran while one was open for 7% of the time, Pallas kernels for 48%

profile of v2, /device:TPU:0, one launch (start us, length us, event | category | flops | bytes accessed | tf_op | source)
XLA Modules:
  0.0 397.2 jit_solution(5900468339859685928)
XLA Ops:
  0.7 3.0 halve.1
  3.7 3.0 collective-permute-start.12
  8.0 3.4 vectors.1
  12.1 3.4 collective-permute-start.10
  17.9 2.8 cut.1
  22.5 4.3 %collective-permute-start.3 = (bf16[128,128]{1,0:T(8,128)(2,1)}, bf16[128,128]{1,0:T(8,128)(2,1)S(1)}, u32[]{:S(2)}, u32[]{:S(2)}) collective-permute-start(bf16[128,128]{1,0:T(8,128)(2,1)} %get-tuple-element.194), channel_id=1, source_target_pairs={{7,3},{11,7},{15,11},{19,15},{23,19},{27,23},{31,27},{0,4},{4,8},{... | collective-permute-start | bytes 98312 | tf_op jit(solution)/shard_map/ppermute | solution.py:1263
  26.8 2.5 collective-permute-start.15
  30.8 3.9 collective-permute-start.1
  34.7 4.9 %collective-permute-start.2 = (bf16[128,1280]{1,0:T(8,128)(2,1)}, bf16[128,1280]{1,0:T(8,128)(2,1)S(1)}, u32[]{:S(2)}, u32[]{:S(2)}) collective-permute-start(bf16[128,1280]{1,0:T(8,128)(2,1)} %get-tuple-element.193), channel_id=1, source_target_pairs={{0,3},{1,2},{2,1},{3,0},{4,7},{5,6},{6,5},{7,4},{8,11},{9,10},{10,... | collective-permute-start | bytes 983048 | tf_op jit(solution)/shard_map/ppermute | solution.py:1195
  41.4 10.0 %collective-permute-done.2.p3 = bf16[128,1280]{1,0:T(8,128)(2,1)S(1)} collective-permute-done((bf16[128,1280]{1,0:T(8,128)(2,1)}, bf16[128,1280]{1,0:T(8,128)(2,1)S(1)}, u32[]{:S(2)}, u32[]{:S(2)}) %collective-permute-start.2) | collective-permute-done | bytes 327712 | tf_op jit(solution)/shard_map/ppermute | solution.py:1195
  58.1 4.8 %enter.1.s_ref.refs_2_ = f32[1280,512]{1,0:T(8,128)} custom-call(bf16[128,1280]{1,0:T(8,128)(2,1)} %get-tuple-element.203.p0, bf16[128,1280]{1,0:T(8,128)(2,1)} %copy-done.17, bf16[128,1280]{1,0:T(8,128)(2,1)} %copy-done.18, bf16[128,1280]{1,0:T(8,128)(2,1)} %copy-done.19, bf16[128,128]{1,0:T(8,128)(2,1)} %copy-done.30, bf16[128,128]{1,0:T(8,128)(2,1)} %copy-done.31, ...), custom_call_target="tpu_custom_call" | custom-call | flops 115000000 | tf_op jit(solution)/shard_map/enter/pallas_call | solution.py:556
  63.6 11.7 %unit_forward_1.1 = (f32[1280,512]{1,0:T(8,128)}, f32[1280,512]{1,0:T(8,128)}, bf16[1376,512]{1,0:T(8,128)(2,1)}, bf16[512,512]{1,0:T(8,128)(2,1)}) custom-call(f32[1280,512]{1,0:T(8,128)} %enter.1.s_ref.refs_2_, bf16[3,7,128,512]{3,2,1,0:T(8,128)(2,1)} %refs_1_.11, bf16[3,128,512]{2,1,0:T(8,128)(2,1)} %refs_2_.5, ...), custom_call_target="tpu_custom_call" | custom-call | flops 13799999488 | tf_op jit(solution)/shard_map/unit_forward_1/pallas_call | solution.py:221
  76.4 8.2 %look_up.1 = (f32[160,128]{1,0:T(8,128)}, f32[256,512]{1,0:T(8,128)}, f32[256,128]{1,0:T(8,128)}) custom-call(s32[672,128]{1,0:T(8,128)} %broadcast_in_dim.91.i_ref, f32[8,8192]{1,0:T(8,128)} %c_ref.1, bf16[256,128]{1,0:T(8,128)(2,1)} %concatenate.12.p_ref, bf16[256,512]{1,0:T(8,128)(2,1)} %t_ref.3), custom_call_target="tpu_custom_call" | custom-call | flops 115000000 | tf_op jit(solution)/shard_map/look_up/pallas_call | solution.py:696
  84.6 4.3 %collective-permute-done.19.refs_5_.refs_9_ = bf16[4,128,512]{2,1,0:T(8,128)(2,1)S(1)} collective-permute-done((bf16[4,128,512]{2,1,0:T(8,128)(2,1)S(1)}, bf16[4,128,512]{2,1,0:T(8,128)(2,1)S(1)}, u32[]{:S(2)}, u32[]{:S(2)}) %collective-permute-start.19) | collective-permute-done | bytes 524320 | tf_op jit(solution)/shard_map/ppermute | solution.py:1057
  91.6 11.7 %unit_forward_3.1 = (f32[1280,512]{1,0:T(8,128)}, f32[1280,512]{1,0:T(8,128)}, bf16[1568,512]{1,0:T(8,128)(2,1)}, bf16[512,512]{1,0:T(8,128)(2,1)}) custom-call(f32[1280,512]{1,0:T(8,128)} %get-tuple-element.218.s_ref.refs_2_, bf16[3,7,128,512]{3,2,1,0:T(8,128)(2,1)} %refs_1_.11, bf16[3,128,512]{2,1,0:T(8,128)(2,1)} %refs_2_.5, ...), custom_call_target="tpu_custom_call" | custom-call | flops 13799999488 | tf_op jit(solution)/shard_map/unit_forward_3/pallas_call | solution.py:221
  103.3 11.2 %collective-permute-done.23.refs_4_.refs_8_ = bf16[8,128,512]{2,1,0:T(8,128)(2,1)S(1)} collective-permute-done((bf16[8,128,512]{2,1,0:T(8,128)(2,1)S(1)}, bf16[8,128,512]{2,1,0:T(8,128)(2,1)S(1)}, u32[]{:S(2)}, u32[]{:S(2)}) %collective-permute-start.23) | collective-permute-done | bytes 1048608 | tf_op jit(solution)/shard_map/ppermute | solution.py:1057
  114.4 5.0 %merge_strided.1 = (f32[136,512]{1,0:T(8,128)}, f32[8,256]{1,0:T(8,128)}) custom-call(bf16[16,256,512]{2,1,0:T(8,128)(2,1)} %w_ref.3, f32[1,256]{1,0:T(1,128)} %bitcast.50, f32[1,256]{1,0:T(1,128)} %bitcast.49, bf16[8,256]{1,0:T(8,128)(2,1)} %p_ref.2), custom_call_target="tpu_custom_call" | custom-call | flops 115000000 | tf_op jit(solution)/shard_map/merge_strided/pallas_call | solution.py:654
  124.0 11.8 %unit_forward_9.1 = (f32[1280,512]{1,0:T(8,128)}, f32[1280,512]{1,0:T(8,128)}, bf16[2144,512]{1,0:T(8,128)(2,1)}, bf16[512,512]{1,0:T(8,128)(2,1)}) custom-call(f32[1280,512]{1,0:T(8,128)} %get-tuple-element.226.s_ref.refs_2_, bf16[3,7,128,512]{3,2,1,0:T(8,128)(2,1)} %refs_1_.11, bf16[3,128,512]{2,1,0:T(8,128)(2,1)} %refs_2_.5, ...), custom_call_target="tpu_custom_call" | custom-call | flops 13799999488 | tf_op jit(solution)/shard_map/unit_forward_9/pallas_call | solution.py:221
  136.6 10.8 %bottleneck.1 = (f32[1280,512]{1,0:T(8,128)}, f32[160,128]{1,0:T(8,128)}, f32[160,128]{1,0:T(8,128)}, f32[16,8,512]{2,1,0:T(8,128)}, f32[8,512]{1,0:T(8,128)}) custom-call(f32[1280,512]{1,0:T(8,128)} %get-tuple-element.230.s_ref, f32[136,512]{1,0:T(8,128)} %add.223.w_ref, f32[8,512]{1,0:T(8,128)} %maximum_maximum_fusion.v_ref, ...), custom_call_target="tpu_custom_call" | custom-call | flops 12650000384 | tf_op jit(solution)/shard_map/bottleneck/pallas_call | solution.py:1031
  147.5 14.9 %units_back_weights_9.1 = (bf16[1280,512]{1,0:T(8,128)(2,1)}, bf16[2,8,128,512]{3,2,1,0:T(8,128)(2,1)}, bf16[2,8,128,512]{3,2,1,0:T(8,128)(2,1)}, f32[8,512]{1,0:T(8,128)}) custom-call(f32[2176,128]{1,0:T(8,128)} %broadcast_in_dim.87.refs_9_.refs_7_.l_ref.refs_0_, f32[1280,512]{1,0:T(8,128)} %get-tuple-element.247.refs_1_, ...), custom_call_target="tpu_custom_call" | custom-call | flops 39099998208 | tf_op jit(solution)/shard_map/units_back_weights_9/pallas_call | solution.py:445
  164.7 6.0 %code_payload.1 = (bf16[128,512]{1,0:T(8,128)(2,1)}, bf16[128,512]{1,0:T(8,128)(2,1)}, bf16[128,512]{1,0:T(8,128)(2,1)}, bf16[128,512]{1,0:T(8,128)(2,1)}) custom-call(f32[160,128]{1,0:T(8,128)} %get-tuple-element.239.d_ref, f32[160,128]{1,0:T(8,128)} %get-tuple-element.240.l_ref, f32[16,8,512]{2,1,0:T(8,128)} %get-tuple-element.241.m_ref, ...), custom_call_target="tpu_custom_call" | custom-call | flops 115000000 | tf_op jit(solution)/shard_map/code_payload/pallas_call | solution.py:758
  172.6 2.3 fusion
  176.3 24.3 %units_back_into_9_weights_3.1 = (f32[1280,512]{1,0:T(8,128)}, f32[8,512]{1,0:T(8,128)}, bf16[1280,512]{1,0:T(8,128)(2,1)}, bf16[2,8,128,512]{3,2,1,0:T(8,128)(2...) custom-call(f32[2176,128]{1,0:T(8,128)} %broadcast_in_dim.87.refs_9_.refs_7_.l_ref.refs_0_, ...), custom_call_target="tpu_custom_call" | custom-call | flops 73600000000 | tf_op jit(solution)/shard_map/units_back_into_9_weights_3/pallas_call | solution.py:445
  202.3 3.6 sum_halves.12
  209.2 24.6 %units_back_into_3_weights_1.1 = (f32[1280,512]{1,0:T(8,128)}, f32[8,512]{1,0:T(8,128)}, bf16[1280,512]{1,0:T(8,128)(2,1)}, bf16[2,8,128,512]{3,2,1,0:T(8,128)(2...) custom-call(f32[2176,128]{1,0:T(8,128)} %broadcast_in_dim.87.refs_9_.refs_7_.l_ref.refs_0_, ...), custom_call_target="tpu_custom_call" | custom-call | flops 73600000000 | tf_op jit(solution)/shard_map/units_back_into_3_weights_1/pallas_call | solution.py:445
  234.6 2.2 sum_halves.13
  236.9 3.7 collective-permute-start.36
  241.6 3.3 sum_halves.14
  246.7 13.8 %units_back_into_1.1 = (f32[1280,512]{1,0:T(8,128)}, f32[56,512]{1,0:T(8,128)}) custom-call(f32[2176,128]{1,0:T(8,128)} %broadcast_in_dim.87.refs_9_.refs_7_.l_ref.refs_0_, f32[1280,512]{1,0:T(8,128)} %get-tuple-element.279.refs_1_, f32[1280,512]{1,0:T(8,128)} %enter.1.s_ref.refs_2_, bf16[1280,512]{1,0:T(8,128)(2,1)} %get-tuple-element.280.refs_3_, ...), custom_call_target="tpu_custom_call" | custom-call | flops 57500000256 | tf_op jit(solution)/shard_map/units_back_into_1/pallas_call | solution.py:445
  263.9 2.3 sum_halves.16
  268.6 2.9 collective-permute-start.38
  271.5 3.5 leave.1
  275.1 3.4 collective-permute-done.38.refs_1_
  280.8 3.4 collective-permute-start.40
  293.8 4.3 %collective-permute-start.48 = (f32[56,512]{1,0:T(8,128)S(1)}, f32[56,512]{1,0:T(8,128)S(1)}, u32[]{:S(2)}, u32[]{:S(2)}) collective-permute-start(f32[56,512]{1,0:T(8,128)S(1)} %add.228), channel_id=1, source_target_pairs={{0,8},{4,12},{8,0},{12,4},{16,24},{20,28},{24,16},{28,20},{1,9},{5... | collective-permute-start | bytes 344072 | tf_op jit(solution)/shard_map/ppermute | solution.py:1057
  298.1 3.2 sum_halves.19
  306.5 2.9 collective-permute-start.52
  311.5 4.2 %collective-permute-done.46.refs_1_ = bf16[512,512]{1,0:T(8,128)(2,1)S(1)} collective-permute-done((bf16[512,512]{1,0:T(8,128)(2,1)}, bf16[512,512]{1,0:T(8,128)(2,1)S(1)}, u32[]{:S(2)}, u32[]{:S(2)}) %collective-permute-start.46) | collective-permute-done | bytes 524320 | tf_op jit(solution)/shard_map/ppermute | solution.py:1057
  328.9 3.4 collective-permute-start.53
  340.8 2.4 collective-permute-start.56
  346.2 2.3 join.13.refs_0_
  351.4 3.6 norm_back_2.1
  359.1 10.2 %strided_back.1 = (f32[16,256,512]{2,1,0:T(8,128)}, f32[16,256]{1,0:T(8,128)}) custom-call(bf16[16,256,512]{2,1,0:T(8,128)(2,1)} %w_ref.3, bf16[16,8,512]{2,1,0:T(8,128)(2,1)} %slice_bitcast_fusion.m_ref, bf16[8,256]{1,0:T(8,128)(2,1)} %p_ref.2, f32[8,256]{1,0:T(8,128)} %get-tuple-element.338.n_ref), custom_call_target="tpu_custom_call" | custom-call | flops 115000000 | tf_op jit(solution)/shard_map/strided_back/pallas_call | solution.py:805
  376.3 2.3 join.17.refs_0_
  381.3 3.6 norm_back_1.1
  385.7 3.2 collective-permute-done.62.g_ref
  389.7 2.3 join.16.refs_0_
  391.9 3.6 norm_back_0.1
  (337 shorter events, 108.4 us)
Async XLA Ops:
  3.7 23.1 %collective-permute-start.12 = (bf16[4,128,512]{2,1,0:T(8,128)(2,1)}, bf16[4,128,512]{2,1,0:T(8,128)(2,1)}, u32[]{:S(2)}, u32[]{:S(2)}) collective-permute-start(bf16[4,128,512]{2,1,0:T(8,128)(2,1)} %get-tuple-element.186), channel_id=1, source_target_pairs={{0,2},{1,3},{2,0},{3,1},{4,6},{5,7},{6,4},{7,5},{8,10},{9,11},{10,... | collective-permute-start | bytes 1572872 | tf_op jit(solution)/shard_map/ppermute | solution.py:1057
  6.7 56.8 %collective-permute-start.13 = (bf16[3,7,128,512]{3,2,1,0:T(8,128)(2,1)S(1)}, bf16[3,7,128,512]{3,2,1,0:T(8,128)(2,1)}, u32[]{:S(2)}, u32[]{:S(2)}) collective-permute-start(bf16[3,7,128,512]{3,2,1,0:T(8,128)(2,1)S(1)} %copy-done), channel_id=1, source_target_pairs={{0,1},{1,0},{2,3},{3,2},{4,5},{5,4},{6,7},{7,6},{8,9},{9,8},{10,11... | collective-permute-start | bytes 8257544 | tf_op jit(solution)/shard_map/ppermute | solution.py:1057
  11.4 11.1 %collective-permute-start.7 = (f32[40,128]{1,0:T(8,128)}, f32[40,128]{1,0:T(8,128)S(1)}, u32[]{:S(2)}, u32[]{:S(2)}) collective-permute-start(f32[40,128]{1,0:T(8,128)} %get-tuple-element.198), channel_id=1, source_target_pairs={{0,1},{1,0},{2,3},{3,2},{4,5},{5,4},{6,7},{7,6},{8,9},{9,8},{10,11... | collective-permute-start | bytes 61448 | tf_op jit(solution)/shard_map/ppermute | solution.py:1195
  12.1 8.9 %collective-permute-start.10 = (s32[16]{0:T(128)S(1)}, s32[16]{0:T(128)S(1)}, u32[]{:S(2)}, u32[]{:S(2)}) collective-permute-start(s32[16]{0:T(128)S(1)} %get-tuple-element.421), channel_id=1, source_target_pairs={{0,4},{4,8},{8,12},{12,16},{16,20},{20,24},{24,28},{1,5},{5,9},{9,... | collective-permute-start | bytes 200 | tf_op jit(solution)/shard_map/ppermute | solution.py:1254
  26.8 12.9 %collective-permute-start.15 = (bf16[4,128,512]{2,1,0:T(8,128)(2,1)}, bf16[4,128,512]{2,1,0:T(8,128)(2,1)}, u32[]{:S(2)}, u32[]{:S(2)}) collective-permute-start(bf16[4,128,512]{2,1,0:T(8,128)(2,1)} %collective-permute-done.12.refs_4_.refs_8_), channel_id=1, source_target_pairs={{0,4},{4,0},{8,12},{12,8},{16,20},{20,16},{24,28},{28,24},{1,5},{5... | collective-permute-start | bytes 1572872 | tf_op jit(solution)/shard_map/ppermute | solution.py:1057
  29.4 10.2 %collective-permute-start = (bf16[128,1280]{1,0:T(8,128)(2,1)}, bf16[128,1280]{1,0:T(8,128)(2,1)S(1)}, u32[]{:S(2)}, u32[]{:S(2)}) collective-permute-start(bf16[128,1280]{1,0:T(8,128)(2,1)} %get-tuple-element.191), channel_id=1, source_target_pairs={{0,1},{1,0},{2,3},{3,2},{4,5},{5,4},{6,7},{7,6},{8,9},{9,8},{10,11... | collective-permute-start | bytes 983048 | tf_op jit(solution)/shard_map/ppermute | solution.py:1195
  30.8 9.4 %collective-permute-start.1 = (bf16[128,1280]{1,0:T(8,128)(2,1)}, bf16[128,1280]{1,0:T(8,128)(2,1)S(1)}, u32[]{:S(2)}, u32[]{:S(2)}) collective-permute-start(bf16[128,1280]{1,0:T(8,128)(2,1)} %get-tuple-element.192), channel_id=1, source_target_pairs={{0,2},{1,3},{2,0},{3,1},{4,6},{5,7},{6,4},{7,5},{8,10},{9,11},{10,... | collective-permute-start | bytes 983048 | tf_op jit(solution)/shard_map/ppermute | solution.py:1195
  34.7 16.8 %collective-permute-start.2 = (bf16[128,1280]{1,0:T(8,128)(2,1)}, bf16[128,1280]{1,0:T(8,128)(2,1)S(1)}, u32[]{:S(2)}, u32[]{:S(2)}) collective-permute-start(bf16[128,1280]{1,0:T(8,128)(2,1)} %get-tuple-element.193), channel_id=1, source_target_pairs={{0,3},{1,2},{2,1},{3,0},{4,7},{5,6},{6,5},{7,4},{8,11},{9,10},{10,... | collective-permute-start | bytes 983048 | tf_op jit(solution)/shard_map/ppermute | solution.py:1195
  39.6 24.0 %collective-permute-start.16 = (bf16[4,128,512]{2,1,0:T(8,128)(2,1)}, bf16[4,128,512]{2,1,0:T(8,128)(2,1)}, u32[]{:S(2)}, u32[]{:S(2)}) collective-permute-start(bf16[4,128,512]{2,1,0:T(8,128)(2,1)} %collective-permute-done.12.refs_4_.refs_8_), channel_id=1, source_target_pairs={{0,1},{1,0},{2,3},{3,2},{4,5},{5,4},{6,7},{7,6},{8,9},{9,8},{10,11... | collective-permute-start | bytes 1572872 | tf_op jit(solution)/shard_map/ppermute | solution.py:1057
  39.7 23.8 %collective-permute-start.17 = (bf16[4,128,512]{2,1,0:T(8,128)(2,1)}, bf16[4,128,512]{2,1,0:T(8,128)(2,1)}, u32[]{:S(2)}, u32[]{:S(2)}) collective-permute-start(bf16[4,128,512]{2,1,0:T(8,128)(2,1)} %collective-permute-done.15.refs_5_.refs_9_), channel_id=1, source_target_pairs={{0,1},{1,0},{2,3},{3,2},{4,5},{5,4},{6,7},{7,6},{8,9},{9,8},{10,11... | collective-permute-start | bytes 1572872 | tf_op jit(solution)/shard_map/ppermute | solution.py:1057
  40.2 12.9 %collective-permute-start.6 = (bf16[128,128]{1,0:T(8,128)(2,1)}, bf16[128,128]{1,0:T(8,128)(2,1)}, u32[]{:S(2)}, u32[]{:S(2)}) collective-permute-start(bf16[128,128]{1,0:T(8,128)(2,1)} %get-tuple-element.197), channel_id=1, source_target_pairs={{4,3},{8,7},{12,11},{16,15},{20,19},{24,23},{28,27},{3,4},{7,8},{1... | collective-permute-start | bytes 98312 | tf_op jit(solution)/shard_map/ppermute | solution.py:1263
  51.5 12.1 %collective-permute-start.14 = (bf16[3,128,512]{2,1,0:T(8,128)(2,1)S(1)}, bf16[3,128,512]{2,1,0:T(8,128)(2,1)}, u32[]{:S(2)}, u32[]{:S(2)}) collective-permute-start(bf16[3,128,512]{2,1,0:T(8,128)(2,1)S(1)} %copy-done.1), channel_id=1, source_target_pairs={{0,1},{1,0},{2,3},{3,2},{4,5},{5,4},{6,7},{7,6},{8,9},{9,8},{10,11... | collective-permute-start | bytes 1179656 | tf_op jit(solution)/shard_map/ppermute | solution.py:1057
  53.0 22.2 %collective-permute-start.18 = (bf16[4,128,512]{2,1,0:T(8,128)(2,1)}, bf16[4,128,512]{2,1,0:T(8,128)(2,1)S(1)}, u32[]{:S(2)}, u32[]{:S(2)}) collective-permute-start(bf16[4,128,512]{2,1,0:T(8,128)(2,1)} %get-tuple-element.220), channel_id=1, source_target_pairs={{0,2},{1,3},{2,0},{3,1},{4,6},{5,7},{6,4},{7,5},{8,10},{9,11},{10,... | collective-permute-start | bytes 1572872 | tf_op jit(solution)/shard_map/ppermute | solution.py:1057
  75.3 13.6 %collective-permute-start.19 = (bf16[4,128,512]{2,1,0:T(8,128)(2,1)S(1)}, bf16[4,128,512]{2,1,0:T(8,128)(2,1)S(1)}, u32[]{:S(2)}, u32[]{:S(2)}) collective-permute-start(bf16[4,128,512]{2,1,0:T(8,128)(2,1)S(1)} %collective-permute-done.18.refs_4_.refs_8_), channel_id=1, source_target_pairs={{0,4},{4,0},{8,12},{12,8},{16,20},{20,16},{24,28},{28,24},{1,5},{5... | collective-permute-start | bytes 1572872 | tf_op jit(solution)/shard_map/ppermute | solution.py:1057
  76.3 13.3 %collective-permute-start.20 = (bf16[4,128,512]{2,1,0:T(8,128)(2,1)S(1)}, bf16[4,128,512]{2,1,0:T(8,128)(2,1)S(1)}, u32[]{:S(2)}, u32[]{:S(2)}) collective-permute-start(bf16[4,128,512]{2,1,0:T(8,128)(2,1)S(1)} %collective-permute-done.18.refs_4_.refs_8_), channel_id=1, source_target_pairs={{0,1},{1,0},{2,3},{3,2},{4,5},{5,4},{6,7},{7,6},{8,9},{9,8},{10,11... | collective-permute-start | bytes 1572872 | tf_op jit(solution)/shard_map/ppermute | solution.py:1057
  88.9 25.6 %collective-permute-start.23 = (bf16[8,128,512]{2,1,0:T(8,128)(2,1)S(1)}, bf16[8,128,512]{2,1,0:T(8,128)(2,1)S(1)}, u32[]{:S(2)}, u32[]{:S(2)}) collective-permute-start(bf16[8,128,512]{2,1,0:T(8,128)(2,1)S(1)} %copy-done.44), channel_id=1, source_target_pairs={{0,2},{1,3},{2,0},{3,1},{4,6},{5,7},{6,4},{7,5},{8,10},{9,11},{10,... | collective-permute-start | bytes 3145736 | tf_op jit(solution)/shard_map/ppermute | solution.py:1057
  122.3 13.6 %collective-permute-start.25 = (f32[136,512]{1,0:T(8,128)S(1)}, f32[136,512]{1,0:T(8,128)S(1)}, u32[]{:S(2)}, u32[]{:S(2)}) collective-permute-start(f32[136,512]{1,0:T(8,128)S(1)} %add.222), channel_id=1, source_target_pairs={{0,2},{1,3},{2,0},{3,1},{4,6},{5,7},{6,4},{7,5},{8,10},{9,11},{10,... | collective-permute-start | bytes 835592 | tf_op jit(solution)/shard_map/ppermute | solution.py:1057
  162.3 10.3 %collective-permute-start.26 = (bf16[2,8,128,512]{3,2,1,0:T(8,128)(2,1)}, bf16[2,8,128,512]{3,2,1,0:T(8,128)(2,1)S(1)}, u32[]{:S(2)}, u32[]{:S(2)}) collective-permute-start(bf16[2,8,128,512]{3,2,1,0:T(8,128)(2,1)} %get-tuple-element.238), channel_id=1, source_target_pairs={{0,1},{1,0},{2,3},{3,2},{4,5},{5,4},{6,7},{7,6},{8,9},{9,8},{10,11... | collective-permute-start | bytes 6291464 | tf_op jit(solution)/shard_map/ppermute | solution.py:1057
  170.7 30.5 %collective-permute-start.29 = (bf16[128,512]{1,0:T(8,128)(2,1)}, bf16[128,512]{1,0:T(8,128)(2,1)S(1)}, u32[]{:S(2)}, u32[]{:S(2)}) collective-permute-start(bf16[128,512]{1,0:T(8,128)(2,1)} %get-tuple-element.255), channel_id=1, source_target_pairs={{0,1},{1,0},{2,3},{3,2},{4,5},{5,4},{6,7},{7,6},{8,9},{9,8},{10,11... | collective-permute-start | bytes 393224 | tf_op jit(solution)/shard_map/ppermute | solution.py:1195
  171.2 30.0 %collective-permute-start.30 = (bf16[128,512]{1,0:T(8,128)(2,1)}, bf16[128,512]{1,0:T(8,128)(2,1)S(1)}, u32[]{:S(2)}, u32[]{:S(2)}) collective-permute-start(bf16[128,512]{1,0:T(8,128)(2,1)} %get-tuple-element.256), channel_id=1, source_target_pairs={{0,2},{1,3},{2,0},{3,1},{4,6},{5,7},{6,4},{7,5},{8,10},{9,11},{10,... | collective-permute-start | bytes 393224 | tf_op jit(solution)/shard_map/ppermute | solution.py:1195
  172.6 28.7 %collective-permute-start.31 = (bf16[128,512]{1,0:T(8,128)(2,1)}, bf16[128,512]{1,0:T(8,128)(2,1)S(1)}, u32[]{:S(2)}, u32[]{:S(2)}) collective-permute-start(bf16[128,512]{1,0:T(8,128)(2,1)} %get-tuple-element.257), channel_id=1, source_target_pairs={{0,3},{1,2},{2,1},{3,0},{4,7},{5,6},{6,5},{7,4},{8,11},{9,10},{10,... | collective-permute-start | bytes 393224 | tf_op jit(solution)/shard_map/ppermute | solution.py:1195
  174.9 27.3 %collective-permute-start.28 = (bf16[8,128,512]{2,1,0:T(8,128)(2,1)S(1)}, bf16[8,128,512]{2,1,0:T(8,128)(2,1)}, u32[]{:S(2)}, u32[]{:S(2)}) collective-permute-start(bf16[8,128,512]{2,1,0:T(8,128)(2,1)S(1)} %fusion), channel_id=1, source_target_pairs={{0,2},{1,3},{2,0},{3,1},{4,6},{5,7},{6,4},{7,5},{8,10},{9,11},{10,... | collective-permute-start | bytes 3145736 | tf_op jit(solution)/shard_map/ppermute | solution.py:1057
  205.9 27.9 %collective-permute-start.33 = (bf16[576,512]{1,0:T(8,128)(2,1)}, bf16[576,512]{1,0:T(8,128)(2,1)S(1)}, u32[]{:S(2)}, u32[]{:S(2)}) collective-permute-start(bf16[576,512]{1,0:T(8,128)(2,1)} %get-tuple-element.264), channel_id=1, source_target_pairs={{0,4},{4,0},{8,12},{12,8},{16,20},{20,16},{24,28},{28,24},{1,5},{5... | collective-permute-start | bytes 1769480 | tf_op jit(solution)/shard_map/ppermute | solution.py:1057
  208.4 32.2 %collective-permute-start.32 = (bf16[8,128,512]{2,1,0:T(8,128)(2,1)S(1)}, bf16[8,128,512]{2,1,0:T(8,128)(2,1)S(1)}, u32[]{:S(2)}, u32[]{:S(2)}) collective-permute-start(bf16[8,128,512]{2,1,0:T(8,128)(2,1)S(1)} %fusion.1), channel_id=1, source_target_pairs={{0,2},{1,3},{2,0},{3,1},{4,6},{5,7},{6,4},{7,5},{8,10},{9,11},{10,... | collective-permute-start | bytes 3145736 | tf_op jit(solution)/shard_map/ppermute | solution.py:1057
  236.9 23.6 %collective-permute-start.36 = (bf16[288,512]{1,0:T(8,128)(2,1)}, bf16[288,512]{1,0:T(8,128)(2,1)S(1)}, u32[]{:S(2)}, u32[]{:S(2)}) collective-permute-start(bf16[288,512]{1,0:T(8,128)(2,1)} %get-tuple-element.275), channel_id=1, source_target_pairs={{0,8},{4,12},{8,0},{12,4},{16,24},{20,28},{24,16},{28,20},{1,9},{5... | collective-permute-start | bytes 884744 | tf_op jit(solution)/shard_map/ppermute | solution.py:1057
  240.6 25.6 %collective-permute-start.34 = (bf16[2,8,128,512]{3,2,1,0:T(8,128)(2,1)}, bf16[2,8,128,512]{3,2,1,0:T(8,128)(2,1)}, u32[]{:S(2)}, u32[]{:S(2)}) collective-permute-start(bf16[2,8,128,512]{3,2,1,0:T(8,128)(2,1)} %get-tuple-element.286), channel_id=1, source_target_pairs={{0,1},{1,0},{2,3},{3,2},{4,5},{5,4},{6,7},{7,6},{8,9},{9,8},{10,11... | collective-permute-start | bytes 6291464 | tf_op jit(solution)/shard_map/ppermute | solution.py:1057
  244.8 18.2 %collective-permute-start.35 = (bf16[576,512]{1,0:T(8,128)(2,1)}, bf16[576,512]{1,0:T(8,128)(2,1)S(1)}, u32[]{:S(2)}, u32[]{:S(2)}) collective-permute-start(bf16[576,512]{1,0:T(8,128)(2,1)} %get-tuple-element.278), channel_id=1, source_target_pairs={{0,4},{4,0},{8,12},{12,8},{16,20},{20,16},{24,28},{28,24},{1,5},{5... | collective-permute-start | bytes 1769480 | tf_op jit(solution)/shard_map/ppermute | solution.py:1057
  267.7 26.1 %collective-permute-start.37 = (bf16[8,128,512]{2,1,0:T(8,128)(2,1)S(1)}, bf16[8,128,512]{2,1,0:T(8,128)(2,1)S(1)}, u32[]{:S(2)}, u32[]{:S(2)}) collective-permute-start(bf16[8,128,512]{2,1,0:T(8,128)(2,1)S(1)} %fusion.2), channel_id=1, source_target_pairs={{0,2},{1,3},{2,0},{3,1},{4,6},{5,7},{6,4},{7,5},{8,10},{9,11},{10,... | collective-permute-start | bytes 3145736 | tf_op jit(solution)/shard_map/ppermute | solution.py:1057
  268.5 16.2 %collective-permute-start.42 = (bf16[288,512]{1,0:T(8,128)(2,1)}, bf16[288,512]{1,0:T(8,128)(2,1)S(1)}, u32[]{:S(2)}, u32[]{:S(2)}) collective-permute-start(bf16[288,512]{1,0:T(8,128)(2,1)} %get-tuple-element.292), channel_id=1, source_target_pairs={{0,8},{4,12},{8,0},{12,4},{16,24},{20,28},{24,16},{28,20},{1,9},{5... | collective-permute-start | bytes 884744 | tf_op jit(solution)/shard_map/ppermute | solution.py:1057
  268.6 9.9 %collective-permute-start.38 = (bf16[144,512]{1,0:T(8,128)(2,1)S(1)}, bf16[144,512]{1,0:T(8,128)(2,1)S(1)}, u32[]{:S(2)}, u32[]{:S(2)}) collective-permute-start(bf16[144,512]{1,0:T(8,128)(2,1)S(1)} %copy-done.51), channel_id=1, source_target_pairs={{0,16},{4,20},{8,24},{12,28},{16,0},{20,4},{24,8},{28,12},{1,17},{... | collective-permute-start | bytes 442376 | tf_op jit(solution)/shard_map/ppermute | solution.py:1057
  284.6 17.8 %collective-permute-start.43 = (bf16[128,1024]{1,0:T(8,128)(2,1)}, bf16[128,1024]{1,0:T(8,128)(2,1)S(1)}, u32[]{:S(2)}, u32[]{:S(2)}) collective-permute-start(bf16[128,1024]{1,0:T(8,128)(2,1)} %get-tuple-element.308), channel_id=1, source_target_pairs={{0,1},{1,0},{2,3},{3,2},{4,5},{5,4},{6,7},{7,6},{8,9},{9,8},{10,11... | collective-permute-start | bytes 786440 | tf_op jit(solution)/shard_map/ppermute | solution.py:1195
  284.7 18.1 %collective-permute-start.45 = (bf16[128,1024]{1,0:T(8,128)(2,1)}, bf16[128,1024]{1,0:T(8,128)(2,1)}, u32[]{:S(2)}, u32[]{:S(2)}) collective-permute-start(bf16[128,1024]{1,0:T(8,128)(2,1)} %get-tuple-element.312), channel_id=1, source_target_pairs={{0,3},{1,2},{2,1},{3,0},{4,7},{5,6},{6,5},{7,4},{8,11},{9,10},{10,... | collective-permute-start | bytes 786440 | tf_op jit(solution)/shard_map/ppermute | solution.py:1195
  289.0 20.4 %collective-permute-start.47 = (bf16[144,512]{1,0:T(8,128)(2,1)}, bf16[144,512]{1,0:T(8,128)(2,1)}, u32[]{:S(2)}, u32[]{:S(2)}) collective-permute-start(bf16[144,512]{1,0:T(8,128)(2,1)} %get-tuple-element.302), channel_id=1, source_target_pairs={{0,16},{4,20},{8,24},{12,28},{16,0},{20,4},{24,8},{28,12},{1,17},{... | collective-permute-start | bytes 442376 | tf_op jit(solution)/shard_map/ppermute | solution.py:1057
  289.1 15.4 %collective-permute-start.44 = (bf16[128,1024]{1,0:T(8,128)(2,1)}, bf16[128,1024]{1,0:T(8,128)(2,1)}, u32[]{:S(2)}, u32[]{:S(2)}) collective-permute-start(bf16[128,1024]{1,0:T(8,128)(2,1)} %get-tuple-element.310), channel_id=1, source_target_pairs={{0,2},{1,3},{2,0},{3,1},{4,6},{5,7},{6,4},{7,5},{8,10},{9,11},{10,... | collective-permute-start | bytes 786440 | tf_op jit(solution)/shard_map/ppermute | solution.py:1195
  293.8 12.7 %collective-permute-start.48 = (f32[56,512]{1,0:T(8,128)S(1)}, f32[56,512]{1,0:T(8,128)S(1)}, u32[]{:S(2)}, u32[]{:S(2)}) collective-permute-start(f32[56,512]{1,0:T(8,128)S(1)} %add.228), channel_id=1, source_target_pairs={{0,8},{4,12},{8,0},{12,4},{16,24},{20,28},{24,16},{28,20},{1,9},{5... | collective-permute-start | bytes 344072 | tf_op jit(solution)/shard_map/ppermute | solution.py:1057
  302.5 13.3 %collective-permute-start.46 = (bf16[512,512]{1,0:T(8,128)(2,1)}, bf16[512,512]{1,0:T(8,128)(2,1)S(1)}, u32[]{:S(2)}, u32[]{:S(2)}) collective-permute-start(bf16[512,512]{1,0:T(8,128)(2,1)} %get-tuple-element.306), channel_id=1, source_target_pairs={{0,4},{4,0},{8,12},{12,8},{16,20},{20,16},{24,28},{28,24},{1,5},{5... | collective-permute-start | bytes 1572872 | tf_op jit(solution)/shard_map/ppermute | solution.py:1057
  302.8 18.3 %collective-permute-start.51 = (bf16[288,512]{1,0:T(8,128)(2,1)S(1)}, bf16[288,512]{1,0:T(8,128)(2,1)S(1)}, u32[]{:S(2)}, u32[]{:S(2)}) collective-permute-start(bf16[288,512]{1,0:T(8,128)(2,1)S(1)} %copy-done.6), channel_id=1, source_target_pairs={{0,8},{4,12},{8,0},{12,4},{16,24},{20,28},{24,16},{28,20},{1,9},{5... | collective-permute-start | bytes 884744 | tf_op jit(solution)/shard_map/ppermute | solution.py:1057
  306.5 13.6 %collective-permute-start.52 = (f32[56,512]{1,0:T(8,128)S(1)}, f32[56,512]{1,0:T(8,128)S(1)}, u32[]{:S(2)}, u32[]{:S(2)}) collective-permute-start(f32[56,512]{1,0:T(8,128)S(1)} %add.233), channel_id=1, source_target_pairs={{0,16},{4,20},{8,24},{12,28},{16,0},{20,4},{24,8},{28,12},{1,17},{... | collective-permute-start | bytes 344072 | tf_op jit(solution)/shard_map/ppermute | solution.py:1057
  311.1 13.5 %collective-permute-start.50 = (bf16[144,512]{1,0:T(8,128)(2,1)}, bf16[144,512]{1,0:T(8,128)(2,1)}, u32[]{:S(2)}, u32[]{:S(2)}) collective-permute-start(bf16[144,512]{1,0:T(8,128)(2,1)} %sum_halves.20.m_ref), channel_id=1, source_target_pairs={{0,16},{4,20},{8,24},{12,28},{16,0},{20,4},{24,8},{28,12},{1,17},{... | collective-permute-start | bytes 442376 | tf_op jit(solution)/shard_map/ppermute | solution.py:1057
  320.1 12.3 %collective-permute-start.55 = (f32[56,512]{1,0:T(8,128)S(1)}, f32[56,512]{1,0:T(8,128)S(1)}, u32[]{:S(2)}, u32[]{:S(2)}) collective-permute-start(f32[56,512]{1,0:T(8,128)S(1)} %add.234), channel_id=1, source_target_pairs={{0,2},{1,3},{2,0},{3,1},{4,6},{5,7},{6,4},{7,5},{8,10},{9,11},{10,... | collective-permute-start | bytes 344072 | tf_op jit(solution)/shard_map/ppermute | solution.py:1057
  323.7 21.6 %collective-permute-start.57 = (bf16[576,512]{1,0:T(8,128)(2,1)}, bf16[576,512]{1,0:T(8,128)(2,1)S(1)}, u32[]{:S(2)}, u32[]{:S(2)}) collective-permute-start(bf16[576,512]{1,0:T(8,128)(2,1)} %join.10.m_ref), channel_id=1, source_target_pairs={{0,4},{4,0},{8,12},{12,8},{16,20},{20,16},{24,28},{28,24},{1,5},{5... | collective-permute-start | bytes 1769480 | tf_op jit(solution)/shard_map/ppermute | solution.py:1057
  326.3 9.5 %collective-permute-start.54 = (bf16[288,512]{1,0:T(8,128)(2,1)}, bf16[288,512]{1,0:T(8,128)(2,1)S(1)}, u32[]{:S(2)}, u32[]{:S(2)}) collective-permute-start(bf16[288,512]{1,0:T(8,128)(2,1)} %join.11.m_ref), channel_id=1, source_target_pairs={{0,8},{4,12},{8,0},{12,4},{16,24},{20,28},{24,16},{28,20},{1,9},{5... | collective-permute-start | bytes 884744 | tf_op jit(solution)/shard_map/ppermute | solution.py:1057
  328.9 9.5 %collective-permute-start.53 = (bf16[128,512]{1,0:T(8,128)(2,1)}, bf16[128,512]{1,0:T(8,128)(2,1)S(1)}, u32[]{:S(2)}, u32[]{:S(2)}) collective-permute-start(bf16[128,512]{1,0:T(8,128)(2,1)} %get-tuple-element.326), channel_id=1, source_target_pairs={{0,16},{4,20},{8,24},{12,28},{16,0},{20,4},{24,8},{28,12},{1,17},{... | collective-permute-start | bytes 393224 | tf_op jit(solution)/shard_map/ppermute | solution.py:1057
  340.8 14.2 %collective-permute-start.56 = (bf16[128,512]{1,0:T(8,128)(2,1)}, bf16[128,512]{1,0:T(8,128)(2,1)S(1)}, u32[]{:S(2)}, u32[]{:S(2)}) collective-permute-start(bf16[128,512]{1,0:T(8,128)(2,1)} %sum_halves.23.m_ref), channel_id=1, source_target_pairs={{0,16},{4,20},{8,24},{12,28},{16,0},{20,4},{24,8},{28,12},{1,17},{... | collective-permute-start | bytes 393224 | tf_op jit(solution)/shard_map/ppermute | solution.py:1057
  343.7 31.8 %collective-permute-start.63 = (bf16[576,512]{1,0:T(8,128)(2,1)}, bf16[576,512]{1,0:T(8,128)(2,1)S(1)}, u32[]{:S(2)}, u32[]{:S(2)}) collective-permute-start(bf16[576,512]{1,0:T(8,128)(2,1)} %join.12.m_ref), channel_id=1, source_target_pairs={{0,4},{4,0},{8,12},{12,8},{16,20},{20,16},{24,28},{28,24},{1,5},{5... | collective-permute-start | bytes 1769480 | tf_op jit(solution)/shard_map/ppermute | solution.py:1057
  349.4 8.9 %collective-permute-start.61 = (bf16[128,512]{1,0:T(8,128)(2,1)S(1)}, bf16[128,512]{1,0:T(8,128)(2,1)S(1)}, u32[]{:S(2)}, u32[]{:S(2)}) collective-permute-start(bf16[128,512]{1,0:T(8,128)(2,1)S(1)} %slice.181), channel_id=1, source_target_pairs={{0,3},{1,2},{2,1},{3,0},{4,7},{5,6},{6,5},{7,4},{8,11},{9,10},{10,... | collective-permute-start | bytes 393224 | tf_op jit(solution)/shard_map/ppermute | solution.py:1195
  357.4 15.2 %collective-permute-start.58 = (bf16[256,512]{1,0:T(8,128)(2,1)}, bf16[256,512]{1,0:T(8,128)(2,1)S(1)}, u32[]{:S(2)}, u32[]{:S(2)}) collective-permute-start(bf16[256,512]{1,0:T(8,128)(2,1)} %join.14.m_ref), channel_id=1, source_target_pairs={{0,8},{4,12},{8,0},{12,4},{16,24},{20,28},{24,16},{28,20},{1,9},{5... | collective-permute-start | bytes 786440 | tf_op jit(solution)/shard_map/ppermute | solution.py:1057
  375.1 13.8 %collective-permute-start.62 = (bf16[512,512]{1,0:T(8,128)(2,1)}, bf16[512,512]{1,0:T(8,128)(2,1)S(1)}, u32[]{:S(2)}, u32[]{:S(2)}) collective-permute-start(bf16[512,512]{1,0:T(8,128)(2,1)} %join.15.m_ref), channel_id=1, source_target_pairs={{0,4},{4,0},{8,12},{12,8},{16,20},{20,16},{24,28},{28,24},{1,5},{5... | collective-permute-start | bytes 1572872 | tf_op jit(solution)/shard_map/ppermute | solution.py:1057
  (75 other events, 607.8 us)

commit v3 on v2

--- a/solution.py
+++ b/solution.py
@@ -89,15 +89,14 @@
         (near7, weights.at[pl.ds(0, 7), place(1), :]),
         (near1, weights.at[7, place(1), :]),
     ]
-    if len(pieces) == 6:
-        moves += [(pieces[4], weights.at[:, place(2), :]), (pieces[5], weights.at[:, place(3), :])]
-    else:
-        moves += [
-            (pieces[4], weights.at[pl.ds(first, 4), place(2), :]),
-            (pieces[5], weights.at[pl.ds(4 - first, 4), place(2), :]),
-            (pieces[6], weights.at[pl.ds(first, 4), place(3), :]),
-            (pieces[7], weights.at[pl.ds(4 - first, 4), place(3), :]),
-        ]
+    if member == 2:
+        first = 0
+    moves += [
+        (pieces[4], weights.at[pl.ds(first, 4), place(2), :]),
+        (pieces[5], weights.at[pl.ds(4 - first, 4), place(2), :]),
+        (pieces[6], weights.at[pl.ds(first, 4), place(3), :]),
+        (pieces[7], weights.at[pl.ds(4 - first, 4), place(3), :]),
+    ]
     copies = []
     for piece, target in moves:
         copy = pltpu.make_async_copy(piece, target, sems.at[len(copies)])
@@ -165,6 +164,7 @@
             v_ref, l_ref, out_ref, mid_ref, wide_ref, w1_ref,
             weights, wide, turn, mask, stream_in, result, middle, total0, total1, sems, s_sems, o_sems, m_sems, end_sems,
         ) = refs
+        v_ref = v_ref.at[pl.ds(8 * member, 8)]
         incoming = Stream(s_ref, stream_in, s_sems)
         outgoing, outgoing_mid = Stream(result, out_ref, o_sems), Stream(middle, mid_ref, m_sems)
         for chunk in range(chunks):
@@ -261,7 +261,7 @@
     chunks = rows // CHUNK
     held, whole = pl.BlockSpec(memory_space=pl.ANY), pl.BlockSpec(memory_space=pltpu.VMEM)
     f32_rows, bf_rows = jax.ShapeDtypeStruct((rows, chans), F32), jax.ShapeDtypeStruct((rows, chans), BF)
-    ins, outs, scratch = {"labels": (labels, whole)}, {}, {"mask": pltpu.VMEM((7, rows, 128), BF)}
+    ins, outs, scratch = {"labels": (labels, whole), "vecs": (vecs, whole)}, {}, {"mask": pltpu.VMEM((7, rows, 128), BF)}
     name, micros = "units_back", 20
     if into is not None:
         member_c, grad, stream, scaled, pieces = into
@@ -270,7 +270,6 @@
         name, micros = f"{name}_into_{spacing_c}", micros + 30
         ins |= {"grad": (grad, held), "stream": (stream, held), "scaled": (scaled, held)}
         ins |= {f"piece{n}": (piece, held) for n, piece in enumerate(pieces)}
-        ins["vec_c"] = (vecs[member_c], whole)
         ins |= {f"other{n}": (other, whole) for n, other in enumerate(others)}
         outs |= {"out": (f32_rows, held), "sums_c": (jax.ShapeDtypeStruct((8 + 8 * len(others), chans), F32), whole)}
         scratch |= {
@@ -293,7 +292,7 @@
         member_a, _, middle, wide_act, weight1 = weights
         spacing_a = 3**member_a
         name, micros = f"{name}_weights_{spacing_a}", micros + 14
-        ins |= {"middle": (middle, held), "wide": (wide_act, held), "w1": (weight1, whole), "vec_a": (vecs[member_a], whole)}
+        ins |= {"middle": (middle, held), "wide": (wide_act, held), "w1": (weight1, whole)}
         outs |= {
             "scaled_out": (bf_rows, held),
             "keep": (jax.ShapeDtypeStruct((2, 8, part, chans), BF), held),
@@ -428,6 +427,10 @@
 
     def kernel(*refs):
         r = Names([*ins, *outs, *scratch], refs)
+        if into is not None:
+            r.vec_c = r.vecs.at[pl.ds(8 * member_c, 8)]
+        if weights is not None:
+            r.vec_a = r.vecs.at[pl.ds(8 * member_a, 8)]
         outgoing = None
         if into is None:
             incoming = Stream(r.grad, r.grad_in, r.g_sems)
@@ -458,7 +461,7 @@
 def halve(dilated, pointwise):
     units, _, part, chans = dilated.shape
 
-    def kernel(d_ref, q_ref, f0, f1, f2, held, sems, out_sems):
+    def kernel(d_ref, q_ref, f0, f1, f2, f3, held, sems, out_sems):
         first = pl.multiple_of((lax.axis_index("frames") & 1) * 4, 4)
         copies = []
         for u in range(units):
@@ -469,9 +472,13 @@
         outs = [
             pltpu.make_async_copy(held.at[0, pl.ds(first, 4)], f0, out_sems.at[0]),
             pltpu.make_async_copy(held.at[1, pl.ds(first, 4)], f1, out_sems.at[1]),
-            pltpu.make_async_copy(held.at[2], f2, out_sems.at[2]),
+            pltpu.make_async_copy(held.at[2, pl.ds(0, 4)], f2, out_sems.at[2]),
+            pltpu.make_async_copy(held.at[2, pl.ds(4, 4)], f3, out_sems.at[3]),
         ]
-        for u, out in enumerate(outs):
+        for u, out in zip((0, 1, 2, 2), outs, strict=True):
+            if u == 2 and out is outs[3]:
+                out.start()
+                continue
             copies[2 * u].wait()
             copies[2 * u + 1].wait()
             out.start()
@@ -483,15 +490,14 @@
         kernel,
         out_shape=[
             jax.ShapeDtypeStruct((4, part, chans), BF),
-            jax.ShapeDtypeStruct((4, part, chans), BF),
-            jax.ShapeDtypeStruct((8, part, chans), BF),
-        ],
+        ]
+        * 4,
         in_specs=[held] * 2,
-        out_specs=[held] * 3,
+        out_specs=[held] * 4,
         scratch_shapes=[
             pltpu.VMEM((units, 8, part, chans), BF),
             pltpu.SemaphoreType.DMA((2 * units,)),
-            pltpu.SemaphoreType.DMA((units,)),
+            pltpu.SemaphoreType.DMA((units + 1,)),
         ],
         compiler_params=pltpu.CompilerParams(vmem_limit_bytes=VMEM),
         cost_estimate=cost(0.1),
@@ -499,13 +505,16 @@
     )(dilated, pointwise)
 
 
-def cut(signal):
+def cut(signal, packed, pulled, codes):
     part, extent = signal.shape
     own = extent // 4
-
-    def kernel(s_ref, p0, p1, p2, p3, e0, e1, e2, e3, low):
+    count = own + 2 * HALO
+    own_frames = pulled.shape[1] // 4
+
+    def kernel(s_ref, v_ref, u_ref, c_ref, p0, p1, p2, p3, e0, e1, e2, e3, low):
         me = lax.axis_index("chan")
         low[...] = s_ref[...].astype(BF)
+        vectors3 = terms(v_ref[...], 3)
         for p, (piece, end) in enumerate(((p0, e0), (p1, e1), (p2, e2), (p3, e3))):
             owner = me ^ p
             start = pl.multiple_of(owner * own, own)
@@ -513,51 +522,81 @@
             before = pl.multiple_of(jnp.maximum(start - HALO, 0), HALO)
             piece[:, 0:HALO] = low[:, pl.ds(before, HALO)]
             behind = pl.multiple_of(jnp.minimum(start + own, extent - HALO), HALO)
-            piece[:, HALO + own : 2 * HALO + own] = low[:, pl.ds(behind, HALO)]
+            piece[:, HALO + own : count] = low[:, pl.ds(behind, HALO)]
+            frames = pl.ds(pl.multiple_of(owner * own_frames, own_frames), own_frames)
+            pulled2 = jnp.concatenate([u_ref[:, frames], jnp.zeros((8, own_frames), F32)], axis=0)
+            high = pulled2.astype(BF).astype(F32)
+            both = jnp.concatenate([high[0:8], (pulled2 - high)[0:8]], axis=0).astype(BF)
+            piece[:, count : count + 128] = jnp.concatenate(
+                [*vectors3, both, jnp.zeros((128 - 3 * packed.shape[0] - 16, 128), BF)], axis=0
+            )
             outer = pl.multiple_of(jnp.where(owner == 0, extent - HALO, 0), HALO)
-            end[...] = low[:, pl.ds(outer, HALO)]
+            end[0:part, :] = low[:, pl.ds(outer, HALO)]
+        first, last = c_ref[0:1, :], c_ref[codes.shape[0] - 1 : codes.shape[0], :]
+        e0[part : part + 16, :] = jnp.concatenate(
+            [row.astype(F32) for row in (first >> 7, first & 127, last >> 7, last & 127)] + [jnp.zeros((12, 128), F32)],
+            axis=0,
+        ).astype(BF)
 
     whole = pl.BlockSpec(memory_space=pltpu.VMEM)
     outs = pl.pallas_call(
         kernel,
-        out_shape=[jax.ShapeDtypeStruct((part, own + 2 * HALO), BF)] * 4 + [jax.ShapeDtypeStruct((part, HALO), BF)] * 4,
-        in_specs=[whole],
+        out_shape=[jax.ShapeDtypeStruct((part, count + 128), BF)] * 4
+        + [jax.ShapeDtypeStruct((part + 16, HALO), BF)]
+        + [jax.ShapeDtypeStruct((part, HALO), BF)] * 3,
+        in_specs=[whole] * 4,
         out_specs=[whole] * 8,
         scratch_shapes=[pltpu.VMEM((part, extent), BF)],
         compiler_params=pltpu.CompilerParams(vmem_limit_bytes=VMEM),
         cost_estimate=cost(0.1),
         name="cut",
-    )(signal)
+    )(signal, packed, pulled, codes)
     return outs[0:4], outs[4:8]
 
 
-def enter(pieces, ends, own):
-    part, count = pieces[0].shape
+def enter(pieces, ends, lines, own):
+    part = pieces[0].shape[0]
+    count = own + 2 * HALO
     span = count // SEG
 
-    def kernel(p0, p1, p2, p3, e0, e1, e2, e3, out_ref, turned, placed):
+    def kernel(p0, p1, p2, p3, e0, e1, e2, e3, out_ref, vec_ref, pull_ref, code_ref, turned, placed):
         me = lax.axis_index("chan")
+        pulled = jnp.zeros((8, part), F32)
         for p, (piece, end) in enumerate(((p0, e0), (p1, e1), (p2, e2), (p3, e3))):
-            turned[...] = piece[...].astype(F32).T
+            turned[...] = piece[:, 0:count].astype(F32).T
 
             @pl.when(me == 0)
             def _(end=end):
-                turned[0:HALO, :] = end[...].astype(F32).T
+                turned[0:HALO, :] = end[0:part, :].astype(F32).T
 
             @pl.when(me == 3)
             def _(end=end):
-                turned[HALO + own : 2 * HALO + own, :] = end[...].astype(F32).T
+                turned[HALO + own : count, :] = end[0:part, :].astype(F32).T
 
             for a in range(SEG):
                 placed[pl.ds(a, span, stride=SEG), :] = turned[pl.ds(a * span, span), :]
-            out_ref[:, pl.ds(pl.multiple_of((me ^ p) * part, part), part)] = placed[...]
+            lanes = pl.ds(pl.multiple_of((me ^ p) * part, part), part)
+            out_ref[:, lanes] = placed[...]
+            tile = piece[:, count : count + 128].astype(F32)
+            vec_ref[:, lanes] = tile[0:lines] + tile[lines : 2 * lines] + tile[2 * lines : 3 * lines]
+            pulled = pulled + tile[3 * lines : 3 * lines + 8] + tile[3 * lines + 8 : 3 * lines + 16]
+        pull_ref[...] = pulled
+        tile = e0[part : part + 16, :].astype(F32)
+        code_ref[...] = jnp.concatenate(
+            [tile[0:1] * 128.0 + tile[1:2], tile[2:3] * 128.0 + tile[3:4], jnp.zeros((6, 128), F32)], axis=0
+        )
 
     whole = pl.BlockSpec(memory_space=pltpu.VMEM)
     return pl.pallas_call(
         kernel,
-        out_shape=jax.ShapeDtypeStruct((count, 4 * part), F32),
+        out_shape=[
+            jax.ShapeDtypeStruct((count, 4 * part), F32),
+            jax.ShapeDtypeStruct((lines, 4 * part), F32),
+            jax.ShapeDtypeStruct((8, part), F32),
+            jax.ShapeDtypeStruct((8, 128), F32),
+        ],
         in_specs=[whole] * 8,
-        out_specs=whole,
+        out_specs=[whole] * 4,
         scratch_shapes=[pltpu.VMEM((count, part), F32)] * 2,
         compiler_params=pltpu.CompilerParams(vmem_limit_bytes=VMEM),
         cost_estimate=cost(0.1),
@@ -571,9 +610,8 @@
 
 def vectors(dilated, pointwise, gains7, gains1, bias7, bias1, first, second, last, project, cotangent):
     units, taps, part, chans = dilated.shape
-    own_frames = cotangent.shape[1] // 4
-
-    def kernel(d_ref, q_ref, g7, g1, b7, b1, a1, a2, a3, p_ref, t_ref, o0, o1, o2, o3, out_ref, pulled):
+
+    def kernel(d_ref, q_ref, g7, g1, b7, b1, a1, a2, a3, p_ref, t_ref, out_ref, pulled):
         out_ref[...] = jnp.zeros_like(out_ref)
         for u in range(units):
             total = jnp.zeros((part, 128), F32)
@@ -603,22 +641,16 @@
         out_ref[8 * units : 8 * units + 1, :] = a3[...] * (1.0 / jnp.pi)
         out_ref[8 * units + 1 : 8 * units + 2, :] = 1.0 / a3[...]
         pulled[...] = dot_tn(p_ref[...], t_ref[...])[0:8, :]
-        me = lax.axis_index("chan")
-        for p, piece in enumerate((o0, o1, o2, o3)):
-            piece[0 : 8 * units + 8, :] = out_ref[...]
-            frames = pl.ds(pl.multiple_of((me ^ p) * own_frames, own_frames), own_frames)
-            piece[8 * units + 8 : 8 * units + 16, :] = pulled[:, frames]
 
     whole = pl.BlockSpec(memory_space=pltpu.VMEM)
     return pl.pallas_call(
         kernel,
-        out_shape=[jax.ShapeDtypeStruct((8 * units + 16, part), F32)] * 4,
+        out_shape=[
+            jax.ShapeDtypeStruct((8 * units + 8, part), F32),
+            jax.ShapeDtypeStruct((8, cotangent.shape[1]), F32),
+        ],
         in_specs=[whole] * 11,
-        out_specs=[whole] * 4,
-        scratch_shapes=[
-            pltpu.VMEM((8 * units + 8, part), F32),
-            pltpu.VMEM((8, cotangent.shape[1]), F32),
-        ],
+        out_specs=[whole] * 2,
         compiler_params=pltpu.CompilerParams(vmem_limit_bytes=VMEM),
         cost_estimate=cost(0.1),
         name="vectors",
@@ -657,7 +689,7 @@
         in_specs=[whole] * 4,
         out_specs=[whole] * 2,
         compiler_params=pltpu.CompilerParams(vmem_limit_bytes=VMEM),
-        cost_estimate=cost(0.1),
+        cost_estimate=cost(5),
         name="merge_strided",
     )(strided, gains[None], bias[None], project)
 
@@ -771,7 +803,7 @@
     taps, rows, chans = strided.shape
     group = 4
 
-    def kernel(w_ref, m_ref, p_ref, n_ref, out_ref, vec_ref, total, factor, split):
+    def kernel(w_ref, m_ref, p_ref, n_ref, out_ref, vec_ref, kept, total, factor, split):
         phase, step = pl.program_id(0), pl.program_id(1)
 
         @pl.when((phase == 0) & (step == 0))
@@ -784,6 +816,7 @@
             for tap in range(group):
                 meeting = meeting + dot_nt(m_ref[tap], w_ref[tap])
             total[...] = meeting
+            kept[step] = w_ref[...]
 
         @pl.when((phase == 1) & (step == 0))
         def _():
@@ -799,7 +832,7 @@
         def _():
             for tap in range(group):
                 three = jnp.concatenate([m_ref[tap]] * 3, axis=0)
-                out_ref[tap] = dot_tn(split[...], three) - w_ref[tap].astype(F32) * lanes4(factor[...])
+                out_ref[tap] = dot_tn(split[...], three) - kept[step, tap].astype(F32) * lanes4(factor[...])
 
     whole = pl.BlockSpec(memory_space=pltpu.VMEM)
     return pl.pallas_call(
@@ -807,7 +840,7 @@
         grid=(2, taps // group),
         out_shape=[jax.ShapeDtypeStruct((taps, rows, chans), F32), jax.ShapeDtypeStruct((16, rows), F32)],
         in_specs=[
-            pl.BlockSpec((group, rows, chans), lambda phase, step: (step, 0, 0)),
+            pl.BlockSpec((group, rows, chans), lambda phase, step: (step * (1 - phase) + (taps // group - 1) * phase, 0, 0)),
             pl.BlockSpec((group, 8, chans), lambda phase, step: (step, 0, 0)),
             whole,
             whole,
@@ -816,60 +849,71 @@
             pl.BlockSpec((group, rows, chans), lambda phase, step: (phase * step, 0, 0)),
             pl.BlockSpec((16, rows), lambda phase, step: (0, 0)),
         ],
-        scratch_shapes=[pltpu.VMEM((8, rows), F32), pltpu.VMEM((rows, 128), F32), pltpu.VMEM((24, rows), BF)],
+        scratch_shapes=[
+            pltpu.VMEM((taps // group, group, rows, chans), BF),
+            pltpu.VMEM((8, rows), F32), pltpu.VMEM((rows, 128), F32),
+            pltpu.VMEM((24, rows), BF),
+        ],
         compiler_params=pltpu.CompilerParams(vmem_limit_bytes=VMEM),
         cost_estimate=cost(0.1),
         name="strided_back",
     )(strided, mixed_grad, project, norms)
 
 
-def norm_back(total, dilated, pointwise, gains, member, earlier):
+def norm_back(chains, dilated, pointwise, gains, members, earlier):
     units, _, part, chans = dilated.shape
+    count = len(members)
 
     def kernel(*refs):
-        held, w_ref, q_ref, g_ref = refs[0], refs[1].at[0], refs[2], refs[3].at[0]
-        out7, out1, out_g, res7, res1, row_g, sems = refs[-7:]
-
-        def grad_of(tap):
-            return held[tap * part : (tap + 1) * part, :].astype(F32)
-
-        def weight_of(tap):
-            return (q_ref[0] if tap == 7 else w_ref[tap]).astype(F32)
-
-        def one(taps):
-            square = jnp.zeros((part, 128), F32)
-            along = jnp.zeros((part, 128), F32)
-            for tap in taps:
-                value, grad = weight_of(tap), grad_of(tap)
-                both, value2 = value * grad, value * value
-                for g in range(chans // 128):
-                    cols = slice(g * 128, (g + 1) * 128)
-                    square = square + value2[:, cols]
-                    along = along + both[:, cols]
-            square_sum = jnp.sum(square, axis=1, keepdims=True) + NORM_EPS
-            factor = jnp.sum(along, axis=1, keepdims=True) / square_sum
-            return lane_sums(along), factor
-
-        along, factor = one(range(7))
-        row_g[...] = jnp.zeros_like(row_g)
-        row_g[0:1, :] = along / g_ref[0:1, :]
+        halves, refs = refs[: 2 * count], refs[2 * count :]
+        w_refs, q_refs, g_refs = (refs[n * count : (n + 1) * count] for n in range(3))
+        out7, out1, out_g, helds, res7, res1, row_g, sems = refs[-8:]
         outs = []
-        for tap in range(7):
-            res7[tap] = grad_of(tap) - weight_of(tap) * factor
-            outs.append(pltpu.make_async_copy(res7.at[tap], out7.at[member, tap], sems.at[tap]))
+
+        def send(value, target):
+            outs.append(pltpu.make_async_copy(value, target, sems.at[len(outs)]))
             outs[-1].start()
-        along, factor = one((7,))
-        row_g[1:2, :] = along / g_ref[1:2, :]
-        res1[...] = grad_of(7) - weight_of(7) * factor
-        outs.append(pltpu.make_async_copy(res1, out1.at[member], sems.at[7]))
-        outs[-1].start()
-        outs.append(pltpu.make_async_copy(row_g, out_g.at[member], sems.at[8]))
-        outs[-1].start()
+
+        for n, member in enumerate(members):
+            rows = halves[2 * n].shape[0]
+            upper = bit_of(*chains[n].last)
+            helds[n, pl.ds(pl.multiple_of(upper * rows, 16), rows), :] = halves[2 * n][...]
+            helds[n, pl.ds(pl.multiple_of((1 - upper) * rows, 16), rows), :] = halves[2 * n + 1][...]
+
+            def grad_of(tap, n=n):
+                return helds[n, tap * part : (tap + 1) * part, :].astype(F32)
+
+            def weight_of(tap, n=n):
+                return (q_refs[n][0] if tap == 7 else w_refs[n][0, tap]).astype(F32)
+
+            row_g[n] = jnp.zeros_like(row_g[n])
+            for which, taps in enumerate((range(7), (7,))):
+                square = jnp.zeros((part, 128), F32)
+                along = jnp.zeros((part, 128), F32)
+                for tap in taps:
+                    value, grad = weight_of(tap), grad_of(tap)
+                    both, value2 = value * grad, value * value
+                    for g in range(chans // 128):
+                        cols = slice(g * 128, (g + 1) * 128)
+                        square = square + value2[:, cols]
+                        along = along + both[:, cols]
+                square_sum = jnp.sum(square, axis=1, keepdims=True) + NORM_EPS
+                factor = jnp.sum(along, axis=1, keepdims=True) / square_sum
+                row_g[n, which : which + 1, :] = lane_sums(along) / g_refs[n][0, which : which + 1, :]
+                for tap in taps:
+                    target = res1.at[n] if tap == 7 else res7.at[n, tap]
+                    target[...] = grad_of(tap) - weight_of(tap) * factor
+                    send(target, out1.at[member] if tap == 7 else out7.at[member, tap])
+            send(row_g.at[n], out_g.at[member])
         for copy in outs:
             copy.wait()
 
     whole = pl.BlockSpec(memory_space=pltpu.VMEM)
     held = pl.BlockSpec(memory_space=pl.ANY)
+
+    def block(shape, member):
+        return pl.BlockSpec((1,) + shape, lambda step: (member,) + (0,) * len(shape))
+
     return pl.pallas_call(
         kernel,
         grid=(1,),
@@ -878,25 +922,24 @@
             jax.ShapeDtypeStruct((units, part, chans), F32),
             jax.ShapeDtypeStruct((units, 8, part), F32),
         ],
-        in_specs=[
-            whole,
-            pl.BlockSpec((1, 7, part, chans), lambda step: (member, 0, 0, 0)),
-            pl.BlockSpec((1, part, chans), lambda step: (member, 0, 0)),
-            pl.BlockSpec((1, 2, part), lambda step: (member, 0, 0)),
-        ]
+        in_specs=[whole] * (2 * count)
+        + [block((7, part, chans), member) for member in members]
+        + [block((part, chans), member) for member in members]
+        + [block((2, part), member) for member in members]
         + [held] * len(earlier),
         out_specs=[held] * 3,
-        input_output_aliases={4 + n: n for n in range(len(earlier))},
+        input_output_aliases={5 * count + n: n for n in range(len(earlier))},
         scratch_shapes=[
-            pltpu.VMEM((7, part, chans), F32),
-            pltpu.VMEM((part, chans), F32),
-            pltpu.VMEM((8, part), F32),
-            pltpu.SemaphoreType.DMA((9,)),
+            pltpu.VMEM((count, max(2 * chain.whole[0].shape[0] for chain in chains), chans), BF),
+            pltpu.VMEM((count, 7, part, chans), F32),
+            pltpu.VMEM((count, part, chans), F32),
+            pltpu.VMEM((count, 8, part), F32),
+            pltpu.SemaphoreType.DMA((9 * count,)),
         ],
         compiler_params=pltpu.CompilerParams(vmem_limit_bytes=VMEM),
         cost_estimate=cost(0.1),
-        name=f"norm_back_{member}",
-    )(total, dilated, pointwise, gains, *earlier)
+        name="norm_back",
+    )(*[half for chain in chains for half in chain.whole], *[dilated] * count, *[pointwise] * count, *[gains] * count, *earlier)
 
 
 def leave(grad, own):
@@ -925,26 +968,48 @@
     )(grad)
 
 
-def bottleneck(stream, merged, vecs, labels, chosen, picked_grad, own):
+def settle(pieces):
+    part, own = pieces[0].shape
+
+    def kernel(p0, p1, p2, p3, out_ref):
+        me = lax.axis_index("chan")
+        for p, piece in enumerate((p0, p1, p2, p3)):
+            out_ref[:, pl.ds(pl.multiple_of((me ^ p) * own, own), own)] = piece[...].astype(F32)
+
+    whole = pl.BlockSpec(memory_space=pltpu.VMEM)
+    return pl.pallas_call(
+        kernel,
+        out_shape=jax.ShapeDtypeStruct((part, 4 * own), F32),
+        in_specs=[whole] * 4,
+        out_specs=whole,
+        compiler_params=pltpu.CompilerParams(vmem_limit_bytes=VMEM),
+        cost_estimate=cost(0.1),
+        name="settle",
+    )(*pieces)
+
+
+def bottleneck(stream, merged, bias, vecs, labels, chosen, picked_grad, own):
     rows, chans = stream.shape
     span = rows // SEG
     groups = span // STRIDE
     count = groups * SEG
-    taps = merged.shape[0] // 8 - 1
+    taps = merged[0].shape[0] // 8 - 1
     edge = 16 * SEG
+    turn_row = vecs.shape[0] - 8
 
     def kernel(
-        s_ref, w_ref, v_ref, l_ref, c_ref, o_ref, g_ref, lat_ref, dch_ref, m_ref, sum_ref,
+        s_ref, wa_ref, wb_ref, bias_ref, v_ref, l_ref, c_ref, o_ref, g_ref, lat_ref, dch_ref, m_ref, sum_ref,
         q_ref, wide, full, codes, sums,
     ):
         blank = jnp.zeros((104, chans), BF)
         for tap in range(taps):
-            high, rest = terms(w_ref[8 * tap : 8 * tap + 8, :], 2)
+            here = slice(8 * tap, 8 * tap + 8)
+            high, rest = terms(wa_ref[here, :] + wb_ref[here, :], 2)
             q_ref[tap] = jnp.concatenate([high, high, rest, blank], axis=0)
         shift = jnp.sum(
             jnp.where(
                 lax.broadcasted_iota(jnp.int32, (8, 128), 0) == lax.broadcasted_iota(jnp.int32, (8, 128), 1),
-                w_ref[8 * taps : 8 * taps + 8, 0:128],
+                wa_ref[8 * taps : 8 * taps + 8, 0:128] + wb_ref[8 * taps : 8 * taps + 8, 0:128],
                 0.0,
             ),
             axis=0,
@@ -954,7 +1019,7 @@
         @pl.loop(0, rows, step=CHUNK)
         def _(start):
             start = pl.multiple_of(start, CHUNK)
-            act = snake(s_ref[pl.ds(start, CHUNK), :], v_ref[0:1, :], v_ref[1:2, :])
+            act = snake(s_ref[pl.ds(start, CHUNK), :], v_ref[turn_row : turn_row + 1, :], v_ref[turn_row + 1 : turn_row + 2, :])
             full[pl.ds(8 + start, CHUNK), :] = act
             wide[pl.ds(edge + start, CHUNK), :] = act.astype(BF)
 
@@ -981,7 +1046,7 @@
         for tap in range(taps):
             total = total + dot_nt(tap_columns(tap), q_ref[tap])
         lane = lax.broadcasted_iota(jnp.int32, (count, 128), 1)
-        latent = jnp.where(lane < 8, total + pltpu.roll(total, 112, 1) + shift + v_ref[2:3, :128], 0.0)
+        latent = jnp.where(lane < 8, total + pltpu.roll(total, 112, 1) + shift + bias_ref[...], 0.0)
         lat_ref[...] = latent
         inverse = lax.rsqrt(jnp.sum(latent * latent, axis=1, keepdims=True) + 1.0)
         normed = latent * inverse
@@ -1020,7 +1085,7 @@
             for g in range(groups):
                 here = pl.ds((g * STRIDE + rest) * SEG, SEG)
                 part = total[g * SEG : (g + 1) * SEG, :]
-                value, slope, by_alpha = snake_parts(s_ref[here, :], v_ref[0:1, :], v_ref[1:2, :])
+                value, slope, by_alpha = snake_parts(s_ref[here, :], v_ref[turn_row : turn_row + 1, :], v_ref[turn_row + 1 : turn_row + 2, :])
                 g_ref[here, :] = part * slope
                 mask = lanes4(own_mask((g * STRIDE + rest) * SEG, SEG, span, own))
                 sums[...] += fold(part * by_alpha * mask)
@@ -1037,7 +1102,7 @@
             jax.ShapeDtypeStruct((taps, 8, chans), F32),
             jax.ShapeDtypeStruct((8, chans), F32),
         ],
-        in_specs=[whole] * 6,
+        in_specs=[whole] * 8,
         out_specs=[whole] * 5,
         scratch_shapes=[
             pltpu.VMEM((taps, 128, chans), BF),
@@ -1049,7 +1114,7 @@
         compiler_params=pltpu.CompilerParams(vmem_limit_bytes=VMEM),
         cost_estimate=cost(11),
         name="bottleneck",
-    )(stream, merged, vecs, labels, chosen, picked_grad)
+    )(stream, *merged, bias, vecs, labels, chosen, picked_grad)
 
 
 def swap(value, axis, bit):
@@ -1180,11 +1245,17 @@
                 self.kept, self.sent = sum_halves(terms_in, self.rows, self.adds[0])
             else:
                 self.sent = sum_halves(terms_in, self.rows, None)[0]
+        elif self.left:
+            self.sent = join(self.sent, got, self.joins.pop(0))
         else:
-            self.sent = self.whole = join(self.sent, got, self.joins.pop(0))
+            self.whole = (self.sent, got)
+            self.last = self.joins.pop(0)
         if self.left:
             self.start()
         return self.sent
+
+    def upper(self):
+        return jnp.where(bit_of(*self.last) == 1, *self.whole)
 
 
 def after(value, *others):
@@ -1243,21 +1314,12 @@
         [output_proj] + [term[:, None] for term in terms(output_bias, 3)] + [jnp.zeros((output_bias.shape[0], 117), BF)],
         axis=1,
     )
-    packed = vectors(
+    packed, pulled = vectors(
         after(dilated_dirs, halves[0]), pointwise_dirs, dilated_gains, pointwise_gains, dilated_bias, pointwise_bias,
         snake_first, snake_second, snake_last, project, cotangent,
     )
-    packed = [packed[0]] + [to_peer(packed[peer], peer) for peer in (1, 2, 3)]
-    code_ends = after(code_index, packed[0])
-    around = jnp.concatenate(
-        [
-            lax.ppermute(code_ends[frames - extra :], "frames", [(i, i + 1) for i in range(ring - 1)]),
-            code_index,
-            lax.ppermute(code_ends[:extra], "frames", [(i + 1, i) for i in range(ring - 1)]),
-        ]
-    )
-
-    pieces, ends = cut(after(signal, packed[0]))
+
+    pieces, ends = cut(signal, packed, pulled, code_index.reshape(-1, 128))
     pieces = [pieces[0]] + [to_peer(pieces[peer], peer) for peer in (1, 2, 3)]
     ends = [
         lax.ppermute(
@@ -1271,17 +1333,8 @@
     rest = [swap(far[0], "frames", 0)]
     far_close = [swap(far[0], "chan", 0)]
     rest_close = [swap(rest[0], "chan", 0)]
-    for member in (1, 2):
-        far.append(swap(after(halves[member], *pieces), "chan", 1))
-    lines = packed[0].shape[0] - 8
-    vecs = jnp.zeros((lines, chans), F32)
-    mine_pulled = None
-    for peer in range(4):
-        got = packed[peer]
-        vecs = lax.dynamic_update_slice(vecs, got[:lines], (0, (me ^ peer) * part))
-        mine_pulled = got[lines:] if mine_pulled is None else mine_pulled + got[lines:]
-    mine_pulled = jnp.pad(mine_pulled, ((0, 120), (extra, extra)))
-    mine_pulled = mine_pulled.reshape(128, SEG, span_frames).transpose(2, 1, 0).reshape(-1, 128)
+    far.append(swap(after(halves[1], *pieces), "chan", 1))
+    far.append(swap(after(halves[2], *pieces), "chan", 1))
 
     bounds = jnp.cumsum(utterances) * STRIDE
     b_place = jnp.arange(-LEAD, span + LEAD, dtype=jnp.int32)
@@ -1297,60 +1350,59 @@
     place = jnp.where(owned, place - extra + block * frames + me * own_frames, -1)
     place = jnp.broadcast_to(place[:, None], (place.shape[0], 128))
     refill = refill_index.reshape(-1, 512)
-    near = lax.dynamic_slice_in_dim(around, me * own_frames, own_frames + 2 * extra)
-    near = near.reshape(SEG, span_frames).T.reshape(-1)
-    wanted = jnp.broadcast_to(jnp.concatenate([near, code_index])[:, None], (near.shape[0] + frames, 128))
-    *held, labels, vecs, mine_pulled, place, refill, wanted, _ = lax.optimization_barrier(
-        (*pieces, *ends, labels, vecs, mine_pulled, place, refill, wanted, far[0])
-    )
-    near_rows = wanted[: near.shape[0]]
-    stream = enter(held[:4], held[4:], own)
+    labels, place, refill, project_in, _ = lax.optimization_barrier((labels, place, refill, latent_proj, halves[0]))
+    merged, norms = merge_strided(strided_dirs, strided_gains, strided_bias, project_in)
+    *held, _, _ = lax.optimization_barrier((*pieces, *ends, far[0], merged))
+    stream, vecs, pulled, edge_codes = enter(held[:4], held[4:], packed.shape[0], own)
 
     def unit(member, stream, *far_pieces):
         pieces = (dilated_dirs, pointwise_dirs, *close, *far_pieces)
-        vec = vecs[8 * member : 8 * member + 8]
-        result, middle, wide, weight1 = unit_forward(stream, pieces, member, vec, labels)
-        saved.append((stream, middle, wide, vec, weight1, pieces))
+        result, middle, wide, weight1 = unit_forward(stream, pieces, member, vecs, labels)
+        saved.append((stream, middle, wide, weight1, pieces))
         return result
 
     saved = []
     stream = unit(0, stream, far[0], rest[0], far_close[0], rest_close[0])
     rest.append(swap(after(far[1], stream), "frames", 0))
     far_close.append(swap(after(far[1], stream), "chan", 0))
-
-    chosen, output, sums_out = look_up(after(wanted, stream), codebook, project, cotangent, near.shape[0])
-    rest_close.append(swap(after(rest[1], chosen), "chan", 0))
+    got = swap(after(merged, stream), "chan", 0)
+
+    edge_codes = edge_codes.astype(jnp.int32)
+    around = jnp.concatenate([edge_codes[1, 128 - extra :], code_index, edge_codes[0, :extra]])
+    near = lax.dynamic_slice_in_dim(around, me * own_frames, own_frames + 2 * extra)
+    near = near.reshape(SEG, span_frames).T.reshape(-1)
+    wanted = jnp.broadcast_to(jnp.concatenate([near, code_index])[:, None], (near.shape[0] + frames, 128))
+    near_rows = wanted[: near.shape[0]]
+    pulled = jnp.pad(pulled, ((0, 120), (extra, extra)))
+    pulled = pulled.reshape(128, SEG, span_frames).transpose(2, 1, 0).reshape(-1, 128)
+    latent_bias = jnp.pad(latent_bias, (0, 128 - latent_bias.shape[0]))[None]
+    wanted, near_rows, pulled, latent_bias, _ = lax.optimization_barrier((wanted, near_rows, pulled, latent_bias, stream))
+    chosen, output, sums_out = look_up(wanted, codebook, project, cotangent, near.shape[0])
+    merged = merged + after(got, chosen)
+    got = swap(merged, "chan", 1)
+    rest_close.append(swap(after(rest[1], merged), "chan", 0))
+    rest.append(swap(after(halves[3], far[2], merged), "chan", 1))
+    far_close.append(swap(after(far[2], merged), "chan", 0))
     stream = unit(1, after(stream, chosen), far[1], rest[1], far_close[1], rest_close[1])
-    far_close.append(swap(after(far[2], stream), "chan", 0))
-    merged, norms = merge_strided(strided_dirs, strided_gains, strided_bias, after(latent_proj, stream))
-    merged = merged + swap(merged, "chan", 0)
-    got = swap(merged, "chan", 1)
-    stream = unit(2, after(stream, merged), far[2], far_close[2])
-    merged = merged + after(got, stream)
-    tail_vecs = jnp.concatenate(
-        [
-            vecs[8 * units : 8 * units + 2],
-            jnp.pad(latent_bias, (0, chans - latent_bias.shape[0]))[None],
-            jnp.zeros((5, chans), F32),
-        ]
+    rest_close.append(swap(after(rest[2], stream), "chan", 0))
+    stream = unit(2, stream, far[2], rest[2], far_close[2], rest_close[2])
+    merged = (merged, after(got, stream))
+    grad, latent, dchosen, mixed_grad, last_sums = bottleneck(
+        stream, merged, latent_bias, vecs, labels, chosen, pulled, own
     )
-    grad, latent, dchosen, mixed_grad, last_sums = bottleneck(
-        stream, merged, tail_vecs, labels, chosen, mine_pulled, own
-    )
 
     bit0, bit1 = over_chan
 
-    unit_vecs = [saved[member][3] for member in range(units)]
     rows = grad.shape[0]
 
     def weights_of(member, grad=None):
-        _, middle, wide, _, weight1, _ = saved[member]
+        _, middle, wide, weight1, _ = saved[member]
         return (member, grad, middle, wide, weight1)
 
     def into_of(member, grad, scaled):
-        return (member, grad, saved[member][0], scaled, saved[member][5])
-
-    back2 = units_back(unit_vecs, labels, own, rows, chans, weights=weights_of(2, grad))
+        return (member, grad, saved[member][0], scaled, saved[member][4])
+
+    back2 = units_back(vecs, labels, own, rows, chans, weights=weights_of(2, grad))
     keep2 = back2["keep"]
     near2 = swap(back2["send"], "chan", 0)
     chain_rows = -(-(8 * part + 128) // (16 * ring)) * 16 * ring
@@ -1360,7 +1412,7 @@
     far2 = add_up(keep2[1], near2[1])
     x2 = swap(far2, "chan", 1)
     back1 = units_back(
-        unit_vecs, labels, own, rows, chans, into_of(2, after(grad, far2), back2["scaled_out"]), weights_of(1)
+        vecs, labels, own, rows, chans, into_of(2, after(grad, far2), back2["scaled_out"]), weights_of(1)
     )
     keep1 = back1["keep"]
     near1 = swap(back1["send"], "chan", 0)
@@ -1371,7 +1423,7 @@
     far1 = add_up(keep1[1], after(near1, chain2.sent)[1])
     x1 = swap(far1, "chan", 1)
     back0 = units_back(
-        unit_vecs, labels, own, rows, chans,
+        vecs, labels, own, rows, chans,
         into_of(1, after(back1["out"], far1), back1["scaled_out"]), weights_of(0),
     )
     keep0 = back0["keep"]
@@ -1381,7 +1433,7 @@
     more = jnp.pad(more, ((0, 16 - more.shape[0]), (0, 0)))
     chain1 = Chain([[(keep1, 0), (near1, 0), (after(x1, token), None)], [(more, None)]], chain_rows, over_frames)
     last = units_back(
-        unit_vecs, labels, own, rows, chans, into_of(0, after(back0["out"], chain1.sent), back0["scaled_out"]),
+        vecs, labels, own, rows, chans, into_of(0, after(back0["out"], chain1.sent), back0["scaled_out"]),
         others=(back0["sums_a"], back0["sums_c"], back1["sums_a"], back1["sums_c"], back2["sums_a"], last_sums),
     )
     grad, small = last["out"], last["sums_c"]
@@ -1405,53 +1457,51 @@
         token = small
 
     half = len(over_frames)
+    while chain2.adds:
+        token = chain2.step(token)
     small_step()
-    token = chain2.step(token)
     token = chain1.step(token)
     small_step()
     token = chain2.step(token)
     chain0 = Chain([[(keep0, 0), (near0, 0), (after(x0, token), None)]], 8 * part, over_frames)
     token = chain0.sent
-    grad_signal = jnp.zeros((part, extent), F32)
-    for peer in range(4):
-        got = after(sent_outs[peer], token).astype(F32)
-        grad_signal = lax.dynamic_update_slice(grad_signal, got, (0, (me ^ peer) * own))
-    token = grad_signal
+    while chain1.left > half:
+        token = chain1.step(token)
+    while chain2.left > 1:
+        token = chain2.step(token)
+    token = chain0.step(token)
     while len(small_steps) > 2:
         small_step()
-    while chain1.left > half:
-        token = chain1.step(token)
-    token = chain0.step(token)
-    small_step()
-    while chain2.left > 1:
-        token = chain2.step(token)
-    token = chain1.step(token)
-    token = chain0.step(token)
-    small_step()
-    while chain1.left > 1:
-        token = chain1.step(token)
-    while chain0.left > half:
+    while chain0.left > half + 1:
         token = chain0.step(token)
     token = chain2.step(token)
     quarter = codes[0].shape[0]
-    total2 = chain2.whole
-    codes_mine = total2[8 * part : 8 * part + quarter]
+    first = 8 * part - chain_rows // 2
+    codes_mine = chain2.upper()[first : first + quarter]
     got_codes = [codes_mine] + [to_peer(codes_mine, peer) for peer in (1, 2, 3)]
-    gains = jnp.stack([dilated_gains, pointwise_gains], axis=1)
-    results = norm_back(after(total2, token), dilated_dirs, pointwise_dirs, gains, 2, ())
-    token = chain0.step(results[0])
+    token = chain1.step(token)
+    small_step()
+    token = chain0.step(token)
     payload = jnp.zeros((4 * quarter, chans), BF)
     for peer in range(4):
         got = after(got_codes[peer], token)
         payload = lax.dynamic_update_slice_in_dim(payload, got, (me ^ peer) * quarter, 0)
     blocks = codebook.shape[1] // 512
     dstrided_dirs, meeting = strided_back(strided_dirs, payload[24 * blocks :].reshape(-1, 8, chans), latent_proj, norms)
-    token = dstrided_dirs
+    token = chain0.step(dstrided_dirs)
+    while chain1.left > 1:
+        token = chain1.step(token)
+    gains = jnp.stack([dilated_gains, pointwise_gains], axis=1)
+    results = norm_back([chain2], after(dilated_dirs, token), pointwise_dirs, gains, (2,), ())
+    token = results[0]
+    small_step()
+    grad_signal = settle(list(lax.optimization_barrier((*sent_outs, token))[:4]))
+    token = grad_signal
     while chain0.left > 1:
         token = chain0.step(token)
     token = chain1.step(token)
-    results = norm_back(chain1.whole, dilated_dirs, pointwise_dirs, gains, 1, results)
-    payload = after(payload, token)
+    results = norm_back([chain1], after(dilated_dirs, token), pointwise_dirs, gains, (1,), results)
+    payload = after(payload, results[0])
     codes = codebook.shape[1]
     blocks = codes // 512
     by_code = payload[: 24 * blocks].reshape(blocks, 24, 512).transpose(1, 0, 2).reshape(24, codes).astype(F32)
@@ -1461,11 +1511,10 @@
     coded = codebook * coded_scale[None, :]
     dcodebook = (dcoded - coded * jnp.sum(coded * dcoded, axis=0)[None, :]) * coded_scale[None, :]
 
-    token = lax.optimization_barrier((results[0], refreshed, dcodebook))[0]
+    token = lax.optimization_barrier((token, refreshed, dcodebook))[0]
     chain0.step(token)
-    total0 = chain0.whole
-    results = norm_back(total0, dilated_dirs, pointwise_dirs, gains, 0, results)
-    sums_out = chain1.whole[8 * part : 8 * part + output_bias.shape[0] * 16 // chans].astype(F32).reshape(-1, 16)
+    results = norm_back([chain0], dilated_dirs, pointwise_dirs, gains, (0,), results)
+    sums_out = chain1.upper()[first : first + output_bias.shape[0] * 16 // chans].astype(F32).reshape(-1, 16)
     mine_small = lax.dynamic_slice_in_dim(small, me * part, part, axis=1)
     dbias_latent = small[6 * 8 + 1, :8]
     dbias1, dbias7, dalpha2 = mine_small[8:48:16], mine_small[9:48:16], mine_small[10:48:16]

time: 403 us -> 379 us (0.940)
  starting transfers between devices: 77.5 us -> 61.5 us
  Pallas kernels: 227 us -> 222 us
    ppermute x15 -> x12, starting transfers between devices: 17.2 us -> 9.73 us  [to_peer(): return lax.ppermute(value, 'chan', [(i, i ^ peer) for i in range(4)])]
    pallas_call x9 -> x6, Pallas kernels: 17.8 us -> 10.8 us  [join(): pl.pallas_call(kernel, out_shape=jax.ShapeDtypeStruct((2 * rows, chans),...]
    ppermute x2 -> x0, starting transfers between devices: 4.7 us -> none  [the longest x1 3.41 us: local(): lax.ppermute(code_ends[frames - extra:], 'frames', [(i, i + 1) for i in r...]
    unnamed x123 -> x145, local copies, waits for them, and re-layouts: 15.7 us -> 20 us
    pallas_call x3 -> x4, Pallas kernels: 11 us -> 14.2 us  [the longest x1 5.23 us: enter(): pl.pallas_call(kernel, out_shape=[jax.ShapeDtypeStruct((count, 4 * part),...]
    ppermute x15 -> x12, waiting for transfers between devices: 10.7 us -> 7.49 us  [to_peer(): return lax.ppermute(value, 'chan', [(i, i ^ peer) for i in range(4)])]
    ppermute x43 -> x45, starting transfers between devices: 48.8 us -> 47.3 us  [swap(): return lax.ppermute(value, axis, [(i, i ^ 1 << bit) for i in range(count)])]
    ppermute x43 -> x45, waiting for transfers between devices: 33 us -> 32.5 us  [swap(): return lax.ppermute(value, axis, [(i, i ^ 1 << bit) for i in range(count)])]
  transfers between devices with their start and end apart: 64 -> 61, of which waited for: 13 -> 13; matrix products, arithmetic and copies ran while one was open for 7% -> 7% of each run, Pallas kernels for 48% -> 50%
where the time goes in v3:
time: 379 us; the launch traced here: 373 us
  Pallas kernels  222 us (59%)
  starting transfers between devices  61.5 us (16%)
  waiting for transfers between devices  40 us (11%)
  local copies, waits for them, and re-layouts  36.2 us (10%)
  other arithmetic  11.5 us (3%)
    pallas_call x4, Pallas kernels, units_back(): pl.pallas_call(kernel, out_shape=[shape for shape, _ in outs.values()], i...  77.6 us
    ppermute x45, starting transfers between devices, swap(): return lax.ppermute(value, axis, [(i, i ^ 1 << bit) for i in range(count)])  47.3 us
    pallas_call x3, Pallas kernels, unit_forward(): pl.pallas_call(kernel, out_shape=[jax.ShapeDtypeStruct((rows, chans), F32...  35.6 us
    ppermute x45, waiting for transfers between devices, swap(): return lax.ppermute(value, axis, [(i, i ^ 1 << bit) for i in range(count)])  32.5 us
    pallas_call x12, Pallas kernels, sum_halves(): pl.pallas_call(kernel, grid=(1,), out_shape=[jax.ShapeDtypeStruct((half,...  27.3 us
    unnamed x145, local copies, waits for them, and re-layouts  20 us
    pallas_call x3, Pallas kernels, norm_back(): pl.pallas_call(kernel, grid=(1,), out_shape=[jax.ShapeDtypeStruct((units,...  11.3 us
    pallas_call x1, Pallas kernels, bottleneck(): pl.pallas_call(kernel, out_shape=[jax.ShapeDtypeStruct((rows, chans), F32...  10.9 us
  transfers between devices with their start and end apart: 61, of which 13 were waited for; matrix products, arithmetic and copies ran while one was open for 7% of the time, Pallas kernels for 50%

profile of v3, /device:TPU:0, one launch (start us, length us, event | category | flops | bytes accessed | tf_op | source)
XLA Modules:
  0.0 372.9 jit_solution(4090720621512432198)
XLA Ops:
  0.7 3.0 halve.1
  4.6 2.5 collective-permute-start.7
  8.3 3.3 vectors.1
  11.6 2.9 cut.1
  18.7 2.9 collective-permute-start
  21.6 2.2 collective-permute-start.1
  23.8 2.6 collective-permute-start.10
  31.0 1.9 collective-permute-start.3
  33.3 7.2 %collective-permute-done.2.p3 = bf16[128,1408]{1,0:T(8,128)(2,1)} collective-permute-done((bf16[128,1408]{1,0:T(8,128)(2,1)}, bf16[128,1408]{1,0:T(8,128)(2,1)}, u32[]{:S(2)}, u32[]{:S(2)}) %collective-permute-start.2) | collective-permute-done | bytes 360480 | tf_op jit(solution)/shard_map/ppermute | solution.py:1266
  40.9 4.7 %merge_strided.1 = (f32[136,512]{1,0:T(8,128)}, f32[8,256]{1,0:T(8,128)}) custom-call(bf16[16,256,512]{2,1,0:T(8,128)(2,1)} %w_ref.3, f32[1,256]{1,0:T(1,128)} %bitcast.58, f32[1,256]{1,0:T(1,128)} %bitcast.55, bf16[8,256]{1,0:T(8,128)(2,1)} %p_ref.2), custom_call_target="tpu_custom_call" | custom-call | flops 5750000128 | tf_op jit(solution)/shard_map/merge_strided/pallas_call | solution.py:686
  47.1 5.2 %enter.1 = (f32[1280,512]{1,0:T(8,128)}, f32[32,512]{1,0:T(8,128)}, f32[8,128]{1,0:T(8,128)}, f32[8,128]{1,0:T(8,128)}) custom-call(bf16[128,1408]{1,0:T(8,128)(2,1)} %get-tuple-element.204.p0, bf16[128,1408]{1,0:T(8,128)(2,1)} %copy-done.17, bf16[128,1408]{1,0:T(8,128)(2,1)} %collective-permute-done.1.p2, bf16[128,1408]{1,0:T(8,128)(2,1)} %collective-permute-done.2.p3, ...), custom_call_target="tpu_custom_call" | custom-call | flops 115000000 | tf_op jit(solution)/shard_map/enter/pallas_call | solution.py:590
  52.4 11.7 %unit_forward_1.1 = (f32[1280,512]{1,0:T(8,128)}, f32[1280,512]{1,0:T(8,128)}, bf16[1376,512]{1,0:T(8,128)(2,1)}, bf16[512,512]{1,0:T(8,128)(2,1)}) custom-call(f32[1280,512]{1,0:T(8,128)} %get-tuple-element.214.s_ref.refs_3_, bf16[3,7,128,512]{3,2,1,0:T(8,128)(2,1)} %refs_2_.3, bf16[3,128,512]{2,1,0:T(8,128)(2,1)} %refs_3_.5, ...), custom_call_target="tpu_custom_call" | custom-call | flops 13799999488 | tf_op jit(solution)/shard_map/unit_forward_1/pallas_call | solution.py:221
  70.1 8.0 %look_up.1 = (f32[160,128]{1,0:T(8,128)}, f32[256,512]{1,0:T(8,128)}, f32[256,128]{1,0:T(8,128)}) custom-call(s32[672,128]{1,0:T(8,128)} %broadcast_in_dim.85.i_ref, f32[8,8192]{1,0:T(8,128)} %c_ref.1, bf16[256,128]{1,0:T(8,128)(2,1)} %concatenate.9.p_ref, bf16[256,512]{1,0:T(8,128)(2,1)} %t_ref.3), custom_call_target="tpu_custom_call" | custom-call | flops 115000000 | tf_op jit(solution)/shard_map/look_up/pallas_call | solution.py:728
  82.5 11.7 %unit_forward_3.1 = (f32[1280,512]{1,0:T(8,128)}, f32[1280,512]{1,0:T(8,128)}, bf16[1568,512]{1,0:T(8,128)(2,1)}, bf16[512,512]{1,0:T(8,128)(2,1)}) custom-call(f32[1280,512]{1,0:T(8,128)} %get-tuple-element.222.s_ref.refs_3_, bf16[3,7,128,512]{3,2,1,0:T(8,128)(2,1)} %refs_2_.3, bf16[3,128,512]{2,1,0:T(8,128)(2,1)} %refs_3_.5, ...), custom_call_target="tpu_custom_call" | custom-call | flops 13799999488 | tf_op jit(solution)/shard_map/unit_forward_3/pallas_call | solution.py:221
  97.2 12.3 %unit_forward_9.1 = (f32[1280,512]{1,0:T(8,128)}, f32[1280,512]{1,0:T(8,128)}, bf16[2144,512]{1,0:T(8,128)(2,1)}, bf16[512,512]{1,0:T(8,128)(2,1)}) custom-call(f32[1280,512]{1,0:T(8,128)} %get-tuple-element.229.s_ref.refs_3_, bf16[3,7,128,512]{3,2,1,0:T(8,128)(2,1)} %refs_2_.3, bf16[3,128,512]{2,1,0:T(8,128)(2,1)} %refs_3_.5, ...), custom_call_target="tpu_custom_call" | custom-call | flops 13799999488 | tf_op jit(solution)/shard_map/unit_forward_9/pallas_call | solution.py:221
  110.2 10.9 %bottleneck.1 = (f32[1280,512]{1,0:T(8,128)}, f32[160,128]{1,0:T(8,128)}, f32[160,128]{1,0:T(8,128)}, f32[16,8,512]{2,1,0:T(8,128)}, f32[8,512]{1,0:T(8,128)}) custom-call(f32[1280,512]{1,0:T(8,128)} %get-tuple-element.236.s_ref, f32[136,512]{1,0:T(8,128)} %copy-done.23, f32[136,512]{1,0:T(8,128)} %copy-done.60, f32[1,128]{1,0:T(1,128)} %pad_bitcast_fusion.bias_ref, ...), custom_call_target="tpu_custom_call" | custom-call | flops 12650000384 | tf_op jit(solution)/shard_map/bottleneck/pallas_call | solution.py:1096
  121.2 14.7 %units_back_weights_9.1 = (bf16[1280,512]{1,0:T(8,128)(2,1)}, bf16[2,8,128,512]{3,2,1,0:T(8,128)(2,1)}, bf16[2,8,128,512]{3,2,1,0:T(8,128)(2,1)}, f32[8,512]{1,0:T(8,128)}) custom-call(f32[2176,128]{1,0:T(8,128)} %broadcast_in_dim.82.refs_9_.l_ref.refs_0_, f32[32,512]{1,0:T(8,128)} %get-tuple-element.216.refs_8_.v_ref.refs_1_, ...), custom_call_target="tpu_custom_call" | custom-call | flops 39099998208 | tf_op jit(solution)/shard_map/units_back_weights_9/pallas_call | solution.py:448
  136.9 6.1 %code_payload.1 = (bf16[128,512]{1,0:T(8,128)(2,1)}, bf16[128,512]{1,0:T(8,128)(2,1)}, bf16[128,512]{1,0:T(8,128)(2,1)}, bf16[128,512]{1,0:T(8,128)(2,1)}) custom-call(f32[160,128]{1,0:T(8,128)} %get-tuple-element.246.d_ref, f32[160,128]{1,0:T(8,128)} %get-tuple-element.247.l_ref, f32[16,8,512]{2,1,0:T(8,128)} %get-tuple-element.248.m_ref, ...), custom_call_target="tpu_custom_call" | custom-call | flops 115000000 | tf_op jit(solution)/shard_map/code_payload/pallas_call | solution.py:790
  144.9 2.3 fusion
  148.2 24.3 %units_back_into_9_weights_3.1 = (f32[1280,512]{1,0:T(8,128)}, f32[8,512]{1,0:T(8,128)}, bf16[1280,512]{1,0:T(8,128)(2,1)}, bf16[2,8,128,512]{3,2,1,0:T(8,128)(2...) custom-call(f32[2176,128]{1,0:T(8,128)} %broadcast_in_dim.82.refs_9_.l_ref.refs_0_, ...), custom_call_target="tpu_custom_call" | custom-call | flops 73600000000 | tf_op jit(solution)/shard_map/units_back_into_9_weights_3/pallas_call | solution.py:448
  174.5 3.6 sum_halves.12
  181.2 24.8 %units_back_into_3_weights_1.1 = (f32[1280,512]{1,0:T(8,128)}, f32[8,512]{1,0:T(8,128)}, bf16[1280,512]{1,0:T(8,128)(2,1)}, bf16[2,8,128,512]{3,2,1,0:T(8,128)(2...) custom-call(f32[2176,128]{1,0:T(8,128)} %broadcast_in_dim.82.refs_9_.l_ref.refs_0_, ...), custom_call_target="tpu_custom_call" | custom-call | flops 73600000000 | tf_op jit(solution)/shard_map/units_back_into_3_weights_1/pallas_call | solution.py:448
  206.9 2.2 sum_halves.13
  211.8 3.3 sum_halves.14
  216.7 13.8 %units_back_into_1.1 = (f32[1280,512]{1,0:T(8,128)}, f32[56,512]{1,0:T(8,128)}) custom-call(f32[2176,128]{1,0:T(8,128)} %broadcast_in_dim.82.refs_9_.l_ref.refs_0_, f32[32,512]{1,0:T(8,128)} %get-tuple-element.216.refs_8_.v_ref.refs_1_, f32[1280,512]{1,0:T(8,128)} %get-tuple-element.287.refs_2_, f32[1280,512]{1,0:T(8,128)} %get-tuple-element.214.s_ref.refs_3_, ...), custom_call_target="tpu_custom_call" | custom-call | flops 57500000256 | tf_op jit(solution)/shard_map/units_back_into_1/pallas_call | solution.py:448
  233.9 2.3 sum_halves.16
  239.4 2.6 collective-permute-start.38
  242.0 3.5 leave.1
  245.5 3.4 collective-permute-done.38.refs_1_
  251.3 3.4 collective-permute-start.43
  264.5 3.2 sum_halves.19
  269.3 3.1 collective-permute-start.46
  272.4 6.1 %collective-permute-done.46.refs_1_ = bf16[144,512]{1,0:T(8,128)(2,1)S(1)} collective-permute-done((bf16[144,512]{1,0:T(8,128)(2,1)S(1)}, bf16[144,512]{1,0:T(8,128)(2,1)S(1)}, u32[]{:S(2)}, u32[]{:S(2)}) %collective-permute-start.46) | collective-permute-done | bytes 147488 | tf_op jit(solution)/shard_map/ppermute | solution.py:1122
  281.5 1.9 join.7.refs_0_
  284.6 2.1 sum_halves.21
  286.7 4.1 %collective-permute-start.51 = (bf16[256,512]{1,0:T(8,128)(2,1)}, bf16[256,512]{1,0:T(8,128)(2,1)S(1)}, u32[]{:S(2)}, u32[]{:S(2)}) collective-permute-start(bf16[256,512]{1,0:T(8,128)(2,1)} %get-tuple-element.323), channel_id=1, source_target_pairs={{0,8},{4,12},{8,0},{12,4},{16,24},{20,28},{24,16},{28,20},{1,9},{5... | collective-permute-start | bytes 786440 | tf_op jit(solution)/shard_map/ppermute | solution.py:1122
  292.5 9.4 %collective-permute-done.41 = f32[56,512]{1,0:T(8,128)S(1)} collective-permute-done((f32[56,512]{1,0:T(8,128)S(1)}, f32[56,512]{1,0:T(8,128)S(1)}, u32[]{:S(2)}, u32[]{:S(2)}) %collective-permute-start.41) | collective-permute-done | bytes 114720 | tf_op jit(solution)/shard_map/ppermute | solution.py:1122
  304.5 3.0 collective-permute-start.53
  317.9 2.3 collective-permute-start.54
  321.0 8.8 %strided_back.1 = (f32[16,256,512]{2,1,0:T(8,128)}, f32[16,256]{1,0:T(8,128)}) custom-call(bf16[16,256,512]{2,1,0:T(8,128)(2,1)} %w_ref.3, bf16[16,8,512]{2,1,0:T(8,128)(2,1)} %slice_bitcast_fusion.m_ref, bf16[8,256]{1,0:T(8,128)(2,1)} %p_ref.2, f32[8,256]{1,0:T(8,128)} %get-tuple-element.337.n_ref), custom_call_target="tpu_custom_call" | custom-call | flops 115000000 | tf_op jit(solution)/shard_map/strided_back/pallas_call | solution.py:838
  334.1 1.9 join.10.refs_0_
  336.0 3.8 %norm_back.3 = (f32[3,7,128,512]{3,2,1,0:T(8,128)}, f32[3,128,512]{2,1,0:T(8,128)}, f32[3,8,128]{2,1,0:T(8,128)}) custom-call(bf16[576,512]{1,0:T(8,128)(2,1)} %join.7.refs_0_, bf16[576,512]{1,0:T(8,128)(2,1)} %copy-done.9, bf16[3,7,128,512]{3,2,1,0:T(8,128)(2,1)} %refs_2_.3, bf16[3,128,512]{2,1,0:T(8,128)(2,1)} %refs_3_.5, f32[3,2,128]{2,1,0:T(2,128)} %pad_maximum_fusion.refs_4_), custom_call_target="tpu_custom_call" | custom-call | flops 115000000 | tf_op jit(solution)/shard_map/norm_back/pallas_call | solution.py:917
  346.1 2.7 settle.1
  350.7 1.9 join.11.refs_0_
  353.0 2.5 collective-permute-done.60.refs_1_
  356.3 3.8 %norm_back.4 = (f32[3,7,128,512]{3,2,1,0:T(8,128)}, f32[3,128,512]{2,1,0:T(8,128)}, f32[3,8,128]{2,1,0:T(8,128)}) custom-call(bf16[576,512]{1,0:T(8,128)(2,1)} %join.10.refs_0_, bf16[576,512]{1,0:T(8,128)(2,1)} %copy-done.10, bf16[3,7,128,512]{3,2,1,0:T(8,128)(2,1)} %refs_2_.3, ...), custom_call_target="tpu_custom_call", output_to_operand_aliasing={{0}: (5, {}), {1}: (6, {}), {2}: (7, {})} | custom-call | flops 115000000 | tf_op jit(solution)/shard_map/norm_back/pallas_call | solution.py:917
  363.6 3.1 collective-permute-done.59.refs_1_
  367.5 3.7 %norm_back.5 = (f32[3,7,128,512]{3,2,1,0:T(8,128)}, f32[3,128,512]{2,1,0:T(8,128)}, f32[3,8,128]{2,1,0:T(8,128)}) custom-call(bf16[512,512]{1,0:T(8,128)(2,1)} %join.11.refs_0_, bf16[512,512]{1,0:T(8,128)(2,1)} %copy-done.15, bf16[3,7,128,512]{3,2,1,0:T(8,128)(2,1)} %refs_2_.3, ...), custom_call_target="tpu_custom_call", output_to_operand_aliasing={{0}: (5, {}), {1}: (6, {}), {2}: (7, {})} | custom-call | flops 115000000 | tf_op jit(solution)/shard_map/norm_back/pallas_call | solution.py:917
  (335 shorter events, 100.3 us)
Async XLA Ops:
  4.1 48.2 %collective-permute-start.8 = (bf16[3,7,128,512]{3,2,1,0:T(8,128)(2,1)S(1)}, bf16[3,7,128,512]{3,2,1,0:T(8,128)(2,1)}, u32[]{:S(2)}, u32[]{:S(2)}) collective-permute-start(bf16[3,7,128,512]{3,2,1,0:T(8,128)(2,1)S(1)} %copy-done), channel_id=1, source_target_pairs={{0,1},{1,0},{2,3},{3,2},{4,5},{5,4},{6,7},{7,6},{8,9},{9,8},{10,11... | collective-permute-start | bytes 8257544 | tf_op jit(solution)/shard_map/ppermute | solution.py:1122
  4.6 19.2 %collective-permute-start.7 = (bf16[4,128,512]{2,1,0:T(8,128)(2,1)}, bf16[4,128,512]{2,1,0:T(8,128)(2,1)}, u32[]{:S(2)}, u32[]{:S(2)}) collective-permute-start(bf16[4,128,512]{2,1,0:T(8,128)(2,1)} %get-tuple-element.190), channel_id=1, source_target_pairs={{0,2},{1,3},{2,0},{3,1},{4,6},{5,7},{6,4},{7,5},{8,10},{9,11},{10,... | collective-permute-start | bytes 1572872 | tf_op jit(solution)/shard_map/ppermute | solution.py:1122
  18.7 12.3 %collective-permute-start = (bf16[128,1408]{1,0:T(8,128)(2,1)}, bf16[128,1408]{1,0:T(8,128)(2,1)S(1)}, u32[]{:S(2)}, u32[]{:S(2)}) collective-permute-start(bf16[128,1408]{1,0:T(8,128)(2,1)} %get-tuple-element.195), channel_id=1, source_target_pairs={{0,1},{1,0},{2,3},{3,2},{4,5},{5,4},{6,7},{7,6},{8,9},{9,8},{10,11... | collective-permute-start | bytes 1081352 | tf_op jit(solution)/shard_map/ppermute | solution.py:1266
  21.6 11.7 %collective-permute-start.1 = (bf16[128,1408]{1,0:T(8,128)(2,1)}, bf16[128,1408]{1,0:T(8,128)(2,1)}, u32[]{:S(2)}, u32[]{:S(2)}) collective-permute-start(bf16[128,1408]{1,0:T(8,128)(2,1)} %get-tuple-element.196), channel_id=1, source_target_pairs={{0,2},{1,3},{2,0},{3,1},{4,6},{5,7},{6,4},{7,5},{8,10},{9,11},{10,... | collective-permute-start | bytes 1081352 | tf_op jit(solution)/shard_map/ppermute | solution.py:1266
  23.8 16.7 %collective-permute-start.2 = (bf16[128,1408]{1,0:T(8,128)(2,1)}, bf16[128,1408]{1,0:T(8,128)(2,1)}, u32[]{:S(2)}, u32[]{:S(2)}) collective-permute-start(bf16[128,1408]{1,0:T(8,128)(2,1)} %get-tuple-element.197), channel_id=1, source_target_pairs={{0,3},{1,2},{2,1},{3,0},{4,7},{5,6},{6,5},{7,4},{8,11},{9,10},{10,... | collective-permute-start | bytes 1081352 | tf_op jit(solution)/shard_map/ppermute | solution.py:1266
  23.8 16.7 %collective-permute-start.10 = (bf16[4,128,512]{2,1,0:T(8,128)(2,1)}, bf16[4,128,512]{2,1,0:T(8,128)(2,1)}, u32[]{:S(2)}, u32[]{:S(2)}) collective-permute-start(bf16[4,128,512]{2,1,0:T(8,128)(2,1)} %collective-permute-done.7.refs_4_.refs_9_), channel_id=1, source_target_pairs={{0,4},{4,0},{8,12},{12,8},{16,20},{20,16},{24,28},{28,24},{1,5},{5... | collective-permute-start | bytes 1572872 | tf_op jit(solution)/shard_map/ppermute | solution.py:1122
  31.0 14.6 %collective-permute-start.3 = (bf16[144,128]{1,0:T(8,128)(2,1)}, bf16[144,128]{1,0:T(8,128)(2,1)S(1)}, u32[]{:S(2)}, u32[]{:S(2)}) collective-permute-start(bf16[144,128]{1,0:T(8,128)(2,1)} %get-tuple-element.198), channel_id=1, source_target_pairs={{7,3},{11,7},{15,11},{19,15},{23,19},{27,23},{31,27},{0,4},{4,8},{... | collective-permute-start | bytes 110600 | tf_op jit(solution)/shard_map/ppermute | solution.py:1325
  33.2 19.1 %collective-permute-start.9 = (bf16[3,128,512]{2,1,0:T(8,128)(2,1)S(1)}, bf16[3,128,512]{2,1,0:T(8,128)(2,1)}, u32[]{:S(2)}, u32[]{:S(2)}) collective-permute-start(bf16[3,128,512]{2,1,0:T(8,128)(2,1)S(1)} %copy-done.1), channel_id=1, source_target_pairs={{0,1},{1,0},{2,3},{3,2},{4,5},{5,4},{6,7},{7,6},{8,9},{9,8},{10,11... | collective-permute-start | bytes 1179656 | tf_op jit(solution)/shard_map/ppermute | solution.py:1122
  40.4 11.9 %collective-permute-start.11 = (bf16[4,128,512]{2,1,0:T(8,128)(2,1)}, bf16[4,128,512]{2,1,0:T(8,128)(2,1)}, u32[]{:S(2)}, u32[]{:S(2)}) collective-permute-start(bf16[4,128,512]{2,1,0:T(8,128)(2,1)} %collective-permute-done.7.refs_4_.refs_9_), channel_id=1, source_target_pairs={{0,1},{1,0},{2,3},{3,2},{4,5},{5,4},{6,7},{7,6},{8,9},{9,8},{10,11... | collective-permute-start | bytes 1572872 | tf_op jit(solution)/shard_map/ppermute | solution.py:1122
  40.5 11.8 %collective-permute-start.12 = (bf16[4,128,512]{2,1,0:T(8,128)(2,1)}, bf16[4,128,512]{2,1,0:T(8,128)(2,1)}, u32[]{:S(2)}, u32[]{:S(2)}) collective-permute-start(bf16[4,128,512]{2,1,0:T(8,128)(2,1)} %collective-permute-done.10.refs_5_.refs_10_), channel_id=1, source_target_pairs={{0,1},{1,0},{2,3},{3,2},{4,5},{5,4},{6,7},{7,6},{8,9},{9,8},{10,11... | collective-permute-start | bytes 1572872 | tf_op jit(solution)/shard_map/ppermute | solution.py:1122
  45.6 18.5 %collective-permute-start.13 = (bf16[4,128,512]{2,1,0:T(8,128)(2,1)}, bf16[4,128,512]{2,1,0:T(8,128)(2,1)}, u32[]{:S(2)}, u32[]{:S(2)}) collective-permute-start(bf16[4,128,512]{2,1,0:T(8,128)(2,1)} %get-tuple-element.224), channel_id=1, source_target_pairs={{0,2},{1,3},{2,0},{3,1},{4,6},{5,7},{6,4},{7,5},{8,10},{9,11},{10,... | collective-permute-start | bytes 1572872 | tf_op jit(solution)/shard_map/ppermute | solution.py:1122
  64.1 14.0 %collective-permute-start.14 = (bf16[4,128,512]{2,1,0:T(8,128)(2,1)}, bf16[4,128,512]{2,1,0:T(8,128)(2,1)S(1)}, u32[]{:S(2)}, u32[]{:S(2)}) collective-permute-start(bf16[4,128,512]{2,1,0:T(8,128)(2,1)} %collective-permute-done.13.refs_4_.refs_9_), channel_id=1, source_target_pairs={{0,4},{4,0},{8,12},{12,8},{16,20},{20,16},{24,28},{28,24},{1,5},{5... | collective-permute-start | bytes 1572872 | tf_op jit(solution)/shard_map/ppermute | solution.py:1122
  66.2 13.4 %collective-permute-start.18 = (bf16[4,128,512]{2,1,0:T(8,128)(2,1)S(1)}, bf16[4,128,512]{2,1,0:T(8,128)(2,1)S(1)}, u32[]{:S(2)}, u32[]{:S(2)}) collective-permute-start(bf16[4,128,512]{2,1,0:T(8,128)(2,1)S(1)} %copy-done.51), channel_id=1, source_target_pairs={{0,2},{1,3},{2,0},{3,1},{4,6},{5,7},{6,4},{7,5},{8,10},{9,11},{10,... | collective-permute-start | bytes 1572872 | tf_op jit(solution)/shard_map/ppermute | solution.py:1122
  66.5 11.6 %collective-permute-start.16 = (f32[136,512]{1,0:T(8,128)S(1)}, f32[136,512]{1,0:T(8,128)S(1)}, u32[]{:S(2)}, u32[]{:S(2)}) collective-permute-start(f32[136,512]{1,0:T(8,128)S(1)} %copy-done.22), channel_id=1, source_target_pairs={{0,1},{1,0},{2,3},{3,2},{4,5},{5,4},{6,7},{7,6},{8,9},{9,8},{10,11... | collective-permute-start | bytes 835592 | tf_op jit(solution)/shard_map/ppermute | solution.py:1122
  68.2 12.7 %collective-permute-start.15 = (bf16[4,128,512]{2,1,0:T(8,128)(2,1)}, bf16[4,128,512]{2,1,0:T(8,128)(2,1)S(1)}, u32[]{:S(2)}, u32[]{:S(2)}) collective-permute-start(bf16[4,128,512]{2,1,0:T(8,128)(2,1)} %collective-permute-done.13.refs_4_.refs_9_), channel_id=1, source_target_pairs={{0,1},{1,0},{2,3},{3,2},{4,5},{5,4},{6,7},{7,6},{8,9},{9,8},{10,11... | collective-permute-start | bytes 1572872 | tf_op jit(solution)/shard_map/ppermute | solution.py:1122
  79.7 14.5 %collective-permute-start.19 = (bf16[4,128,512]{2,1,0:T(8,128)(2,1)S(1)}, bf16[4,128,512]{2,1,0:T(8,128)(2,1)S(1)}, u32[]{:S(2)}, u32[]{:S(2)}) collective-permute-start(bf16[4,128,512]{2,1,0:T(8,128)(2,1)S(1)} %copy-done.50), channel_id=1, source_target_pairs={{0,2},{1,3},{2,0},{3,1},{4,6},{5,7},{6,4},{7,5},{8,10},{9,11},{10,... | collective-permute-start | bytes 1572872 | tf_op jit(solution)/shard_map/ppermute | solution.py:1122
  80.9 14.7 %collective-permute-start.20 = (bf16[4,128,512]{2,1,0:T(8,128)(2,1)S(1)}, bf16[4,128,512]{2,1,0:T(8,128)(2,1)S(1)}, u32[]{:S(2)}, u32[]{:S(2)}) collective-permute-start(bf16[4,128,512]{2,1,0:T(8,128)(2,1)S(1)} %collective-permute-done.18.refs_4_.refs_9_), channel_id=1, source_target_pairs={{0,1},{1,0},{2,3},{3,2},{4,5},{5,4},{6,7},{7,6},{8,9},{9,8},{10,11... | collective-permute-start | bytes 1572872 | tf_op jit(solution)/shard_map/ppermute | solution.py:1122
  94.8 14.8 %collective-permute-start.22 = (f32[136,512]{1,0:T(8,128)S(1)}, f32[136,512]{1,0:T(8,128)S(1)}, u32[]{:S(2)}, u32[]{:S(2)}) collective-permute-start(f32[136,512]{1,0:T(8,128)S(1)} %add.187.wa_ref), channel_id=1, source_target_pairs={{0,2},{1,3},{2,0},{3,1},{4,6},{5,7},{6,4},{7,5},{8,10},{9,11},{10,... | collective-permute-start | bytes 835592 | tf_op jit(solution)/shard_map/ppermute | solution.py:1122
  143.0 30.0 %collective-permute-start.26 = (bf16[128,512]{1,0:T(8,128)(2,1)}, bf16[128,512]{1,0:T(8,128)(2,1)S(1)}, u32[]{:S(2)}, u32[]{:S(2)}) collective-permute-start(bf16[128,512]{1,0:T(8,128)(2,1)} %get-tuple-element.263), channel_id=1, source_target_pairs={{0,1},{1,0},{2,3},{3,2},{4,5},{5,4},{6,7},{7,6},{8,9},{9,8},{10,11... | collective-permute-start | bytes 393224 | tf_op jit(solution)/shard_map/ppermute | solution.py:1266
  143.2 29.8 %collective-permute-start.27 = (bf16[128,512]{1,0:T(8,128)(2,1)}, bf16[128,512]{1,0:T(8,128)(2,1)S(1)}, u32[]{:S(2)}, u32[]{:S(2)}) collective-permute-start(bf16[128,512]{1,0:T(8,128)(2,1)} %get-tuple-element.264), channel_id=1, source_target_pairs={{0,2},{1,3},{2,0},{3,1},{4,6},{5,7},{6,4},{7,5},{8,10},{9,11},{10,... | collective-permute-start | bytes 393224 | tf_op jit(solution)/shard_map/ppermute | solution.py:1266
  144.4 28.6 %collective-permute-start.28 = (bf16[128,512]{1,0:T(8,128)(2,1)}, bf16[128,512]{1,0:T(8,128)(2,1)S(1)}, u32[]{:S(2)}, u32[]{:S(2)}) collective-permute-start(bf16[128,512]{1,0:T(8,128)(2,1)} %get-tuple-element.265), channel_id=1, source_target_pairs={{0,3},{1,2},{2,1},{3,0},{4,7},{5,6},{6,5},{7,4},{8,11},{9,10},{10,... | collective-permute-start | bytes 393224 | tf_op jit(solution)/shard_map/ppermute | solution.py:1266
  147.2 27.3 %collective-permute-start.25 = (bf16[8,128,512]{2,1,0:T(8,128)(2,1)S(1)}, bf16[8,128,512]{2,1,0:T(8,128)(2,1)}, u32[]{:S(2)}, u32[]{:S(2)}) collective-permute-start(bf16[8,128,512]{2,1,0:T(8,128)(2,1)S(1)} %fusion), channel_id=1, source_target_pairs={{0,2},{1,3},{2,0},{3,1},{4,6},{5,7},{6,4},{7,5},{8,10},{9,11},{10,... | collective-permute-start | bytes 3145736 | tf_op jit(solution)/shard_map/ppermute | solution.py:1122
  178.1 27.9 %collective-permute-start.30 = (bf16[576,512]{1,0:T(8,128)(2,1)}, bf16[576,512]{1,0:T(8,128)(2,1)S(1)}, u32[]{:S(2)}, u32[]{:S(2)}) collective-permute-start(bf16[576,512]{1,0:T(8,128)(2,1)} %get-tuple-element.272), channel_id=1, source_target_pairs={{0,4},{4,0},{8,12},{12,8},{16,20},{20,16},{24,28},{28,24},{1,5},{5... | collective-permute-start | bytes 1769480 | tf_op jit(solution)/shard_map/ppermute | solution.py:1122
  180.2 30.6 %collective-permute-start.29 = (bf16[8,128,512]{2,1,0:T(8,128)(2,1)S(1)}, bf16[8,128,512]{2,1,0:T(8,128)(2,1)S(1)}, u32[]{:S(2)}, u32[]{:S(2)}) collective-permute-start(bf16[8,128,512]{2,1,0:T(8,128)(2,1)S(1)} %fusion.1), channel_id=1, source_target_pairs={{0,2},{1,3},{2,0},{3,1},{4,6},{5,7},{6,4},{7,5},{8,10},{9,11},{10,... | collective-permute-start | bytes 3145736 | tf_op jit(solution)/shard_map/ppermute | solution.py:1122
  209.2 21.3 %collective-permute-start.33 = (bf16[288,512]{1,0:T(8,128)(2,1)}, bf16[288,512]{1,0:T(8,128)(2,1)S(1)}, u32[]{:S(2)}, u32[]{:S(2)}) collective-permute-start(bf16[288,512]{1,0:T(8,128)(2,1)} %get-tuple-element.283), channel_id=1, source_target_pairs={{0,8},{4,12},{8,0},{12,4},{16,24},{20,28},{24,16},{28,20},{1,9},{5... | collective-permute-start | bytes 884744 | tf_op jit(solution)/shard_map/ppermute | solution.py:1122
  210.8 25.4 %collective-permute-start.31 = (bf16[2,8,128,512]{3,2,1,0:T(8,128)(2,1)}, bf16[2,8,128,512]{3,2,1,0:T(8,128)(2,1)}, u32[]{:S(2)}, u32[]{:S(2)}) collective-permute-start(bf16[2,8,128,512]{3,2,1,0:T(8,128)(2,1)} %get-tuple-element.294), channel_id=1, source_target_pairs={{0,1},{1,0},{2,3},{3,2},{4,5},{5,4},{6,7},{7,6},{8,9},{9,8},{10,11... | collective-permute-start | bytes 6291464 | tf_op jit(solution)/shard_map/ppermute | solution.py:1122
  215.1 18.0 %collective-permute-start.32 = (bf16[576,512]{1,0:T(8,128)(2,1)}, bf16[576,512]{1,0:T(8,128)(2,1)S(1)}, u32[]{:S(2)}, u32[]{:S(2)}) collective-permute-start(bf16[576,512]{1,0:T(8,128)(2,1)} %get-tuple-element.286), channel_id=1, source_target_pairs={{0,4},{4,0},{8,12},{12,8},{16,20},{20,16},{24,28},{28,24},{1,5},{5... | collective-permute-start | bytes 1769480 | tf_op jit(solution)/shard_map/ppermute | solution.py:1122
  237.8 25.8 %collective-permute-start.42 = (bf16[8,128,512]{2,1,0:T(8,128)(2,1)S(1)}, bf16[8,128,512]{2,1,0:T(8,128)(2,1)S(1)}, u32[]{:S(2)}, u32[]{:S(2)}) collective-permute-start(bf16[8,128,512]{2,1,0:T(8,128)(2,1)S(1)} %fusion.2), channel_id=1, source_target_pairs={{0,2},{1,3},{2,0},{3,1},{4,6},{5,7},{6,4},{7,5},{8,10},{9,11},{10,... | collective-permute-start | bytes 3145736 | tf_op jit(solution)/shard_map/ppermute | solution.py:1122
  238.9 16.3 %collective-permute-start.40 = (bf16[288,512]{1,0:T(8,128)(2,1)S(1)}, bf16[288,512]{1,0:T(8,128)(2,1)S(1)}, u32[]{:S(2)}, u32[]{:S(2)}) collective-permute-start(bf16[288,512]{1,0:T(8,128)(2,1)S(1)} %copy-done.59), channel_id=1, source_target_pairs={{0,8},{4,12},{8,0},{12,4},{16,24},{20,28},{24,16},{28,20},{1,9},{5... | collective-permute-start | bytes 884744 | tf_op jit(solution)/shard_map/ppermute | solution.py:1122
  242.0 12.7 %collective-permute-start.37 = (f32[56,512]{1,0:T(8,128)S(1)}, f32[56,512]{1,0:T(8,128)S(1)}, u32[]{:S(2)}, u32[]{:S(2)}) collective-permute-start(f32[56,512]{1,0:T(8,128)S(1)} %copy-done.34), channel_id=1, source_target_pairs={{0,1},{1,0},{2,3},{3,2},{4,5},{5,4},{6,7},{7,6},{8,9},{9,8},{10,11... | collective-permute-start | bytes 344072 | tf_op jit(solution)/shard_map/ppermute | solution.py:1122
  251.3 9.9 %collective-permute-start.43 = (bf16[144,512]{1,0:T(8,128)(2,1)}, bf16[144,512]{1,0:T(8,128)(2,1)S(1)}, u32[]{:S(2)}, u32[]{:S(2)}) collective-permute-start(bf16[144,512]{1,0:T(8,128)(2,1)} %sum_halves.17.m_ref), channel_id=1, source_target_pairs={{0,16},{4,20},{8,24},{12,28},{16,0},{20,4},{24,8},{28,12},{1,17},{... | collective-permute-start | bytes 442376 | tf_op jit(solution)/shard_map/ppermute | solution.py:1122
  267.8 16.0 %collective-permute-start.44 = (bf16[512,512]{1,0:T(8,128)(2,1)}, bf16[512,512]{1,0:T(8,128)(2,1)S(1)}, u32[]{:S(2)}, u32[]{:S(2)}) collective-permute-start(bf16[512,512]{1,0:T(8,128)(2,1)} %get-tuple-element.318), channel_id=1, source_target_pairs={{0,4},{4,0},{8,12},{12,8},{16,20},{20,16},{24,28},{28,24},{1,5},{5... | collective-permute-start | bytes 1572872 | tf_op jit(solution)/shard_map/ppermute | solution.py:1122
  267.9 12.9 %collective-permute-start.45 = (bf16[288,512]{1,0:T(8,128)(2,1)S(1)}, bf16[288,512]{1,0:T(8,128)(2,1)S(1)}, u32[]{:S(2)}, u32[]{:S(2)}) collective-permute-start(bf16[288,512]{1,0:T(8,128)(2,1)S(1)} %copy-done.6), channel_id=1, source_target_pairs={{0,8},{4,12},{8,0},{12,4},{16,24},{20,28},{24,16},{28,20},{1,9},{5... | collective-permute-start | bytes 884744 | tf_op jit(solution)/shard_map/ppermute | solution.py:1122
  283.4 24.1 %collective-permute-start.50 = (bf16[576,512]{1,0:T(8,128)(2,1)}, bf16[576,512]{1,0:T(8,128)(2,1)S(1)}, u32[]{:S(2)}, u32[]{:S(2)}) collective-permute-start(bf16[576,512]{1,0:T(8,128)(2,1)} %join.7.refs_0_), channel_id=1, source_target_pairs={{0,4},{4,0},{8,12},{12,8},{16,20},{20,16},{24,28},{28,24},{1,5},{5... | collective-permute-start | bytes 1769480 | tf_op jit(solution)/shard_map/ppermute | solution.py:1122
  286.7 15.3 %collective-permute-start.51 = (bf16[256,512]{1,0:T(8,128)(2,1)}, bf16[256,512]{1,0:T(8,128)(2,1)S(1)}, u32[]{:S(2)}, u32[]{:S(2)}) collective-permute-start(bf16[256,512]{1,0:T(8,128)(2,1)} %get-tuple-element.323), channel_id=1, source_target_pairs={{0,8},{4,12},{8,0},{12,4},{16,24},{20,28},{24,16},{28,20},{1,9},{5... | collective-permute-start | bytes 786440 | tf_op jit(solution)/shard_map/ppermute | solution.py:1122
  290.9 10.9 %collective-permute-start.41 = (f32[56,512]{1,0:T(8,128)S(1)}, f32[56,512]{1,0:T(8,128)S(1)}, u32[]{:S(2)}, u32[]{:S(2)}) collective-permute-start(f32[56,512]{1,0:T(8,128)S(1)} %add.192), channel_id=1, source_target_pairs={{0,8},{4,12},{8,0},{12,4},{16,24},{20,28},{24,16},{28,20},{1,9},{5... | collective-permute-start | bytes 344072 | tf_op jit(solution)/shard_map/ppermute | solution.py:1122
  291.1 18.3 %collective-permute-start.48 = (bf16[144,512]{1,0:T(8,128)(2,1)S(1)}, bf16[144,512]{1,0:T(8,128)(2,1)S(1)}, u32[]{:S(2)}, u32[]{:S(2)}) collective-permute-start(bf16[144,512]{1,0:T(8,128)(2,1)S(1)} %copy-done.13), channel_id=1, source_target_pairs={{0,16},{4,20},{8,24},{12,28},{16,0},{20,4},{24,8},{28,12},{1,17},{... | collective-permute-start | bytes 442376 | tf_op jit(solution)/shard_map/ppermute | solution.py:1122
  301.9 10.9 %collective-permute-start.47 = (f32[56,512]{1,0:T(8,128)S(1)}, f32[56,512]{1,0:T(8,128)S(1)}, u32[]{:S(2)}, u32[]{:S(2)}) collective-permute-start(f32[56,512]{1,0:T(8,128)S(1)} %add.193), channel_id=1, source_target_pairs={{0,16},{4,20},{8,24},{12,28},{16,0},{20,4},{24,8},{28,12},{1,17},{... | collective-permute-start | bytes 344072 | tf_op jit(solution)/shard_map/ppermute | solution.py:1122
  304.5 9.6 %collective-permute-start.53 = (bf16[128,512]{1,0:T(8,128)(2,1)}, bf16[128,512]{1,0:T(8,128)(2,1)S(1)}, u32[]{:S(2)}, u32[]{:S(2)}) collective-permute-start(bf16[128,512]{1,0:T(8,128)(2,1)} %get-tuple-element.329), channel_id=1, source_target_pairs={{0,16},{4,20},{8,24},{12,28},{16,0},{20,4},{24,8},{28,12},{1,17},{... | collective-permute-start | bytes 393224 | tf_op jit(solution)/shard_map/ppermute | solution.py:1122
  312.8 31.8 %collective-permute-start.34 = (bf16[128,1024]{1,0:T(8,128)(2,1)}, bf16[128,1024]{1,0:T(8,128)(2,1)S(1)}, u32[]{:S(2)}, u32[]{:S(2)}) collective-permute-start(bf16[128,1024]{1,0:T(8,128)(2,1)} %get-tuple-element.304), channel_id=1, source_target_pairs={{0,1},{1,0},{2,3},{3,2},{4,5},{5,4},{6,7},{7,6},{8,9},{9,8},{10,11... | collective-permute-start | bytes 786440 | tf_op jit(solution)/shard_map/ppermute | solution.py:1266
  314.1 30.4 %collective-permute-start.35 = (bf16[128,1024]{1,0:T(8,128)(2,1)}, bf16[128,1024]{1,0:T(8,128)(2,1)S(1)}, u32[]{:S(2)}, u32[]{:S(2)}) collective-permute-start(bf16[128,1024]{1,0:T(8,128)(2,1)} %get-tuple-element.305), channel_id=1, source_target_pairs={{0,2},{1,3},{2,0},{3,1},{4,6},{5,7},{6,4},{7,5},{8,10},{9,11},{10,... | collective-permute-start | bytes 786440 | tf_op jit(solution)/shard_map/ppermute | solution.py:1266
  316.5 16.9 %collective-permute-start.52 = (bf16[288,512]{1,0:T(8,128)(2,1)}, bf16[288,512]{1,0:T(8,128)(2,1)S(1)}, u32[]{:S(2)}, u32[]{:S(2)}) collective-permute-start(bf16[288,512]{1,0:T(8,128)(2,1)} %join.8.m_ref), channel_id=1, source_target_pairs={{0,8},{4,12},{8,0},{12,4},{16,24},{20,28},{24,16},{28,20},{1,9},{5... | collective-permute-start | bytes 884744 | tf_op jit(solution)/shard_map/ppermute | solution.py:1122
  316.5 23.4 %collective-permute-start.49 = (f32[56,512]{1,0:T(8,128)S(1)}, f32[56,512]{1,0:T(8,128)S(1)}, u32[]{:S(2)}, u32[]{:S(2)}) collective-permute-start(f32[56,512]{1,0:T(8,128)S(1)} %add.194), channel_id=1, source_target_pairs={{0,2},{1,3},{2,0},{3,1},{4,6},{5,7},{6,4},{7,5},{8,10},{9,11},{10,... | collective-permute-start | bytes 344072 | tf_op jit(solution)/shard_map/ppermute | solution.py:1122
  317.9 13.2 %collective-permute-start.54 = (bf16[128,512]{1,0:T(8,128)(2,1)}, bf16[128,512]{1,0:T(8,128)(2,1)S(1)}, u32[]{:S(2)}, u32[]{:S(2)}) collective-permute-start(bf16[128,512]{1,0:T(8,128)(2,1)} %sum_halves.23.m_ref), channel_id=1, source_target_pairs={{0,16},{4,20},{8,24},{12,28},{16,0},{20,4},{24,8},{28,12},{1,17},{... | collective-permute-start | bytes 393224 | tf_op jit(solution)/shard_map/ppermute | solution.py:1122
  331.1 13.5 %collective-permute-start.36 = (bf16[128,1024]{1,0:T(8,128)(2,1)S(1)}, bf16[128,1024]{1,0:T(8,128)(2,1)S(1)}, u32[]{:S(2)}, u32[]{:S(2)}) collective-permute-start(bf16[128,1024]{1,0:T(8,128)(2,1)S(1)} %copy-done.61), channel_id=1, source_target_pairs={{0,3},{1,2},{2,1},{3,0},{4,7},{5,6},{6,5},{7,4},{8,11},{9,10},{10,... | collective-permute-start | bytes 786440 | tf_op jit(solution)/shard_map/ppermute | solution.py:1266
  333.4 16.6 %collective-permute-start.58 = (bf16[256,512]{1,0:T(8,128)(2,1)}, bf16[256,512]{1,0:T(8,128)(2,1)S(1)}, u32[]{:S(2)}, u32[]{:S(2)}) collective-permute-start(bf16[256,512]{1,0:T(8,128)(2,1)} %join.9.m_ref), channel_id=1, source_target_pairs={{0,8},{4,12},{8,0},{12,4},{16,24},{20,28},{24,16},{28,20},{1,9},{5... | collective-permute-start | bytes 786440 | tf_op jit(solution)/shard_map/ppermute | solution.py:1122
  339.9 15.6 %collective-permute-start.60 = (bf16[576,512]{1,0:T(8,128)(2,1)S(1)}, bf16[576,512]{1,0:T(8,128)(2,1)S(1)}, u32[]{:S(2)}, u32[]{:S(2)}) collective-permute-start(bf16[576,512]{1,0:T(8,128)(2,1)S(1)} %copy-done.5), channel_id=1, source_target_pairs={{0,4},{4,0},{8,12},{12,8},{16,20},{20,16},{24,28},{28,24},{1,5},{5... | collective-permute-start | bytes 1769480 | tf_op jit(solution)/shard_map/ppermute | solution.py:1122
  352.6 14.1 %collective-permute-start.59 = (bf16[512,512]{1,0:T(8,128)(2,1)}, bf16[512,512]{1,0:T(8,128)(2,1)S(1)}, u32[]{:S(2)}, u32[]{:S(2)}) collective-permute-start(bf16[512,512]{1,0:T(8,128)(2,1)} %join.11.refs_0_), channel_id=1, source_target_pairs={{0,4},{4,0},{8,12},{12,8},{16,20},{20,16},{24,28},{28,24},{1,5},{5... | collective-permute-start | bytes 1572872 | tf_op jit(solution)/shard_map/ppermute | solution.py:1122
  (83 other events, 563.8 us)

commit v4 on v3

--- a/solution.py
+++ b/solution.py
@@ -76,7 +76,6 @@
 
 def load_weights(pieces, member, weights, sems):
     me = lax.axis_index("chan")
-    first = (lax.axis_index("frames") & 1) * 4
     own7, own1, near7, near1 = (piece.at[member] for piece in pieces[:4])
     rows = own1.shape[0]
 
@@ -89,13 +88,14 @@
         (near7, weights.at[pl.ds(0, 7), place(1), :]),
         (near1, weights.at[7, place(1), :]),
     ]
-    if member == 2:
-        first = 0
+    size = pieces[4].shape[0]
+    side = 0 if member == 2 else lax.axis_index("frames") & 1
+    first, second = side * (8 - size), (1 - side) * size
     moves += [
-        (pieces[4], weights.at[pl.ds(first, 4), place(2), :]),
-        (pieces[5], weights.at[pl.ds(4 - first, 4), place(2), :]),
-        (pieces[6], weights.at[pl.ds(first, 4), place(3), :]),
-        (pieces[7], weights.at[pl.ds(4 - first, 4), place(3), :]),
+        (pieces[4], weights.at[pl.ds(first, size), place(2), :]),
+        (pieces[5], weights.at[pl.ds(second, 8 - size), place(2), :]),
+        (pieces[6], weights.at[pl.ds(first, size), place(3), :]),
+        (pieces[7], weights.at[pl.ds(second, 8 - size), place(3), :]),
     ]
     copies = []
     for piece, target in moves:
@@ -270,8 +270,8 @@
         name, micros = f"{name}_into_{spacing_c}", micros + 30
         ins |= {"grad": (grad, held), "stream": (stream, held), "scaled": (scaled, held)}
         ins |= {f"piece{n}": (piece, held) for n, piece in enumerate(pieces)}
-        ins |= {f"other{n}": (other, whole) for n, other in enumerate(others)}
-        outs |= {"out": (f32_rows, held), "sums_c": (jax.ShapeDtypeStruct((8 + 8 * len(others), chans), F32), whole)}
+        ins |= {f"other{n}": (other, whole) for n, (other, _) in enumerate(others)}
+        outs |= {"out": (f32_rows, held), "sums_c": (jax.ShapeDtypeStruct((16 if others else 8, chans), F32), whole)}
         scratch |= {
             "weights": pltpu.VMEM((8, chans, chans), BF),
             "wide_c": pltpu.VMEM((rows + 2 * margin_c * SEG, chans), BF),
@@ -357,8 +357,12 @@
         r.sums_c[0:8, :] = jnp.concatenate(
             [r.total_c[...].sum(axis=0, keepdims=True), jnp.zeros((7, chans), F32)], axis=0
         )
-        for n in range(len(others)):
-            r.sums_c[8 * n + 8 : 8 * n + 16, :] = getattr(r, f"other{n}")[...]
+        start = 1
+        for n, (_, count) in enumerate(others):
+            r.sums_c[start : start + count, :] = getattr(r, f"other{n}")[0:count, :]
+            start += count
+        if others:
+            r.sums_c[start:16, :] = jnp.zeros((16 - start, chans), F32)
         return outgoing
 
     def start_weights(r):
@@ -462,7 +466,7 @@
     units, _, part, chans = dilated.shape
 
     def kernel(d_ref, q_ref, f0, f1, f2, f3, held, sems, out_sems):
-        first = pl.multiple_of((lax.axis_index("frames") & 1) * 4, 4)
+        side = lax.axis_index("frames") & 1
         copies = []
         for u in range(units):
             copies.append(pltpu.make_async_copy(d_ref.at[u], held.at[u, pl.ds(0, 7)], sems.at[u]))
@@ -470,8 +474,8 @@
         for copy in copies:
             copy.start()
         outs = [
-            pltpu.make_async_copy(held.at[0, pl.ds(first, 4)], f0, out_sems.at[0]),
-            pltpu.make_async_copy(held.at[1, pl.ds(first, 4)], f1, out_sems.at[1]),
+            pltpu.make_async_copy(held.at[0, pl.ds(side * 4, 4)], f0, out_sems.at[0]),
+            pltpu.make_async_copy(held.at[1, pl.ds(side * 4, 4)], f1, out_sems.at[1]),
             pltpu.make_async_copy(held.at[2, pl.ds(0, 4)], f2, out_sems.at[2]),
             pltpu.make_async_copy(held.at[2, pl.ds(4, 4)], f3, out_sems.at[3]),
         ]
@@ -489,9 +493,8 @@
     return pl.pallas_call(
         kernel,
         out_shape=[
-            jax.ShapeDtypeStruct((4, part, chans), BF),
-        ]
-        * 4,
+            jax.ShapeDtypeStruct((taps, part, chans), BF) for taps in (4, 4, 4, 4)
+        ],
         in_specs=[held] * 2,
         out_specs=[held] * 4,
         scratch_shapes=[
@@ -799,75 +802,92 @@
     )(dchosen, latent, mixed_grad, near, place, refill, after_this)
 
 
-def strided_back(strided, mixed_grad, project, norms):
+def strided_meet(strided, mixed_grad, project, norms):
     taps, rows, chans = strided.shape
     group = 4
 
-    def kernel(w_ref, m_ref, p_ref, n_ref, out_ref, vec_ref, kept, total, factor, split):
-        phase, step = pl.program_id(0), pl.program_id(1)
-
-        @pl.when((phase == 0) & (step == 0))
+    def kernel(w_ref, m_ref, p_ref, n_ref, vec_ref, factor_ref, total):
+        step = pl.program_id(0)
+
+        @pl.when(step == 0)
         def _():
             total[...] = jnp.zeros_like(total)
 
-        @pl.when(phase == 0)
-        def _():
-            meeting = total[...]
-            for tap in range(group):
-                meeting = meeting + dot_nt(m_ref[tap], w_ref[tap])
-            total[...] = meeting
-            kept[step] = w_ref[...]
-
-        @pl.when((phase == 1) & (step == 0))
+        meeting = total[...]
+        for tap in range(group):
+            meeting = meeting + dot_nt(m_ref[tap], w_ref[tap])
+        total[...] = meeting
+
+        @pl.when(step == taps // group - 1)
         def _():
             plain = p_ref[...].astype(F32)
             along = jnp.sum(plain * total[...], axis=0, keepdims=True)
             vec_ref[...] = jnp.zeros_like(vec_ref)
             vec_ref[0:8, :] = total[...] * n_ref[0:1, :]
             vec_ref[8:9, :] = along * n_ref[2:3, :]
-            factor[...] = jnp.broadcast_to(along * n_ref[1:2, :], (128, rows)).T
-            split[...] = jnp.concatenate(terms(plain * n_ref[0:1, :], 3), axis=0)
-
-        @pl.when(phase == 1)
-        def _():
-            for tap in range(group):
-                three = jnp.concatenate([m_ref[tap]] * 3, axis=0)
-                out_ref[tap] = dot_tn(split[...], three) - kept[step, tap].astype(F32) * lanes4(factor[...])
+            factor_ref[...] = jnp.broadcast_to(along * n_ref[1:2, :], (128, rows)).T
 
     whole = pl.BlockSpec(memory_space=pltpu.VMEM)
     return pl.pallas_call(
         kernel,
-        grid=(2, taps // group),
-        out_shape=[jax.ShapeDtypeStruct((taps, rows, chans), F32), jax.ShapeDtypeStruct((16, rows), F32)],
+        grid=(taps // group,),
+        out_shape=[jax.ShapeDtypeStruct((16, rows), F32), jax.ShapeDtypeStruct((rows, 128), F32)],
         in_specs=[
-            pl.BlockSpec((group, rows, chans), lambda phase, step: (step * (1 - phase) + (taps // group - 1) * phase, 0, 0)),
-            pl.BlockSpec((group, 8, chans), lambda phase, step: (step, 0, 0)),
+            pl.BlockSpec((group, rows, chans), lambda step: (step, 0, 0)),
+            pl.BlockSpec((group, 8, chans), lambda step: (step, 0, 0)),
             whole,
             whole,
         ],
         out_specs=[
-            pl.BlockSpec((group, rows, chans), lambda phase, step: (phase * step, 0, 0)),
-            pl.BlockSpec((16, rows), lambda phase, step: (0, 0)),
+            pl.BlockSpec((16, rows), lambda step: (0, 0)),
+            pl.BlockSpec((rows, 128), lambda step: (0, 0)),
         ],
-        scratch_shapes=[
-            pltpu.VMEM((taps // group, group, rows, chans), BF),
-            pltpu.VMEM((8, rows), F32), pltpu.VMEM((rows, 128), F32),
-            pltpu.VMEM((24, rows), BF),
+        scratch_shapes=[pltpu.VMEM((8, rows), F32)],
+        compiler_params=pltpu.CompilerParams(vmem_limit_bytes=VMEM),
+        cost_estimate=cost(0.1),
+        name="strided_meet",
+    )(strided, mixed_grad, project, norms)
+
+
+def strided_back(strided, mixed_grad, project, norms, factors):
+    taps, rows, chans = strided.shape
+    group = 4
+
+    def kernel(w_ref, m_ref, p_ref, n_ref, f_ref, out_ref):
+        split = jnp.concatenate(terms(p_ref[...].astype(F32) * n_ref[0:1, :], 3), axis=0)
+        for tap in range(group):
+            three = jnp.concatenate([m_ref[tap]] * 3, axis=0)
+            out_ref[tap] = dot_tn(split, three) - w_ref[tap].astype(F32) * lanes4(f_ref[...])
+
+    whole = pl.BlockSpec(memory_space=pltpu.VMEM)
+    return pl.pallas_call(
+        kernel,
+        grid=(taps // group,),
+        out_shape=jax.ShapeDtypeStruct((taps, rows, chans), F32),
+        in_specs=[
+            pl.BlockSpec((group, rows, chans), lambda step: (step, 0, 0)),
+            pl.BlockSpec((group, 8, chans), lambda step: (step, 0, 0)),
+            whole,
+            whole,
+            whole,
         ],
+        out_specs=pl.BlockSpec((group, rows, chans), lambda step: (step, 0, 0)),
         compiler_params=pltpu.CompilerParams(vmem_limit_bytes=VMEM),
         cost_estimate=cost(0.1),
         name="strided_back",
-    )(strided, mixed_grad, project, norms)
+    )(strided, mixed_grad, project, norms, factors)
 
 
 def norm_back(chains, dilated, pointwise, gains, members, earlier):
     units, _, part, chans = dilated.shape
     count = len(members)
+    others = earlier[2:]
 
     def kernel(*refs):
         halves, refs = refs[: 2 * count], refs[2 * count :]
         w_refs, q_refs, g_refs = (refs[n * count : (n + 1) * count] for n in range(3))
-        out7, out1, out_g, helds, res7, res1, row_g, sems = refs[-8:]
+        out7, out1, out_g7, out_g1, helds, res7, res1, sems = refs[-8:]
+        given = refs[3 * count + 2 : 3 * count + 2 + len(others)] if earlier else ()
         outs = []
 
         def send(value, target):
@@ -886,7 +906,6 @@
             def weight_of(tap, n=n):
                 return (q_refs[n][0] if tap == 7 else w_refs[n][0, tap]).astype(F32)
 
-            row_g[n] = jnp.zeros_like(row_g[n])
             for which, taps in enumerate((range(7), (7,))):
                 square = jnp.zeros((part, 128), F32)
                 along = jnp.zeros((part, 128), F32)
@@ -899,12 +918,17 @@
                         along = along + both[:, cols]
                 square_sum = jnp.sum(square, axis=1, keepdims=True) + NORM_EPS
                 factor = jnp.sum(along, axis=1, keepdims=True) / square_sum
-                row_g[n, which : which + 1, :] = lane_sums(along) / g_refs[n][0, which : which + 1, :]
+                row = lane_sums(along) / g_refs[n][0, which : which + 1, :]
+                out_g = (out_g7, out_g1)[which]
+                place = member if others else 0
+                out_g[place : place + 1, :] = row
+                for other in range(len(others) // 2):
+                    place = units - 1 - other
+                    out_g[place : place + 1, :] = given[2 * other + which][...]
                 for tap in taps:
                     target = res1.at[n] if tap == 7 else res7.at[n, tap]
                     target[...] = grad_of(tap) - weight_of(tap) * factor
                     send(target, out1.at[member] if tap == 7 else out7.at[member, tap])
-            send(row_g.at[n], out_g.at[member])
         for copy in outs:
             copy.wait()
 
@@ -920,21 +944,21 @@
         out_shape=[
             jax.ShapeDtypeStruct((units, 7, part, chans), F32),
             jax.ShapeDtypeStruct((units, part, chans), F32),
-            jax.ShapeDtypeStruct((units, 8, part), F32),
-        ],
+        ]
+        + [jax.ShapeDtypeStruct((units if others else 1, part), F32)] * 2,
         in_specs=[whole] * (2 * count)
         + [block((7, part, chans), member) for member in members]
         + [block((part, chans), member) for member in members]
         + [block((2, part), member) for member in members]
-        + [held] * len(earlier),
-        out_specs=[held] * 3,
-        input_output_aliases={5 * count + n: n for n in range(len(earlier))},
+        + [held] * len(earlier[:2])
+        + [whole] * len(others),
+        out_specs=[held, held, whole, whole],
+        input_output_aliases={5 * count + n: n for n in range(len(earlier[:2]))},
         scratch_shapes=[
             pltpu.VMEM((count, max(2 * chain.whole[0].shape[0] for chain in chains), chans), BF),
             pltpu.VMEM((count, 7, part, chans), F32),
             pltpu.VMEM((count, part, chans), F32),
-            pltpu.VMEM((count, 8, part), F32),
-            pltpu.SemaphoreType.DMA((9 * count,)),
+            pltpu.SemaphoreType.DMA((8 * count,)),
         ],
         compiler_params=pltpu.CompilerParams(vmem_limit_bytes=VMEM),
         cost_estimate=cost(0.1),
@@ -1434,7 +1458,10 @@
     chain1 = Chain([[(keep1, 0), (near1, 0), (after(x1, token), None)], [(more, None)]], chain_rows, over_frames)
     last = units_back(
         vecs, labels, own, rows, chans, into_of(0, after(back0["out"], chain1.sent), back0["scaled_out"]),
-        others=(back0["sums_a"], back0["sums_c"], back1["sums_a"], back1["sums_c"], back2["sums_a"], last_sums),
+        others=(
+            (back0["sums_a"], 3), (back0["sums_c"], 1), (back1["sums_a"], 3), (back1["sums_c"], 1),
+            (back2["sums_a"], 3), (last_sums, 2),
+        ),
     )
     grad, small = last["out"], last["sums_c"]
 
@@ -1487,21 +1514,20 @@
         got = after(got_codes[peer], token)
         payload = lax.dynamic_update_slice_in_dim(payload, got, (me ^ peer) * quarter, 0)
     blocks = codebook.shape[1] // 512
-    dstrided_dirs, meeting = strided_back(strided_dirs, payload[24 * blocks :].reshape(-1, 8, chans), latent_proj, norms)
-    token = chain0.step(dstrided_dirs)
+    mixed_total = payload[24 * blocks :].reshape(-1, 8, chans)
+    meeting, factors = strided_meet(strided_dirs, mixed_total, latent_proj, norms)
+    token = chain0.step(meeting)
     while chain1.left > 1:
         token = chain1.step(token)
+    small_step()
     gains = jnp.stack([dilated_gains, pointwise_gains], axis=1)
     results = norm_back([chain2], after(dilated_dirs, token), pointwise_dirs, gains, (2,), ())
-    token = results[0]
-    small_step()
-    grad_signal = settle(list(lax.optimization_barrier((*sent_outs, token))[:4]))
+    gains2 = results[2:]
+    grad_signal = settle(list(lax.optimization_barrier((*sent_outs, results[0]))[:4]))
     token = grad_signal
     while chain0.left > 1:
         token = chain0.step(token)
-    token = chain1.step(token)
-    results = norm_back([chain1], after(dilated_dirs, token), pointwise_dirs, gains, (1,), results)
-    payload = after(payload, results[0])
+    payload = after(payload, token)
     codes = codebook.shape[1]
     blocks = codes // 512
     by_code = payload[: 24 * blocks].reshape(blocks, 24, 512).transpose(1, 0, 2).reshape(24, codes).astype(F32)
@@ -1511,27 +1537,30 @@
     coded = codebook * coded_scale[None, :]
     dcodebook = (dcoded - coded * jnp.sum(coded * dcoded, axis=0)[None, :]) * coded_scale[None, :]
 
-    token = lax.optimization_barrier((token, refreshed, dcodebook))[0]
+    factors = lax.optimization_barrier((factors, token, refreshed, dcodebook))[0]
+    dstrided_dirs = strided_back(strided_dirs, mixed_total, latent_proj, norms, factors)
+    token = chain1.step(dstrided_dirs)
+    results = norm_back([chain1], after(dilated_dirs, token), pointwise_dirs, gains, (1,), results[:2])
+    token = results[0]
     chain0.step(token)
-    results = norm_back([chain0], dilated_dirs, pointwise_dirs, gains, (0,), results)
+    results = norm_back([chain0], dilated_dirs, pointwise_dirs, gains, (0,), (*results[:2], *gains2, *results[2:]))
     sums_out = chain1.upper()[first : first + output_bias.shape[0] * 16 // chans].astype(F32).reshape(-1, 16)
     mine_small = lax.dynamic_slice_in_dim(small, me * part, part, axis=1)
-    dbias_latent = small[6 * 8 + 1, :8]
-    dbias1, dbias7, dalpha2 = mine_small[8:48:16], mine_small[9:48:16], mine_small[10:48:16]
-    dalpha1 = mine_small[0:48:16]
-    dalpha_last = mine_small[6 * 8]
+    dbias_latent = small[4 * units + 1, :8]
+    dalpha1, dbias1, dbias7, dalpha2 = (mine_small[n : 4 * units : 4] for n in range(4))
+    dalpha_last = mine_small[4 * units]
     dproj_latent = meeting[0:8] + dbias_latent[:, None] * strided_bias[None, :]
     dbias_strided = jnp.sum(latent_proj.astype(F32) * dbias_latent[:, None], axis=0)
     return (
         output,
         grad_signal,
         results[0],
-        results[2][:, 0],
+        results[2],
         dbias7,
         dalpha1,
         dalpha2,
         results[1],
-        results[2][:, 1],
+        results[3],
         dbias1,
         dalpha_last,
         dstrided_dirs,

time: 379 us -> 373 us (0.984)
  waiting for transfers between devices: 40 us -> 33.4 us
  Pallas kernels: 222 us -> 226 us
    ppermute x45, waiting for transfers between devices: 32.5 us -> 25.2 us  [swap(): return lax.ppermute(value, axis, [(i, i ^ 1 << bit) for i in range(count)])]
    pallas_call x2 -> x3, Pallas kernels: 11.8 us -> 14.2 us  [the longest x1 6.68 us: strided_back(): pl.pallas_call(kernel, grid=(taps // group,), out_shape=jax.ShapeDtypeStr...]
    unnamed x145 -> x146, local copies, waits for them, and re-layouts: 20 us -> 18.5 us
  transfers between devices with their start and end apart: 61 -> 61, of which waited for: 13 -> 13; matrix products, arithmetic and copies ran while one was open for 7% -> 7% of each run, Pallas kernels for 50% -> 52%
where the time goes in v4:
time: 373 us; the launch traced here: 367 us
  Pallas kernels  226 us (61%)
  starting transfers between devices  60.9 us (16%)
  local copies, waits for them, and re-layouts  33.9 us (9%)
  waiting for transfers between devices  33.4 us (9%)
  other arithmetic  11.5 us (3%)
    pallas_call x4, Pallas kernels, units_back(): pl.pallas_call(kernel, out_shape=[shape for shape, _ in outs.values()], i...  77.5 us
    ppermute x45, starting transfers between devices, swap(): return lax.ppermute(value, axis, [(i, i ^ 1 << bit) for i in range(count)])  46.1 us
    pallas_call x3, Pallas kernels, unit_forward(): pl.pallas_call(kernel, out_shape=[jax.ShapeDtypeStruct((rows, chans), F32...  35.6 us
    pallas_call x12, Pallas kernels, sum_halves(): pl.pallas_call(kernel, grid=(1,), out_shape=[jax.ShapeDtypeStruct((half,...  27.2 us
    ppermute x45, waiting for transfers between devices, swap(): return lax.ppermute(value, axis, [(i, i ^ 1 << bit) for i in range(count)])  25.2 us
    unnamed x146, local copies, waits for them, and re-layouts  18.5 us
    pallas_call x3, Pallas kernels, norm_back(): pl.pallas_call(kernel, grid=(1,), out_shape=[jax.ShapeDtypeStruct((units,...  13 us
    pallas_call x1, Pallas kernels, bottleneck(): pl.pallas_call(kernel, out_shape=[jax.ShapeDtypeStruct((rows, chans), F32...  10.9 us
  transfers between devices with their start and end apart: 61, of which 13 were waited for; matrix products, arithmetic and copies ran while one was open for 7% of the time, Pallas kernels for 52%

profile of v4, /device:TPU:0, one launch (start us, length us, event | category | flops | bytes accessed | tf_op | source)
XLA Modules:
  0.0 367.4 jit_solution(13304876621627524243)
XLA Ops:
  0.7 3.0 halve.1
  4.6 2.5 collective-permute-start.7
  8.3 3.3 vectors.1
  11.6 2.9 cut.1
  18.7 2.9 collective-permute-start
  21.6 2.2 collective-permute-start.1
  23.8 2.6 collective-permute-start.10
  31.0 1.9 collective-permute-start.3
  33.2 7.2 %collective-permute-done.2.p3 = bf16[128,1408]{1,0:T(8,128)(2,1)} collective-permute-done((bf16[128,1408]{1,0:T(8,128)(2,1)}, bf16[128,1408]{1,0:T(8,128)(2,1)}, u32[]{:S(2)}, u32[]{:S(2)}) %collective-permute-start.2) | collective-permute-done | bytes 360480 | tf_op jit(solution)/shard_map/ppermute | solution.py:1290
  40.9 4.7 %merge_strided.1 = (f32[136,512]{1,0:T(8,128)}, f32[8,256]{1,0:T(8,128)}) custom-call(bf16[16,256,512]{2,1,0:T(8,128)(2,1)} %w_ref.5, f32[1,256]{1,0:T(1,128)} %bitcast.54, f32[1,256]{1,0:T(1,128)} %bitcast.51, bf16[8,256]{1,0:T(8,128)(2,1)} %p_ref.4), custom_call_target="tpu_custom_call" | custom-call | flops 5750000128 | tf_op jit(solution)/shard_map/merge_strided/pallas_call | solution.py:689
  47.1 5.2 %enter.1 = (f32[1280,512]{1,0:T(8,128)}, f32[32,512]{1,0:T(8,128)}, f32[8,128]{1,0:T(8,128)}, f32[8,128]{1,0:T(8,128)}) custom-call(bf16[128,1408]{1,0:T(8,128)(2,1)} %get-tuple-element.210.p0, bf16[128,1408]{1,0:T(8,128)(2,1)} %copy-done.16, bf16[128,1408]{1,0:T(8,128)(2,1)} %collective-permute-done.1.p2, bf16[128,1408]{1,0:T(8,128)(2,1)} %collective-permute-done.2.p3, ...), custom_call_target="tpu_custom_call" | custom-call | flops 115000000 | tf_op jit(solution)/shard_map/enter/pallas_call | solution.py:593
  52.4 11.7 %unit_forward_1.1 = (f32[1280,512]{1,0:T(8,128)}, f32[1280,512]{1,0:T(8,128)}, bf16[1376,512]{1,0:T(8,128)(2,1)}, bf16[512,512]{1,0:T(8,128)(2,1)}) custom-call(f32[1280,512]{1,0:T(8,128)} %get-tuple-element.220.s_ref.refs_3_, bf16[3,7,128,512]{3,2,1,0:T(8,128)(2,1)} %refs_2_.3, bf16[3,128,512]{2,1,0:T(8,128)(2,1)} %refs_3_.5, ...), custom_call_target="tpu_custom_call" | custom-call | flops 13799999488 | tf_op jit(solution)/shard_map/unit_forward_1/pallas_call | solution.py:221
  70.0 8.0 %look_up.1 = (f32[160,128]{1,0:T(8,128)}, f32[256,512]{1,0:T(8,128)}, f32[256,128]{1,0:T(8,128)}) custom-call(s32[672,128]{1,0:T(8,128)} %broadcast_in_dim.85.i_ref, f32[8,8192]{1,0:T(8,128)} %c_ref.1, bf16[256,128]{1,0:T(8,128)(2,1)} %concatenate.9.p_ref, bf16[256,512]{1,0:T(8,128)(2,1)} %t_ref.3), custom_call_target="tpu_custom_call" | custom-call | flops 115000000 | tf_op jit(solution)/shard_map/look_up/pallas_call | solution.py:731
  82.4 11.7 %unit_forward_3.1 = (f32[1280,512]{1,0:T(8,128)}, f32[1280,512]{1,0:T(8,128)}, bf16[1568,512]{1,0:T(8,128)(2,1)}, bf16[512,512]{1,0:T(8,128)(2,1)}) custom-call(f32[1280,512]{1,0:T(8,128)} %get-tuple-element.228.s_ref.refs_3_, bf16[3,7,128,512]{3,2,1,0:T(8,128)(2,1)} %refs_2_.3, bf16[3,128,512]{2,1,0:T(8,128)(2,1)} %refs_3_.5, ...), custom_call_target="tpu_custom_call" | custom-call | flops 13799999488 | tf_op jit(solution)/shard_map/unit_forward_3/pallas_call | solution.py:221
  97.2 12.3 %unit_forward_9.1 = (f32[1280,512]{1,0:T(8,128)}, f32[1280,512]{1,0:T(8,128)}, bf16[2144,512]{1,0:T(8,128)(2,1)}, bf16[512,512]{1,0:T(8,128)(2,1)}) custom-call(f32[1280,512]{1,0:T(8,128)} %get-tuple-element.235.s_ref.refs_3_, bf16[3,7,128,512]{3,2,1,0:T(8,128)(2,1)} %refs_2_.3, bf16[3,128,512]{2,1,0:T(8,128)(2,1)} %refs_3_.5, ...), custom_call_target="tpu_custom_call" | custom-call | flops 13799999488 | tf_op jit(solution)/shard_map/unit_forward_9/pallas_call | solution.py:221
  110.1 10.9 %bottleneck.1 = (f32[1280,512]{1,0:T(8,128)}, f32[160,128]{1,0:T(8,128)}, f32[160,128]{1,0:T(8,128)}, f32[16,8,512]{2,1,0:T(8,128)}, f32[8,512]{1,0:T(8,128)}) custom-call(f32[1280,512]{1,0:T(8,128)} %get-tuple-element.242.s_ref, f32[136,512]{1,0:T(8,128)} %copy-done.22, f32[136,512]{1,0:T(8,128)} %copy-done.59, f32[1,128]{1,0:T(1,128)} %pad_bitcast_fusion.bias_ref, ...), custom_call_target="tpu_custom_call" | custom-call | flops 12650000384 | tf_op jit(solution)/shard_map/bottleneck/pallas_call | solution.py:1120
  121.1 14.6 %units_back_weights_9.1 = (bf16[1280,512]{1,0:T(8,128)(2,1)}, bf16[2,8,128,512]{3,2,1,0:T(8,128)(2,1)}, bf16[2,8,128,512]{3,2,1,0:T(8,128)(2,1)}, f32[8,512]{1,0:T(8,128)}) custom-call(f32[2176,128]{1,0:T(8,128)} %broadcast_in_dim.82.refs_9_.l_ref.refs_0_, f32[32,512]{1,0:T(8,128)} %get-tuple-element.222.refs_8_.v_ref.refs_1_, ...), custom_call_target="tpu_custom_call" | custom-call | flops 39099998208 | tf_op jit(solution)/shard_map/units_back_weights_9/pallas_call | solution.py:452
  136.8 6.1 %code_payload.1 = (bf16[128,512]{1,0:T(8,128)(2,1)}, bf16[128,512]{1,0:T(8,128)(2,1)}, bf16[128,512]{1,0:T(8,128)(2,1)}, bf16[128,512]{1,0:T(8,128)(2,1)}) custom-call(f32[160,128]{1,0:T(8,128)} %get-tuple-element.252.d_ref, f32[160,128]{1,0:T(8,128)} %get-tuple-element.253.l_ref, f32[16,8,512]{2,1,0:T(8,128)} %get-tuple-element.254.m_ref, ...), custom_call_target="tpu_custom_call" | custom-call | flops 115000000 | tf_op jit(solution)/shard_map/code_payload/pallas_call | solution.py:793
  144.7 2.3 fusion
  148.0 24.3 %units_back_into_9_weights_3.1 = (f32[1280,512]{1,0:T(8,128)}, f32[8,512]{1,0:T(8,128)}, bf16[1280,512]{1,0:T(8,128)(2,1)}, bf16[2,8,128,512]{3,2,1,0:T(8,128)(2...) custom-call(f32[2176,128]{1,0:T(8,128)} %broadcast_in_dim.82.refs_9_.l_ref.refs_0_, ...), custom_call_target="tpu_custom_call" | custom-call | flops 73600000000 | tf_op jit(solution)/shard_map/units_back_into_9_weights_3/pallas_call | solution.py:452
  174.4 3.6 sum_halves.12
  181.1 24.8 %units_back_into_3_weights_1.1 = (f32[1280,512]{1,0:T(8,128)}, f32[8,512]{1,0:T(8,128)}, bf16[1280,512]{1,0:T(8,128)(2,1)}, bf16[2,8,128,512]{3,2,1,0:T(8,128)(2...) custom-call(f32[2176,128]{1,0:T(8,128)} %broadcast_in_dim.82.refs_9_.l_ref.refs_0_, ...), custom_call_target="tpu_custom_call" | custom-call | flops 73600000000 | tf_op jit(solution)/shard_map/units_back_into_3_weights_1/pallas_call | solution.py:452
  206.8 2.2 sum_halves.13
  211.6 3.3 sum_halves.14
  216.5 13.8 %units_back_into_1.1 = (f32[1280,512]{1,0:T(8,128)}, f32[16,512]{1,0:T(8,128)}) custom-call(f32[2176,128]{1,0:T(8,128)} %broadcast_in_dim.82.refs_9_.l_ref.refs_0_, f32[32,512]{1,0:T(8,128)} %get-tuple-element.222.refs_8_.v_ref.refs_1_, f32[1280,512]{1,0:T(8,128)} %get-tuple-element.293.refs_2_, f32[1280,512]{1,0:T(8,128)} %get-tuple-element.220.s_ref.refs_3_, ...), custom_call_target="tpu_custom_call" | custom-call | flops 57500000256 | tf_op jit(solution)/shard_map/units_back_into_1/pallas_call | solution.py:452
  231.0 1.8 sum_halves.15
  233.7 2.2 sum_halves.16
  239.2 2.6 collective-permute-start.37
  241.8 3.5 leave.1
  245.3 3.5 collective-permute-done.37.refs_1_
  251.1 3.4 collective-permute-start.38
  264.3 3.2 sum_halves.19
  269.2 3.1 collective-permute-start.43
  272.2 6.4 %collective-permute-done.43.refs_1_ = bf16[144,512]{1,0:T(8,128)(2,1)S(1)} collective-permute-done((bf16[144,512]{1,0:T(8,128)(2,1)S(1)}, bf16[144,512]{1,0:T(8,128)(2,1)S(1)}, u32[]{:S(2)}, u32[]{:S(2)}) %collective-permute-start.43) | collective-permute-done | bytes 147488 | tf_op jit(solution)/shard_map/ppermute | solution.py:1146
  281.6 1.9 join.7.refs_0_
  285.0 2.1 sum_halves.21
  287.3 2.1 collective-permute-start.48
  290.5 8.4 %collective-permute-done.48 = f32[16,512]{1,0:T(8,128)S(1)} collective-permute-done((f32[16,512]{1,0:T(8,128)S(1)}, f32[16,512]{1,0:T(8,128)S(1)}, u32[]{:S(2)}, u32[]{:S(2)}) %collective-permute-start.48) | collective-permute-done | bytes 32800 | tf_op jit(solution)/shard_map/ppermute | solution.py:1146
  301.4 3.0 collective-permute-start.53
  316.4 4.5 %strided_meet.1 = (f32[16,256]{1,0:T(8,128)}, f32[256,128]{1,0:T(8,128)}) custom-call(bf16[16,256,512]{2,1,0:T(8,128)(2,1)} %w_ref.5, bf16[16,8,512]{2,1,0:T(8,128)(2,1)} %slice_bitcast_fusion.m_ref, bf16[8,256]{1,0:T(8,128)(2,1)} %p_ref.4, f32[8,256]{1,0:T(8,128)} %get-tuple-element.343.n_ref), custom_call_target="tpu_custom_call" | custom-call | flops 115000000 | tf_op jit(solution)/shard_map/strided_meet/pallas_call | solution.py:831
  325.5 1.9 join.10.refs_0_
  328.0 2.4 collective-permute-start.58
  334.5 4.3 %norm_back.3 = (f32[3,7,128,512]{3,2,1,0:T(8,128)}, f32[3,128,512]{2,1,0:T(8,128)}, f32[1,128]{1,0:T(1,128)}, f32[1,128]{1,0:T(1,128)}) custom-call(bf16[576,512]{1,0:T(8,128)(2,1)} %join.7.refs_0_, bf16[576,512]{1,0:T(8,128)(2,1)} %copy-done.8, bf16[3,7,128,512]{3,2,1,0:T(8,128)(2,1)} %refs_2_.3, bf16[3,128,512]{2,1,0:T(8,128)(2,1)} %refs_3_.5, ...), custom_call_target="tpu_custom_call" | custom-call | flops 115000000 | tf_op jit(solution)/shard_map/norm_back/pallas_call | solution.py:941
  339.8 2.7 settle.1
  344.5 1.9 join.11.refs_0_
  348.7 6.7 %strided_back.1 = f32[16,256,512]{2,1,0:T(8,128)} custom-call(bf16[16,256,512]{2,1,0:T(8,128)(2,1)} %w_ref.5, bf16[16,8,512]{2,1,0:T(8,128)(2,1)} %slice_bitcast_fusion.m_ref, bf16[8,256]{1,0:T(8,128)(2,1)} %p_ref.4, f32[8,256]{1,0:T(8,128)} %get-tuple-element.343.n_ref, f32[256,128]{1,0:T(8,128)} %get-tuple-element.357.f_ref), custom_call_target="tpu_custom_call" | custom-call | flops 115000000 | tf_op jit(solution)/shard_map/strided_back/pallas_call | solution.py:863
  356.9 4.3 %norm_back.4 = (f32[3,7,128,512]{3,2,1,0:T(8,128)}, f32[3,128,512]{2,1,0:T(8,128)}, f32[1,128]{1,0:T(1,128)}, f32[1,128]{1,0:T(1,128)}) custom-call(bf16[576,512]{1,0:T(8,128)(2,1)} %join.10.refs_0_, bf16[576,512]{1,0:T(8,128)(2,1)} %copy-done.9, bf16[3,7,128,512]{3,2,1,0:T(8,128)(2,1)} %refs_2_.3, ...), custom_call_target="tpu_custom_call", output_to_operand_aliasing={{0}: (5, {}), {1}: (6, {})} | custom-call | flops 115000000 | tf_op jit(solution)/shard_map/norm_back/pallas_call | solution.py:941
  362.8 4.3 %norm_back.5 = (f32[3,7,128,512]{3,2,1,0:T(8,128)}, f32[3,128,512]{2,1,0:T(8,128)}, f32[3,128]{1,0:T(4,128)}, f32[3,128]{1,0:T(4,128)}) custom-call(bf16[512,512]{1,0:T(8,128)(2,1)} %join.11.refs_0_, bf16[512,512]{1,0:T(8,128)(2,1)} %copy-done.14, bf16[3,7,128,512]{3,2,1,0:T(8,128)(2,1)} %refs_2_.3, ...), custom_call_target="tpu_custom_call", output_to_operand_aliasing={{0}: (5, {}), {1}: (6, {})} | custom-call | flops 115000000 | tf_op jit(solution)/shard_map/norm_back/pallas_call | solution.py:941
  (336 shorter events, 97.3 us)
Async XLA Ops:
  4.1 48.2 %collective-permute-start.8 = (bf16[3,7,128,512]{3,2,1,0:T(8,128)(2,1)S(1)}, bf16[3,7,128,512]{3,2,1,0:T(8,128)(2,1)}, u32[]{:S(2)}, u32[]{:S(2)}) collective-permute-start(bf16[3,7,128,512]{3,2,1,0:T(8,128)(2,1)S(1)} %copy-done), channel_id=1, source_target_pairs={{0,1},{1,0},{2,3},{3,2},{4,5},{5,4},{6,7},{7,6},{8,9},{9,8},{10,11... | collective-permute-start | bytes 8257544 | tf_op jit(solution)/shard_map/ppermute | solution.py:1146
  4.6 19.2 %collective-permute-start.7 = (bf16[4,128,512]{2,1,0:T(8,128)(2,1)}, bf16[4,128,512]{2,1,0:T(8,128)(2,1)}, u32[]{:S(2)}, u32[]{:S(2)}) collective-permute-start(bf16[4,128,512]{2,1,0:T(8,128)(2,1)} %get-tuple-element.196), channel_id=1, source_target_pairs={{0,2},{1,3},{2,0},{3,1},{4,6},{5,7},{6,4},{7,5},{8,10},{9,11},{10,... | collective-permute-start | bytes 1572872 | tf_op jit(solution)/shard_map/ppermute | solution.py:1146
  18.7 12.3 %collective-permute-start = (bf16[128,1408]{1,0:T(8,128)(2,1)}, bf16[128,1408]{1,0:T(8,128)(2,1)S(1)}, u32[]{:S(2)}, u32[]{:S(2)}) collective-permute-start(bf16[128,1408]{1,0:T(8,128)(2,1)} %get-tuple-element.201), channel_id=1, source_target_pairs={{0,1},{1,0},{2,3},{3,2},{4,5},{5,4},{6,7},{7,6},{8,9},{9,8},{10,11... | collective-permute-start | bytes 1081352 | tf_op jit(solution)/shard_map/ppermute | solution.py:1290
  21.6 11.6 %collective-permute-start.1 = (bf16[128,1408]{1,0:T(8,128)(2,1)}, bf16[128,1408]{1,0:T(8,128)(2,1)}, u32[]{:S(2)}, u32[]{:S(2)}) collective-permute-start(bf16[128,1408]{1,0:T(8,128)(2,1)} %get-tuple-element.202), channel_id=1, source_target_pairs={{0,2},{1,3},{2,0},{3,1},{4,6},{5,7},{6,4},{7,5},{8,10},{9,11},{10,... | collective-permute-start | bytes 1081352 | tf_op jit(solution)/shard_map/ppermute | solution.py:1290
  23.8 16.7 %collective-permute-start.2 = (bf16[128,1408]{1,0:T(8,128)(2,1)}, bf16[128,1408]{1,0:T(8,128)(2,1)}, u32[]{:S(2)}, u32[]{:S(2)}) collective-permute-start(bf16[128,1408]{1,0:T(8,128)(2,1)} %get-tuple-element.203), channel_id=1, source_target_pairs={{0,3},{1,2},{2,1},{3,0},{4,7},{5,6},{6,5},{7,4},{8,11},{9,10},{10,... | collective-permute-start | bytes 1081352 | tf_op jit(solution)/shard_map/ppermute | solution.py:1290
  23.8 16.7 %collective-permute-start.10 = (bf16[4,128,512]{2,1,0:T(8,128)(2,1)}, bf16[4,128,512]{2,1,0:T(8,128)(2,1)}, u32[]{:S(2)}, u32[]{:S(2)}) collective-permute-start(bf16[4,128,512]{2,1,0:T(8,128)(2,1)} %collective-permute-done.7.refs_4_.refs_9_), channel_id=1, source_target_pairs={{0,4},{4,0},{8,12},{12,8},{16,20},{20,16},{24,28},{28,24},{1,5},{5... | collective-permute-start | bytes 1572872 | tf_op jit(solution)/shard_map/ppermute | solution.py:1146
  31.0 14.6 %collective-permute-start.3 = (bf16[144,128]{1,0:T(8,128)(2,1)}, bf16[144,128]{1,0:T(8,128)(2,1)S(1)}, u32[]{:S(2)}, u32[]{:S(2)}) collective-permute-start(bf16[144,128]{1,0:T(8,128)(2,1)} %get-tuple-element.204), channel_id=1, source_target_pairs={{7,3},{11,7},{15,11},{19,15},{23,19},{27,23},{31,27},{0,4},{4,8},{... | collective-permute-start | bytes 110600 | tf_op jit(solution)/shard_map/ppermute | solution.py:1349
  33.2 19.0 %collective-permute-start.9 = (bf16[3,128,512]{2,1,0:T(8,128)(2,1)S(1)}, bf16[3,128,512]{2,1,0:T(8,128)(2,1)}, u32[]{:S(2)}, u32[]{:S(2)}) collective-permute-start(bf16[3,128,512]{2,1,0:T(8,128)(2,1)S(1)} %copy-done.1), channel_id=1, source_target_pairs={{0,1},{1,0},{2,3},{3,2},{4,5},{5,4},{6,7},{7,6},{8,9},{9,8},{10,11... | collective-permute-start | bytes 1179656 | tf_op jit(solution)/shard_map/ppermute | solution.py:1146
  40.4 11.9 %collective-permute-start.11 = (bf16[4,128,512]{2,1,0:T(8,128)(2,1)}, bf16[4,128,512]{2,1,0:T(8,128)(2,1)}, u32[]{:S(2)}, u32[]{:S(2)}) collective-permute-start(bf16[4,128,512]{2,1,0:T(8,128)(2,1)} %collective-permute-done.7.refs_4_.refs_9_), channel_id=1, source_target_pairs={{0,1},{1,0},{2,3},{3,2},{4,5},{5,4},{6,7},{7,6},{8,9},{9,8},{10,11... | collective-permute-start | bytes 1572872 | tf_op jit(solution)/shard_map/ppermute | solution.py:1146
  40.5 11.8 %collective-permute-start.12 = (bf16[4,128,512]{2,1,0:T(8,128)(2,1)}, bf16[4,128,512]{2,1,0:T(8,128)(2,1)}, u32[]{:S(2)}, u32[]{:S(2)}) collective-permute-start(bf16[4,128,512]{2,1,0:T(8,128)(2,1)} %collective-permute-done.10.refs_5_.refs_10_), channel_id=1, source_target_pairs={{0,1},{1,0},{2,3},{3,2},{4,5},{5,4},{6,7},{7,6},{8,9},{9,8},{10,11... | collective-permute-start | bytes 1572872 | tf_op jit(solution)/shard_map/ppermute | solution.py:1146
  45.6 18.5 %collective-permute-start.13 = (bf16[4,128,512]{2,1,0:T(8,128)(2,1)}, bf16[4,128,512]{2,1,0:T(8,128)(2,1)}, u32[]{:S(2)}, u32[]{:S(2)}) collective-permute-start(bf16[4,128,512]{2,1,0:T(8,128)(2,1)} %get-tuple-element.230), channel_id=1, source_target_pairs={{0,2},{1,3},{2,0},{3,1},{4,6},{5,7},{6,4},{7,5},{8,10},{9,11},{10,... | collective-permute-start | bytes 1572872 | tf_op jit(solution)/shard_map/ppermute | solution.py:1146
  64.1 14.0 %collective-permute-start.14 = (bf16[4,128,512]{2,1,0:T(8,128)(2,1)}, bf16[4,128,512]{2,1,0:T(8,128)(2,1)S(1)}, u32[]{:S(2)}, u32[]{:S(2)}) collective-permute-start(bf16[4,128,512]{2,1,0:T(8,128)(2,1)} %collective-permute-done.13.refs_4_.refs_9_), channel_id=1, source_target_pairs={{0,4},{4,0},{8,12},{12,8},{16,20},{20,16},{24,28},{28,24},{1,5},{5... | collective-permute-start | bytes 1572872 | tf_op jit(solution)/shard_map/ppermute | solution.py:1146
  66.2 13.4 %collective-permute-start.18 = (bf16[4,128,512]{2,1,0:T(8,128)(2,1)S(1)}, bf16[4,128,512]{2,1,0:T(8,128)(2,1)S(1)}, u32[]{:S(2)}, u32[]{:S(2)}) collective-permute-start(bf16[4,128,512]{2,1,0:T(8,128)(2,1)S(1)} %copy-done.50), channel_id=1, source_target_pairs={{0,2},{1,3},{2,0},{3,1},{4,6},{5,7},{6,4},{7,5},{8,10},{9,11},{10,... | collective-permute-start | bytes 1572872 | tf_op jit(solution)/shard_map/ppermute | solution.py:1146
  66.5 11.6 %collective-permute-start.16 = (f32[136,512]{1,0:T(8,128)S(1)}, f32[136,512]{1,0:T(8,128)S(1)}, u32[]{:S(2)}, u32[]{:S(2)}) collective-permute-start(f32[136,512]{1,0:T(8,128)S(1)} %copy-done.21), channel_id=1, source_target_pairs={{0,1},{1,0},{2,3},{3,2},{4,5},{5,4},{6,7},{7,6},{8,9},{9,8},{10,11... | collective-permute-start | bytes 835592 | tf_op jit(solution)/shard_map/ppermute | solution.py:1146
  68.1 12.7 %collective-permute-start.15 = (bf16[4,128,512]{2,1,0:T(8,128)(2,1)}, bf16[4,128,512]{2,1,0:T(8,128)(2,1)S(1)}, u32[]{:S(2)}, u32[]{:S(2)}) collective-permute-start(bf16[4,128,512]{2,1,0:T(8,128)(2,1)} %collective-permute-done.13.refs_4_.refs_9_), channel_id=1, source_target_pairs={{0,1},{1,0},{2,3},{3,2},{4,5},{5,4},{6,7},{7,6},{8,9},{9,8},{10,11... | collective-permute-start | bytes 1572872 | tf_op jit(solution)/shard_map/ppermute | solution.py:1146
  79.6 14.5 %collective-permute-start.19 = (bf16[4,128,512]{2,1,0:T(8,128)(2,1)S(1)}, bf16[4,128,512]{2,1,0:T(8,128)(2,1)S(1)}, u32[]{:S(2)}, u32[]{:S(2)}) collective-permute-start(bf16[4,128,512]{2,1,0:T(8,128)(2,1)S(1)} %copy-done.49), channel_id=1, source_target_pairs={{0,2},{1,3},{2,0},{3,1},{4,6},{5,7},{6,4},{7,5},{8,10},{9,11},{10,... | collective-permute-start | bytes 1572872 | tf_op jit(solution)/shard_map/ppermute | solution.py:1146
  80.8 14.7 %collective-permute-start.20 = (bf16[4,128,512]{2,1,0:T(8,128)(2,1)S(1)}, bf16[4,128,512]{2,1,0:T(8,128)(2,1)S(1)}, u32[]{:S(2)}, u32[]{:S(2)}) collective-permute-start(bf16[4,128,512]{2,1,0:T(8,128)(2,1)S(1)} %collective-permute-done.18.refs_4_.refs_9_), channel_id=1, source_target_pairs={{0,1},{1,0},{2,3},{3,2},{4,5},{5,4},{6,7},{7,6},{8,9},{9,8},{10,11... | collective-permute-start | bytes 1572872 | tf_op jit(solution)/shard_map/ppermute | solution.py:1146
  94.7 14.7 %collective-permute-start.22 = (f32[136,512]{1,0:T(8,128)S(1)}, f32[136,512]{1,0:T(8,128)S(1)}, u32[]{:S(2)}, u32[]{:S(2)}) collective-permute-start(f32[136,512]{1,0:T(8,128)S(1)} %add.187.wa_ref), channel_id=1, source_target_pairs={{0,2},{1,3},{2,0},{3,1},{4,6},{5,7},{6,4},{7,5},{8,10},{9,11},{10,... | collective-permute-start | bytes 835592 | tf_op jit(solution)/shard_map/ppermute | solution.py:1146
  135.7 9.0 %collective-permute-start.23 = (bf16[2,8,128,512]{3,2,1,0:T(8,128)(2,1)}, bf16[2,8,128,512]{3,2,1,0:T(8,128)(2,1)S(1)}, u32[]{:S(2)}, u32[]{:S(2)}) collective-permute-start(bf16[2,8,128,512]{3,2,1,0:T(8,128)(2,1)} %get-tuple-element.251), channel_id=1, source_target_pairs={{0,1},{1,0},{2,3},{3,2},{4,5},{5,4},{6,7},{7,6},{8,9},{9,8},{10,11... | collective-permute-start | bytes 6291464 | tf_op jit(solution)/shard_map/ppermute | solution.py:1146
  142.9 30.0 %collective-permute-start.26 = (bf16[128,512]{1,0:T(8,128)(2,1)}, bf16[128,512]{1,0:T(8,128)(2,1)S(1)}, u32[]{:S(2)}, u32[]{:S(2)}) collective-permute-start(bf16[128,512]{1,0:T(8,128)(2,1)} %get-tuple-element.269), channel_id=1, source_target_pairs={{0,1},{1,0},{2,3},{3,2},{4,5},{5,4},{6,7},{7,6},{8,9},{9,8},{10,11... | collective-permute-start | bytes 393224 | tf_op jit(solution)/shard_map/ppermute | solution.py:1290
  143.1 29.8 %collective-permute-start.27 = (bf16[128,512]{1,0:T(8,128)(2,1)}, bf16[128,512]{1,0:T(8,128)(2,1)S(1)}, u32[]{:S(2)}, u32[]{:S(2)}) collective-permute-start(bf16[128,512]{1,0:T(8,128)(2,1)} %get-tuple-element.270), channel_id=1, source_target_pairs={{0,2},{1,3},{2,0},{3,1},{4,6},{5,7},{6,4},{7,5},{8,10},{9,11},{10,... | collective-permute-start | bytes 393224 | tf_op jit(solution)/shard_map/ppermute | solution.py:1290
  144.3 28.6 %collective-permute-start.28 = (bf16[128,512]{1,0:T(8,128)(2,1)}, bf16[128,512]{1,0:T(8,128)(2,1)S(1)}, u32[]{:S(2)}, u32[]{:S(2)}) collective-permute-start(bf16[128,512]{1,0:T(8,128)(2,1)} %get-tuple-element.271), channel_id=1, source_target_pairs={{0,3},{1,2},{2,1},{3,0},{4,7},{5,6},{6,5},{7,4},{8,11},{9,10},{10,... | collective-permute-start | bytes 393224 | tf_op jit(solution)/shard_map/ppermute | solution.py:1290
  147.0 27.3 %collective-permute-start.25 = (bf16[8,128,512]{2,1,0:T(8,128)(2,1)S(1)}, bf16[8,128,512]{2,1,0:T(8,128)(2,1)}, u32[]{:S(2)}, u32[]{:S(2)}) collective-permute-start(bf16[8,128,512]{2,1,0:T(8,128)(2,1)S(1)} %fusion), channel_id=1, source_target_pairs={{0,2},{1,3},{2,0},{3,1},{4,6},{5,7},{6,4},{7,5},{8,10},{9,11},{10,... | collective-permute-start | bytes 3145736 | tf_op jit(solution)/shard_map/ppermute | solution.py:1146
  178.0 27.9 %collective-permute-start.30 = (bf16[576,512]{1,0:T(8,128)(2,1)}, bf16[576,512]{1,0:T(8,128)(2,1)S(1)}, u32[]{:S(2)}, u32[]{:S(2)}) collective-permute-start(bf16[576,512]{1,0:T(8,128)(2,1)} %get-tuple-element.278), channel_id=1, source_target_pairs={{0,4},{4,0},{8,12},{12,8},{16,20},{20,16},{24,28},{28,24},{1,5},{5... | collective-permute-start | bytes 1769480 | tf_op jit(solution)/shard_map/ppermute | solution.py:1146
  180.1 30.5 %collective-permute-start.29 = (bf16[8,128,512]{2,1,0:T(8,128)(2,1)S(1)}, bf16[8,128,512]{2,1,0:T(8,128)(2,1)S(1)}, u32[]{:S(2)}, u32[]{:S(2)}) collective-permute-start(bf16[8,128,512]{2,1,0:T(8,128)(2,1)S(1)} %fusion.1), channel_id=1, source_target_pairs={{0,2},{1,3},{2,0},{3,1},{4,6},{5,7},{6,4},{7,5},{8,10},{9,11},{10,... | collective-permute-start | bytes 3145736 | tf_op jit(solution)/shard_map/ppermute | solution.py:1146
  209.0 21.3 %collective-permute-start.33 = (bf16[288,512]{1,0:T(8,128)(2,1)}, bf16[288,512]{1,0:T(8,128)(2,1)S(1)}, u32[]{:S(2)}, u32[]{:S(2)}) collective-permute-start(bf16[288,512]{1,0:T(8,128)(2,1)} %get-tuple-element.289), channel_id=1, source_target_pairs={{0,8},{4,12},{8,0},{12,4},{16,24},{20,28},{24,16},{28,20},{1,9},{5... | collective-permute-start | bytes 884744 | tf_op jit(solution)/shard_map/ppermute | solution.py:1146
  210.6 25.3 %collective-permute-start.31 = (bf16[2,8,128,512]{3,2,1,0:T(8,128)(2,1)}, bf16[2,8,128,512]{3,2,1,0:T(8,128)(2,1)}, u32[]{:S(2)}, u32[]{:S(2)}) collective-permute-start(bf16[2,8,128,512]{3,2,1,0:T(8,128)(2,1)} %get-tuple-element.300), channel_id=1, source_target_pairs={{0,1},{1,0},{2,3},{3,2},{4,5},{5,4},{6,7},{7,6},{8,9},{9,8},{10,11... | collective-permute-start | bytes 6291464 | tf_op jit(solution)/shard_map/ppermute | solution.py:1146
  214.9 17.9 %collective-permute-start.32 = (bf16[576,512]{1,0:T(8,128)(2,1)}, bf16[576,512]{1,0:T(8,128)(2,1)S(1)}, u32[]{:S(2)}, u32[]{:S(2)}) collective-permute-start(bf16[576,512]{1,0:T(8,128)(2,1)} %get-tuple-element.292), channel_id=1, source_target_pairs={{0,4},{4,0},{8,12},{12,8},{16,20},{20,16},{24,28},{28,24},{1,5},{5... | collective-permute-start | bytes 1769480 | tf_op jit(solution)/shard_map/ppermute | solution.py:1146
  237.6 25.8 %collective-permute-start.44 = (bf16[8,128,512]{2,1,0:T(8,128)(2,1)S(1)}, bf16[8,128,512]{2,1,0:T(8,128)(2,1)S(1)}, u32[]{:S(2)}, u32[]{:S(2)}) collective-permute-start(bf16[8,128,512]{2,1,0:T(8,128)(2,1)S(1)} %fusion.2), channel_id=1, source_target_pairs={{0,2},{1,3},{2,0},{3,1},{4,6},{5,7},{6,4},{7,5},{8,10},{9,11},{10,... | collective-permute-start | bytes 3145736 | tf_op jit(solution)/shard_map/ppermute | solution.py:1146
  238.7 17.4 %collective-permute-start.41 = (bf16[288,512]{1,0:T(8,128)(2,1)S(1)}, bf16[288,512]{1,0:T(8,128)(2,1)S(1)}, u32[]{:S(2)}, u32[]{:S(2)}) collective-permute-start(bf16[288,512]{1,0:T(8,128)(2,1)S(1)} %copy-done.58), channel_id=1, source_target_pairs={{0,8},{4,12},{8,0},{12,4},{16,24},{20,28},{24,16},{28,20},{1,9},{5... | collective-permute-start | bytes 884744 | tf_op jit(solution)/shard_map/ppermute | solution.py:1146
  239.2 9.6 %collective-permute-start.37 = (bf16[144,512]{1,0:T(8,128)(2,1)S(1)}, bf16[144,512]{1,0:T(8,128)(2,1)S(1)}, u32[]{:S(2)}, u32[]{:S(2)}) collective-permute-start(bf16[144,512]{1,0:T(8,128)(2,1)S(1)} %copy-done.63), channel_id=1, source_target_pairs={{0,16},{4,20},{8,24},{12,28},{16,0},{20,4},{24,8},{28,12},{1,17},{... | collective-permute-start | bytes 442376 | tf_op jit(solution)/shard_map/ppermute | solution.py:1146
  251.1 9.9 %collective-permute-start.38 = (bf16[144,512]{1,0:T(8,128)(2,1)}, bf16[144,512]{1,0:T(8,128)(2,1)S(1)}, u32[]{:S(2)}, u32[]{:S(2)}) collective-permute-start(bf16[144,512]{1,0:T(8,128)(2,1)} %sum_halves.17.m_ref), channel_id=1, source_target_pairs={{0,16},{4,20},{8,24},{12,28},{16,0},{20,4},{24,8},{28,12},{1,17},{... | collective-permute-start | bytes 442376 | tf_op jit(solution)/shard_map/ppermute | solution.py:1146
  263.3 17.6 %collective-permute-start.42 = (bf16[288,512]{1,0:T(8,128)(2,1)}, bf16[288,512]{1,0:T(8,128)(2,1)S(1)}, u32[]{:S(2)}, u32[]{:S(2)}) collective-permute-start(bf16[288,512]{1,0:T(8,128)(2,1)} %join.6.m_ref), channel_id=1, source_target_pairs={{0,8},{4,12},{8,0},{12,4},{16,24},{20,28},{24,16},{28,20},{1,9},{5... | collective-permute-start | bytes 884744 | tf_op jit(solution)/shard_map/ppermute | solution.py:1146
  267.6 16.6 %collective-permute-start.46 = (bf16[512,512]{1,0:T(8,128)(2,1)}, bf16[512,512]{1,0:T(8,128)(2,1)S(1)}, u32[]{:S(2)}, u32[]{:S(2)}) collective-permute-start(bf16[512,512]{1,0:T(8,128)(2,1)} %get-tuple-element.324), channel_id=1, source_target_pairs={{0,4},{4,0},{8,12},{12,8},{16,20},{20,16},{24,28},{28,24},{1,5},{5... | collective-permute-start | bytes 1572872 | tf_op jit(solution)/shard_map/ppermute | solution.py:1146
  269.2 9.4 %collective-permute-start.43 = (bf16[144,512]{1,0:T(8,128)(2,1)S(1)}, bf16[144,512]{1,0:T(8,128)(2,1)S(1)}, u32[]{:S(2)}, u32[]{:S(2)}) collective-permute-start(bf16[144,512]{1,0:T(8,128)(2,1)S(1)} %copy-done.64), channel_id=1, source_target_pairs={{0,16},{4,20},{8,24},{12,28},{16,0},{20,4},{24,8},{28,12},{1,17},{... | collective-permute-start | bytes 442376 | tf_op jit(solution)/shard_map/ppermute | solution.py:1146
  283.5 20.8 %collective-permute-start.45 = (bf16[576,512]{1,0:T(8,128)(2,1)}, bf16[576,512]{1,0:T(8,128)(2,1)S(1)}, u32[]{:S(2)}, u32[]{:S(2)}) collective-permute-start(bf16[576,512]{1,0:T(8,128)(2,1)} %join.7.refs_0_), channel_id=1, source_target_pairs={{0,4},{4,0},{8,12},{12,8},{16,20},{20,16},{24,28},{28,24},{1,5},{5... | collective-permute-start | bytes 1769480 | tf_op jit(solution)/shard_map/ppermute | solution.py:1146
  287.1 11.7 %collective-permute-start.47 = (bf16[256,512]{1,0:T(8,128)(2,1)}, bf16[256,512]{1,0:T(8,128)(2,1)S(1)}, u32[]{:S(2)}, u32[]{:S(2)}) collective-permute-start(bf16[256,512]{1,0:T(8,128)(2,1)} %get-tuple-element.330), channel_id=1, source_target_pairs={{0,8},{4,12},{8,0},{12,4},{16,24},{20,28},{24,16},{28,20},{1,9},{5... | collective-permute-start | bytes 786440 | tf_op jit(solution)/shard_map/ppermute | solution.py:1146
  287.3 11.6 %collective-permute-start.48 = (f32[16,512]{1,0:T(8,128)S(1)}, f32[16,512]{1,0:T(8,128)S(1)}, u32[]{:S(2)}, u32[]{:S(2)}) collective-permute-start(f32[16,512]{1,0:T(8,128)S(1)} %add.192), channel_id=1, source_target_pairs={{0,8},{4,12},{8,0},{12,4},{16,24},{20,28},{24,16},{28,20},{1,9},{5... | collective-permute-start | bytes 98312 | tf_op jit(solution)/shard_map/ppermute | solution.py:1146
  289.4 17.1 %collective-permute-start.50 = (bf16[144,512]{1,0:T(8,128)(2,1)S(1)}, bf16[144,512]{1,0:T(8,128)(2,1)S(1)}, u32[]{:S(2)}, u32[]{:S(2)}) collective-permute-start(bf16[144,512]{1,0:T(8,128)(2,1)S(1)} %copy-done.12), channel_id=1, source_target_pairs={{0,16},{4,20},{8,24},{12,28},{16,0},{20,4},{24,8},{28,12},{1,17},{... | collective-permute-start | bytes 442376 | tf_op jit(solution)/shard_map/ppermute | solution.py:1146
  298.9 10.8 %collective-permute-start.49 = (f32[16,512]{1,0:T(8,128)S(1)}, f32[16,512]{1,0:T(8,128)S(1)}, u32[]{:S(2)}, u32[]{:S(2)}) collective-permute-start(f32[16,512]{1,0:T(8,128)S(1)} %add.193), channel_id=1, source_target_pairs={{0,16},{4,20},{8,24},{12,28},{16,0},{20,4},{24,8},{28,12},{1,17},{... | collective-permute-start | bytes 98312 | tf_op jit(solution)/shard_map/ppermute | solution.py:1146
  309.7 29.2 %collective-permute-start.34 = (bf16[128,1024]{1,0:T(8,128)(2,1)S(1)}, bf16[128,1024]{1,0:T(8,128)(2,1)S(1)}, u32[]{:S(2)}, u32[]{:S(2)}) collective-permute-start(bf16[128,1024]{1,0:T(8,128)(2,1)S(1)} %copy-done.62), channel_id=1, source_target_pairs={{0,1},{1,0},{2,3},{3,2},{4,5},{5,4},{6,7},{7,6},{8,9},{9,8},{10,11... | collective-permute-start | bytes 786440 | tf_op jit(solution)/shard_map/ppermute | solution.py:1290
  309.8 29.2 %collective-permute-start.35 = (bf16[128,1024]{1,0:T(8,128)(2,1)S(1)}, bf16[128,1024]{1,0:T(8,128)(2,1)S(1)}, u32[]{:S(2)}, u32[]{:S(2)}) collective-permute-start(bf16[128,1024]{1,0:T(8,128)(2,1)S(1)} %copy-done.61), channel_id=1, source_target_pairs={{0,2},{1,3},{2,0},{3,1},{4,6},{5,7},{6,4},{7,5},{8,10},{9,11},{10,... | collective-permute-start | bytes 786440 | tf_op jit(solution)/shard_map/ppermute | solution.py:1290
  312.4 12.3 %collective-permute-start.52 = (bf16[288,512]{1,0:T(8,128)(2,1)}, bf16[288,512]{1,0:T(8,128)(2,1)S(1)}, u32[]{:S(2)}, u32[]{:S(2)}) collective-permute-start(bf16[288,512]{1,0:T(8,128)(2,1)} %join.8.m_ref), channel_id=1, source_target_pairs={{0,8},{4,12},{8,0},{12,4},{16,24},{20,28},{24,16},{28,20},{1,9},{5... | collective-permute-start | bytes 884744 | tf_op jit(solution)/shard_map/ppermute | solution.py:1146
  313.1 14.3 %collective-permute-start.51 = (f32[16,512]{1,0:T(8,128)S(1)}, f32[16,512]{1,0:T(8,128)S(1)}, u32[]{:S(2)}, u32[]{:S(2)}) collective-permute-start(f32[16,512]{1,0:T(8,128)S(1)} %add.194), channel_id=1, source_target_pairs={{0,2},{1,3},{2,0},{3,1},{4,6},{5,7},{6,4},{7,5},{8,10},{9,11},{10,... | collective-permute-start | bytes 98312 | tf_op jit(solution)/shard_map/ppermute | solution.py:1146
  322.4 16.5 %collective-permute-start.36 = (bf16[128,1024]{1,0:T(8,128)(2,1)S(1)}, bf16[128,1024]{1,0:T(8,128)(2,1)S(1)}, u32[]{:S(2)}, u32[]{:S(2)}) collective-permute-start(bf16[128,1024]{1,0:T(8,128)(2,1)S(1)} %copy-done.60), channel_id=1, source_target_pairs={{0,3},{1,2},{2,1},{3,0},{4,7},{5,6},{6,5},{7,4},{8,11},{9,10},{10,... | collective-permute-start | bytes 786440 | tf_op jit(solution)/shard_map/ppermute | solution.py:1290
  328.0 15.8 %collective-permute-start.58 = (bf16[256,512]{1,0:T(8,128)(2,1)}, bf16[256,512]{1,0:T(8,128)(2,1)S(1)}, u32[]{:S(2)}, u32[]{:S(2)}) collective-permute-start(bf16[256,512]{1,0:T(8,128)(2,1)} %join.9.m_ref), channel_id=1, source_target_pairs={{0,8},{4,12},{8,0},{12,4},{16,24},{20,28},{24,16},{28,20},{1,9},{5... | collective-permute-start | bytes 786440 | tf_op jit(solution)/shard_map/ppermute | solution.py:1146
  330.5 24.9 %collective-permute-start.60 = (bf16[576,512]{1,0:T(8,128)(2,1)}, bf16[576,512]{1,0:T(8,128)(2,1)S(1)}, u32[]{:S(2)}, u32[]{:S(2)}) collective-permute-start(bf16[576,512]{1,0:T(8,128)(2,1)} %join.10.refs_0_), channel_id=1, source_target_pairs={{0,4},{4,0},{8,12},{12,8},{16,20},{20,16},{24,28},{28,24},{1,5},{5... | collective-permute-start | bytes 1769480 | tf_op jit(solution)/shard_map/ppermute | solution.py:1146
  347.4 14.6 %collective-permute-start.59 = (bf16[512,512]{1,0:T(8,128)(2,1)S(1)}, bf16[512,512]{1,0:T(8,128)(2,1)S(1)}, u32[]{:S(2)}, u32[]{:S(2)}) collective-permute-start(bf16[512,512]{1,0:T(8,128)(2,1)S(1)} %copy-done.5), channel_id=1, source_target_pairs={{0,4},{4,0},{8,12},{12,8},{16,20},{20,16},{24,28},{28,24},{1,5},{5... | collective-permute-start | bytes 1572872 | tf_op jit(solution)/shard_map/ppermute | solution.py:1146
  (84 other events, 577.0 us)

commit v5 on v4

--- a/solution.py
+++ b/solution.py
@@ -1494,9 +1494,9 @@
     token = chain0.sent
     while chain1.left > half:
         token = chain1.step(token)
+    token = chain0.step(token)
     while chain2.left > 1:
         token = chain2.step(token)
-    token = chain0.step(token)
     while len(small_steps) > 2:
         small_step()
     while chain0.left > half + 1:

time: 373 us -> 378 us (1.013)
    unnamed x146 -> x148, local copies, waits for them, and re-layouts: 18.5 us -> 18.9 us
  transfers between devices with their start and end apart: 61 -> 61, of which waited for: 13 -> 14; matrix products, arithmetic and copies ran while one was open for 7% -> 7% of each run, Pallas kernels for 52% -> 51%
where the time goes in v5:
time: 378 us; the launch traced here: 372 us
  Pallas kernels  226 us (60%)
  starting transfers between devices  63.7 us (17%)
  waiting for transfers between devices  34.5 us (9%)
  local copies, waits for them, and re-layouts  34.3 us (9%)
  other arithmetic  11.5 us (3%)
    pallas_call x4, Pallas kernels, units_back(): pl.pallas_call(kernel, out_shape=[shape for shape, _ in outs.values()], i...  77.6 us
    ppermute x45, starting transfers between devices, swap(): return lax.ppermute(value, axis, [(i, i ^ 1 << bit) for i in range(count)])  49.7 us
    pallas_call x3, Pallas kernels, unit_forward(): pl.pallas_call(kernel, out_shape=[jax.ShapeDtypeStruct((rows, chans), F32...  35.6 us
    pallas_call x12, Pallas kernels, sum_halves(): pl.pallas_call(kernel, grid=(1,), out_shape=[jax.ShapeDtypeStruct((half,...  27.3 us
    ppermute x45, waiting for transfers between devices, swap(): return lax.ppermute(value, axis, [(i, i ^ 1 << bit) for i in range(count)])  27 us
    unnamed x148, local copies, waits for them, and re-layouts  18.9 us
    pallas_call x3, Pallas kernels, norm_back(): pl.pallas_call(kernel, grid=(1,), out_shape=[jax.ShapeDtypeStruct((units,...  13 us
    pallas_call x1, Pallas kernels, bottleneck(): pl.pallas_call(kernel, out_shape=[jax.ShapeDtypeStruct((rows, chans), F32...  10.9 us
  transfers between devices with their start and end apart: 61, of which 14 were waited for; matrix products, arithmetic and copies ran while one was open for 7% of the time, Pallas kernels for 51%

profile of v5, /device:TPU:0, one launch (start us, length us, event | category | flops | bytes accessed | tf_op | source)
XLA Modules:
  0.0 371.8 jit_solution(13543799740513315374)
XLA Ops:
  0.7 3.0 halve.1
  4.6 2.5 collective-permute-start.7
  8.3 3.3 vectors.1
  11.6 2.9 cut.1
  18.7 2.9 collective-permute-start
  21.6 2.2 collective-permute-start.1
  23.8 2.6 collective-permute-start.10
  31.0 1.9 collective-permute-start.3
  33.3 7.2 %collective-permute-done.2.p3 = bf16[128,1408]{1,0:T(8,128)(2,1)} collective-permute-done((bf16[128,1408]{1,0:T(8,128)(2,1)}, bf16[128,1408]{1,0:T(8,128)(2,1)}, u32[]{:S(2)}, u32[]{:S(2)}) %collective-permute-start.2) | collective-permute-done | bytes 360480 | tf_op jit(solution)/shard_map/ppermute | solution.py:1290
  40.9 4.7 %merge_strided.1 = (f32[136,512]{1,0:T(8,128)}, f32[8,256]{1,0:T(8,128)}) custom-call(bf16[16,256,512]{2,1,0:T(8,128)(2,1)} %w_ref.5, f32[1,256]{1,0:T(1,128)} %bitcast.54, f32[1,256]{1,0:T(1,128)} %bitcast.51, bf16[8,256]{1,0:T(8,128)(2,1)} %p_ref.4), custom_call_target="tpu_custom_call" | custom-call | flops 5750000128 | tf_op jit(solution)/shard_map/merge_strided/pallas_call | solution.py:689
  47.1 5.2 %enter.1 = (f32[1280,512]{1,0:T(8,128)}, f32[32,512]{1,0:T(8,128)}, f32[8,128]{1,0:T(8,128)}, f32[8,128]{1,0:T(8,128)}) custom-call(bf16[128,1408]{1,0:T(8,128)(2,1)} %get-tuple-element.210.p0, bf16[128,1408]{1,0:T(8,128)(2,1)} %copy-done.17, bf16[128,1408]{1,0:T(8,128)(2,1)} %collective-permute-done.1.p2, bf16[128,1408]{1,0:T(8,128)(2,1)} %collective-permute-done.2.p3, ...), custom_call_target="tpu_custom_call" | custom-call | flops 115000000 | tf_op jit(solution)/shard_map/enter/pallas_call | solution.py:593
  52.4 11.7 %unit_forward_1.1 = (f32[1280,512]{1,0:T(8,128)}, f32[1280,512]{1,0:T(8,128)}, bf16[1376,512]{1,0:T(8,128)(2,1)}, bf16[512,512]{1,0:T(8,128)(2,1)}) custom-call(f32[1280,512]{1,0:T(8,128)} %get-tuple-element.220.s_ref.refs_3_, bf16[3,7,128,512]{3,2,1,0:T(8,128)(2,1)} %refs_2_.3, bf16[3,128,512]{2,1,0:T(8,128)(2,1)} %refs_3_.5, ...), custom_call_target="tpu_custom_call" | custom-call | flops 13799999488 | tf_op jit(solution)/shard_map/unit_forward_1/pallas_call | solution.py:221
  70.0 8.0 %look_up.1 = (f32[160,128]{1,0:T(8,128)}, f32[256,512]{1,0:T(8,128)}, f32[256,128]{1,0:T(8,128)}) custom-call(s32[672,128]{1,0:T(8,128)} %broadcast_in_dim.85.i_ref, f32[8,8192]{1,0:T(8,128)} %c_ref.1, bf16[256,128]{1,0:T(8,128)(2,1)} %concatenate.9.p_ref, bf16[256,512]{1,0:T(8,128)(2,1)} %t_ref.3), custom_call_target="tpu_custom_call" | custom-call | flops 115000000 | tf_op jit(solution)/shard_map/look_up/pallas_call | solution.py:731
  82.4 11.7 %unit_forward_3.1 = (f32[1280,512]{1,0:T(8,128)}, f32[1280,512]{1,0:T(8,128)}, bf16[1568,512]{1,0:T(8,128)(2,1)}, bf16[512,512]{1,0:T(8,128)(2,1)}) custom-call(f32[1280,512]{1,0:T(8,128)} %get-tuple-element.228.s_ref.refs_3_, bf16[3,7,128,512]{3,2,1,0:T(8,128)(2,1)} %refs_2_.3, bf16[3,128,512]{2,1,0:T(8,128)(2,1)} %refs_3_.5, ...), custom_call_target="tpu_custom_call" | custom-call | flops 13799999488 | tf_op jit(solution)/shard_map/unit_forward_3/pallas_call | solution.py:221
  97.2 12.3 %unit_forward_9.1 = (f32[1280,512]{1,0:T(8,128)}, f32[1280,512]{1,0:T(8,128)}, bf16[2144,512]{1,0:T(8,128)(2,1)}, bf16[512,512]{1,0:T(8,128)(2,1)}) custom-call(f32[1280,512]{1,0:T(8,128)} %get-tuple-element.235.s_ref.refs_3_, bf16[3,7,128,512]{3,2,1,0:T(8,128)(2,1)} %refs_2_.3, bf16[3,128,512]{2,1,0:T(8,128)(2,1)} %refs_3_.5, ...), custom_call_target="tpu_custom_call" | custom-call | flops 13799999488 | tf_op jit(solution)/shard_map/unit_forward_9/pallas_call | solution.py:221
  110.2 10.9 %bottleneck.1 = (f32[1280,512]{1,0:T(8,128)}, f32[160,128]{1,0:T(8,128)}, f32[160,128]{1,0:T(8,128)}, f32[16,8,512]{2,1,0:T(8,128)}, f32[8,512]{1,0:T(8,128)}) custom-call(f32[1280,512]{1,0:T(8,128)} %get-tuple-element.242.s_ref, f32[136,512]{1,0:T(8,128)} %copy-done.23, f32[136,512]{1,0:T(8,128)} %copy-done.60, f32[1,128]{1,0:T(1,128)} %pad_bitcast_fusion.bias_ref, ...), custom_call_target="tpu_custom_call" | custom-call | flops 12650000384 | tf_op jit(solution)/shard_map/bottleneck/pallas_call | solution.py:1120
  121.1 14.7 %units_back_weights_9.1 = (bf16[1280,512]{1,0:T(8,128)(2,1)}, bf16[2,8,128,512]{3,2,1,0:T(8,128)(2,1)}, bf16[2,8,128,512]{3,2,1,0:T(8,128)(2,1)}, f32[8,512]{1,0:T(8,128)}) custom-call(f32[2176,128]{1,0:T(8,128)} %broadcast_in_dim.82.refs_9_.l_ref.refs_0_, f32[32,512]{1,0:T(8,128)} %get-tuple-element.222.refs_8_.v_ref.refs_1_, ...), custom_call_target="tpu_custom_call" | custom-call | flops 39099998208 | tf_op jit(solution)/shard_map/units_back_weights_9/pallas_call | solution.py:452
  136.9 6.1 %code_payload.1 = (bf16[128,512]{1,0:T(8,128)(2,1)}, bf16[128,512]{1,0:T(8,128)(2,1)}, bf16[128,512]{1,0:T(8,128)(2,1)}, bf16[128,512]{1,0:T(8,128)(2,1)}) custom-call(f32[160,128]{1,0:T(8,128)} %get-tuple-element.252.d_ref, f32[160,128]{1,0:T(8,128)} %get-tuple-element.253.l_ref, f32[16,8,512]{2,1,0:T(8,128)} %get-tuple-element.254.m_ref, ...), custom_call_target="tpu_custom_call" | custom-call | flops 115000000 | tf_op jit(solution)/shard_map/code_payload/pallas_call | solution.py:793
  144.8 2.3 fusion
  148.1 24.3 %units_back_into_9_weights_3.1 = (f32[1280,512]{1,0:T(8,128)}, f32[8,512]{1,0:T(8,128)}, bf16[1280,512]{1,0:T(8,128)(2,1)}, bf16[2,8,128,512]{3,2,1,0:T(8,128)(2...) custom-call(f32[2176,128]{1,0:T(8,128)} %broadcast_in_dim.82.refs_9_.l_ref.refs_0_, ...), custom_call_target="tpu_custom_call" | custom-call | flops 73600000000 | tf_op jit(solution)/shard_map/units_back_into_9_weights_3/pallas_call | solution.py:452
  174.5 3.6 sum_halves.12
  181.2 24.8 %units_back_into_3_weights_1.1 = (f32[1280,512]{1,0:T(8,128)}, f32[8,512]{1,0:T(8,128)}, bf16[1280,512]{1,0:T(8,128)(2,1)}, bf16[2,8,128,512]{3,2,1,0:T(8,128)(2...) custom-call(f32[2176,128]{1,0:T(8,128)} %broadcast_in_dim.82.refs_9_.l_ref.refs_0_, ...), custom_call_target="tpu_custom_call" | custom-call | flops 73600000000 | tf_op jit(solution)/shard_map/units_back_into_3_weights_1/pallas_call | solution.py:452
  206.9 2.2 sum_halves.13
  211.7 3.3 sum_halves.14
  216.6 13.8 %units_back_into_1.1 = (f32[1280,512]{1,0:T(8,128)}, f32[16,512]{1,0:T(8,128)}) custom-call(f32[2176,128]{1,0:T(8,128)} %broadcast_in_dim.82.refs_9_.l_ref.refs_0_, f32[32,512]{1,0:T(8,128)} %get-tuple-element.222.refs_8_.v_ref.refs_1_, f32[1280,512]{1,0:T(8,128)} %get-tuple-element.293.refs_2_, f32[1280,512]{1,0:T(8,128)} %get-tuple-element.220.s_ref.refs_3_, ...), custom_call_target="tpu_custom_call" | custom-call | flops 57500000256 | tf_op jit(solution)/shard_map/units_back_into_1/pallas_call | solution.py:452
  233.8 2.2 sum_halves.16
  239.3 2.6 collective-permute-start.37
  241.9 3.5 leave.1
  245.4 3.5 collective-permute-done.37.refs_1_
  251.2 3.4 collective-permute-start.38
  264.4 3.2 sum_halves.19
  269.3 3.1 collective-permute-start.45
  272.3 6.1 %collective-permute-done.45.refs_1_ = bf16[144,512]{1,0:T(8,128)(2,1)S(1)} collective-permute-done((bf16[144,512]{1,0:T(8,128)(2,1)S(1)}, bf16[144,512]{1,0:T(8,128)(2,1)S(1)}, u32[]{:S(2)}, u32[]{:S(2)}) %collective-permute-start.45) | collective-permute-done | bytes 147488 | tf_op jit(solution)/shard_map/ppermute | solution.py:1146
  281.6 2.2 sum_halves.21
  284.5 1.9 join.7.refs_0_
  287.0 3.2 collective-permute-start.50
  290.3 1.9 collective-permute-start.47
  293.0 6.7 %collective-permute-done.48 = f32[16,512]{1,0:T(8,128)S(1)} collective-permute-done((f32[16,512]{1,0:T(8,128)S(1)}, f32[16,512]{1,0:T(8,128)S(1)}, u32[]{:S(2)}, u32[]{:S(2)}) %collective-permute-start.48) | collective-permute-done | bytes 32800 | tf_op jit(solution)/shard_map/ppermute | solution.py:1146
  299.7 3.1 collective-permute-start.49
  310.2 3.5 collective-permute-done.53.refs_1_
  319.6 4.5 %strided_meet.1 = (f32[16,256]{1,0:T(8,128)}, f32[256,128]{1,0:T(8,128)}) custom-call(bf16[16,256,512]{2,1,0:T(8,128)(2,1)} %w_ref.5, bf16[16,8,512]{2,1,0:T(8,128)(2,1)} %slice_bitcast_fusion.m_ref, bf16[8,256]{1,0:T(8,128)(2,1)} %p_ref.4, f32[8,256]{1,0:T(8,128)} %get-tuple-element.343.n_ref), custom_call_target="tpu_custom_call" | custom-call | flops 115000000 | tf_op jit(solution)/shard_map/strided_meet/pallas_call | solution.py:831
  327.6 1.9 join.10.refs_0_
  330.2 3.5 collective-permute-start.58
  338.7 4.3 %norm_back.3 = (f32[3,7,128,512]{3,2,1,0:T(8,128)}, f32[3,128,512]{2,1,0:T(8,128)}, f32[1,128]{1,0:T(1,128)}, f32[1,128]{1,0:T(1,128)}) custom-call(bf16[576,512]{1,0:T(8,128)(2,1)} %join.7.refs_0_, bf16[576,512]{1,0:T(8,128)(2,1)} %copy-done.9, bf16[3,7,128,512]{3,2,1,0:T(8,128)(2,1)} %refs_2_.3, bf16[3,128,512]{2,1,0:T(8,128)(2,1)} %refs_3_.5, ...), custom_call_target="tpu_custom_call" | custom-call | flops 115000000 | tf_op jit(solution)/shard_map/norm_back/pallas_call | solution.py:941
  344.0 2.7 settle.1
  353.1 6.7 %strided_back.1 = f32[16,256,512]{2,1,0:T(8,128)} custom-call(bf16[16,256,512]{2,1,0:T(8,128)(2,1)} %w_ref.5, bf16[16,8,512]{2,1,0:T(8,128)(2,1)} %slice_bitcast_fusion.m_ref, bf16[8,256]{1,0:T(8,128)(2,1)} %p_ref.4, f32[8,256]{1,0:T(8,128)} %get-tuple-element.343.n_ref, f32[256,128]{1,0:T(8,128)} %get-tuple-element.357.f_ref), custom_call_target="tpu_custom_call" | custom-call | flops 115000000 | tf_op jit(solution)/shard_map/strided_back/pallas_call | solution.py:863
  361.3 4.3 %norm_back.4 = (f32[3,7,128,512]{3,2,1,0:T(8,128)}, f32[3,128,512]{2,1,0:T(8,128)}, f32[1,128]{1,0:T(1,128)}, f32[1,128]{1,0:T(1,128)}) custom-call(bf16[576,512]{1,0:T(8,128)(2,1)} %join.10.refs_0_, bf16[576,512]{1,0:T(8,128)(2,1)} %copy-done.10, bf16[3,7,128,512]{3,2,1,0:T(8,128)(2,1)} %refs_2_.3, ...), custom_call_target="tpu_custom_call", output_to_operand_aliasing={{0}: (5, {}), {1}: (6, {})} | custom-call | flops 115000000 | tf_op jit(solution)/shard_map/norm_back/pallas_call | solution.py:941
  367.2 4.3 %norm_back.5 = (f32[3,7,128,512]{3,2,1,0:T(8,128)}, f32[3,128,512]{2,1,0:T(8,128)}, f32[3,128]{1,0:T(4,128)}, f32[3,128]{1,0:T(4,128)}) custom-call(bf16[512,512]{1,0:T(8,128)(2,1)} %join.11.refs_0_, bf16[512,512]{1,0:T(8,128)(2,1)} %copy-done.15, bf16[3,7,128,512]{3,2,1,0:T(8,128)(2,1)} %refs_2_.3, ...), custom_call_target="tpu_custom_call", output_to_operand_aliasing={{0}: (5, {}), {1}: (6, {})} | custom-call | flops 115000000 | tf_op jit(solution)/shard_map/norm_back/pallas_call | solution.py:941
  (338 shorter events, 99.6 us)
Async XLA Ops:
  4.1 48.2 %collective-permute-start.8 = (bf16[3,7,128,512]{3,2,1,0:T(8,128)(2,1)S(1)}, bf16[3,7,128,512]{3,2,1,0:T(8,128)(2,1)}, u32[]{:S(2)}, u32[]{:S(2)}) collective-permute-start(bf16[3,7,128,512]{3,2,1,0:T(8,128)(2,1)S(1)} %copy-done), channel_id=1, source_target_pairs={{0,1},{1,0},{2,3},{3,2},{4,5},{5,4},{6,7},{7,6},{8,9},{9,8},{10,11... | collective-permute-start | bytes 8257544 | tf_op jit(solution)/shard_map/ppermute | solution.py:1146
  4.6 19.2 %collective-permute-start.7 = (bf16[4,128,512]{2,1,0:T(8,128)(2,1)}, bf16[4,128,512]{2,1,0:T(8,128)(2,1)}, u32[]{:S(2)}, u32[]{:S(2)}) collective-permute-start(bf16[4,128,512]{2,1,0:T(8,128)(2,1)} %get-tuple-element.196), channel_id=1, source_target_pairs={{0,2},{1,3},{2,0},{3,1},{4,6},{5,7},{6,4},{7,5},{8,10},{9,11},{10,... | collective-permute-start | bytes 1572872 | tf_op jit(solution)/shard_map/ppermute | solution.py:1146
  18.7 12.3 %collective-permute-start = (bf16[128,1408]{1,0:T(8,128)(2,1)}, bf16[128,1408]{1,0:T(8,128)(2,1)S(1)}, u32[]{:S(2)}, u32[]{:S(2)}) collective-permute-start(bf16[128,1408]{1,0:T(8,128)(2,1)} %get-tuple-element.201), channel_id=1, source_target_pairs={{0,1},{1,0},{2,3},{3,2},{4,5},{5,4},{6,7},{7,6},{8,9},{9,8},{10,11... | collective-permute-start | bytes 1081352 | tf_op jit(solution)/shard_map/ppermute | solution.py:1290
  21.6 11.7 %collective-permute-start.1 = (bf16[128,1408]{1,0:T(8,128)(2,1)}, bf16[128,1408]{1,0:T(8,128)(2,1)}, u32[]{:S(2)}, u32[]{:S(2)}) collective-permute-start(bf16[128,1408]{1,0:T(8,128)(2,1)} %get-tuple-element.202), channel_id=1, source_target_pairs={{0,2},{1,3},{2,0},{3,1},{4,6},{5,7},{6,4},{7,5},{8,10},{9,11},{10,... | collective-permute-start | bytes 1081352 | tf_op jit(solution)/shard_map/ppermute | solution.py:1290
  23.8 16.7 %collective-permute-start.2 = (bf16[128,1408]{1,0:T(8,128)(2,1)}, bf16[128,1408]{1,0:T(8,128)(2,1)}, u32[]{:S(2)}, u32[]{:S(2)}) collective-permute-start(bf16[128,1408]{1,0:T(8,128)(2,1)} %get-tuple-element.203), channel_id=1, source_target_pairs={{0,3},{1,2},{2,1},{3,0},{4,7},{5,6},{6,5},{7,4},{8,11},{9,10},{10,... | collective-permute-start | bytes 1081352 | tf_op jit(solution)/shard_map/ppermute | solution.py:1290
  23.8 16.7 %collective-permute-start.10 = (bf16[4,128,512]{2,1,0:T(8,128)(2,1)}, bf16[4,128,512]{2,1,0:T(8,128)(2,1)}, u32[]{:S(2)}, u32[]{:S(2)}) collective-permute-start(bf16[4,128,512]{2,1,0:T(8,128)(2,1)} %collective-permute-done.7.refs_4_.refs_9_), channel_id=1, source_target_pairs={{0,4},{4,0},{8,12},{12,8},{16,20},{20,16},{24,28},{28,24},{1,5},{5... | collective-permute-start | bytes 1572872 | tf_op jit(solution)/shard_map/ppermute | solution.py:1146
  31.0 14.6 %collective-permute-start.3 = (bf16[144,128]{1,0:T(8,128)(2,1)}, bf16[144,128]{1,0:T(8,128)(2,1)S(1)}, u32[]{:S(2)}, u32[]{:S(2)}) collective-permute-start(bf16[144,128]{1,0:T(8,128)(2,1)} %get-tuple-element.204), channel_id=1, source_target_pairs={{7,3},{11,7},{15,11},{19,15},{23,19},{27,23},{31,27},{0,4},{4,8},{... | collective-permute-start | bytes 110600 | tf_op jit(solution)/shard_map/ppermute | solution.py:1349
  33.2 19.0 %collective-permute-start.9 = (bf16[3,128,512]{2,1,0:T(8,128)(2,1)S(1)}, bf16[3,128,512]{2,1,0:T(8,128)(2,1)}, u32[]{:S(2)}, u32[]{:S(2)}) collective-permute-start(bf16[3,128,512]{2,1,0:T(8,128)(2,1)S(1)} %copy-done.1), channel_id=1, source_target_pairs={{0,1},{1,0},{2,3},{3,2},{4,5},{5,4},{6,7},{7,6},{8,9},{9,8},{10,11... | collective-permute-start | bytes 1179656 | tf_op jit(solution)/shard_map/ppermute | solution.py:1146
  40.4 11.9 %collective-permute-start.11 = (bf16[4,128,512]{2,1,0:T(8,128)(2,1)}, bf16[4,128,512]{2,1,0:T(8,128)(2,1)}, u32[]{:S(2)}, u32[]{:S(2)}) collective-permute-start(bf16[4,128,512]{2,1,0:T(8,128)(2,1)} %collective-permute-done.7.refs_4_.refs_9_), channel_id=1, source_target_pairs={{0,1},{1,0},{2,3},{3,2},{4,5},{5,4},{6,7},{7,6},{8,9},{9,8},{10,11... | collective-permute-start | bytes 1572872 | tf_op jit(solution)/shard_map/ppermute | solution.py:1146
  40.5 11.8 %collective-permute-start.12 = (bf16[4,128,512]{2,1,0:T(8,128)(2,1)}, bf16[4,128,512]{2,1,0:T(8,128)(2,1)}, u32[]{:S(2)}, u32[]{:S(2)}) collective-permute-start(bf16[4,128,512]{2,1,0:T(8,128)(2,1)} %collective-permute-done.10.refs_5_.refs_10_), channel_id=1, source_target_pairs={{0,1},{1,0},{2,3},{3,2},{4,5},{5,4},{6,7},{7,6},{8,9},{9,8},{10,11... | collective-permute-start | bytes 1572872 | tf_op jit(solution)/shard_map/ppermute | solution.py:1146
  45.6 18.5 %collective-permute-start.13 = (bf16[4,128,512]{2,1,0:T(8,128)(2,1)}, bf16[4,128,512]{2,1,0:T(8,128)(2,1)}, u32[]{:S(2)}, u32[]{:S(2)}) collective-permute-start(bf16[4,128,512]{2,1,0:T(8,128)(2,1)} %get-tuple-element.230), channel_id=1, source_target_pairs={{0,2},{1,3},{2,0},{3,1},{4,6},{5,7},{6,4},{7,5},{8,10},{9,11},{10,... | collective-permute-start | bytes 1572872 | tf_op jit(solution)/shard_map/ppermute | solution.py:1146
  64.1 14.0 %collective-permute-start.14 = (bf16[4,128,512]{2,1,0:T(8,128)(2,1)}, bf16[4,128,512]{2,1,0:T(8,128)(2,1)S(1)}, u32[]{:S(2)}, u32[]{:S(2)}) collective-permute-start(bf16[4,128,512]{2,1,0:T(8,128)(2,1)} %collective-permute-done.13.refs_4_.refs_9_), channel_id=1, source_target_pairs={{0,4},{4,0},{8,12},{12,8},{16,20},{20,16},{24,28},{28,24},{1,5},{5... | collective-permute-start | bytes 1572872 | tf_op jit(solution)/shard_map/ppermute | solution.py:1146
  66.2 13.4 %collective-permute-start.18 = (bf16[4,128,512]{2,1,0:T(8,128)(2,1)S(1)}, bf16[4,128,512]{2,1,0:T(8,128)(2,1)S(1)}, u32[]{:S(2)}, u32[]{:S(2)}) collective-permute-start(bf16[4,128,512]{2,1,0:T(8,128)(2,1)S(1)} %copy-done.51), channel_id=1, source_target_pairs={{0,2},{1,3},{2,0},{3,1},{4,6},{5,7},{6,4},{7,5},{8,10},{9,11},{10,... | collective-permute-start | bytes 1572872 | tf_op jit(solution)/shard_map/ppermute | solution.py:1146
  66.5 11.6 %collective-permute-start.16 = (f32[136,512]{1,0:T(8,128)S(1)}, f32[136,512]{1,0:T(8,128)S(1)}, u32[]{:S(2)}, u32[]{:S(2)}) collective-permute-start(f32[136,512]{1,0:T(8,128)S(1)} %copy-done.22), channel_id=1, source_target_pairs={{0,1},{1,0},{2,3},{3,2},{4,5},{5,4},{6,7},{7,6},{8,9},{9,8},{10,11... | collective-permute-start | bytes 835592 | tf_op jit(solution)/shard_map/ppermute | solution.py:1146
  68.2 12.7 %collective-permute-start.15 = (bf16[4,128,512]{2,1,0:T(8,128)(2,1)}, bf16[4,128,512]{2,1,0:T(8,128)(2,1)S(1)}, u32[]{:S(2)}, u32[]{:S(2)}) collective-permute-start(bf16[4,128,512]{2,1,0:T(8,128)(2,1)} %collective-permute-done.13.refs_4_.refs_9_), channel_id=1, source_target_pairs={{0,1},{1,0},{2,3},{3,2},{4,5},{5,4},{6,7},{7,6},{8,9},{9,8},{10,11... | collective-permute-start | bytes 1572872 | tf_op jit(solution)/shard_map/ppermute | solution.py:1146
  79.6 14.5 %collective-permute-start.19 = (bf16[4,128,512]{2,1,0:T(8,128)(2,1)S(1)}, bf16[4,128,512]{2,1,0:T(8,128)(2,1)S(1)}, u32[]{:S(2)}, u32[]{:S(2)}) collective-permute-start(bf16[4,128,512]{2,1,0:T(8,128)(2,1)S(1)} %copy-done.50), channel_id=1, source_target_pairs={{0,2},{1,3},{2,0},{3,1},{4,6},{5,7},{6,4},{7,5},{8,10},{9,11},{10,... | collective-permute-start | bytes 1572872 | tf_op jit(solution)/shard_map/ppermute | solution.py:1146
  80.8 14.7 %collective-permute-start.20 = (bf16[4,128,512]{2,1,0:T(8,128)(2,1)S(1)}, bf16[4,128,512]{2,1,0:T(8,128)(2,1)S(1)}, u32[]{:S(2)}, u32[]{:S(2)}) collective-permute-start(bf16[4,128,512]{2,1,0:T(8,128)(2,1)S(1)} %collective-permute-done.18.refs_4_.refs_9_), channel_id=1, source_target_pairs={{0,1},{1,0},{2,3},{3,2},{4,5},{5,4},{6,7},{7,6},{8,9},{9,8},{10,11... | collective-permute-start | bytes 1572872 | tf_op jit(solution)/shard_map/ppermute | solution.py:1146
  94.7 14.8 %collective-permute-start.22 = (f32[136,512]{1,0:T(8,128)S(1)}, f32[136,512]{1,0:T(8,128)S(1)}, u32[]{:S(2)}, u32[]{:S(2)}) collective-permute-start(f32[136,512]{1,0:T(8,128)S(1)} %add.187.wa_ref), channel_id=1, source_target_pairs={{0,2},{1,3},{2,0},{3,1},{4,6},{5,7},{6,4},{7,5},{8,10},{9,11},{10,... | collective-permute-start | bytes 835592 | tf_op jit(solution)/shard_map/ppermute | solution.py:1146
  142.9 30.0 %collective-permute-start.26 = (bf16[128,512]{1,0:T(8,128)(2,1)}, bf16[128,512]{1,0:T(8,128)(2,1)S(1)}, u32[]{:S(2)}, u32[]{:S(2)}) collective-permute-start(bf16[128,512]{1,0:T(8,128)(2,1)} %get-tuple-element.269), channel_id=1, source_target_pairs={{0,1},{1,0},{2,3},{3,2},{4,5},{5,4},{6,7},{7,6},{8,9},{9,8},{10,11... | collective-permute-start | bytes 393224 | tf_op jit(solution)/shard_map/ppermute | solution.py:1290
  143.2 29.8 %collective-permute-start.27 = (bf16[128,512]{1,0:T(8,128)(2,1)}, bf16[128,512]{1,0:T(8,128)(2,1)S(1)}, u32[]{:S(2)}, u32[]{:S(2)}) collective-permute-start(bf16[128,512]{1,0:T(8,128)(2,1)} %get-tuple-element.270), channel_id=1, source_target_pairs={{0,2},{1,3},{2,0},{3,1},{4,6},{5,7},{6,4},{7,5},{8,10},{9,11},{10,... | collective-permute-start | bytes 393224 | tf_op jit(solution)/shard_map/ppermute | solution.py:1290
  144.4 28.6 %collective-permute-start.28 = (bf16[128,512]{1,0:T(8,128)(2,1)}, bf16[128,512]{1,0:T(8,128)(2,1)S(1)}, u32[]{:S(2)}, u32[]{:S(2)}) collective-permute-start(bf16[128,512]{1,0:T(8,128)(2,1)} %get-tuple-element.271), channel_id=1, source_target_pairs={{0,3},{1,2},{2,1},{3,0},{4,7},{5,6},{6,5},{7,4},{8,11},{9,10},{10,... | collective-permute-start | bytes 393224 | tf_op jit(solution)/shard_map/ppermute | solution.py:1290
  147.1 27.3 %collective-permute-start.25 = (bf16[8,128,512]{2,1,0:T(8,128)(2,1)S(1)}, bf16[8,128,512]{2,1,0:T(8,128)(2,1)}, u32[]{:S(2)}, u32[]{:S(2)}) collective-permute-start(bf16[8,128,512]{2,1,0:T(8,128)(2,1)S(1)} %fusion), channel_id=1, source_target_pairs={{0,2},{1,3},{2,0},{3,1},{4,6},{5,7},{6,4},{7,5},{8,10},{9,11},{10,... | collective-permute-start | bytes 3145736 | tf_op jit(solution)/shard_map/ppermute | solution.py:1146
  178.1 28.0 %collective-permute-start.30 = (bf16[576,512]{1,0:T(8,128)(2,1)}, bf16[576,512]{1,0:T(8,128)(2,1)S(1)}, u32[]{:S(2)}, u32[]{:S(2)}) collective-permute-start(bf16[576,512]{1,0:T(8,128)(2,1)} %get-tuple-element.278), channel_id=1, source_target_pairs={{0,4},{4,0},{8,12},{12,8},{16,20},{20,16},{24,28},{28,24},{1,5},{5... | collective-permute-start | bytes 1769480 | tf_op jit(solution)/shard_map/ppermute | solution.py:1146
  180.2 30.6 %collective-permute-start.29 = (bf16[8,128,512]{2,1,0:T(8,128)(2,1)S(1)}, bf16[8,128,512]{2,1,0:T(8,128)(2,1)S(1)}, u32[]{:S(2)}, u32[]{:S(2)}) collective-permute-start(bf16[8,128,512]{2,1,0:T(8,128)(2,1)S(1)} %fusion.1), channel_id=1, source_target_pairs={{0,2},{1,3},{2,0},{3,1},{4,6},{5,7},{6,4},{7,5},{8,10},{9,11},{10,... | collective-permute-start | bytes 3145736 | tf_op jit(solution)/shard_map/ppermute | solution.py:1146
  209.1 21.3 %collective-permute-start.33 = (bf16[288,512]{1,0:T(8,128)(2,1)}, bf16[288,512]{1,0:T(8,128)(2,1)S(1)}, u32[]{:S(2)}, u32[]{:S(2)}) collective-permute-start(bf16[288,512]{1,0:T(8,128)(2,1)} %get-tuple-element.289), channel_id=1, source_target_pairs={{0,8},{4,12},{8,0},{12,4},{16,24},{20,28},{24,16},{28,20},{1,9},{5... | collective-permute-start | bytes 884744 | tf_op jit(solution)/shard_map/ppermute | solution.py:1146
  210.8 25.3 %collective-permute-start.31 = (bf16[2,8,128,512]{3,2,1,0:T(8,128)(2,1)}, bf16[2,8,128,512]{3,2,1,0:T(8,128)(2,1)}, u32[]{:S(2)}, u32[]{:S(2)}) collective-permute-start(bf16[2,8,128,512]{3,2,1,0:T(8,128)(2,1)} %get-tuple-element.300), channel_id=1, source_target_pairs={{0,1},{1,0},{2,3},{3,2},{4,5},{5,4},{6,7},{7,6},{8,9},{9,8},{10,11... | collective-permute-start | bytes 6291464 | tf_op jit(solution)/shard_map/ppermute | solution.py:1146
  215.0 18.0 %collective-permute-start.32 = (bf16[576,512]{1,0:T(8,128)(2,1)}, bf16[576,512]{1,0:T(8,128)(2,1)S(1)}, u32[]{:S(2)}, u32[]{:S(2)}) collective-permute-start(bf16[576,512]{1,0:T(8,128)(2,1)} %get-tuple-element.292), channel_id=1, source_target_pairs={{0,4},{4,0},{8,12},{12,8},{16,20},{20,16},{24,28},{28,24},{1,5},{5... | collective-permute-start | bytes 1769480 | tf_op jit(solution)/shard_map/ppermute | solution.py:1146
  237.7 25.7 %collective-permute-start.43 = (bf16[8,128,512]{2,1,0:T(8,128)(2,1)S(1)}, bf16[8,128,512]{2,1,0:T(8,128)(2,1)S(1)}, u32[]{:S(2)}, u32[]{:S(2)}) collective-permute-start(bf16[8,128,512]{2,1,0:T(8,128)(2,1)S(1)} %fusion.2), channel_id=1, source_target_pairs={{0,2},{1,3},{2,0},{3,1},{4,6},{5,7},{6,4},{7,5},{8,10},{9,11},{10,... | collective-permute-start | bytes 3145736 | tf_op jit(solution)/shard_map/ppermute | solution.py:1146
  238.9 17.4 %collective-permute-start.41 = (bf16[288,512]{1,0:T(8,128)(2,1)S(1)}, bf16[288,512]{1,0:T(8,128)(2,1)S(1)}, u32[]{:S(2)}, u32[]{:S(2)}) collective-permute-start(bf16[288,512]{1,0:T(8,128)(2,1)S(1)} %copy-done.59), channel_id=1, source_target_pairs={{0,8},{4,12},{8,0},{12,4},{16,24},{20,28},{24,16},{28,20},{1,9},{5... | collective-permute-start | bytes 884744 | tf_op jit(solution)/shard_map/ppermute | solution.py:1146
  239.3 9.5 %collective-permute-start.37 = (bf16[144,512]{1,0:T(8,128)(2,1)S(1)}, bf16[144,512]{1,0:T(8,128)(2,1)S(1)}, u32[]{:S(2)}, u32[]{:S(2)}) collective-permute-start(bf16[144,512]{1,0:T(8,128)(2,1)S(1)} %copy-done.64), channel_id=1, source_target_pairs={{0,16},{4,20},{8,24},{12,28},{16,0},{20,4},{24,8},{28,12},{1,17},{... | collective-permute-start | bytes 442376 | tf_op jit(solution)/shard_map/ppermute | solution.py:1146
  251.2 9.9 %collective-permute-start.38 = (bf16[144,512]{1,0:T(8,128)(2,1)}, bf16[144,512]{1,0:T(8,128)(2,1)S(1)}, u32[]{:S(2)}, u32[]{:S(2)}) collective-permute-start(bf16[144,512]{1,0:T(8,128)(2,1)} %sum_halves.17.m_ref), channel_id=1, source_target_pairs={{0,16},{4,20},{8,24},{12,28},{16,0},{20,4},{24,8},{28,12},{1,17},{... | collective-permute-start | bytes 442376 | tf_op jit(solution)/shard_map/ppermute | solution.py:1146
  267.7 13.1 %collective-permute-start.44 = (bf16[512,512]{1,0:T(8,128)(2,1)}, bf16[512,512]{1,0:T(8,128)(2,1)S(1)}, u32[]{:S(2)}, u32[]{:S(2)}) collective-permute-start(bf16[512,512]{1,0:T(8,128)(2,1)} %get-tuple-element.324), channel_id=1, source_target_pairs={{0,4},{4,0},{8,12},{12,8},{16,20},{20,16},{24,28},{28,24},{1,5},{5... | collective-permute-start | bytes 1572872 | tf_op jit(solution)/shard_map/ppermute | solution.py:1146
  267.8 15.9 %collective-permute-start.42 = (bf16[288,512]{1,0:T(8,128)(2,1)S(1)}, bf16[288,512]{1,0:T(8,128)(2,1)S(1)}, u32[]{:S(2)}, u32[]{:S(2)}) collective-permute-start(bf16[288,512]{1,0:T(8,128)(2,1)S(1)} %copy-done.6), channel_id=1, source_target_pairs={{0,8},{4,12},{8,0},{12,4},{16,24},{20,28},{24,16},{28,20},{1,9},{5... | collective-permute-start | bytes 884744 | tf_op jit(solution)/shard_map/ppermute | solution.py:1146
  286.4 19.0 %collective-permute-start.46 = (bf16[576,512]{1,0:T(8,128)(2,1)}, bf16[576,512]{1,0:T(8,128)(2,1)S(1)}, u32[]{:S(2)}, u32[]{:S(2)}) collective-permute-start(bf16[576,512]{1,0:T(8,128)(2,1)} %join.7.refs_0_), channel_id=1, source_target_pairs={{0,4},{4,0},{8,12},{12,8},{16,20},{20,16},{24,28},{28,24},{1,5},{5... | collective-permute-start | bytes 1769480 | tf_op jit(solution)/shard_map/ppermute | solution.py:1146
  287.0 12.7 %collective-permute-start.50 = (bf16[144,512]{1,0:T(8,128)(2,1)S(1)}, bf16[144,512]{1,0:T(8,128)(2,1)S(1)}, u32[]{:S(2)}, u32[]{:S(2)}) collective-permute-start(bf16[144,512]{1,0:T(8,128)(2,1)S(1)} %copy-done.13), channel_id=1, source_target_pairs={{0,16},{4,20},{8,24},{12,28},{16,0},{20,4},{24,8},{28,12},{1,17},{... | collective-permute-start | bytes 442376 | tf_op jit(solution)/shard_map/ppermute | solution.py:1146
  290.3 12.5 %collective-permute-start.47 = (bf16[256,512]{1,0:T(8,128)(2,1)}, bf16[256,512]{1,0:T(8,128)(2,1)S(1)}, u32[]{:S(2)}, u32[]{:S(2)}) collective-permute-start(bf16[256,512]{1,0:T(8,128)(2,1)} %get-tuple-element.328), channel_id=1, source_target_pairs={{0,8},{4,12},{8,0},{12,4},{16,24},{20,28},{24,16},{28,20},{1,9},{5... | collective-permute-start | bytes 786440 | tf_op jit(solution)/shard_map/ppermute | solution.py:1146
  299.7 10.4 %collective-permute-start.49 = (f32[16,512]{1,0:T(8,128)S(1)}, f32[16,512]{1,0:T(8,128)S(1)}, u32[]{:S(2)}, u32[]{:S(2)}) collective-permute-start(f32[16,512]{1,0:T(8,128)S(1)} %add.193), channel_id=1, source_target_pairs={{0,16},{4,20},{8,24},{12,28},{16,0},{20,4},{24,8},{28,12},{1,17},{... | collective-permute-start | bytes 98312 | tf_op jit(solution)/shard_map/ppermute | solution.py:1146
  306.5 9.6 %collective-permute-start.57 = (bf16[128,512]{1,0:T(8,128)(2,1)S(1)}, bf16[128,512]{1,0:T(8,128)(2,1)S(1)}, u32[]{:S(2)}, u32[]{:S(2)}) collective-permute-start(bf16[128,512]{1,0:T(8,128)(2,1)S(1)} %slice_select_fusion), channel_id=1, source_target_pairs={{0,3},{1,2},{2,1},{3,0},{4,7},{5,6},{6,5},{7,4},{8,11},{9,10},{10,... | collective-permute-start | bytes 393224 | tf_op jit(solution)/shard_map/ppermute | solution.py:1290
  306.6 9.6 %collective-permute-start.56 = (bf16[128,512]{1,0:T(8,128)(2,1)S(1)}, bf16[128,512]{1,0:T(8,128)(2,1)S(1)}, u32[]{:S(2)}, u32[]{:S(2)}) collective-permute-start(bf16[128,512]{1,0:T(8,128)(2,1)S(1)} %slice_select_fusion), channel_id=1, source_target_pairs={{0,2},{1,3},{2,0},{3,1},{4,6},{5,7},{6,4},{7,5},{8,10},{9,11},{10,... | collective-permute-start | bytes 393224 | tf_op jit(solution)/shard_map/ppermute | solution.py:1290
  307.4 10.1 %collective-permute-start.55 = (bf16[128,512]{1,0:T(8,128)(2,1)S(1)}, bf16[128,512]{1,0:T(8,128)(2,1)S(1)}, u32[]{:S(2)}, u32[]{:S(2)}) collective-permute-start(bf16[128,512]{1,0:T(8,128)(2,1)S(1)} %slice_select_fusion), channel_id=1, source_target_pairs={{0,1},{1,0},{2,3},{3,2},{4,5},{5,4},{6,7},{7,6},{8,9},{9,8},{10,11... | collective-permute-start | bytes 393224 | tf_op jit(solution)/shard_map/ppermute | solution.py:1290
  310.2 33.0 %collective-permute-start.34 = (bf16[128,1024]{1,0:T(8,128)(2,1)S(1)}, bf16[128,1024]{1,0:T(8,128)(2,1)S(1)}, u32[]{:S(2)}, u32[]{:S(2)}) collective-permute-start(bf16[128,1024]{1,0:T(8,128)(2,1)S(1)} %copy-done.63), channel_id=1, source_target_pairs={{0,1},{1,0},{2,3},{3,2},{4,5},{5,4},{6,7},{7,6},{8,9},{9,8},{10,11... | collective-permute-start | bytes 786440 | tf_op jit(solution)/shard_map/ppermute | solution.py:1290
  313.6 29.5 %collective-permute-start.35 = (bf16[128,1024]{1,0:T(8,128)(2,1)S(1)}, bf16[128,1024]{1,0:T(8,128)(2,1)S(1)}, u32[]{:S(2)}, u32[]{:S(2)}) collective-permute-start(bf16[128,1024]{1,0:T(8,128)(2,1)S(1)} %copy-done.62), channel_id=1, source_target_pairs={{0,2},{1,3},{2,0},{3,1},{4,6},{5,7},{6,4},{7,5},{8,10},{9,11},{10,... | collective-permute-start | bytes 786440 | tf_op jit(solution)/shard_map/ppermute | solution.py:1290
  316.1 10.9 %collective-permute-start.52 = (bf16[288,512]{1,0:T(8,128)(2,1)}, bf16[288,512]{1,0:T(8,128)(2,1)S(1)}, u32[]{:S(2)}, u32[]{:S(2)}) collective-permute-start(bf16[288,512]{1,0:T(8,128)(2,1)} %join.8.m_ref), channel_id=1, source_target_pairs={{0,8},{4,12},{8,0},{12,4},{16,24},{20,28},{24,16},{28,20},{1,9},{5... | collective-permute-start | bytes 884744 | tf_op jit(solution)/shard_map/ppermute | solution.py:1146
  316.2 13.4 %collective-permute-start.51 = (f32[16,512]{1,0:T(8,128)S(1)}, f32[16,512]{1,0:T(8,128)S(1)}, u32[]{:S(2)}, u32[]{:S(2)}) collective-permute-start(f32[16,512]{1,0:T(8,128)S(1)} %add.194), channel_id=1, source_target_pairs={{0,2},{1,3},{2,0},{3,1},{4,6},{5,7},{6,4},{7,5},{8,10},{9,11},{10,... | collective-permute-start | bytes 98312 | tf_op jit(solution)/shard_map/ppermute | solution.py:1146
  324.6 18.6 %collective-permute-start.36 = (bf16[128,1024]{1,0:T(8,128)(2,1)S(1)}, bf16[128,1024]{1,0:T(8,128)(2,1)S(1)}, u32[]{:S(2)}, u32[]{:S(2)}) collective-permute-start(bf16[128,1024]{1,0:T(8,128)(2,1)S(1)} %copy-done.61), channel_id=1, source_target_pairs={{0,3},{1,2},{2,1},{3,0},{4,7},{5,6},{6,5},{7,4},{8,11},{9,10},{10,... | collective-permute-start | bytes 786440 | tf_op jit(solution)/shard_map/ppermute | solution.py:1290
  330.2 17.8 %collective-permute-start.58 = (bf16[256,512]{1,0:T(8,128)(2,1)}, bf16[256,512]{1,0:T(8,128)(2,1)S(1)}, u32[]{:S(2)}, u32[]{:S(2)}) collective-permute-start(bf16[256,512]{1,0:T(8,128)(2,1)} %join.9.m_ref), channel_id=1, source_target_pairs={{0,8},{4,12},{8,0},{12,4},{16,24},{20,28},{24,16},{28,20},{1,9},{5... | collective-permute-start | bytes 786440 | tf_op jit(solution)/shard_map/ppermute | solution.py:1146
  333.6 26.2 %collective-permute-start.60 = (bf16[576,512]{1,0:T(8,128)(2,1)}, bf16[576,512]{1,0:T(8,128)(2,1)S(1)}, u32[]{:S(2)}, u32[]{:S(2)}) collective-permute-start(bf16[576,512]{1,0:T(8,128)(2,1)} %join.10.refs_0_), channel_id=1, source_target_pairs={{0,4},{4,0},{8,12},{12,8},{16,20},{20,16},{24,28},{28,24},{1,5},{5... | collective-permute-start | bytes 1769480 | tf_op jit(solution)/shard_map/ppermute | solution.py:1146
  351.6 14.8 %collective-permute-start.59 = (bf16[512,512]{1,0:T(8,128)(2,1)S(1)}, bf16[512,512]{1,0:T(8,128)(2,1)S(1)}, u32[]{:S(2)}, u32[]{:S(2)}) collective-permute-start(bf16[512,512]{1,0:T(8,128)(2,1)S(1)} %copy-done.5), channel_id=1, source_target_pairs={{0,4},{4,0},{8,12},{12,8},{16,20},{20,16},{24,28},{28,24},{1,5},{5... | collective-permute-start | bytes 1572872 | tf_op jit(solution)/shard_map/ppermute | solution.py:1146
  (85 other events, 598.5 us)
